TPU v7x, 256 devices: a whole 4x4x8 slice. The times are simulated.
256 devices in a mesh: band: 128 (over z, x, y), mp: 2 (over core).
Axes of the slice: x: 4, y: 4, z: 8, core: 2. Of those that a mesh axis runs over, the one named last changes fastest.
Arguments:
- grid: bfloat16 [163840, 512], P('band', 'mp'), may hold values from -6 to 6
- interp: bfloat16 [1280, 4, 128, 128], P('band'), may hold values from -0.5 to 0.5
- mesh_init: bfloat16 [32768, 512], P('band', 'mp'), may hold values from -6 to 6
- w_enc: bfloat16 [512, 512], P(None, 'mp'), may hold values from -0.25 to 0.25
- w_dec: bfloat16 [512, 512], P(None, 'mp'), may hold values from -0.25 to 0.25
- cotangent: bfloat16 [163840, 512], P('band', 'mp'), may hold values from -6 to 6
- pair_mesh: int32 [1280, 4], P('band'), may hold values from 0 to 255, as said below
- pair_count: int32 [1280], P('band'), may hold values from 2 to 4, as said below
Outputs:
- grid_out: bfloat16 [163840, 512], P('band', 'mp')
- grad_enc: float32 [512, 512], P(None, 'mp')
- grad_dec: float32 [512, 512], P(None, 'mp')
Inputs may be any that keep to these rules, and one draw needn't show every extreme that they name: The owner of mesh block pair_mesh[b, k], device pair_mesh[b, k] // 2 of band, lies at most 2 devices from grid block b's device b // 10; in every band some slot reaches 2 devices up and some 2 devices down, where such devices exist. Slots k < pair_count[b] of grid block b are used, the others are not.
All inputs are finite; a program needn't handle non-finite values.
Results may differ from a plain program's by a relative error of at most 0.0075.
Values may be sent and summed in bfloat16 or wider, within the bound.
No kernel may reach another device: no remote copies, remote signals or barrier semaphores. Data moves between devices by JAX's collectives and lax.ppermute only.
A program may use at most 128 MiB of HBM per device.

v0:
```python
import jax
import jax.numpy as jnp
from jax import lax
from jax.sharding import PartitionSpec as P

REACH = 2


def shifted(value, axis, steps):
    count = lax.axis_size(axis)
    first, last = (max(0, -steps), min(count, count - steps))
    return lax.ppermute(value, axis, [(source, source + steps) for source in range(first, last)])


def silu_slope(pre, sig):
    return sig * (1.0 + pre * (1.0 - sig))


def local(grid, interp, mesh_init, w_enc, w_dec, cotangent, pair_mesh, pair_count):
    fl = jnp.float32
    blocks, pair_slots, mesh_rows, block_rows = interp.shape
    half_width = grid.shape[1]
    full_width = w_enc.shape[0]
    count_pairs = blocks * pair_slots
    reach_devs = REACH
    slab_count = 2 * reach_devs + 1
    owner_rows = mesh_init.shape[0]
    owner_blocks = owner_rows // mesh_rows
    slot_total = slab_count * owner_blocks
    offsets = [offset for offset in range(-reach_devs, reach_devs + 1) if offset != 0]
    band_index = lax.axis_index("band")
    targets = pair_mesh.reshape(count_pairs)
    slot_index = (
        targets // owner_blocks - band_index + reach_devs
    ) * owner_blocks + targets % owner_blocks
    onehot = (slot_index[None, :] == jnp.arange(slot_total)[:, None]).astype(fl)
    live_mask = (jnp.arange(pair_slots)[None, :] < pair_count[:, None]).astype(fl)
    live_pairs = live_mask.reshape(count_pairs, 1, 1)
    weights = interp.reshape(count_pairs, mesh_rows, block_rows)
    local_msgs = jnp.einsum(
        "bkrg,bgf->bkrf",
        interp,
        grid.reshape(blocks, block_rows, half_width),
        preferred_element_type=fl,
    ).astype(jnp.bfloat16)
    messages = lax.all_gather(local_msgs, "mp", axis=3, tiled=True)
    messages = messages.reshape(count_pairs, mesh_rows, full_width)
    pre_enc = jnp.dot(
        messages.reshape(count_pairs * mesh_rows, full_width), w_enc, preferred_element_type=fl
    ).reshape(count_pairs, mesh_rows, half_width)
    sig_enc = jax.nn.sigmoid(pre_enc)
    edge_out = pre_enc * sig_enc * live_pairs
    slabs = jnp.einsum("sp,prh->srh", onehot, edge_out, precision=lax.Precision.HIGHEST)
    slabs = slabs.reshape(slab_count, owner_rows, half_width)
    aggregate = slabs[reach_devs]
    for offset in offsets:
        aggregate = aggregate + shifted(slabs[reach_devs + offset], "band", offset)
    mesh_lat = (mesh_init.astype(fl) + 0.25 * aggregate).astype(jnp.bfloat16)
    pieces = []
    for offset in range(-reach_devs, reach_devs + 1):
        if offset == 0:
            pieces.append(mesh_lat)
        else:
            pieces.append(shifted(mesh_lat, "band", -offset))
    nearby = lax.all_gather(jnp.stack(pieces), "mp", axis=2, tiled=True)
    nearby = nearby.reshape(slot_total, mesh_rows, full_width)
    chosen = jnp.take(nearby, slot_index, axis=0)
    decoded = jnp.einsum("prg,prf->pgf", weights, chosen, preferred_element_type=fl).astype(
        jnp.bfloat16
    )
    pre_dec = jnp.dot(
        decoded.reshape(count_pairs * block_rows, full_width), w_dec, preferred_element_type=fl
    ).reshape(count_pairs, block_rows, half_width)
    sig_dec = jax.nn.sigmoid(pre_dec)
    node_out = (
        (pre_dec * sig_dec * live_pairs)
        .reshape(blocks, pair_slots, block_rows, half_width)
        .sum(axis=1)
    )
    grid_out = grid.astype(fl).reshape(blocks, block_rows, half_width) + node_out
    grid_out = grid_out.reshape(blocks * block_rows, half_width).astype(jnp.bfloat16)
    upstream = cotangent.astype(fl).reshape(blocks, 1, block_rows, half_width)
    slope_dec = (silu_slope(pre_dec, sig_dec) * live_pairs).reshape(
        blocks, pair_slots, block_rows, half_width
    )
    grad_pre = (
        (upstream * slope_dec).astype(jnp.bfloat16).reshape(count_pairs, block_rows, half_width)
    )
    grad_dec = jnp.einsum("pgf,pgh->fh", decoded, grad_pre, preferred_element_type=fl)
    lifted = jnp.einsum("prg,pgh->prh", weights, grad_pre, preferred_element_type=fl)
    grad_slabs = jnp.einsum("sp,prh->srh", onehot, lifted, precision=lax.Precision.HIGHEST)
    grad_slabs = grad_slabs.reshape(slab_count, owner_rows, half_width)
    collected = grad_slabs[reach_devs]
    for offset in offsets:
        collected = collected + shifted(grad_slabs[reach_devs + offset], "band", offset)
    mesh_terms = jnp.dot(collected, w_dec.astype(fl).T, precision=lax.Precision.HIGHEST)
    grad_mesh = lax.psum_scatter(mesh_terms, "mp", scatter_dimension=1, tiled=True)
    grad_pieces = []
    for offset in range(-reach_devs, reach_devs + 1):
        if offset == 0:
            grad_pieces.append(grad_mesh)
        else:
            grad_pieces.append(shifted(grad_mesh, "band", -offset))
    grad_nearby = jnp.stack(grad_pieces).reshape(slot_total, mesh_rows, half_width)
    picked = jnp.take(grad_nearby, slot_index, axis=0)
    grad_edge = (0.25 * picked * silu_slope(pre_enc, sig_enc) * live_pairs).astype(jnp.bfloat16)
    grad_enc = jnp.einsum("prf,prh->fh", messages, grad_edge, preferred_element_type=fl)
    grad_enc, grad_dec = lax.psum((grad_enc, grad_dec), "band")
    return (grid_out, grad_enc, grad_dec)


def solution(mesh):
    placed = (
        P("band", "mp"),
        P("band", None, None, None),
        P("band", "mp"),
        P(None, "mp"),
        P(None, "mp"),
        P("band", "mp"),
        P("band", None),
        P("band"),
    )
    return jax.shard_map(
        local,
        mesh=mesh,
        in_specs=placed,
        out_specs=(P("band", "mp"), P(None, "mp"), P(None, "mp")),
        check_vma=False,
    )
```

profile of v0, /device:TPU:8, one launch (start us, length us, event | category | flops | bytes accessed | tf_op | source)
XLA Modules:
  0.0 468.3 jit_solution(9597718689260473274)
XLA Ops:
  8.5 3.4 convolution_convert_fusion
  12.4 22.3 %all-gather.3.cloned.1.call-done = bf16[10,4,128,512]{3,2,1,0:T(8,128)(2,1)} async-done(((bf16[10,4,128,256]{3,2,1,0:T(8,128)(2,1)}), bf16[10,4,128,512]{3,2,1,0:T(8,128)(2,1)}) %all-gather.3.cloned.1.call-update) | async-done | bytes 5242896 | tf_op jit(solution)/shard_map/all_gather | solution.py:46
  34.6 6.4 %multiply_multiply_fusion.1 = (f32[40,128,256]{2,1,0:T(8,128)S(1)}, f32[40,128,256]{2,1,0:T(8,128)}) fusion(f32[40]{0:T(128)S(1)} %reshape.264, bf16[40,128,512]{2,1,0:T(8,128)(2,1)} %bitcast.127, bf16[512,256]{1,0:T(8,128)(2,1)S(1)} %copy-done.11), kind=kOutput, calls=%fused_computation.17 | convolution fusion | flops 1348730880 | bytes 15990944 | tf_op jit(solution)/shard_map/dot_general | solution.py:48
  41.0 4.9 %fusion.7 = f32[10,128,256]{2,0,1:T(8,128)S(1)} fusion(f32[40,128,256]{2,1,0:T(8,128)S(1)} %get-tuple-element.19, s32[40]{0:T(128)S(1)} %get-tuple-element.6), kind=kOutput, calls=%fused_computation.10 | convolution fusion | flops 157286800 | bytes 6553760 | tf_op jit(solution)/shard_map/sp,prh->srh/dot_general | solution.py:53
  47.8 2.7 collective-permute-start.1
  50.5 4.0 collective-permute-start.2
  54.5 7.3 %collective-permute-start.3 = (f32[256,256]{1,0:T(8,128)S(1)}, f32[256,256]{1,0:T(8,128)S(1)}, u32[]{:S(2)}, u32[]{:S(2)}) collective-permute-start(f32[256,256]{1,0:T(8,128)S(1)} %bitcast.119), channel_id=1, source_target_pairs={{0,4},{2,6},{4,8},{6,10},{8,12},{10,14},{12,16},{14,18},{16,20},{1... | collective-permute-start | bytes 786440 | tf_op jit(solution)/shard_map/ppermute | solution.py:12
  65.0 3.7 collective-permute-done.3
  68.8 6.0 %collective-permute-start.4 = (bf16[256,256]{1,0:T(8,128)(2,1)S(1)}, bf16[256,256]{1,0:T(8,128)(2,1)S(1)}, u32[]{:S(2)}, u32[]{:S(2)}) collective-permute-start(bf16[256,256]{1,0:T(8,128)(2,1)S(1)} %fusion.31), channel_id=1, source_target_pairs={{0,4},{2,6},{4,8},{6,10},{8,12},{10,14},{12,16},{14,18},{16,20},{1... | collective-permute-start | bytes 393224 | tf_op jit(solution)/shard_map/ppermute | solution.py:12
  76.0 3.3 collective-permute-start.6
  79.4 4.0 collective-permute-start.5
  83.4 4.1 collective-permute-done.5
  90.0 25.5 %all-gather.5.cloned.1.call-done = bf16[5,256,512]{2,1,0:T(8,128)(2,1)} async-done(((bf16[5,256,256]{2,1,0:T(8,128)(2,1)}), bf16[5,256,512]{2,1,0:T(8,128)(2,1)}) %all-gather.5.cloned.1.call-update) | async-done | bytes 1310736 | tf_op jit(solution)/shard_map/all_gather | solution.py:65
  115.5 5.9 %gather_fusion = bf16[40,128,512]{2,1,0:T(8,128)(2,1)} fusion(bf16[10,128,512]{2,1,0:T(8,128)(2,1)} %bitcast.116, s32[1024]{0:T(1024)S(1)} %pad_clamp_fusion), kind=kCustom, calls=%fused_computation | custom fusion | bytes 10485920 | tf_op jit(solution)/shard_map/jit(_take)/gather | solution.py:67
  121.4 4.3 fusion.12
  125.7 5.8 %fusion.2 = (bf16[40,128,256]{2,1,0:T(8,128)(2,1)S(1)}, f32[40,128,256]{2,1,0:T(8,128)}) fusion(f32[10,128,256]{2,1,0:T(8,128)S(1)} %convert.2, f32[40]{0:T(128)S(1)} %reshape.264, bf16[512,256]{1,0:T(8,128)(2,1)S(1)} %copy-done.5, bf16[40,512,128]{2,1,0:T(8,128)(2,1)S(1)} %fusion.12), kind=kOutput, calls=%fused_computation.5 | convolution fusion | flops 1357905920 | bytes 14680224 | tf_op jit(solution)/shard_map/dot_general | solution.py:71
  132.9 3.2 fusion.50
  136.2 6.2 %copy.35 = f32[40,256,128]{1,0,2:T(8,128)} copy(f32[40,256,128]{2,1,0:T(8,128)} %fusion.50) | data formatting | bytes 10485760 | tf_op jit(solution)/shard_map/prg,pgh->prh/dot_general | solution.py:90
  142.4 4.5 fusion
  151.4 4.0 collective-permute-start.10
  155.4 7.3 %collective-permute-start.11 = (f32[256,256]{1,0:T(8,128)S(1)}, f32[256,256]{1,0:T(8,128)S(1)}, u32[]{:S(2)}, u32[]{:S(2)}) collective-permute-start(f32[256,256]{1,0:T(8,128)S(1)} %bitcast.120), channel_id=1, source_target_pairs={{0,4},{2,6},{4,8},{6,10},{8,12},{10,14},{12,16},{14,18},{16,20},{1... | collective-permute-start | bytes 786440 | tf_op jit(solution)/shard_map/ppermute | solution.py:12
  165.9 3.7 collective-permute-done.11
  171.0 18.8 %reduce-scatter.2.cloned.1.call-done = f32[256,256]{1,0:T(8,128)} async-done(((f32[256,512]{1,0:T(8,128)}), f32[256,256]{1,0:T(8,128)}) %reduce-scatter.2.cloned.1.call-update) | async-done | bytes 262160 | tf_op jit(solution)/shard_map/reduce_scatter | solution.py:97
  189.8 3.5 collective-permute-start.13
  193.3 4.0 collective-permute-start.12
  197.3 5.6 %fusion.19 = f32[512,256]{1,0:T(8,128)} fusion(bf16[40,128,256]{2,1,0:T(8,128)(2,1)} %copy-done.3, bf16[40,512,128]{2,1,0:T(8,128)(2,1)} %copy-done.2), kind=kOutput, calls=%fused_computation.27 | convolution fusion | flops 1342177280 | bytes 8388608 | tf_op jit(solution)/shard_map/pgf,pgh->fh/dot_general | solution.py:89
  204.2 3.4 collective-permute-start.14
  207.6 12.2 %collective-permute-done.14 = f32[256,256]{1,0:T(8,128)S(1)} collective-permute-done((f32[256,256]{1,0:T(8,128)S(1)}, f32[256,256]{1,0:T(8,128)S(1)}, u32[]{:S(2)}, u32[]{:S(2)}) %collective-permute-start.14) | collective-permute-done | bytes 262176 | tf_op jit(solution)/shard_map/ppermute | solution.py:12
  219.9 3.2 gather_fusion.1
  223.1 9.1 %fusion.18 = f32[512,256]{1,0:T(8,128)} fusion(bf16[40,128,512]{2,1,0:T(8,128)(2,1)} %bitcast.128, f32[40,128,256]{2,1,0:T(8,128)} %get-tuple-element.20, f32[40,128,256]{2,1,0:T(8,128)} %gather_fusion.1, f32[40]{0:T(128)S(1)} %reshape.264, pred[40]{0:T(512)(128)(4,1)S(1)} %get-tuple-element.5), kind=kOutput, calls=%fused_computation.26 | convolution fusion | flops 1357905920 | bytes 16253128 | tf_op jit(solution)/shard_map/prf,prh->fh/dot_general | solution.py:107
  232.2 3.1 reduce_sum.11
  236.3 221.7 %all-reduce.3.cloned.1.call-done = (f32[512,256]{1,0:T(8,128)}, f32[512,256]{1,0:T(8,128)}) async-done(((f32[512,256]{1,0:T(8,128)}, f32[512,256]{1,0:T(8,128)}), (f32[512,256]{1,0:T(8,128)}, f32[512,256]{1,0:T(8,128)})) %all-reduce.3.cloned.1.call-update) | async-done | bytes 1048592 | tf_op jit(solution)/shard_map/psum | solution.py:108
  (86 shorter events, 27.1 us)
Async XLA Ops:
  7.2 1.3 copy-start
  7.2 4.8 %copy-start.9 = (s32[10,4]{0,1:T(4,128)S(1)}, s32[10,4]{0,1:T(4,128)}, u32[]{:S(2)}) copy-start(s32[10,4]{0,1:T(4,128)} %param.14) | copy-start | bytes 484
  7.2 5.0 %copy-start.10 = (s32[10]{0:T(128)S(1)}, s32[10]{0:T(128)}, u32[]{:S(2)}) copy-start(s32[10]{0:T(128)} %param.15) | copy-start | bytes 124
  7.2 27.4 %copy-start.11 = (bf16[512,256]{1,0:T(8,128)(2,1)S(1)}, bf16[512,256]{1,0:T(8,128)(2,1)}, u32[]{:S(2)}) copy-start(bf16[512,256]{1,0:T(8,128)(2,1)} %param.11) | copy-start | bytes 786436
  7.2 27.4 %all-gather.3.cloned.1.call-start = ((), (), s32[]{:S(2)}) async-start(), calls=%async_computation.1 | async-start | bytes 7864320 | tf_op jit(solution)/shard_map/all_gather | solution.py:46
  11.9 103.6 %all-gather.5.cloned.1.call-start = ((), (), s32[]{:S(2)}) async-start(), calls=%async_computation.2 | async-start | bytes 1966080 | tf_op jit(solution)/shard_map/all_gather | solution.py:65
  41.0 27.6 %copy-start.8 = (bf16[256,256]{1,0:T(8,128)(2,1)S(1)}, bf16[256,256]{1,0:T(8,128)(2,1)}, u32[]{:S(2)}) copy-start(bf16[256,256]{1,0:T(8,128)(2,1)} %param.10) | copy-start | bytes 393220
  46.5 15.4 %collective-permute-start = (f32[256,256]{1,0:T(8,128)S(1)}, f32[256,256]{1,0:T(8,128)S(1)}, u32[]{:S(2)}, u32[]{:S(2)}) collective-permute-start(f32[256,256]{1,0:T(8,128)S(1)} %bitcast.125), channel_id=1, source_target_pairs={{4,0},{6,2},{8,4},{10,6},{12,8},{14,10},{16,12},{18,14},{20,16},{2... | collective-permute-start | bytes 786440 | tf_op jit(solution)/shard_map/ppermute | solution.py:12
  47.8 16.2 %collective-permute-start.1 = (f32[256,256]{1,0:T(8,128)S(1)}, f32[256,256]{1,0:T(8,128)S(1)}, u32[]{:S(2)}, u32[]{:S(2)}) collective-permute-start(f32[256,256]{1,0:T(8,128)S(1)} %bitcast.123), channel_id=1, source_target_pairs={{2,0},{4,2},{6,4},{8,6},{10,8},{12,10},{14,12},{16,14},{18,16},{20... | collective-permute-start | bytes 786440 | tf_op jit(solution)/shard_map/ppermute | solution.py:12
  50.5 14.5 %collective-permute-start.2 = (f32[256,256]{1,0:T(8,128)S(1)}, f32[256,256]{1,0:T(8,128)S(1)}, u32[]{:S(2)}, u32[]{:S(2)}) collective-permute-start(f32[256,256]{1,0:T(8,128)S(1)} %bitcast.121), channel_id=1, source_target_pairs={{0,2},{2,4},{4,6},{6,8},{8,10},{10,12},{12,14},{14,16},{16,18},{18... | collective-permute-start | bytes 786440 | tf_op jit(solution)/shard_map/ppermute | solution.py:12
  54.5 14.2 %collective-permute-start.3 = (f32[256,256]{1,0:T(8,128)S(1)}, f32[256,256]{1,0:T(8,128)S(1)}, u32[]{:S(2)}, u32[]{:S(2)}) collective-permute-start(f32[256,256]{1,0:T(8,128)S(1)} %bitcast.119), channel_id=1, source_target_pairs={{0,4},{2,6},{4,8},{6,10},{8,12},{10,14},{12,16},{14,18},{16,20},{1... | collective-permute-start | bytes 786440 | tf_op jit(solution)/shard_map/ppermute | solution.py:12
  68.8 14.6 %collective-permute-start.4 = (bf16[256,256]{1,0:T(8,128)(2,1)S(1)}, bf16[256,256]{1,0:T(8,128)(2,1)S(1)}, u32[]{:S(2)}, u32[]{:S(2)}) collective-permute-start(bf16[256,256]{1,0:T(8,128)(2,1)S(1)} %fusion.31), channel_id=1, source_target_pairs={{0,4},{2,6},{4,8},{6,10},{8,12},{10,14},{12,16},{14,18},{16,20},{1... | collective-permute-start | bytes 393224 | tf_op jit(solution)/shard_map/ppermute | solution.py:12
  74.7 12.8 %collective-permute-start.7 = (bf16[256,256]{1,0:T(8,128)(2,1)S(1)}, bf16[256,256]{1,0:T(8,128)(2,1)S(1)}, u32[]{:S(2)}, u32[]{:S(2)}) collective-permute-start(bf16[256,256]{1,0:T(8,128)(2,1)S(1)} %fusion.31), channel_id=1, source_target_pairs={{4,0},{6,2},{8,4},{10,6},{12,8},{14,10},{16,12},{18,14},{20,16},{2... | collective-permute-start | bytes 393224 | tf_op jit(solution)/shard_map/ppermute | solution.py:12
  76.0 11.5 %collective-permute-start.6 = (bf16[256,256]{1,0:T(8,128)(2,1)S(1)}, bf16[256,256]{1,0:T(8,128)(2,1)S(1)}, u32[]{:S(2)}, u32[]{:S(2)}) collective-permute-start(bf16[256,256]{1,0:T(8,128)(2,1)S(1)} %fusion.31), channel_id=1, source_target_pairs={{2,0},{4,2},{6,4},{8,6},{10,8},{12,10},{14,12},{16,14},{18,16},{20... | collective-permute-start | bytes 393224 | tf_op jit(solution)/shard_map/ppermute | solution.py:12
  79.4 8.1 %collective-permute-start.5 = (bf16[256,256]{1,0:T(8,128)(2,1)S(1)}, bf16[256,256]{1,0:T(8,128)(2,1)S(1)}, u32[]{:S(2)}, u32[]{:S(2)}) collective-permute-start(bf16[256,256]{1,0:T(8,128)(2,1)S(1)} %fusion.31), channel_id=1, source_target_pairs={{0,2},{2,4},{4,6},{6,8},{8,10},{10,12},{12,14},{14,16},{16,18},{18... | collective-permute-start | bytes 393224 | tf_op jit(solution)/shard_map/ppermute | solution.py:12
  87.6 0.8 copy-start.6
  88.4 101.3 %reduce-scatter.2.cloned.1.call-start = ((), (), s32[]{:S(2)}) async-start(), calls=%async_computation.3 | async-start | bytes 786432 | tf_op jit(solution)/shard_map/reduce_scatter | solution.py:97
  121.4 4.3 copy-start.5
  125.7 5.8 %copy-start.2 = (bf16[40,512,128]{2,1,0:T(8,128)(2,1)}, bf16[40,512,128]{2,1,0:T(8,128)(2,1)S(1)}, u32[]{:S(2)}) copy-start(bf16[40,512,128]{2,1,0:T(8,128)(2,1)S(1)} %fusion.12) | copy-start | bytes 15728644
  131.5 1.4 copy-start.3
  147.4 15.4 %collective-permute-start.8 = (f32[256,256]{1,0:T(8,128)S(1)}, f32[256,256]{1,0:T(8,128)S(1)}, u32[]{:S(2)}, u32[]{:S(2)}) collective-permute-start(f32[256,256]{1,0:T(8,128)S(1)} %bitcast.126), channel_id=1, source_target_pairs={{4,0},{6,2},{8,4},{10,6},{12,8},{14,10},{16,12},{18,14},{20,16},{2... | collective-permute-start | bytes 786440 | tf_op jit(solution)/shard_map/ppermute | solution.py:12
  148.7 16.2 %collective-permute-start.9 = (f32[256,256]{1,0:T(8,128)S(1)}, f32[256,256]{1,0:T(8,128)S(1)}, u32[]{:S(2)}, u32[]{:S(2)}) collective-permute-start(f32[256,256]{1,0:T(8,128)S(1)} %bitcast.124), channel_id=1, source_target_pairs={{2,0},{4,2},{6,4},{8,6},{10,8},{12,10},{14,12},{16,14},{18,16},{20... | collective-permute-start | bytes 786440 | tf_op jit(solution)/shard_map/ppermute | solution.py:12
  151.4 14.5 %collective-permute-start.10 = (f32[256,256]{1,0:T(8,128)S(1)}, f32[256,256]{1,0:T(8,128)S(1)}, u32[]{:S(2)}, u32[]{:S(2)}) collective-permute-start(f32[256,256]{1,0:T(8,128)S(1)} %bitcast.122), channel_id=1, source_target_pairs={{0,2},{2,4},{4,6},{6,8},{8,10},{10,12},{12,14},{14,16},{16,18},{18... | collective-permute-start | bytes 786440 | tf_op jit(solution)/shard_map/ppermute | solution.py:12
  155.4 14.2 %collective-permute-start.11 = (f32[256,256]{1,0:T(8,128)S(1)}, f32[256,256]{1,0:T(8,128)S(1)}, u32[]{:S(2)}, u32[]{:S(2)}) collective-permute-start(f32[256,256]{1,0:T(8,128)S(1)} %bitcast.120), channel_id=1, source_target_pairs={{0,4},{2,6},{4,8},{6,10},{8,12},{10,14},{12,16},{14,18},{16,20},{1... | collective-permute-start | bytes 786440 | tf_op jit(solution)/shard_map/ppermute | solution.py:12
  170.9 287.0 %all-reduce.3.cloned.1.call-start = ((), (), s32[]{:S(2)}) async-start(), calls=%async_computation.4 | async-start | bytes 2097152 | tf_op jit(solution)/shard_map/psum | solution.py:108
  189.8 13.1 %copy-start.7 = (f32[256,256]{1,0:T(8,128)S(1)}, f32[256,256]{1,0:T(8,128)}, u32[]{:S(2)}) copy-start(f32[256,256]{1,0:T(8,128)} %reduce-scatter.2.cloned.1.call-done) | copy-start | bytes 786436
  189.8 17.8 %collective-permute-start.13 = (f32[256,256]{1,0:T(8,128)}, f32[256,256]{1,0:T(8,128)S(1)}, u32[]{:S(2)}, u32[]{:S(2)}) collective-permute-start(f32[256,256]{1,0:T(8,128)} %reduce-scatter.2.cloned.1.call-done), channel_id=1, source_target_pairs={{0,2},{2,4},{4,6},{6,8},{8,10},{10,12},{12,14},{14,16},{16,18},{18... | collective-permute-start | bytes 786440 | tf_op jit(solution)/shard_map/ppermute | solution.py:12
  193.3 14.2 %collective-permute-start.12 = (f32[256,256]{1,0:T(8,128)}, f32[256,256]{1,0:T(8,128)S(1)}, u32[]{:S(2)}, u32[]{:S(2)}) collective-permute-start(f32[256,256]{1,0:T(8,128)} %reduce-scatter.2.cloned.1.call-done), channel_id=1, source_target_pairs={{0,4},{2,6},{4,8},{6,10},{8,12},{10,14},{12,16},{14,18},{16,20},{1... | collective-permute-start | bytes 786440 | tf_op jit(solution)/shard_map/ppermute | solution.py:12
  202.9 17.0 %collective-permute-start.15 = (f32[256,256]{1,0:T(8,128)S(1)}, f32[256,256]{1,0:T(8,128)S(1)}, u32[]{:S(2)}, u32[]{:S(2)}) collective-permute-start(f32[256,256]{1,0:T(8,128)S(1)} %copy-done.7), channel_id=1, source_target_pairs={{4,0},{6,2},{8,4},{10,6},{12,8},{14,10},{16,12},{18,14},{20,16},{2... | collective-permute-start | bytes 786440 | tf_op jit(solution)/shard_map/ppermute | solution.py:12
  204.2 15.7 %collective-permute-start.14 = (f32[256,256]{1,0:T(8,128)S(1)}, f32[256,256]{1,0:T(8,128)S(1)}, u32[]{:S(2)}, u32[]{:S(2)}) collective-permute-start(f32[256,256]{1,0:T(8,128)S(1)} %copy-done.7), channel_id=1, source_target_pairs={{2,0},{4,2},{6,4},{8,6},{10,8},{12,10},{14,12},{16,14},{18,16},{20... | collective-permute-start | bytes 786440 | tf_op jit(solution)/shard_map/ppermute | solution.py:12
  232.1 3.2 copy-start.4
  232.2 229.6 %copy-start.1 = (bf16[10,4,128,128]{3,2,1,0:T(8,128)(2,1)S(1)}, bf16[10,4,128,128]{3,2,1,0:T(8,128)(2,1)}, u32[]{:S(2)}) copy-start(bf16[10,4,128,128]{3,2,1,0:T(8,128)(2,1)} %param.9) | copy-start | bytes 3932164
Sparse Core Ops, SparseCore 0:
  12.1 22.5 all-gather.2
  88.5 26.9 all-gather.4
  171.1 18.6 reduce-scatter.1
  232.3 225.6 all-reduce.2
where the time goes:
time: 469 us; the launch traced here: 468 us
  waiting for transfers between devices  318 us (68%)
  starting transfers between devices  57.6 us (12%)
  matrix products  48.4 us (10%)
  local copies, waits for them, and re-layouts  24 us (5%)
  between operations  14.3 us (3%)
  other arithmetic  5.63 us (1%)
    psum x1, waiting for transfers between devices, local(): grad_enc, grad_dec = lax.psum((grad_enc, grad_dec), 'band')  222 us
    ppermute x16, starting transfers between devices, shifted(): lax.ppermute(value, axis, [(source, source + steps) for source in range(f...  57.3 us
    ppermute x16, waiting for transfers between devices, shifted(): lax.ppermute(value, axis, [(source, source + steps) for source in range(f...  29.9 us
    all_gather x1, waiting for transfers between devices, local(): nearby = lax.all_gather(jnp.stack(pieces), 'mp', axis=2, tiled=True)  25.5 us
    all_gather x1, waiting for transfers between devices, local(): messages = lax.all_gather(local_msgs, 'mp', axis=3, tiled=True)  22.3 us
    reduce_scatter x1, waiting for transfers between devices, local(): lax.psum_scatter(mesh_terms, 'mp', scatter_dimension=1, tiled=True)  18.8 us
  transfers between devices with their start and end apart: 20, of which 12 were waited for; matrix products, arithmetic and copies ran while one was open for 2% of the time, Pallas kernels for 0%

commit v1 on v0

--- a/solution.py
+++ b/solution.py
@@ -16,8 +16,27 @@
     return sig * (1.0 + pre * (1.0 - sig))
 
 
+def halves(value):
+    width = value.shape[1] // 2
+    return [value[:, :width], value[:, width:]]
+
+
+def band_sum(values):
+    fl, bf = jnp.float32, jnp.bfloat16
+    count = lax.axis_size("band")
+    rows, width = values[0].shape
+    flat = jnp.concatenate([half for value in values for half in halves(value)], axis=0)
+    chunks = flat.astype(bf).reshape(count, -1, width // 2)
+    parts = lax.all_to_all(chunks, "band", 0, 0, tiled=True)
+    total = parts.astype(fl).sum(axis=0).astype(bf)
+    spread = jnp.broadcast_to(total[None], parts.shape)
+    flat = lax.all_to_all(spread, "band", 0, 0, tiled=True).reshape(-1, rows, width // 2)
+    flat = flat.astype(fl)
+    return [jnp.concatenate([flat[2 * i], flat[2 * i + 1]], axis=1) for i in range(len(values))]
+
+
 def local(grid, interp, mesh_init, w_enc, w_dec, cotangent, pair_mesh, pair_count):
-    fl = jnp.float32
+    fl, bf = jnp.float32, jnp.bfloat16
     blocks, pair_slots, mesh_rows, block_rows = interp.shape
     half_width = grid.shape[1]
     full_width = w_enc.shape[0]
@@ -37,13 +56,13 @@
     live_mask = (jnp.arange(pair_slots)[None, :] < pair_count[:, None]).astype(fl)
     live_pairs = live_mask.reshape(count_pairs, 1, 1)
     weights = interp.reshape(count_pairs, mesh_rows, block_rows)
-    local_msgs = jnp.einsum(
+    grid_full = lax.all_gather(grid, "mp", axis=1, tiled=True)
+    messages = jnp.einsum(
         "bkrg,bgf->bkrf",
         interp,
-        grid.reshape(blocks, block_rows, half_width),
+        grid_full.reshape(blocks, block_rows, full_width),
         preferred_element_type=fl,
-    ).astype(jnp.bfloat16)
-    messages = lax.all_gather(local_msgs, "mp", axis=3, tiled=True)
+    ).astype(bf)
     messages = messages.reshape(count_pairs, mesh_rows, full_width)
     pre_enc = jnp.dot(
         messages.reshape(count_pairs * mesh_rows, full_width), w_enc, preferred_element_type=fl
@@ -54,20 +73,19 @@
     slabs = slabs.reshape(slab_count, owner_rows, half_width)
     aggregate = slabs[reach_devs]
     for offset in offsets:
-        aggregate = aggregate + shifted(slabs[reach_devs + offset], "band", offset)
-    mesh_lat = (mesh_init.astype(fl) + 0.25 * aggregate).astype(jnp.bfloat16)
+        sent = slabs[reach_devs + offset].astype(bf)
+        aggregate = aggregate + shifted(sent, "band", offset).astype(fl)
+    mesh_lat = (mesh_init.astype(fl) + 0.25 * aggregate).astype(bf)
     pieces = []
     for offset in range(-reach_devs, reach_devs + 1):
         if offset == 0:
             pieces.append(mesh_lat)
         else:
             pieces.append(shifted(mesh_lat, "band", -offset))
-    nearby = lax.all_gather(jnp.stack(pieces), "mp", axis=2, tiled=True)
+    nearby = lax.all_gather(jnp.concatenate(pieces, axis=0), "mp", axis=1, tiled=True)
     nearby = nearby.reshape(slot_total, mesh_rows, full_width)
     chosen = jnp.take(nearby, slot_index, axis=0)
-    decoded = jnp.einsum("prg,prf->pgf", weights, chosen, preferred_element_type=fl).astype(
-        jnp.bfloat16
-    )
+    decoded = jnp.einsum("prg,prf->pgf", weights, chosen, preferred_element_type=fl).astype(bf)
     pre_dec = jnp.dot(
         decoded.reshape(count_pairs * block_rows, full_width), w_dec, preferred_element_type=fl
     ).reshape(count_pairs, block_rows, half_width)
@@ -78,23 +96,25 @@
         .sum(axis=1)
     )
     grid_out = grid.astype(fl).reshape(blocks, block_rows, half_width) + node_out
-    grid_out = grid_out.reshape(blocks * block_rows, half_width).astype(jnp.bfloat16)
+    grid_out = grid_out.reshape(blocks * block_rows, half_width).astype(bf)
     upstream = cotangent.astype(fl).reshape(blocks, 1, block_rows, half_width)
     slope_dec = (silu_slope(pre_dec, sig_dec) * live_pairs).reshape(
         blocks, pair_slots, block_rows, half_width
     )
-    grad_pre = (
-        (upstream * slope_dec).astype(jnp.bfloat16).reshape(count_pairs, block_rows, half_width)
-    )
+    grad_pre = (upstream * slope_dec).astype(bf).reshape(count_pairs, block_rows, half_width)
     grad_dec = jnp.einsum("pgf,pgh->fh", decoded, grad_pre, preferred_element_type=fl)
     lifted = jnp.einsum("prg,pgh->prh", weights, grad_pre, preferred_element_type=fl)
     grad_slabs = jnp.einsum("sp,prh->srh", onehot, lifted, precision=lax.Precision.HIGHEST)
     grad_slabs = grad_slabs.reshape(slab_count, owner_rows, half_width)
     collected = grad_slabs[reach_devs]
     for offset in offsets:
-        collected = collected + shifted(grad_slabs[reach_devs + offset], "band", offset)
-    mesh_terms = jnp.dot(collected, w_dec.astype(fl).T, precision=lax.Precision.HIGHEST)
-    grad_mesh = lax.psum_scatter(mesh_terms, "mp", scatter_dimension=1, tiled=True)
+        sent = grad_slabs[reach_devs + offset].astype(bf)
+        collected = collected + shifted(sent, "band", offset).astype(fl)
+    w_dec_full = lax.all_gather(w_dec, "mp", axis=1, tiled=True)
+    mesh_half = w_dec_full.reshape(2, -1, full_width)
+    w_rows = lax.dynamic_index_in_dim(mesh_half, lax.axis_index("mp"), 0, keepdims=False)
+    lift = lax.all_gather(collected.astype(bf), "mp", axis=1, tiled=True)
+    grad_mesh = jnp.dot(lift, w_rows.T, preferred_element_type=fl).astype(bf)
     grad_pieces = []
     for offset in range(-reach_devs, reach_devs + 1):
         if offset == 0:
@@ -102,10 +122,10 @@
         else:
             grad_pieces.append(shifted(grad_mesh, "band", -offset))
     grad_nearby = jnp.stack(grad_pieces).reshape(slot_total, mesh_rows, half_width)
-    picked = jnp.take(grad_nearby, slot_index, axis=0)
-    grad_edge = (0.25 * picked * silu_slope(pre_enc, sig_enc) * live_pairs).astype(jnp.bfloat16)
+    picked = jnp.take(grad_nearby, slot_index, axis=0).astype(fl)
+    grad_edge = (0.25 * picked * silu_slope(pre_enc, sig_enc) * live_pairs).astype(bf)
     grad_enc = jnp.einsum("prf,prh->fh", messages, grad_edge, preferred_element_type=fl)
-    grad_enc, grad_dec = lax.psum((grad_enc, grad_dec), "band")
+    grad_enc, grad_dec = band_sum([grad_enc, grad_dec])
     return (grid_out, grad_enc, grad_dec)
 
 

time: 469 us -> 263 us (0.56)
  waiting for transfers between devices: 318 us -> 75.5 us
  blocking collectives: 0 us -> 48 us
  matrix products: 48.4 us -> 39.1 us
    psum x1 -> x0, waiting for transfers between devices: 222 us -> none  [local(): grad_enc, grad_dec = lax.psum((grad_enc, grad_dec), 'band')]
    all_to_all x0 -> x1, blocking collectives: none -> 43.8 us  [band_sum(): parts = lax.all_to_all(chunks, 'band', 0, 0, tiled=True)]
    reduce_scatter x1 -> x0, waiting for transfers between devices: 18.8 us -> none  [local(): lax.psum_scatter(mesh_terms, 'mp', scatter_dimension=1, tiled=True)]
    all_to_all x0 -> x1, waiting for transfers between devices: none -> 12.3 us  [band_sum(): lax.all_to_all(spread, 'band', 0, 0, tiled=True)]
    ppermute x16, waiting for transfers between devices: 29.9 us -> 20.9 us  [shifted(): lax.ppermute(value, axis, [(source, source + steps) for source in range(f...]
    ppermute x16, starting transfers between devices: 57.3 us -> 48.8 us  [shifted(): lax.ppermute(value, axis, [(source, source + steps) for source in range(f...]
    all_to_all x0 -> x1, starting transfers between devices: none -> 6.63 us  [band_sum(): lax.all_to_all(spread, 'band', 0, 0, tiled=True)]
    all_gather x2, waiting for transfers between devices: 47.8 us -> 41.6 us  [the longest x1 23.8 us: local(): lax.all_gather(jnp.concatenate(pieces, axis=0), 'mp', axis=1, tiled=True)]
  transfers between devices with their start and end apart: 20 -> 19, of which waited for: 12 -> 8; matrix products, arithmetic and copies ran while one was open for 2% -> 4% of each run, Pallas kernels for 0% -> 0%
where the time goes in v1:
time: 263 us; the launch traced here: 262 us
  waiting for transfers between devices  75.5 us (29%)
  starting transfers between devices  55.5 us (21%)
  blocking collectives  48 us (18%)
  matrix products  39.1 us (15%)
  local copies, waits for them, and re-layouts  20.1 us (8%)
  between operations  14.7 us (6%)
  other arithmetic  9.31 us (4%)
    ppermute x16, starting transfers between devices, shifted(): lax.ppermute(value, axis, [(source, source + steps) for source in range(f...  48.8 us
    all_to_all x1, blocking collectives, band_sum(): parts = lax.all_to_all(chunks, 'band', 0, 0, tiled=True)  43.8 us
    all_gather x1, waiting for transfers between devices, local(): lax.all_gather(jnp.concatenate(pieces, axis=0), 'mp', axis=1, tiled=True)  23.8 us
    ppermute x16, waiting for transfers between devices, shifted(): lax.ppermute(value, axis, [(source, source + steps) for source in range(f...  20.9 us
    all_gather x1, waiting for transfers between devices, local(): grid_full = lax.all_gather(grid, 'mp', axis=1, tiled=True)  17.7 us
    all_to_all x1, waiting for transfers between devices, band_sum(): lax.all_to_all(spread, 'band', 0, 0, tiled=True)  12.3 us
    dot_general x1, matrix products, local(): jnp.einsum('prf,prh->fh', messages, grad_edge, preferred_element_type=fl)  7.69 us
    all_to_all x1, starting transfers between devices, band_sum(): lax.all_to_all(spread, 'band', 0, 0, tiled=True)  6.63 us
  transfers between devices with their start and end apart: 19, of which 8 were waited for; matrix products, arithmetic and copies ran while one was open for 4% of the time, Pallas kernels for 0%

profile of v1, /device:TPU:8, one launch (start us, length us, event | category | flops | bytes accessed | tf_op | source)
XLA Modules:
  0.0 262.2 jit_solution(18316261906790465327)
XLA Ops:
  9.7 17.7 %all-gather.3.cloned.1.call-done = bf16[1280,512]{1,0:T(8,128)(2,1)} async-done(((bf16[1280,256]{1,0:T(8,128)(2,1)}), bf16[1280,512]{1,0:T(8,128)(2,1)}) %all-gather.3.cloned.1.call-update) | async-done | bytes 1310736 | tf_op jit(solution)/shard_map/all_gather | solution.py:59
  27.4 2.8 %convolution_convert_fusion = bf16[10,4,128,512]{3,2,1,0:T(8,128)(2,1)S(1)} fusion(bf16[10,4,128,128]{3,2,1,0:T(8,128)(2,1)S(1)} %copy-done, bf16[10,128,512,1]{2,1,3,0:T(8,128)(2,1)} %bitcast.134), kind=kOutput, calls=%fused_computation.21 | convolution fusion | flops 673710080 | bytes 7864320 | tf_op jit(solution)/shard_map/bkrg,bgf->bkrf/dot_general | solution.py:60
  30.3 3.9 %multiply_multiply_fusion.1 = (f32[40,128,256]{2,1,0:T(8,128)S(1)}, f32[40,128,256]{2,1,0:T(8,128)}) fusion(f32[40]{0:T(128)S(1)} %reshape.290, bf16[40,128,512]{2,1,0:T(8,128)(2,1)S(1)} %bitcast.131, bf16[512,256]{1,0:T(8,128)(2,1)S(1)} %copy-done.9), kind=kOutput, calls=%fused_computation.17 | convolution fusion | flops 1348730880 | bytes 15990944 | tf_op jit(solution)/shard_map/dot_general | solution.py:67
  34.2 4.9 %fusion.62 = (bf16[10,128,256]{2,0,1:T(8,128)(2,1)S(1)}, f32[10,128,256]{2,0,1:T(8,128)S(1)}) fusion(f32[40,128,256]{2,1,0:T(8,128)S(1)} %get-tuple-element.23, s32[40]{0:T(128)S(1)} %get-tuple-element.4), kind=kOutput, calls=%fused_computation.95 | convolution fusion | flops 157614480 | bytes 7209120 | tf_op jit(solution)/shard_map/sp,prh->srh/dot_general | solution.py:72
  39.6 2.7 %collective-permute-start.1 = (bf16[256,256]{1,0:T(8,128)(2,1)S(1)}, bf16[256,256]{1,0:T(8,128)(2,1)S(1)}, u32[]{:S(2)}, u32[]{:S(2)}) collective-permute-start(bf16[256,256]{1,0:T(8,128)(2,1)S(1)} %bitcast.148), channel_id=1, source_target_pairs={{2,0},{4,2},{6,4},{8,6},{10,8},{12,10},{14,12},{16,14},{18,16},{20... | collective-permute-start | bytes 393224 | tf_op jit(solution)/shard_map/ppermute | solution.py:12
  42.3 3.1 %collective-permute-start.2 = (bf16[256,256]{1,0:T(8,128)(2,1)S(1)}, bf16[256,256]{1,0:T(8,128)(2,1)S(1)}, u32[]{:S(2)}, u32[]{:S(2)}) collective-permute-start(bf16[256,256]{1,0:T(8,128)(2,1)S(1)} %bitcast.146), channel_id=1, source_target_pairs={{0,2},{2,4},{4,6},{6,8},{8,10},{10,12},{12,14},{14,16},{16,18},{18... | collective-permute-start | bytes 393224 | tf_op jit(solution)/shard_map/ppermute | solution.py:12
  45.4 6.1 %collective-permute-start.3 = (bf16[256,256]{1,0:T(8,128)(2,1)S(1)}, bf16[256,256]{1,0:T(8,128)(2,1)S(1)}, u32[]{:S(2)}, u32[]{:S(2)}) collective-permute-start(bf16[256,256]{1,0:T(8,128)(2,1)S(1)} %bitcast.144), channel_id=1, source_target_pairs={{0,4},{2,6},{4,8},{6,10},{8,12},{10,14},{12,16},{14,18},{16,20},{1... | collective-permute-start | bytes 393224 | tf_op jit(solution)/shard_map/ppermute | solution.py:12
  54.2 5.8 %collective-permute-done = bf16[256,256]{1,0:T(8,128)(2,1)S(1)} collective-permute-done((bf16[256,256]{1,0:T(8,128)(2,1)S(1)}, bf16[256,256]{1,0:T(8,128)(2,1)S(1)}, u32[]{:S(2)}, u32[]{:S(2)}) %collective-permute-start) | collective-permute-done | bytes 131104 | tf_op jit(solution)/shard_map/ppermute | solution.py:12
  60.1 3.0 %collective-permute-start.4 = (bf16[256,256]{1,0:T(8,128)(2,1)S(1)}, bf16[256,256]{1,0:T(8,128)(2,1)S(1)}, u32[]{:S(2)}, u32[]{:S(2)}) collective-permute-start(bf16[256,256]{1,0:T(8,128)(2,1)S(1)} %fusion.38), channel_id=1, source_target_pairs={{0,4},{2,6},{4,8},{6,10},{8,12},{10,14},{12,16},{14,18},{16,20},{1... | collective-permute-start | bytes 393224 | tf_op jit(solution)/shard_map/ppermute | solution.py:12
  63.1 3.2 %collective-permute-start.5 = (bf16[256,256]{1,0:T(8,128)(2,1)S(1)}, bf16[256,256]{1,0:T(8,128)(2,1)S(1)}, u32[]{:S(2)}, u32[]{:S(2)}) collective-permute-start(bf16[256,256]{1,0:T(8,128)(2,1)S(1)} %fusion.38), channel_id=1, source_target_pairs={{0,2},{2,4},{4,6},{6,8},{8,10},{10,12},{12,14},{14,16},{16,18},{18... | collective-permute-start | bytes 393224 | tf_op jit(solution)/shard_map/ppermute | solution.py:12
  67.6 2.9 %collective-permute-start.6 = (bf16[256,256]{1,0:T(8,128)(2,1)S(1)}, bf16[256,256]{1,0:T(8,128)(2,1)S(1)}, u32[]{:S(2)}, u32[]{:S(2)}) collective-permute-start(bf16[256,256]{1,0:T(8,128)(2,1)S(1)} %fusion.38), channel_id=1, source_target_pairs={{2,0},{4,2},{6,4},{8,6},{10,8},{12,10},{14,12},{16,14},{18,16},{20... | collective-permute-start | bytes 393224 | tf_op jit(solution)/shard_map/ppermute | solution.py:12
  70.5 6.0 %collective-permute-done.6 = bf16[256,256]{1,0:T(8,128)(2,1)S(1)} collective-permute-done((bf16[256,256]{1,0:T(8,128)(2,1)S(1)}, bf16[256,256]{1,0:T(8,128)(2,1)S(1)}, u32[]{:S(2)}, u32[]{:S(2)}) %collective-permute-start.6) | collective-permute-done | bytes 131104 | tf_op jit(solution)/shard_map/ppermute | solution.py:12
  78.8 23.8 %all-gather.5.cloned.1.call-done = bf16[1280,512]{1,0:T(8,128)(2,1)} async-done(((bf16[1280,256]{1,0:T(8,128)(2,1)}), bf16[1280,512]{1,0:T(8,128)(2,1)}) %all-gather.5.cloned.1.call-update) | async-done | bytes 1310736 | tf_op jit(solution)/shard_map/all_gather | solution.py:85
  102.6 5.9 %gather_fusion = bf16[40,128,512]{2,1,0:T(8,128)(2,1)} fusion(bf16[10,128,512]{2,1,0:T(8,128)(2,1)} %bitcast.129, s32[1024]{0:T(1024)S(1)} %pad_clamp_fusion), kind=kCustom, calls=%fused_computation | custom fusion | bytes 10485920 | tf_op jit(solution)/shard_map/jit(_take)/gather | solution.py:87
  108.4 4.3 %fusion.12 = bf16[40,512,128]{2,1,0:T(8,128)(2,1)S(1)} fusion(bf16[40,128,128]{2,1,0:T(8,128)(2,1)S(1)} %bitcast.124, bf16[40,128,512]{2,1,0:T(8,128)(2,1)} %gather_fusion, pred[40]{0:T(512)(128)(4,1)S(1)} %get-tuple-element.3), kind=kOutput, calls=%fused_computation.20 | convolution fusion | flops 676331520 | bytes 11796520 | tf_op jit(solution)/shard_map/prg,prf->pgf/dot_general | solution.py:88
  112.7 5.8 %fusion.2 = (bf16[40,128,256]{2,1,0:T(8,128)(2,1)S(1)}, f32[40,128,256]{2,1,0:T(8,128)}) fusion(f32[10,128,256]{2,1,0:T(8,128)S(1)} %convert.31, f32[40]{0:T(128)S(1)} %reshape.290, bf16[512,256]{1,0:T(8,128)(2,1)S(1)} %copy-done.6, bf16[40,512,128]{2,1,0:T(8,128)(2,1)S(1)} %fusion.12), kind=kOutput, calls=%fused_computation.5 | convolution fusion | flops 1357905920 | bytes 14680224 | tf_op jit(solution)/shard_map/dot_general | solution.py:89
  120.0 3.2 %fusion.64 = f32[40,256,128]{2,1,0:T(8,128)} fusion(bf16[40,128,256]{2,1,0:T(8,128)(2,1)S(1)} %get-tuple-element.5, bf16[40,128,128]{2,1,0:T(8,128)(2,1)S(1)} %bitcast.125), kind=kOutput, calls=%fused_computation.97 | convolution fusion | flops 335544320 | bytes 9175040 | tf_op jit(solution)/shard_map/prg,pgh->prh/dot_general | solution.py:106
  123.3 6.2 %copy.35 = f32[40,256,128]{1,0,2:T(8,128)} copy(f32[40,256,128]{2,1,0:T(8,128)} %fusion.64) | data formatting | bytes 10485760 | tf_op jit(solution)/shard_map/prg,pgh->prh/dot_general | solution.py:106
  129.5 4.7 %fusion.63 = (bf16[10,128,256]{2,0,1:T(8,128)(2,1)S(1)}, f32[10,128,256]{2,0,1:T(8,128)S(1)}) fusion(f32[40,256,128]{1,0,2:T(8,128)} %copy.35, s32[40]{0:T(128)S(1)} %get-tuple-element.4), kind=kOutput, calls=%fused_computation.96 | convolution fusion | flops 157614480 | bytes 7209120 | tf_op jit(solution)/shard_map/sp,prh->srh/dot_general | solution.py:107
  134.6 2.7 %collective-permute-start.9 = (bf16[256,256]{1,0:T(8,128)(2,1)S(1)}, bf16[256,256]{1,0:T(8,128)(2,1)S(1)}, u32[]{:S(2)}, u32[]{:S(2)}) collective-permute-start(bf16[256,256]{1,0:T(8,128)(2,1)S(1)} %bitcast.147), channel_id=1, source_target_pairs={{2,0},{4,2},{6,4},{8,6},{10,8},{12,10},{14,12},{16,14},{18,16},{20... | collective-permute-start | bytes 393224 | tf_op jit(solution)/shard_map/ppermute | solution.py:12
  137.4 3.1 %collective-permute-start.10 = (bf16[256,256]{1,0:T(8,128)(2,1)S(1)}, bf16[256,256]{1,0:T(8,128)(2,1)S(1)}, u32[]{:S(2)}, u32[]{:S(2)}) collective-permute-start(bf16[256,256]{1,0:T(8,128)(2,1)S(1)} %bitcast.145), channel_id=1, source_target_pairs={{0,2},{2,4},{4,6},{6,8},{8,10},{10,12},{12,14},{14,16},{16,18},{18... | collective-permute-start | bytes 393224 | tf_op jit(solution)/shard_map/ppermute | solution.py:12
  140.5 6.2 %collective-permute-start.11 = (bf16[256,256]{1,0:T(8,128)(2,1)S(1)}, bf16[256,256]{1,0:T(8,128)(2,1)S(1)}, u32[]{:S(2)}, u32[]{:S(2)}) collective-permute-start(bf16[256,256]{1,0:T(8,128)(2,1)S(1)} %bitcast.143), channel_id=1, source_target_pairs={{0,4},{2,6},{4,8},{6,10},{8,12},{10,14},{12,16},{14,18},{16,20},{1... | collective-permute-start | bytes 393224 | tf_op jit(solution)/shard_map/ppermute | solution.py:12
  150.3 4.7 %collective-permute-done.8 = bf16[256,256]{1,0:T(8,128)(2,1)S(1)} collective-permute-done((bf16[256,256]{1,0:T(8,128)(2,1)S(1)}, bf16[256,256]{1,0:T(8,128)(2,1)S(1)}, u32[]{:S(2)}, u32[]{:S(2)}) %collective-permute-start.8) | collective-permute-done | bytes 131104 | tf_op jit(solution)/shard_map/ppermute | solution.py:12
  157.4 3.0 %collective-permute-start.12 = (bf16[256,256]{1,0:T(8,128)(2,1)S(1)}, bf16[256,256]{1,0:T(8,128)(2,1)S(1)}, u32[]{:S(2)}, u32[]{:S(2)}) collective-permute-start(bf16[256,256]{1,0:T(8,128)(2,1)S(1)} %convolution_convert_fusion.1), channel_id=1, source_target_pairs={{0,4},{2,6},{4,8},{6,10},{8,12},{10,14},{12,16},{14,18},{16,20},{1... | collective-permute-start | bytes 393224 | tf_op jit(solution)/shard_map/ppermute | solution.py:12
  163.2 3.4 %collective-permute-start.14 = (bf16[256,256]{1,0:T(8,128)(2,1)S(1)}, bf16[256,256]{1,0:T(8,128)(2,1)S(1)}, u32[]{:S(2)}, u32[]{:S(2)}) collective-permute-start(bf16[256,256]{1,0:T(8,128)(2,1)S(1)} %convolution_convert_fusion.1), channel_id=1, source_target_pairs={{2,0},{4,2},{6,4},{8,6},{10,8},{12,10},{14,12},{16,14},{18,16},{20... | collective-permute-start | bytes 393224 | tf_op jit(solution)/shard_map/ppermute | solution.py:12
  166.6 4.2 %collective-permute-start.13 = (bf16[256,256]{1,0:T(8,128)(2,1)S(1)}, bf16[256,256]{1,0:T(8,128)(2,1)S(1)}, u32[]{:S(2)}, u32[]{:S(2)}) collective-permute-start(bf16[256,256]{1,0:T(8,128)(2,1)S(1)} %convolution_convert_fusion.1), channel_id=1, source_target_pairs={{0,2},{2,4},{4,6},{6,8},{8,10},{10,12},{12,14},{14,16},{16,18},{18... | collective-permute-start | bytes 393224 | tf_op jit(solution)/shard_map/ppermute | solution.py:12
  170.9 3.3 %collective-permute-done.13 = bf16[256,256]{1,0:T(8,128)(2,1)S(1)} collective-permute-done((bf16[256,256]{1,0:T(8,128)(2,1)S(1)}, bf16[256,256]{1,0:T(8,128)(2,1)S(1)}, u32[]{:S(2)}, u32[]{:S(2)}) %collective-permute-start.13) | collective-permute-done | bytes 131104 | tf_op jit(solution)/shard_map/ppermute | solution.py:12
  176.6 7.7 %fusion.26 = bf16[512,256]{1,0:T(8,128)(2,1)S(1)} fusion(bf16[40,128,512]{2,1,0:T(8,128)(2,1)} %bitcast.132, f32[40,128,256]{2,1,0:T(8,128)} %get-tuple-element.24, bf16[40,128,256]{2,1,0:T(8,128)(2,1)} %gather_fusion.1, f32[40]{0:T(128)S(1)} %reshape.290, pred[40]{0:T(512)(128)(4,1)S(1)} %get-tuple-element.3), kind=kOutput, calls=%fused_computation.30 | convolution fusion | flops 1359347712 | bytes 13369544 | tf_op jit(solution)/shard_map/prf,prh->fh/dot_general | solution.py:127
  184.4 43.8 %all_to_all.10 = bf16[128,16,128]{2,1,0:T(8,128)(2,1)S(1)} all-to-all(bf16[128,16,128]{2,1,0:T(8,128)(2,1)S(1)} %bitcast.133), channel_id=1, replica_groups=mesh['band'=128,'mp'=2] {'band'}, dimensions={0} | all-to-all | bytes 1048576 | tf_op jit(solution)/shard_map/all_to_all | solution.py:30
  229.3 6.6 %all-to-all-start.1 = ((bf16[128,16,128]{2,1,0:T(8,128)(2,1)}), bf16[128,16,128]{2,1,0:T(8,128)(2,1)S(1)}, u32[]{:S(2)}, u32[]{:S(2)}) async-start(bf16[128,16,128]{2,1,0:T(8,128)(2,1)} %broadcast_in_dim.34), calls=%async_computation.1 | async-start | bytes 1048576 | tf_op jit(solution)/shard_map/all_to_all | solution.py:33
  235.9 3.1 %reduce_sum.23 = f32[10,128,256]{2,1,0:T(8,128)S(1)} reduce(f32[10,4,128,256]{3,2,1,0:T(8,128)} %bitcast.126, f32[]{:T(128)} %constant.77.clone.1), dimensions={1}, to_apply=%region_0.1 | reduce | flops 983040 | bytes 6553604 | tf_op jit(solution)/shard_map/reduce_sum | solution.py:96
  241.3 12.3 %all-to-all-done.1 = bf16[128,16,128]{2,1,0:T(8,128)(2,1)S(1)} async-done(((bf16[128,16,128]{2,1,0:T(8,128)(2,1)}), bf16[128,16,128]{2,1,0:T(8,128)(2,1)S(1)}, u32[]{:S(2)}, u32[]{:S(2)}) %all-to-all-start.1) | async-done | bytes 524320 | tf_op jit(solution)/shard_map/all_to_all | solution.py:33
  (93 shorter events, 27.3 us)
Async XLA Ops:
  7.2 20.3 %copy-start = (bf16[10,4,128,128]{3,2,1,0:T(8,128)(2,1)S(1)}, bf16[10,4,128,128]{3,2,1,0:T(8,128)(2,1)}, u32[]{:S(2)}) copy-start(bf16[10,4,128,128]{3,2,1,0:T(8,128)(2,1)} %param.9) | copy-start | bytes 3932164
  7.2 23.1 %copy-start.9 = (bf16[512,256]{1,0:T(8,128)(2,1)S(1)}, bf16[512,256]{1,0:T(8,128)(2,1)}, u32[]{:S(2)}) copy-start(bf16[512,256]{1,0:T(8,128)(2,1)} %param.11) | copy-start | bytes 786436
  7.2 20.2 %all-gather.3.cloned.1.call-start = ((), (), s32[]{:S(2)}) async-start(), calls=%async_computation.2 | async-start | bytes 1966080 | tf_op jit(solution)/shard_map/all_gather | solution.py:59
  7.9 94.6 %all-gather.5.cloned.1.call-start = ((), (), s32[]{:S(2)}) async-start(), calls=%async_computation.3 | async-start | bytes 1966080 | tf_op jit(solution)/shard_map/all_gather | solution.py:85
  30.3 4.0 %copy-start.5 = (bf16[10,4,128,512]{3,2,1,0:T(8,128)(2,1)}, bf16[10,4,128,512]{3,2,1,0:T(8,128)(2,1)S(1)}, u32[]{:S(2)}) copy-start(bf16[10,4,128,512]{3,2,1,0:T(8,128)(2,1)S(1)} %convolution_convert_fusion) | copy-start | bytes 15728644
  34.2 25.7 %copy-start.8 = (bf16[256,256]{1,0:T(8,128)(2,1)S(1)}, bf16[256,256]{1,0:T(8,128)(2,1)}, u32[]{:S(2)}) copy-start(bf16[256,256]{1,0:T(8,128)(2,1)} %param.10) | copy-start | bytes 393220
  39.6 13.5 %collective-permute-start.1 = (bf16[256,256]{1,0:T(8,128)(2,1)S(1)}, bf16[256,256]{1,0:T(8,128)(2,1)S(1)}, u32[]{:S(2)}, u32[]{:S(2)}) collective-permute-start(bf16[256,256]{1,0:T(8,128)(2,1)S(1)} %bitcast.148), channel_id=1, source_target_pairs={{2,0},{4,2},{6,4},{8,6},{10,8},{12,10},{14,12},{16,14},{18,16},{20... | collective-permute-start | bytes 393224 | tf_op jit(solution)/shard_map/ppermute | solution.py:12
  42.3 10.8 %collective-permute-start.2 = (bf16[256,256]{1,0:T(8,128)(2,1)S(1)}, bf16[256,256]{1,0:T(8,128)(2,1)S(1)}, u32[]{:S(2)}, u32[]{:S(2)}) collective-permute-start(bf16[256,256]{1,0:T(8,128)(2,1)S(1)} %bitcast.146), channel_id=1, source_target_pairs={{0,2},{2,4},{4,6},{6,8},{8,10},{10,12},{12,14},{14,16},{16,18},{18... | collective-permute-start | bytes 393224 | tf_op jit(solution)/shard_map/ppermute | solution.py:12
  45.4 8.7 %collective-permute-start.3 = (bf16[256,256]{1,0:T(8,128)(2,1)S(1)}, bf16[256,256]{1,0:T(8,128)(2,1)S(1)}, u32[]{:S(2)}, u32[]{:S(2)}) collective-permute-start(bf16[256,256]{1,0:T(8,128)(2,1)S(1)} %bitcast.144), channel_id=1, source_target_pairs={{0,4},{2,6},{4,8},{6,10},{8,12},{10,14},{12,16},{14,18},{16,20},{1... | collective-permute-start | bytes 393224 | tf_op jit(solution)/shard_map/ppermute | solution.py:12
  51.6 8.4 %collective-permute-start = (bf16[256,256]{1,0:T(8,128)(2,1)S(1)}, bf16[256,256]{1,0:T(8,128)(2,1)S(1)}, u32[]{:S(2)}, u32[]{:S(2)}) collective-permute-start(bf16[256,256]{1,0:T(8,128)(2,1)S(1)} %bitcast.142), channel_id=1, source_target_pairs={{4,0},{6,2},{8,4},{10,6},{12,8},{14,10},{16,12},{18,14},{20,16},{2... | collective-permute-start | bytes 393224 | tf_op jit(solution)/shard_map/ppermute | solution.py:12
  60.1 10.4 %collective-permute-start.4 = (bf16[256,256]{1,0:T(8,128)(2,1)S(1)}, bf16[256,256]{1,0:T(8,128)(2,1)S(1)}, u32[]{:S(2)}, u32[]{:S(2)}) collective-permute-start(bf16[256,256]{1,0:T(8,128)(2,1)S(1)} %fusion.38), channel_id=1, source_target_pairs={{0,4},{2,6},{4,8},{6,10},{8,12},{10,14},{12,16},{14,18},{16,20},{1... | collective-permute-start | bytes 393224 | tf_op jit(solution)/shard_map/ppermute | solution.py:12
  63.1 7.4 %collective-permute-start.5 = (bf16[256,256]{1,0:T(8,128)(2,1)S(1)}, bf16[256,256]{1,0:T(8,128)(2,1)S(1)}, u32[]{:S(2)}, u32[]{:S(2)}) collective-permute-start(bf16[256,256]{1,0:T(8,128)(2,1)S(1)} %fusion.38), channel_id=1, source_target_pairs={{0,2},{2,4},{4,6},{6,8},{8,10},{10,12},{12,14},{14,16},{16,18},{18... | collective-permute-start | bytes 393224 | tf_op jit(solution)/shard_map/ppermute | solution.py:12
  66.3 10.3 %collective-permute-start.7 = (bf16[256,256]{1,0:T(8,128)(2,1)S(1)}, bf16[256,256]{1,0:T(8,128)(2,1)S(1)}, u32[]{:S(2)}, u32[]{:S(2)}) collective-permute-start(bf16[256,256]{1,0:T(8,128)(2,1)S(1)} %fusion.38), channel_id=1, source_target_pairs={{4,0},{6,2},{8,4},{10,6},{12,8},{14,10},{16,12},{18,14},{20,16},{2... | collective-permute-start | bytes 393224 | tf_op jit(solution)/shard_map/ppermute | solution.py:12
  67.6 9.0 %collective-permute-start.6 = (bf16[256,256]{1,0:T(8,128)(2,1)S(1)}, bf16[256,256]{1,0:T(8,128)(2,1)S(1)}, u32[]{:S(2)}, u32[]{:S(2)}) collective-permute-start(bf16[256,256]{1,0:T(8,128)(2,1)S(1)} %fusion.38), channel_id=1, source_target_pairs={{2,0},{4,2},{6,4},{8,6},{10,8},{12,10},{14,12},{16,14},{18,16},{20... | collective-permute-start | bytes 393224 | tf_op jit(solution)/shard_map/ppermute | solution.py:12
  76.6 0.8 copy-start.7
  108.4 4.3 %copy-start.6 = (bf16[512,256]{1,0:T(8,128)(2,1)S(1)}, bf16[512,256]{1,0:T(8,128)(2,1)}, u32[]{:S(2)}) copy-start(bf16[512,256]{1,0:T(8,128)(2,1)} %param.12) | copy-start | bytes 786436
  112.7 5.8 %copy-start.2 = (bf16[40,512,128]{2,1,0:T(8,128)(2,1)}, bf16[40,512,128]{2,1,0:T(8,128)(2,1)S(1)}, u32[]{:S(2)}) copy-start(bf16[40,512,128]{2,1,0:T(8,128)(2,1)S(1)} %fusion.12) | copy-start | bytes 15728644
  118.6 1.5 copy-start.3
  123.3 37.1 %slice-start = ((s8[5242880]{0:T(1024)(128)(4,1)}), s8[1048576]{0:T(1024)(128)(4,1)S(1)}, s32[]{:S(2)}) async-start(s8[5242880]{0:T(1024)(128)(4,1)} %bitcast.127), calls=%async_computation.4 | async-start | bytes 2097152
  129.5 30.9 %slice-start.1 = ((s8[5242880]{0:T(1024)(128)(4,1)}), s8[4194304]{0:T(1024)(128)(4,1)S(1)}, s32[]{:S(2)}) async-start(s8[5242880]{0:T(1024)(128)(4,1)} %bitcast.127), calls=%async_computation.5 | async-start | bytes 8388608
  129.5 30.9 %copy-start.4 = (bf16[40,128,256]{2,1,0:T(8,128)(2,1)S(1)}, bf16[40,128,256]{2,1,0:T(8,128)(2,1)}, u32[]{:S(2)}) copy-start(bf16[40,128,256]{2,1,0:T(8,128)(2,1)} %copy-done.3) | copy-start | bytes 7864324
  134.6 15.7 %collective-permute-start.9 = (bf16[256,256]{1,0:T(8,128)(2,1)S(1)}, bf16[256,256]{1,0:T(8,128)(2,1)S(1)}, u32[]{:S(2)}, u32[]{:S(2)}) collective-permute-start(bf16[256,256]{1,0:T(8,128)(2,1)S(1)} %bitcast.147), channel_id=1, source_target_pairs={{2,0},{4,2},{6,4},{8,6},{10,8},{12,10},{14,12},{16,14},{18,16},{20... | collective-permute-start | bytes 393224 | tf_op jit(solution)/shard_map/ppermute | solution.py:12
  137.4 13.0 %collective-permute-start.10 = (bf16[256,256]{1,0:T(8,128)(2,1)S(1)}, bf16[256,256]{1,0:T(8,128)(2,1)S(1)}, u32[]{:S(2)}, u32[]{:S(2)}) collective-permute-start(bf16[256,256]{1,0:T(8,128)(2,1)S(1)} %bitcast.145), channel_id=1, source_target_pairs={{0,2},{2,4},{4,6},{6,8},{8,10},{10,12},{12,14},{14,16},{16,18},{18... | collective-permute-start | bytes 393224 | tf_op jit(solution)/shard_map/ppermute | solution.py:12
  140.5 9.9 %collective-permute-start.11 = (bf16[256,256]{1,0:T(8,128)(2,1)S(1)}, bf16[256,256]{1,0:T(8,128)(2,1)S(1)}, u32[]{:S(2)}, u32[]{:S(2)}) collective-permute-start(bf16[256,256]{1,0:T(8,128)(2,1)S(1)} %bitcast.143), channel_id=1, source_target_pairs={{0,4},{2,6},{4,8},{6,10},{8,12},{10,14},{12,16},{14,18},{16,20},{1... | collective-permute-start | bytes 393224 | tf_op jit(solution)/shard_map/ppermute | solution.py:12
  146.7 8.4 %collective-permute-start.8 = (bf16[256,256]{1,0:T(8,128)(2,1)S(1)}, bf16[256,256]{1,0:T(8,128)(2,1)S(1)}, u32[]{:S(2)}, u32[]{:S(2)}) collective-permute-start(bf16[256,256]{1,0:T(8,128)(2,1)S(1)} %bitcast.141), channel_id=1, source_target_pairs={{4,0},{6,2},{8,4},{10,6},{12,8},{14,10},{16,12},{18,14},{20,16},{2... | collective-permute-start | bytes 393224 | tf_op jit(solution)/shard_map/ppermute | solution.py:12
  157.4 13.5 %collective-permute-start.12 = (bf16[256,256]{1,0:T(8,128)(2,1)S(1)}, bf16[256,256]{1,0:T(8,128)(2,1)S(1)}, u32[]{:S(2)}, u32[]{:S(2)}) collective-permute-start(bf16[256,256]{1,0:T(8,128)(2,1)S(1)} %convolution_convert_fusion.1), channel_id=1, source_target_pairs={{0,4},{2,6},{4,8},{6,10},{8,12},{10,14},{12,16},{14,18},{16,20},{1... | collective-permute-start | bytes 393224 | tf_op jit(solution)/shard_map/ppermute | solution.py:12
  161.9 12.3 %collective-permute-start.15 = (bf16[256,256]{1,0:T(8,128)(2,1)S(1)}, bf16[256,256]{1,0:T(8,128)(2,1)S(1)}, u32[]{:S(2)}, u32[]{:S(2)}) collective-permute-start(bf16[256,256]{1,0:T(8,128)(2,1)S(1)} %convolution_convert_fusion.1), channel_id=1, source_target_pairs={{4,0},{6,2},{8,4},{10,6},{12,8},{14,10},{16,12},{18,14},{20,16},{2... | collective-permute-start | bytes 393224 | tf_op jit(solution)/shard_map/ppermute | solution.py:12
  163.2 10.9 %collective-permute-start.14 = (bf16[256,256]{1,0:T(8,128)(2,1)S(1)}, bf16[256,256]{1,0:T(8,128)(2,1)S(1)}, u32[]{:S(2)}, u32[]{:S(2)}) collective-permute-start(bf16[256,256]{1,0:T(8,128)(2,1)S(1)} %convolution_convert_fusion.1), channel_id=1, source_target_pairs={{2,0},{4,2},{6,4},{8,6},{10,8},{12,10},{14,12},{16,14},{18,16},{20... | collective-permute-start | bytes 393224 | tf_op jit(solution)/shard_map/ppermute | solution.py:12
  166.6 7.5 %collective-permute-start.13 = (bf16[256,256]{1,0:T(8,128)(2,1)S(1)}, bf16[256,256]{1,0:T(8,128)(2,1)S(1)}, u32[]{:S(2)}, u32[]{:S(2)}) collective-permute-start(bf16[256,256]{1,0:T(8,128)(2,1)S(1)} %convolution_convert_fusion.1), channel_id=1, source_target_pairs={{0,2},{2,4},{4,6},{6,8},{8,10},{10,12},{12,14},{14,16},{16,18},{18... | collective-permute-start | bytes 393224 | tf_op jit(solution)/shard_map/ppermute | solution.py:12
  229.3 24.3 %all-to-all-start.1 = ((bf16[128,16,128]{2,1,0:T(8,128)(2,1)}), bf16[128,16,128]{2,1,0:T(8,128)(2,1)S(1)}, u32[]{:S(2)}, u32[]{:S(2)}) async-start(bf16[128,16,128]{2,1,0:T(8,128)(2,1)} %broadcast_in_dim.34), calls=%async_computation.1 | async-start | bytes 1048576 | tf_op jit(solution)/shard_map/all_to_all | solution.py:33
  235.9 19.4 %copy-start.1 = (bf16[10,4,128,128]{3,2,1,0:T(8,128)(2,1)S(1)}, bf16[10,4,128,128]{3,2,1,0:T(8,128)(2,1)}, u32[]{:S(2)}) copy-start(bf16[10,4,128,128]{3,2,1,0:T(8,128)(2,1)} %param.9) | copy-start | bytes 3932164
Sparse Core Ops, SparseCore 0:
  9.8 17.5 all-gather.2
  77.5 24.9 all-gather.4

commit v2 on v0

v2 whole, which is shorter than its diff:
```python
import functools

import jax
import jax.numpy as jnp
from jax import lax
from jax.experimental import pallas as pl
from jax.experimental.pallas import tpu as pltpu
from jax.sharding import PartitionSpec as P

REACH = 2
FL, BF = jnp.float32, jnp.bfloat16
ROWS_BY_ROWS = (((0,), (0,)), ((), ()))
COLS_BY_COLS = (((1,), (1,)), ((), ()))


def dot(left, right, dims=(((1,), (0,)), ((), ()))):
    return lax.dot_general(left, right, dims, preferred_element_type=FL)


def swap(value):
    return lax.ppermute(value, "mp", [(0, 1), (1, 0)])


def outward(value, steps):
    count = lax.axis_size("band")
    pairs = []
    for band in range(count):
        pairs.append((2 * band, 2 * ((band + steps) % count)))
        pairs.append((2 * band + 1, 2 * ((band - steps) % count) + 1))
    return lax.ppermute(value, ("band", "mp"), pairs)


def place(pm, block, slot, owner_blocks, facing):
    target = pm[block, slot]
    offset = target // owner_blocks - lax.axis_index("band")
    along = jnp.where(lax.axis_index("mp") == 0, offset, -offset) * facing
    along = jnp.clip(along, -REACH, REACH)
    stored = jnp.where(along >= 0, along, REACH - along)
    return stored * owner_blocks + target % owner_blocks


def live_of(pc, block, slot):
    return jnp.where(slot < pc[block], 1.0, 0.0).astype(FL)


def split_slabs(total, own, mine, other):
    blocks = own.shape[0] // total.shape[1]
    own[...] = total[:blocks].reshape(own.shape).astype(own.dtype)
    mine[...] = total[blocks : 3 * blocks].reshape(mine.shape).astype(mine.dtype)
    other[...] = total[3 * blocks :].reshape(other.shape).astype(other.dtype)


def encode_kernel(pm, pc, a_ref, g_ref, w_ref, x_ref, slope_ref, own, mine, other, total):
    block = pl.program_id(0)
    slots, rows, points = a_ref.shape[1:]
    owner_blocks = own.shape[0] // rows

    @pl.when(block == 0)
    def _():
        total[...] = jnp.zeros_like(total)

    x = dot(a_ref[0].reshape(slots * rows, points), g_ref[...]).astype(BF)
    x_ref[...] = x
    u = dot(x, w_ref[...])
    sig = jax.nn.sigmoid(u)
    edge = u * sig
    slope = sig + edge * (1.0 - sig)
    for slot in range(slots):
        part = slice(slot * rows, (slot + 1) * rows)
        live = live_of(pc, block, slot)
        total[place(pm, block, slot, owner_blocks, 1)] += edge[part] * live
        slope_ref[part] = (slope[part] * (0.25 * live)).astype(BF)

    @pl.when(block == pl.num_programs(0) - 1)
    def _():
        split_slabs(total, own, mine, other)


def gather_near(near, refs, picks):
    blocks = near.shape[0] // len(refs)
    rows, width = near.shape[1], near.shape[2] // 2

    def fill(own_at):
        for at, (ref, pick) in enumerate(zip(refs, picks)):
            for half in range(2):
                column = (own_at + half) % 2 * width
                value = ref[half ^ pick].reshape(blocks, rows, width)
                near[at * blocks : (at + 1) * blocks, :, column : column + width] = value

    core = lax.axis_index("mp")
    pl.when(core == 0)(lambda: fill(0))
    pl.when(core == 1)(lambda: fill(1))


def decode_kernel(
    pm, pc, a_ref, g_ref, cot_ref, w_ref, m, q1, q2, t1, t2,
    out_ref, y_ref, dz_ref, own, mine, other, near, total,
):
    block = pl.program_id(0)
    slots, rows, points = a_ref.shape[1:]
    owner_blocks = own.shape[0] // rows

    @pl.when(block == 0)
    def _():
        total[...] = jnp.zeros_like(total)
        gather_near(near, (m, q1, q2, t1, t2), (0, 0, 0, 1, 1))

    for slot in range(slots):
        chosen = near[place(pm, block, slot, owner_blocks, -1)]
        y = dot(a_ref[0, slot], chosen, ROWS_BY_ROWS).astype(BF)
        y_ref[slot * points : (slot + 1) * points] = y
    z = dot(y_ref[...], w_ref[...])
    sig = jax.nn.sigmoid(z)
    edge = z * sig
    slope = sig + edge * (1.0 - sig)
    result = g_ref[...].astype(FL)
    upstream = cot_ref[...].astype(FL)
    for slot in range(slots):
        part = slice(slot * points, (slot + 1) * points)
        live = live_of(pc, block, slot)
        result = result + edge[part] * live
        dz = ((upstream * live) * slope[part]).astype(BF)
        dz_ref[part] = dz
        total[place(pm, block, slot, owner_blocks, 1)] += dot(a_ref[0, slot], dz)
    out_ref[...] = result.astype(BF)

    @pl.when(block == pl.num_programs(0) - 1)
    def _():
        split_slabs(total, own, mine, other)


def outer_kernel(left_ref, right_ref, out_ref):
    @pl.when(pl.program_id(0) == 0)
    def _():
        out_ref[...] = jnp.zeros_like(out_ref)

    out_ref[...] += dot(left_ref[...], right_ref[...], ROWS_BY_ROWS)


def mesh_grad_kernel(s, t, w_own, w_other, out):
    half = out.shape[2]
    lift_own = (s[0].astype(FL) + t[1].astype(FL)).astype(BF)
    lift_other = (s[1].astype(FL) + t[0].astype(FL)).astype(BF)
    grad = dot(lift_own, w_own[...], COLS_BY_COLS) + dot(lift_other, w_other[...], COLS_BY_COLS)
    grad = grad.astype(BF)
    core = lax.axis_index("mp")

    @pl.when(core == 0)
    def _():
        out[0], out[1] = grad[:, :half], grad[:, half:]

    @pl.when(core == 1)
    def _():
        out[0], out[1] = grad[:, half:], grad[:, :half]


def encoder_grad_kernel(
    pm, pc, x_ref, slope_ref, m, q1, q2, t1, t2, dec_ref, out_ref, near, total
):
    block = pl.program_id(0)
    slots = pm.shape[1]
    rows = near.shape[1]
    owner_blocks = m.shape[1] // rows

    @pl.when(block == 0)
    def _():
        total[...] = jnp.zeros_like(total)
        for at, ref in enumerate((m, q1, q2, t1, t2)):
            near[at * owner_blocks : (at + 1) * owner_blocks] = ref[0].reshape(owner_blocks, rows, -1)

    parts = []
    for slot in range(slots):
        picked = near[place(pm, block, slot, owner_blocks, -1)].astype(FL)
        slope = slope_ref[slot * rows : (slot + 1) * rows].astype(FL)
        parts.append((picked * slope).astype(BF))
    total[...] += dot(x_ref[...], jnp.concatenate(parts, axis=0), ROWS_BY_ROWS)

    @pl.when(block == pl.num_programs(0) - 1)
    def _():
        count, width = total.shape
        for at, value in enumerate((total, dec_ref)):
            for half in range(2):
                start = (2 * at + half) * count
                piece = value[:, half * width // 2 : (half + 1) * width // 2]
                out_ref[start : start + count] = piece.astype(BF)


def sum_kernel(parts_ref, out_ref):
    total = parts_ref[...].astype(FL).sum(axis=0).astype(BF)
    out_ref[...] = jnp.broadcast_to(total[None], out_ref.shape)


def finish_kernel(flat_ref, enc_ref, dec_ref):
    count, width = enc_ref.shape
    for at, out in enumerate((enc_ref, dec_ref)):
        for half in range(2):
            start = (2 * at + half) * count
            out[:, half * width // 2 : (half + 1) * width // 2] = flat_ref[start : start + count].astype(FL)


def params():
    return pltpu.CompilerParams(vmem_limit_bytes=40 * 2**20)


def whole(shape):
    return pl.BlockSpec(shape, lambda *_: (0,) * len(shape))


def shape_of(*shape, dtype=BF):
    return jax.ShapeDtypeStruct(shape, dtype)


def simple(kernel, out_shape):
    return pl.pallas_call(kernel, out_shape=out_shape, compiler_params=params())


def combine(own, parts):
    first, second = (part.astype(FL) for part in parts)
    total = first + second
    return jnp.stack([total[0] + own.astype(FL), total[1]]).astype(BF)


def reduce_to_owner(own, mine, other):
    got = swap(other)
    parts = [outward(jnp.stack([mine[i], got[i]]), i + 1) for i in range(REACH)]
    sums = combine(own, parts)
    return sums, swap(sums)


def spread_from_owner(value):
    near = [outward(value, i + 1) for i in range(REACH)]
    return [value, *near, *(swap(part) for part in near)]


def local(grid, interp, mesh_init, w_enc, w_dec, cotangent, pair_mesh, pair_count):
    blocks, slots, rows, points = interp.shape
    half = grid.shape[1]
    full = w_enc.shape[0]
    owner_rows = mesh_init.shape[0]
    owner_blocks = owner_rows // rows
    near_blocks = (2 * REACH + 1) * owner_blocks
    pairs = blocks * slots

    grid_full = lax.all_gather(grid, "mp", axis=1, tiled=True)
    mesh_both = jnp.stack([mesh_init, swap(mesh_init)])
    w_dec_other = swap(w_dec)

    by_block = lambda *shape: pl.BlockSpec(shape, lambda b, *_: (b,) + (0,) * (len(shape) - 1))
    weights = by_block(1, slots, rows, points)
    slabs = (
        shape_of(owner_rows, half),
        shape_of(REACH, owner_rows, half),
        shape_of(REACH, owner_rows, half),
    )
    slab_specs = [whole(slab.shape) for slab in slabs]
    slab_total = pltpu.VMEM((near_blocks, rows, half), FL)

    x, slope, own, mine, other = pl.pallas_call(
        encode_kernel,
        grid_spec=pltpu.PrefetchScalarGridSpec(
            num_scalar_prefetch=2,
            grid=(blocks,),
            in_specs=[weights, by_block(points, full), whole((full, half))],
            out_specs=[by_block(slots * rows, full), by_block(slots * rows, half), *slab_specs],
            scratch_shapes=[slab_total],
        ),
        out_shape=[shape_of(pairs * rows, full), shape_of(pairs * rows, half), *slabs],
        compiler_params=params(),
    )(pair_mesh, pair_count, interp, grid_full, w_enc)

    sums, got = reduce_to_owner(own, mine, other)
    agg = sums.astype(FL) + got.astype(FL)[::-1]
    mesh_lat = (mesh_both.astype(FL) + 0.25 * agg).astype(BF)
    near = spread_from_owner(mesh_lat)

    out, y, dz, own, mine, other = pl.pallas_call(
        decode_kernel,
        grid_spec=pltpu.PrefetchScalarGridSpec(
            num_scalar_prefetch=2,
            grid=(blocks,),
            in_specs=[
                weights, by_block(points, half), by_block(points, half), whole((full, half)),
                *[whole((2, owner_rows, half))] * 5,
            ],
            out_specs=[
                by_block(points, half), by_block(slots * points, full),
                by_block(slots * points, half), *slab_specs,
            ],
            scratch_shapes=[pltpu.VMEM((near_blocks, rows, full), BF), slab_total],
        ),
        out_shape=[
            shape_of(*grid.shape), shape_of(pairs * points, full),
            shape_of(pairs * points, half), *slabs,
        ],
        compiler_params=params(),
    )(pair_mesh, pair_count, interp, grid, cotangent, w_dec, *near)

    grad_dec = pl.pallas_call(
        outer_kernel,
        grid=(blocks,),
        in_specs=[by_block(slots * points, full), by_block(slots * points, half)],
        out_specs=whole((full, half)),
        out_shape=shape_of(full, half, dtype=FL),
        compiler_params=params(),
        cost_estimate=pl.CostEstimate(
            flops=2 * pairs * points * full * half,
            bytes_accessed=2 * pairs * points * (full + half),
            transcendentals=0,
        ),
    )(y, dz)

    sums, got = reduce_to_owner(own, mine, other)
    grad_mesh = simple(mesh_grad_kernel, shape_of(2, owner_rows, half))(sums, got, w_dec, w_dec_other)
    near = spread_from_owner(grad_mesh)

    pick = lambda at: pl.BlockSpec((1, owner_rows, half), lambda *_: (at, 0, 0))
    flat = pl.pallas_call(
        encoder_grad_kernel,
        grid_spec=pltpu.PrefetchScalarGridSpec(
            num_scalar_prefetch=2,
            grid=(blocks,),
            in_specs=[
                by_block(slots * rows, full), by_block(slots * rows, half),
                pick(0), pick(0), pick(0), pick(1), pick(1), whole((full, half)),
            ],
            out_specs=whole((4 * full, half // 2)),
            scratch_shapes=[pltpu.VMEM((near_blocks, rows, half), BF), pltpu.VMEM((full, half), FL)],
        ),
        out_shape=shape_of(4 * full, half // 2),
        compiler_params=params(),
    )(pair_mesh, pair_count, x, slope, *near, grad_dec)

    count = lax.axis_size("band")
    chunks = lax.all_to_all(flat.reshape(count, -1, half // 2), "band", 0, 0, tiled=True)
    spread = simple(sum_kernel, shape_of(*chunks.shape))(chunks)
    flat = lax.all_to_all(spread, "band", 0, 0, tiled=True).reshape(flat.shape)
    grads = [shape_of(full, half, dtype=FL)] * 2
    grad_enc, grad_dec = simple(finish_kernel, grads)(flat)
    return (out, grad_enc, grad_dec)


def solution(mesh):
    placed = (
        P("band", "mp"),
        P("band", None, None, None),
        P("band", "mp"),
        P(None, "mp"),
        P(None, "mp"),
        P("band", "mp"),
        P("band", None),
        P("band"),
    )
    return jax.shard_map(
        local,
        mesh=mesh,
        in_specs=placed,
        out_specs=(P("band", "mp"), P(None, "mp"), P(None, "mp")),
        check_vma=False,
    )
```

time: 469 us -> 196 us (0.42)
  waiting for transfers between devices: 318 us -> 73.5 us
  blocking collectives: 0 us -> 58.3 us
  matrix products: 48.4 us -> 0 us
  starting transfers between devices: 57.6 us -> 18.8 us
  Pallas kernels: 0 us -> 25.1 us
  local copies, waits for them, and re-layouts: 24 us -> 5.15 us
  other arithmetic: 5.63 us -> 0.47 us
    psum x1 -> x0, waiting for transfers between devices: 222 us -> none  [local(): grad_enc, grad_dec = lax.psum((grad_enc, grad_dec), 'band')]
    all_to_all x0 -> x2, blocking collectives: none -> 58.3 us  [the longest x1 32.8 us: local(): lax.all_to_all(flat.reshape(count, -1, half // 2), 'band', 0, 0, tiled=True)]
    dot_general x10 -> x0, matrix products: 48.4 us -> none  [the longest x1 9.08 us: local(): jnp.einsum('prf,prh->fh', messages, grad_edge, preferred_element_type=fl)]
    ppermute x16 -> x18, starting transfers between devices: 57.3 us -> 18.8 us  [the longest x10 9.78 us: swap(): return lax.ppermute(value, 'mp', [(0, 1), (1, 0)])]
    all_gather x2 -> x1, waiting for transfers between devices: 47.8 us -> 18.7 us  [local(): grid_full = lax.all_gather(grid, 'mp', axis=1, tiled=True)]
    pallas_call x0 -> x7, Pallas kernels: none -> 25.1 us  [the longest x1 9.54 us: local(): pl.pallas_call(decode_kernel, grid_spec=pltpu.PrefetchScalarGridSpec(num_...]
    ppermute x16 -> x18, waiting for transfers between devices: 29.9 us -> 54.1 us  [the longest x8 47.3 us: outward(): return lax.ppermute(value, ('band', 'mp'), pairs)]
    reduce_scatter x1 -> x0, waiting for transfers between devices: 18.8 us -> none  [local(): lax.psum_scatter(mesh_terms, 'mp', scatter_dimension=1, tiled=True)]
  transfers between devices with their start and end apart: 20 -> 19, of which waited for: 12 -> 15; matrix products, arithmetic and copies ran while one was open for 2% -> 1% of each run, Pallas kernels for 0% -> 2%
where the time goes in v2:
time: 196 us
  waiting for transfers between devices  73.5 us (38%)
  blocking collectives  58.3 us (30%)
  Pallas kernels  25.1 us (13%)
  starting transfers between devices  18.8 us (10%)
  between operations  14.3 us (7%)
  local copies, waits for them, and re-layouts  5.15 us (3%)
    ppermute x8, waiting for transfers between devices, outward(): return lax.ppermute(value, ('band', 'mp'), pairs)  47.3 us
    all_to_all x1, blocking collectives, local(): lax.all_to_all(flat.reshape(count, -1, half // 2), 'band', 0, 0, tiled=True)  32.8 us
    all_to_all x1, blocking collectives, local(): flat = lax.all_to_all(spread, 'band', 0, 0, tiled=True).reshape(flat.shape)  25.5 us
    all_gather x1, waiting for transfers between devices, local(): grid_full = lax.all_gather(grid, 'mp', axis=1, tiled=True)  18.7 us
    ppermute x10, starting transfers between devices, swap(): return lax.ppermute(value, 'mp', [(0, 1), (1, 0)])  9.78 us
    pallas_call x1, Pallas kernels, local(): pl.pallas_call(decode_kernel, grid_spec=pltpu.PrefetchScalarGridSpec(num_...  9.54 us
    ppermute x8, starting transfers between devices, outward(): return lax.ppermute(value, ('band', 'mp'), pairs)  8.98 us
    ppermute x10, waiting for transfers between devices, swap(): return lax.ppermute(value, 'mp', [(0, 1), (1, 0)])  6.84 us
  transfers between devices with their start and end apart: 19, of which 15 were waited for; matrix products, arithmetic and copies ran while one was open for 1% of the time, Pallas kernels for 2%

profile of v2, /device:TPU:8, one launch (start us, length us, event | category | flops | bytes accessed | tf_op | source)
XLA Modules:
  0.0 195.7 jit_solution(15760076681467444485)
XLA Ops:
  7.9 0.8 copy.12.pm
  8.7 18.7 %all-gather.2.cloned.1.call-done.g_ref = bf16[1280,512]{1,0:T(8,128)(2,1)} async-done(((bf16[1280,256]{1,0:T(8,128)(2,1)}), bf16[1280,512]{1,0:T(8,128)(2,1)}) %all-gather.2.cloned.1.call-update) | async-done | bytes 1310736 | tf_op jit(solution)/shard_map/all_gather | solution.py:244
  27.4 1.3 copy-done
  28.7 1.3 copy-done.4
  30.0 0.9 copy-done.7
  31.6 5.9 %shard_map.103 = (bf16[5120,512]{1,0:T(8,128)(2,1)S(1)}, bf16[5120,256]{1,0:T(8,128)(2,1)S(1)}, bf16[256,256]{1,0:T(8,128)(2,1)S(1)}, bf16[2,256,256]{2,1,0:T(8,128)(2,1)S(1)}, bf16[2,256,256]{2,1,0:T(8,128)(2,1)S(1)}) custom-call(s32[10,4]{1,0:T(8,128)S(1)} %copy.12.pm, s32[10]{0:T(128)S(1)} %copy-done.8, bf16[10,4,128,128]{3,2,1,0:T(8,128)(2,1)S(1)} %copy-done, ...), custom_call_target="tpu_custom_call" | custom-call | tf_op jit(solution)/shard_map/pallas_call | solution.py:258
  37.9 1.2 collective-permute-done.1
  39.3 1.6 collective-permute-start.2
  40.9 2.1 %collective-permute-start.3 = (bf16[2,256,256]{2,1,0:T(8,128)(2,1)S(1)}, bf16[2,256,256]{2,1,0:T(8,128)(2,1)S(1)}, u32[]{:S(2)}, u32[]{:S(2)}) collective-permute-start(bf16[2,256,256]{2,1,0:T(8,128)(2,1)S(1)} %pad_maximum_fusion.1), channel_id=1, source_target_pairs={{0,4},{1,253},{2,6},{3,255},{4,8},{5,1},{6,10},{7,3},{8,12},{9,5},... | collective-permute-start | bytes 786440 | tf_op jit(solution)/shard_map/ppermute | solution.py:30
  43.0 2.8 %collective-permute-done.2 = bf16[2,256,256]{2,1,0:T(8,128)(2,1)S(1)} collective-permute-done((bf16[2,256,256]{2,1,0:T(8,128)(2,1)S(1)}, bf16[2,256,256]{2,1,0:T(8,128)(2,1)S(1)}, u32[]{:S(2)}, u32[]{:S(2)}) %collective-permute-start.2) | collective-permute-done | bytes 262176 | tf_op jit(solution)/shard_map/ppermute | solution.py:30
  45.7 7.9 %collective-permute-done.3 = bf16[2,256,256]{2,1,0:T(8,128)(2,1)S(1)} collective-permute-done((bf16[2,256,256]{2,1,0:T(8,128)(2,1)S(1)}, bf16[2,256,256]{2,1,0:T(8,128)(2,1)S(1)}, u32[]{:S(2)}, u32[]{:S(2)}) %collective-permute-start.3) | collective-permute-done | bytes 262176 | tf_op jit(solution)/shard_map/ppermute | solution.py:30
  54.3 1.0 collective-permute-done.4
  55.7 1.2 collective-permute-start.5
  56.9 2.9 %collective-permute-start.6 = (bf16[2,256,256]{2,1,0:T(8,128)(2,1)S(1)}, bf16[2,256,256]{2,1,0:T(8,128)(2,1)S(1)}, u32[]{:S(2)}, u32[]{:S(2)}) collective-permute-start(bf16[2,256,256]{2,1,0:T(8,128)(2,1)S(1)} %add_convert_fusion.m), channel_id=1, source_target_pairs={{0,4},{1,253},{2,6},{3,255},{4,8},{5,1},{6,10},{7,3},{8,12},{9,5},... | collective-permute-start | bytes 786440 | tf_op jit(solution)/shard_map/ppermute | solution.py:30
  59.7 6.6 %collective-permute-done.5.q1 = bf16[2,256,256]{2,1,0:T(8,128)(2,1)S(1)} collective-permute-done((bf16[2,256,256]{2,1,0:T(8,128)(2,1)S(1)}, bf16[2,256,256]{2,1,0:T(8,128)(2,1)S(1)}, u32[]{:S(2)}, u32[]{:S(2)}) %collective-permute-start.5) | collective-permute-done | bytes 262176 | tf_op jit(solution)/shard_map/ppermute | solution.py:30
  66.3 2.5 %collective-permute-start.7 = (bf16[2,256,256]{2,1,0:T(8,128)(2,1)S(1)}, bf16[2,256,256]{2,1,0:T(8,128)(2,1)S(1)}, u32[]{:S(2)}, u32[]{:S(2)}) collective-permute-start(bf16[2,256,256]{2,1,0:T(8,128)(2,1)S(1)} %collective-permute-done.5.q1), channel_id=1, source_target_pairs={{0,1},{1,0},{2,3},{3,2},{4,5},{5,4},{6,7},{7,6},{8,9},{9,8},{10,11... | collective-permute-start | bytes 786440 | tf_op jit(solution)/shard_map/ppermute | solution.py:21
  68.8 4.4 %collective-permute-done.6.q2 = bf16[2,256,256]{2,1,0:T(8,128)(2,1)S(1)} collective-permute-done((bf16[2,256,256]{2,1,0:T(8,128)(2,1)S(1)}, bf16[2,256,256]{2,1,0:T(8,128)(2,1)S(1)}, u32[]{:S(2)}, u32[]{:S(2)}) %collective-permute-start.6) | collective-permute-done | bytes 262176 | tf_op jit(solution)/shard_map/ppermute | solution.py:30
  73.2 1.5 collective-permute-done.8.t2
  74.8 9.5 %shard_map.104 = (bf16[1280,256]{1,0:T(8,128)(2,1)}, bf16[5120,512]{1,0:T(8,128)(2,1)S(1)}, bf16[5120,256]{1,0:T(8,128)(2,1)S(1)}, bf16[256,256]{1,0:T(8,128)(2,...) custom-call(s32[10,4]{1,0:T(8,128)S(1)} %copy.12.pm, s32[10]{0:T(128)S(1)} %copy-done.8, ...), custom_call_target="tpu_custom_call" | custom-call | tf_op jit(solution)/shard_map/pallas_call | solution.py:276
  84.5 1.4 collective-permute-done.9
  86.6 4.9 %collective-permute-start.13 = (bf16[512,256]{1,0:T(8,128)(2,1)S(1)}, bf16[512,256]{1,0:T(8,128)(2,1)S(1)}, u32[]{:S(2)}, u32[]{:S(2)}) collective-permute-start(bf16[512,256]{1,0:T(8,128)(2,1)S(1)} %copy-done.5), channel_id=1, source_target_pairs={{0,1},{1,0},{2,3},{3,2},{4,5},{5,4},{6,7},{7,6},{8,9},{9,8},{10,11... | collective-permute-start | bytes 786440 | tf_op jit(solution)/shard_map/ppermute | solution.py:21
  91.5 3.7 %collective-permute-done.10 = bf16[2,256,256]{2,1,0:T(8,128)(2,1)S(1)} collective-permute-done((bf16[2,256,256]{2,1,0:T(8,128)(2,1)S(1)}, bf16[2,256,256]{2,1,0:T(8,128)(2,1)S(1)}, u32[]{:S(2)}, u32[]{:S(2)}) %collective-permute-start.10) | collective-permute-done | bytes 262176 | tf_op jit(solution)/shard_map/ppermute | solution.py:30
  95.2 6.9 %collective-permute-done.11 = bf16[2,256,256]{2,1,0:T(8,128)(2,1)S(1)} collective-permute-done((bf16[2,256,256]{2,1,0:T(8,128)(2,1)S(1)}, bf16[2,256,256]{2,1,0:T(8,128)(2,1)S(1)}, u32[]{:S(2)}, u32[]{:S(2)}) %collective-permute-start.11) | collective-permute-done | bytes 262176 | tf_op jit(solution)/shard_map/ppermute | solution.py:30
  102.3 1.5 collective-permute-done.12.t
  104.8 9.4 %collective-permute-done.14.q1 = bf16[2,256,256]{2,1,0:T(8,128)(2,1)S(1)} collective-permute-done((bf16[2,256,256]{2,1,0:T(8,128)(2,1)S(1)}, bf16[2,256,256]{2,1,0:T(8,128)(2,1)S(1)}, u32[]{:S(2)}, u32[]{:S(2)}) %collective-permute-start.14) | collective-permute-done | bytes 262176 | tf_op jit(solution)/shard_map/ppermute | solution.py:30
  114.2 1.2 collective-permute-start.16
  115.4 5.7 %collective-permute-done.15.q2 = bf16[2,256,256]{2,1,0:T(8,128)(2,1)S(1)} collective-permute-done((bf16[2,256,256]{2,1,0:T(8,128)(2,1)S(1)}, bf16[2,256,256]{2,1,0:T(8,128)(2,1)S(1)}, u32[]{:S(2)}, u32[]{:S(2)}) %collective-permute-start.15) | collective-permute-done | bytes 262176 | tf_op jit(solution)/shard_map/ppermute | solution.py:30
  121.1 3.6 %shard_map.106.dec_ref = f32[512,256]{1,0:T(8,128)S(1)} custom-call(bf16[5120,512]{1,0:T(8,128)(2,1)S(1)} %get-tuple-element.25.left_ref, bf16[5120,256]{1,0:T(8,128)(2,1)S(1)} %get-tuple-element.26.right_ref), custom_call_target="tpu_custom_call" | custom-call | flops 1342177280 | bytes 7864320 | tf_op jit(solution)/shard_map/pallas_call | solution.py:298
  124.8 4.5 %shard_map.107 = bf16[2048,128]{1,0:T(8,128)(2,1)S(1)} custom-call(s32[10,4]{1,0:T(8,128)S(1)} %copy.12.pm, s32[10]{0:T(128)S(1)} %copy-done.9, bf16[5120,512]{1,0:T(8,128)(2,1)S(1)} %get-tuple-element.20.x_ref, bf16[5120,256]{1,0:T(8,128)(2,1)S(1)} %copy-done.3, bf16[2,256,256]{2,1,0:T(8,128)(2,1)S(1)} %shard_map.105.m, ...), custom_call_target="tpu_custom_call" | custom-call | tf_op jit(solution)/shard_map/pallas_call | solution.py:317
  129.3 32.8 %all_to_all.10.parts_ref = bf16[128,16,128]{2,1,0:T(8,128)(2,1)S(1)} all-to-all(bf16[128,16,128]{2,1,0:T(8,128)(2,1)S(1)} %bitcast.24), channel_id=1, replica_groups=mesh['band'=128,'mp'=2] {'band'}, dimensions={0} | all-to-all | bytes 1048576 | tf_op jit(solution)/shard_map/all_to_all | solution.py:334
  162.4 25.5 %all_to_all.11 = bf16[128,16,128]{2,1,0:T(8,128)(2,1)S(1)} all-to-all(bf16[128,16,128]{2,1,0:T(8,128)(2,1)S(1)} %shard_map.108), channel_id=1, replica_groups=mesh['band'=128,'mp'=2] {'band'}, dimensions={0} | all-to-all | bytes 1048576 | tf_op jit(solution)/shard_map/all_to_all | solution.py:336
  187.8 1.0 shard_map.109
  (57 shorter events, 5.1 us)
Async XLA Ops:
  7.2 20.2 %all-gather.2.cloned.1.call-start = ((), (), s32[]{:S(2)}) async-start(), calls=%async_computation.2 | async-start | bytes 1966080 | tf_op jit(solution)/shard_map/all_gather | solution.py:244
  27.4 1.3 copy-start
  28.7 1.3 copy-start.4
  30.0 0.9 copy-start.7
  31.0 0.7 copy-start.8
  37.5 17.9 %copy-start.2 = (bf16[5120,256]{1,0:T(8,128)(2,1)}, bf16[5120,256]{1,0:T(8,128)(2,1)S(1)}, u32[]{:S(2)}) copy-start(bf16[5120,256]{1,0:T(8,128)(2,1)S(1)} %get-tuple-element.21.slope_ref) | copy-start | bytes 7864324
  37.5 16.3 %copy-start.10 = (bf16[256,256]{1,0:T(8,128)(2,1)S(1)}, bf16[256,256]{1,0:T(8,128)(2,1)}, u32[]{:S(2)}) copy-start(bf16[256,256]{1,0:T(8,128)(2,1)} %param.10) | copy-start | bytes 393220
  37.6 1.6 collective-permute-start.1
  39.2 35.5 %copy-start.1 = (bf16[1280,256]{1,0:T(8,128)(2,1)S(1)}, bf16[1280,256]{1,0:T(8,128)(2,1)}, u32[]{:S(2)}) copy-start(bf16[1280,256]{1,0:T(8,128)(2,1)} %g_ref.1) | copy-start | bytes 1966084
  39.2 35.5 %copy-start.5 = (bf16[512,256]{1,0:T(8,128)(2,1)S(1)}, bf16[512,256]{1,0:T(8,128)(2,1)}, u32[]{:S(2)}) copy-start(bf16[512,256]{1,0:T(8,128)(2,1)} %w_own.1) | copy-start | bytes 786436
  39.3 35.5 %copy-start.6 = (bf16[1280,256]{1,0:T(8,128)(2,1)S(1)}, bf16[1280,256]{1,0:T(8,128)(2,1)}, u32[]{:S(2)}) copy-start(bf16[1280,256]{1,0:T(8,128)(2,1)} %cot_ref.1) | copy-start | bytes 1966084
  39.3 6.4 %collective-permute-start.2 = (bf16[2,256,256]{2,1,0:T(8,128)(2,1)S(1)}, bf16[2,256,256]{2,1,0:T(8,128)(2,1)S(1)}, u32[]{:S(2)}, u32[]{:S(2)}) collective-permute-start(bf16[2,256,256]{2,1,0:T(8,128)(2,1)S(1)} %pad_maximum_fusion), channel_id=1, source_target_pairs={{0,2},{1,255},{2,4},{3,1},{4,6},{5,3},{6,8},{7,5},{8,10},{9,7},{10... | collective-permute-start | bytes 786440 | tf_op jit(solution)/shard_map/ppermute | solution.py:30
  40.9 12.7 %collective-permute-start.3 = (bf16[2,256,256]{2,1,0:T(8,128)(2,1)S(1)}, bf16[2,256,256]{2,1,0:T(8,128)(2,1)S(1)}, u32[]{:S(2)}, u32[]{:S(2)}) collective-permute-start(bf16[2,256,256]{2,1,0:T(8,128)(2,1)S(1)} %pad_maximum_fusion.1), channel_id=1, source_target_pairs={{0,4},{1,253},{2,6},{3,255},{4,8},{5,1},{6,10},{7,3},{8,12},{9,5},... | collective-permute-start | bytes 786440 | tf_op jit(solution)/shard_map/ppermute | solution.py:30
  53.7 1.6 collective-permute-start.4
  53.9 1.7 collective-permute-start
  55.7 10.7 %collective-permute-start.5 = (bf16[2,256,256]{2,1,0:T(8,128)(2,1)S(1)}, bf16[2,256,256]{2,1,0:T(8,128)(2,1)S(1)}, u32[]{:S(2)}, u32[]{:S(2)}) collective-permute-start(bf16[2,256,256]{2,1,0:T(8,128)(2,1)S(1)} %add_convert_fusion.m), channel_id=1, source_target_pairs={{0,2},{1,255},{2,4},{3,1},{4,6},{5,3},{6,8},{7,5},{8,10},{9,7},{10... | collective-permute-start | bytes 786440 | tf_op jit(solution)/shard_map/ppermute | solution.py:30
  56.9 16.4 %collective-permute-start.6 = (bf16[2,256,256]{2,1,0:T(8,128)(2,1)S(1)}, bf16[2,256,256]{2,1,0:T(8,128)(2,1)S(1)}, u32[]{:S(2)}, u32[]{:S(2)}) collective-permute-start(bf16[2,256,256]{2,1,0:T(8,128)(2,1)S(1)} %add_convert_fusion.m), channel_id=1, source_target_pairs={{0,4},{1,253},{2,6},{3,255},{4,8},{5,1},{6,10},{7,3},{8,12},{9,5},... | collective-permute-start | bytes 786440 | tf_op jit(solution)/shard_map/ppermute | solution.py:30
  66.3 6.9 %collective-permute-start.7 = (bf16[2,256,256]{2,1,0:T(8,128)(2,1)S(1)}, bf16[2,256,256]{2,1,0:T(8,128)(2,1)S(1)}, u32[]{:S(2)}, u32[]{:S(2)}) collective-permute-start(bf16[2,256,256]{2,1,0:T(8,128)(2,1)S(1)} %collective-permute-done.5.q1), channel_id=1, source_target_pairs={{0,1},{1,0},{2,3},{3,2},{4,5},{5,4},{6,7},{7,6},{8,9},{9,8},{10,11... | collective-permute-start | bytes 786440 | tf_op jit(solution)/shard_map/ppermute | solution.py:21
  73.2 1.5 collective-permute-start.8
  84.3 1.5 collective-permute-start.9
  85.9 9.3 %collective-permute-start.10 = (bf16[2,256,256]{2,1,0:T(8,128)(2,1)S(1)}, bf16[2,256,256]{2,1,0:T(8,128)(2,1)S(1)}, u32[]{:S(2)}, u32[]{:S(2)}) collective-permute-start(bf16[2,256,256]{2,1,0:T(8,128)(2,1)S(1)} %pad_maximum_fusion.3), channel_id=1, source_target_pairs={{0,2},{1,255},{2,4},{3,1},{4,6},{5,3},{6,8},{7,5},{8,10},{9,7},{10... | collective-permute-start | bytes 786440 | tf_op jit(solution)/shard_map/ppermute | solution.py:30
  86.1 16.0 %collective-permute-start.11 = (bf16[2,256,256]{2,1,0:T(8,128)(2,1)S(1)}, bf16[2,256,256]{2,1,0:T(8,128)(2,1)S(1)}, u32[]{:S(2)}, u32[]{:S(2)}) collective-permute-start(bf16[2,256,256]{2,1,0:T(8,128)(2,1)S(1)} %pad_maximum_fusion.4), channel_id=1, source_target_pairs={{0,4},{1,253},{2,6},{3,255},{4,8},{5,1},{6,10},{7,3},{8,12},{9,5},... | collective-permute-start | bytes 786440 | tf_op jit(solution)/shard_map/ppermute | solution.py:30
  86.6 15.7 %collective-permute-start.13 = (bf16[512,256]{1,0:T(8,128)(2,1)S(1)}, bf16[512,256]{1,0:T(8,128)(2,1)S(1)}, u32[]{:S(2)}, u32[]{:S(2)}) collective-permute-start(bf16[512,256]{1,0:T(8,128)(2,1)S(1)} %copy-done.5), channel_id=1, source_target_pairs={{0,1},{1,0},{2,3},{3,2},{4,5},{5,4},{6,7},{7,6},{8,9},{9,8},{10,11... | collective-permute-start | bytes 786440 | tf_op jit(solution)/shard_map/ppermute | solution.py:21
  102.2 1.6 collective-permute-start.12
  104.2 10.0 %collective-permute-start.14 = (bf16[2,256,256]{2,1,0:T(8,128)(2,1)S(1)}, bf16[2,256,256]{2,1,0:T(8,128)(2,1)S(1)}, u32[]{:S(2)}, u32[]{:S(2)}) collective-permute-start(bf16[2,256,256]{2,1,0:T(8,128)(2,1)S(1)} %shard_map.105.m), channel_id=1, source_target_pairs={{0,2},{1,255},{2,4},{3,1},{4,6},{5,3},{6,8},{7,5},{8,10},{9,7},{10... | collective-permute-start | bytes 786440 | tf_op jit(solution)/shard_map/ppermute | solution.py:30
  104.8 16.4 %collective-permute-start.15 = (bf16[2,256,256]{2,1,0:T(8,128)(2,1)S(1)}, bf16[2,256,256]{2,1,0:T(8,128)(2,1)S(1)}, u32[]{:S(2)}, u32[]{:S(2)}) collective-permute-start(bf16[2,256,256]{2,1,0:T(8,128)(2,1)S(1)} %shard_map.105.m), channel_id=1, source_target_pairs={{0,4},{1,253},{2,6},{3,255},{4,8},{5,1},{6,10},{7,3},{8,12},{9,5},... | collective-permute-start | bytes 786440 | tf_op jit(solution)/shard_map/ppermute | solution.py:30
  114.2 10.6 %collective-permute-start.16 = (bf16[2,256,256]{2,1,0:T(8,128)(2,1)S(1)}, bf16[2,256,256]{2,1,0:T(8,128)(2,1)S(1)}, u32[]{:S(2)}, u32[]{:S(2)}) collective-permute-start(bf16[2,256,256]{2,1,0:T(8,128)(2,1)S(1)} %collective-permute-done.14.q1), channel_id=1, source_target_pairs={{0,1},{1,0},{2,3},{3,2},{4,5},{5,4},{6,7},{7,6},{8,9},{9,8},{10,11... | collective-permute-start | bytes 786440 | tf_op jit(solution)/shard_map/ppermute | solution.py:21
  121.1 3.7 %collective-permute-start.17 = (bf16[2,256,256]{2,1,0:T(8,128)(2,1)S(1)}, bf16[2,256,256]{2,1,0:T(8,128)(2,1)S(1)}, u32[]{:S(2)}, u32[]{:S(2)}) collective-permute-start(bf16[2,256,256]{2,1,0:T(8,128)(2,1)S(1)} %collective-permute-done.15.q2), channel_id=1, source_target_pairs={{0,1},{1,0},{2,3},{3,2},{4,5},{5,4},{6,7},{7,6},{8,9},{9,8},{10,11... | collective-permute-start | bytes 786440 | tf_op jit(solution)/shard_map/ppermute | solution.py:21
  121.1 3.7 %copy-start.3 = (bf16[5120,256]{1,0:T(8,128)(2,1)S(1)}, bf16[5120,256]{1,0:T(8,128)(2,1)}, u32[]{:S(2)}) copy-start(bf16[5120,256]{1,0:T(8,128)(2,1)} %copy-done.2) | copy-start | bytes 7864324
  121.1 3.7 %copy-start.9 = (s32[10]{0:T(128)S(1)}, s32[10]{0:T(128)}, u32[]{:S(2)}) copy-start(s32[10]{0:T(128)} %pc.5) | copy-start | bytes 124
Sparse Core Ops, SparseCore 0:
  9.8 17.5 all-gather.1

commit v3 on v2

--- a/solution.py
+++ b/solution.py
@@ -1,5 +1,3 @@
-import functools
-
 import jax
 import jax.numpy as jnp
 from jax import lax
@@ -24,9 +22,9 @@
 def outward(value, steps):
     count = lax.axis_size("band")
     pairs = []
-    for band in range(count):
-        pairs.append((2 * band, 2 * ((band + steps) % count)))
-        pairs.append((2 * band + 1, 2 * ((band - steps) % count) + 1))
+    for band in range(count - steps):
+        pairs.append((2 * band, 2 * (band + steps)))
+        pairs.append((2 * (band + steps) + 1, 2 * band + 1))
     return lax.ppermute(value, ("band", "mp"), pairs)
 
 
@@ -50,7 +48,9 @@
     other[...] = total[3 * blocks :].reshape(other.shape).astype(other.dtype)
 
 
-def encode_kernel(pm, pc, a_ref, g_ref, w_ref, x_ref, slope_ref, own, mine, other, total):
+def encode_kernel(
+    pm, pc, a_ref, g_ref, g_other_ref, w_ref, x_ref, slope_ref, own, mine, other, total
+):
     block = pl.program_id(0)
     slots, rows, points = a_ref.shape[1:]
     owner_blocks = own.shape[0] // rows
@@ -59,7 +59,11 @@
     def _():
         total[...] = jnp.zeros_like(total)
 
-    x = dot(a_ref[0].reshape(slots * rows, points), g_ref[...]).astype(BF)
+    first = lax.axis_index("mp") == 0
+    g_own, g_other = g_ref[...], g_other_ref[...]
+    low, high = jnp.where(first, g_own, g_other), jnp.where(first, g_other, g_own)
+    weights = a_ref[0].reshape(slots * rows, points)
+    x = dot(weights, jnp.concatenate([low, high], axis=1)).astype(BF)
     x_ref[...] = x
     u = dot(x, w_ref[...])
     sig = jax.nn.sigmoid(u)
@@ -198,6 +202,17 @@
             out[:, half * width // 2 : (half + 1) * width // 2] = flat_ref[start : start + count].astype(FL)
 
 
+def plane_groups(count):
+    across = min(16, count // 2)
+    plane = [list(range(at, at + across)) for at in range(0, count, across)]
+    line = [list(range(at, count, across)) for at in range(across)]
+    return plane, line
+
+
+def exchange(value, groups):
+    return lax.all_to_all(value, "band", 0, 0, tiled=True, axis_index_groups=groups)
+
+
 def params():
     return pltpu.CompilerParams(vmem_limit_bytes=40 * 2**20)
 
@@ -220,11 +235,12 @@
     return jnp.stack([total[0] + own.astype(FL), total[1]]).astype(BF)
 
 
-def reduce_to_owner(own, mine, other):
+def reduce_to_owner(own, mine, other, beside=None):
     got = swap(other)
     parts = [outward(jnp.stack([mine[i], got[i]]), i + 1) for i in range(REACH)]
+    parts, beside = lax.optimization_barrier((parts, beside))
     sums = combine(own, parts)
-    return sums, swap(sums)
+    return sums, swap(sums), beside
 
 
 def spread_from_owner(value):
@@ -241,7 +257,7 @@
     near_blocks = (2 * REACH + 1) * owner_blocks
     pairs = blocks * slots
 
-    grid_full = lax.all_gather(grid, "mp", axis=1, tiled=True)
+    grid_other = swap(grid)
     mesh_both = jnp.stack([mesh_init, swap(mesh_init)])
     w_dec_other = swap(w_dec)
 
@@ -260,15 +276,15 @@
         grid_spec=pltpu.PrefetchScalarGridSpec(
             num_scalar_prefetch=2,
             grid=(blocks,),
-            in_specs=[weights, by_block(points, full), whole((full, half))],
+            in_specs=[weights, by_block(points, half), by_block(points, half), whole((full, half))],
             out_specs=[by_block(slots * rows, full), by_block(slots * rows, half), *slab_specs],
             scratch_shapes=[slab_total],
         ),
         out_shape=[shape_of(pairs * rows, full), shape_of(pairs * rows, half), *slabs],
         compiler_params=params(),
-    )(pair_mesh, pair_count, interp, grid_full, w_enc)
-
-    sums, got = reduce_to_owner(own, mine, other)
+    )(pair_mesh, pair_count, interp, grid, grid_other, w_enc)
+
+    sums, got, _ = reduce_to_owner(own, mine, other)
     agg = sums.astype(FL) + got.astype(FL)[::-1]
     mesh_lat = (mesh_both.astype(FL) + 0.25 * agg).astype(BF)
     near = spread_from_owner(mesh_lat)
@@ -309,7 +325,7 @@
         ),
     )(y, dz)
 
-    sums, got = reduce_to_owner(own, mine, other)
+    sums, got, grad_dec = reduce_to_owner(own, mine, other, grad_dec)
     grad_mesh = simple(mesh_grad_kernel, shape_of(2, owner_rows, half))(sums, got, w_dec, w_dec_other)
     near = spread_from_owner(grad_mesh)
 
@@ -330,10 +346,13 @@
         compiler_params=params(),
     )(pair_mesh, pair_count, x, slope, *near, grad_dec)
 
-    count = lax.axis_size("band")
-    chunks = lax.all_to_all(flat.reshape(count, -1, half // 2), "band", 0, 0, tiled=True)
-    spread = simple(sum_kernel, shape_of(*chunks.shape))(chunks)
-    flat = lax.all_to_all(spread, "band", 0, 0, tiled=True).reshape(flat.shape)
+    plane, line = plane_groups(lax.axis_size("band"))
+    across = len(plane[0])
+    chunks = exchange(flat.reshape(across, -1, half // 2), plane)
+    piece = simple(sum_kernel, shape_of(len(line[0]), *chunks.shape[1:]))(chunks)
+    pieces = exchange(piece, line)
+    spread = simple(sum_kernel, shape_of(*chunks.shape))(pieces)
+    flat = exchange(spread, plane).reshape(flat.shape)
     grads = [shape_of(full, half, dtype=FL)] * 2
     grad_enc, grad_dec = simple(finish_kernel, grads)(flat)
     return (out, grad_enc, grad_dec)

time: 196 us -> 158 us (0.81)
  waiting for transfers between devices: 73.5 us -> 34.9 us
  between operations: 14.3 us -> 0.96 us
  starting transfers between devices: 18.8 us -> 32 us
    ppermute x8, waiting for transfers between devices: 47.3 us -> 24.9 us  [outward(): return lax.ppermute(value, ('band', 'mp'), pairs)]
    ppermute x8, starting transfers between devices: 8.98 us -> 30.8 us  [outward(): return lax.ppermute(value, ('band', 'mp'), pairs)]
    all_gather x1 -> x0, waiting for transfers between devices: 18.7 us -> none  [local(): grid_full = lax.all_gather(grid, 'mp', axis=1, tiled=True)]
    ppermute x10 -> x11, starting transfers between devices: 9.78 us -> 1.22 us  [swap(): return lax.ppermute(value, 'mp', [(0, 1), (1, 0)])]
    ppermute x10 -> x11, waiting for transfers between devices: 6.84 us -> 10 us  [swap(): return lax.ppermute(value, 'mp', [(0, 1), (1, 0)])]
    all_to_all x2 -> x3, blocking collectives: 58.3 us -> 59.3 us  [exchange(): lax.all_to_all(value, 'band', 0, 0, tiled=True, axis_index_groups=groups)]
    unnamed x23 -> x21, local copies, waits for them, and re-layouts: 5.04 us -> 4.81 us
  transfers between devices with their start and end apart: 19 -> 19, of which waited for: 15 -> 16; matrix products, arithmetic and copies ran while one was open for 1% -> 1% of each run, Pallas kernels for 2% -> 2%
where the time goes in v3:
time: 158 us
  blocking collectives  59.3 us (38%)
  waiting for transfers between devices  34.9 us (22%)
  starting transfers between devices  32 us (20%)
  Pallas kernels  25.3 us (16%)
  local copies, waits for them, and re-layouts  4.91 us (3%)
    all_to_all x3, blocking collectives, exchange(): lax.all_to_all(value, 'band', 0, 0, tiled=True, axis_index_groups=groups)  59.3 us
    ppermute x8, starting transfers between devices, outward(): return lax.ppermute(value, ('band', 'mp'), pairs)  30.8 us
    ppermute x8, waiting for transfers between devices, outward(): return lax.ppermute(value, ('band', 'mp'), pairs)  24.9 us
    ppermute x11, waiting for transfers between devices, swap(): return lax.ppermute(value, 'mp', [(0, 1), (1, 0)])  10 us
    pallas_call x1, Pallas kernels, local(): pl.pallas_call(decode_kernel, grid_spec=pltpu.PrefetchScalarGridSpec(num_...  9.54 us
    pallas_call x1, Pallas kernels, local(): pl.pallas_call(encode_kernel, grid_spec=pltpu.PrefetchScalarGridSpec(num_...  6.02 us
    unnamed x21, local copies, waits for them, and re-layouts  4.81 us
    pallas_call x1, Pallas kernels, local(): pl.pallas_call(encoder_grad_kernel, grid_spec=pltpu.PrefetchScalarGridSpe...  4.6 us
  transfers between devices with their start and end apart: 19, of which 16 were waited for; matrix products, arithmetic and copies ran while one was open for 1% of the time, Pallas kernels for 2%

profile of v3, /device:TPU:8, one launch (start us, length us, event | category | flops | bytes accessed | tf_op | source)
XLA Modules:
  0.0 157.9 jit_solution(4570571166592433849)
XLA Ops:
  1.5 1.5 collective-permute-done.1.g_other_ref
  3.0 1.3 copy-done
  4.3 1.1 copy-done.1
  7.0 6.0 %shard_map.103 = (bf16[5120,512]{1,0:T(8,128)(2,1)S(1)}, bf16[5120,256]{1,0:T(8,128)(2,1)S(1)}, bf16[256,256]{1,0:T(8,128)(2,1)S(1)}, bf16[2,256,256]{2,1,0:T(8,128)(2,1)S(1)}, bf16[2,256,256]{2,1,0:T(8,128)(2,1)S(1)}) custom-call(s32[10,4]{1,0:T(8,128)S(1)} %copy.12.pm, s32[10]{0:T(128)S(1)} %copy-done.7, bf16[10,4,128,128]{3,2,1,0:T(8,128)(2,1)S(1)} %copy-done, ...), custom_call_target="tpu_custom_call" | custom-call | tf_op jit(solution)/shard_map/pallas_call | solution.py:274
  13.3 1.4 collective-permute-done.2
  14.8 4.3 %collective-permute-start.4 = (bf16[2,256,256]{2,1,0:T(8,128)(2,1)S(1)}, bf16[2,256,256]{2,1,0:T(8,128)(2,1)S(1)}, u32[]{:S(2)}, u32[]{:S(2)}) collective-permute-start(bf16[2,256,256]{2,1,0:T(8,128)(2,1)S(1)} %pad_maximum_fusion.1), channel_id=1, source_target_pairs={{0,4},{5,1},{2,6},{7,3},{4,8},{9,5},{6,10},{11,7},{8,12},{13,9},{1... | collective-permute-start | bytes 786440 | tf_op jit(solution)/shard_map/ppermute | solution.py:28
  19.2 2.4 %collective-permute-start.3 = (bf16[2,256,256]{2,1,0:T(8,128)(2,1)S(1)}, bf16[2,256,256]{2,1,0:T(8,128)(2,1)S(1)}, u32[]{:S(2)}, u32[]{:S(2)}) collective-permute-start(bf16[2,256,256]{2,1,0:T(8,128)(2,1)S(1)} %pad_maximum_fusion), channel_id=1, source_target_pairs={{0,2},{3,1},{2,4},{5,3},{4,6},{7,5},{6,8},{9,7},{8,10},{11,9},{10,... | collective-permute-start | bytes 786440 | tf_op jit(solution)/shard_map/ppermute | solution.py:28
  21.6 6.8 %collective-permute-done.4 = bf16[2,256,256]{2,1,0:T(8,128)(2,1)S(1)} collective-permute-done((bf16[2,256,256]{2,1,0:T(8,128)(2,1)S(1)}, bf16[2,256,256]{2,1,0:T(8,128)(2,1)S(1)}, u32[]{:S(2)}, u32[]{:S(2)}) %collective-permute-start.4) | collective-permute-done | bytes 262176 | tf_op jit(solution)/shard_map/ppermute | solution.py:28
  28.5 2.0 %collective-permute-done.3 = bf16[2,256,256]{2,1,0:T(8,128)(2,1)S(1)} collective-permute-done((bf16[2,256,256]{2,1,0:T(8,128)(2,1)S(1)}, bf16[2,256,256]{2,1,0:T(8,128)(2,1)S(1)}, u32[]{:S(2)}, u32[]{:S(2)}) %collective-permute-start.3) | collective-permute-done | bytes 262176 | tf_op jit(solution)/shard_map/ppermute | solution.py:28
  31.2 1.0 collective-permute-done.5
  32.5 3.3 %collective-permute-start.6 = (bf16[2,256,256]{2,1,0:T(8,128)(2,1)S(1)}, bf16[2,256,256]{2,1,0:T(8,128)(2,1)S(1)}, u32[]{:S(2)}, u32[]{:S(2)}) collective-permute-start(bf16[2,256,256]{2,1,0:T(8,128)(2,1)S(1)} %add_convert_fusion.m), channel_id=1, source_target_pairs={{0,2},{3,1},{2,4},{5,3},{4,6},{7,5},{6,8},{9,7},{8,10},{11,9},{10,... | collective-permute-start | bytes 786440 | tf_op jit(solution)/shard_map/ppermute | solution.py:28
  35.9 3.9 %collective-permute-start.7 = (bf16[2,256,256]{2,1,0:T(8,128)(2,1)S(1)}, bf16[2,256,256]{2,1,0:T(8,128)(2,1)S(1)}, u32[]{:S(2)}, u32[]{:S(2)}) collective-permute-start(bf16[2,256,256]{2,1,0:T(8,128)(2,1)S(1)} %add_convert_fusion.m), channel_id=1, source_target_pairs={{0,4},{5,1},{2,6},{7,3},{4,8},{9,5},{6,10},{11,7},{8,12},{13,9},{1... | collective-permute-start | bytes 786440 | tf_op jit(solution)/shard_map/ppermute | solution.py:28
  39.8 1.0 collective-permute-done.6.q1
  40.8 5.0 %collective-permute-done.7.q2 = bf16[2,256,256]{2,1,0:T(8,128)(2,1)S(1)} collective-permute-done((bf16[2,256,256]{2,1,0:T(8,128)(2,1)S(1)}, bf16[2,256,256]{2,1,0:T(8,128)(2,1)S(1)}, u32[]{:S(2)}, u32[]{:S(2)}) %collective-permute-start.7) | collective-permute-done | bytes 262176 | tf_op jit(solution)/shard_map/ppermute | solution.py:28
  45.8 1.5 collective-permute-done.9.t2
  47.3 9.5 %shard_map.104 = (bf16[1280,256]{1,0:T(8,128)(2,1)}, bf16[5120,512]{1,0:T(8,128)(2,1)S(1)}, bf16[5120,256]{1,0:T(8,128)(2,1)S(1)}, bf16[256,256]{1,0:T(8,128)(2,...) custom-call(s32[10,4]{1,0:T(8,128)S(1)} %copy.12.pm, s32[10]{0:T(128)S(1)} %copy-done.7, ...), custom_call_target="tpu_custom_call" | custom-call | tf_op jit(solution)/shard_map/pallas_call | solution.py:292
  57.0 1.4 collective-permute-done.10
  58.5 6.0 %collective-permute-start.12 = (bf16[2,256,256]{2,1,0:T(8,128)(2,1)S(1)}, bf16[2,256,256]{2,1,0:T(8,128)(2,1)S(1)}, u32[]{:S(2)}, u32[]{:S(2)}) collective-permute-start(bf16[2,256,256]{2,1,0:T(8,128)(2,1)S(1)} %pad_maximum_fusion.4), channel_id=1, source_target_pairs={{0,4},{5,1},{2,6},{7,3},{4,8},{9,5},{6,10},{11,7},{8,12},{13,9},{1... | collective-permute-start | bytes 786440 | tf_op jit(solution)/shard_map/ppermute | solution.py:28
  64.5 3.1 %collective-permute-start.11 = (bf16[2,256,256]{2,1,0:T(8,128)(2,1)S(1)}, bf16[2,256,256]{2,1,0:T(8,128)(2,1)S(1)}, u32[]{:S(2)}, u32[]{:S(2)}) collective-permute-start(bf16[2,256,256]{2,1,0:T(8,128)(2,1)S(1)} %pad_maximum_fusion.3), channel_id=1, source_target_pairs={{0,2},{3,1},{2,4},{5,3},{4,6},{7,5},{6,8},{9,7},{8,10},{11,9},{10,... | collective-permute-start | bytes 786440 | tf_op jit(solution)/shard_map/ppermute | solution.py:28
  67.7 3.6 %shard_map.105.dec_ref = f32[512,256]{1,0:T(8,128)S(1)} custom-call(bf16[5120,512]{1,0:T(8,128)(2,1)S(1)} %get-tuple-element.31.left_ref, bf16[5120,256]{1,0:T(8,128)(2,1)S(1)} %get-tuple-element.32.right_ref), custom_call_target="tpu_custom_call" | custom-call | flops 1342177280 | bytes 7864320 | tf_op jit(solution)/shard_map/pallas_call | solution.py:314
  71.3 2.2 %collective-permute-done.12 = bf16[2,256,256]{2,1,0:T(8,128)(2,1)S(1)} collective-permute-done((bf16[2,256,256]{2,1,0:T(8,128)(2,1)S(1)}, bf16[2,256,256]{2,1,0:T(8,128)(2,1)S(1)}, u32[]{:S(2)}, u32[]{:S(2)}) %collective-permute-start.12) | collective-permute-done | bytes 262176 | tf_op jit(solution)/shard_map/ppermute | solution.py:28
  73.5 2.4 %collective-permute-done.11 = bf16[2,256,256]{2,1,0:T(8,128)(2,1)S(1)} collective-permute-done((bf16[2,256,256]{2,1,0:T(8,128)(2,1)S(1)}, bf16[2,256,256]{2,1,0:T(8,128)(2,1)S(1)}, u32[]{:S(2)}, u32[]{:S(2)}) %collective-permute-start.11) | collective-permute-done | bytes 262176 | tf_op jit(solution)/shard_map/ppermute | solution.py:28
  76.1 1.5 collective-permute-done.13.t
  78.0 3.3 %collective-permute-start.15 = (bf16[2,256,256]{2,1,0:T(8,128)(2,1)S(1)}, bf16[2,256,256]{2,1,0:T(8,128)(2,1)S(1)}, u32[]{:S(2)}, u32[]{:S(2)}) collective-permute-start(bf16[2,256,256]{2,1,0:T(8,128)(2,1)S(1)} %shard_map.106.m), channel_id=1, source_target_pairs={{0,2},{3,1},{2,4},{5,3},{4,6},{7,5},{6,8},{9,7},{8,10},{11,9},{10,... | collective-permute-start | bytes 786440 | tf_op jit(solution)/shard_map/ppermute | solution.py:28
  81.4 4.4 %collective-permute-start.16 = (bf16[2,256,256]{2,1,0:T(8,128)(2,1)S(1)}, bf16[2,256,256]{2,1,0:T(8,128)(2,1)S(1)}, u32[]{:S(2)}, u32[]{:S(2)}) collective-permute-start(bf16[2,256,256]{2,1,0:T(8,128)(2,1)S(1)} %shard_map.106.m), channel_id=1, source_target_pairs={{0,4},{5,1},{2,6},{7,3},{4,8},{9,5},{6,10},{11,7},{8,12},{13,9},{1... | collective-permute-start | bytes 786440 | tf_op jit(solution)/shard_map/ppermute | solution.py:28
  86.3 5.0 %collective-permute-done.16.q2 = bf16[2,256,256]{2,1,0:T(8,128)(2,1)S(1)} collective-permute-done((bf16[2,256,256]{2,1,0:T(8,128)(2,1)S(1)}, bf16[2,256,256]{2,1,0:T(8,128)(2,1)S(1)}, u32[]{:S(2)}, u32[]{:S(2)}) %collective-permute-start.16) | collective-permute-done | bytes 262176 | tf_op jit(solution)/shard_map/ppermute | solution.py:28
  91.3 1.5 collective-permute-done.18.t2
  92.8 4.6 %shard_map.107 = bf16[2048,128]{1,0:T(8,128)(2,1)S(1)} custom-call(s32[10,4]{1,0:T(8,128)S(1)} %copy.12.pm, s32[10]{0:T(128)S(1)} %copy-done.8, bf16[5120,512]{1,0:T(8,128)(2,1)S(1)} %get-tuple-element.27.x_ref, bf16[5120,256]{1,0:T(8,128)(2,1)S(1)} %copy-done.3, bf16[2,256,256]{2,1,0:T(8,128)(2,1)S(1)} %shard_map.106.m, ...), custom_call_target="tpu_custom_call" | custom-call | tf_op jit(solution)/shard_map/pallas_call | solution.py:333
  97.4 23.7 %all_to_all.15.parts_ref = bf16[16,128,128]{2,1,0:T(8,128)(2,1)S(1)} all-to-all(bf16[16,128,128]{2,1,0:T(8,128)(2,1)S(1)} %bitcast.24), channel_id=1, replica_groups={{0,2,4,6,8,10,12,14,16,18,20,22,24,26,28,30},{32,34,36,38,40,42,44,46,4..., dimensions={0} | all-to-all | bytes 1048576 | tf_op jit(solution)/shard_map/all_to_all | solution.py:213
  121.3 21.3 %all_to_all.16.parts_ref = bf16[8,128,128]{2,1,0:T(8,128)(2,1)S(1)} all-to-all(bf16[8,128,128]{2,1,0:T(8,128)(2,1)S(1)} %shard_map.108), channel_id=1, replica_groups={{0,32,64,96,128,160,192,224},{2,34,66,98,130,162,194,226},{4,36,68,100,..., dimensions={0} | all-to-all | bytes 524288 | tf_op jit(solution)/shard_map/all_to_all | solution.py:213
  142.6 14.3 %all_to_all.17 = bf16[16,128,128]{2,1,0:T(8,128)(2,1)S(1)} all-to-all(bf16[16,128,128]{2,1,0:T(8,128)(2,1)S(1)} %shard_map.109), channel_id=1, replica_groups={{0,2,4,6,8,10,12,14,16,18,20,22,24,26,28,30},{32,34,36,38,40,42,44,46,4..., dimensions={0} | all-to-all | bytes 1048576 | tf_op jit(solution)/shard_map/all_to_all | solution.py:213
  156.9 1.0 shard_map.110
  (56 shorter events, 5.4 us)
Async XLA Ops:
  0.6 2.4 %collective-permute-start.1 = (bf16[1280,256]{1,0:T(8,128)(2,1)}, bf16[1280,256]{1,0:T(8,128)(2,1)S(1)}, u32[]{:S(2)}, u32[]{:S(2)}) collective-permute-start(bf16[1280,256]{1,0:T(8,128)(2,1)} %g_ref.3), channel_id=1, source_target_pairs={{0,1},{1,0},{2,3},{3,2},{4,5},{5,4},{6,7},{7,6},{8,9},{9,8},{10,11... | collective-permute-start | bytes 1966088 | tf_op jit(solution)/shard_map/ppermute | solution.py:19
  3.0 1.3 copy-start
  4.3 1.1 copy-start.1
  5.4 0.9 copy-start.6
  6.4 0.7 copy-start.7
  13.1 19.2 %copy-start.2 = (bf16[5120,256]{1,0:T(8,128)(2,1)}, bf16[5120,256]{1,0:T(8,128)(2,1)S(1)}, u32[]{:S(2)}) copy-start(bf16[5120,256]{1,0:T(8,128)(2,1)S(1)} %get-tuple-element.28.slope_ref) | copy-start | bytes 7864324
  13.1 17.6 %copy-start.9 = (bf16[256,256]{1,0:T(8,128)(2,1)S(1)}, bf16[256,256]{1,0:T(8,128)(2,1)}, u32[]{:S(2)}) copy-start(bf16[256,256]{1,0:T(8,128)(2,1)} %param.10) | copy-start | bytes 393220
  13.1 1.6 %collective-permute-start.2 = (bf16[2,256,256]{2,1,0:T(8,128)(2,1)S(1)}, bf16[2,256,256]{2,1,0:T(8,128)(2,1)S(1)}, u32[]{:S(2)}, u32[]{:S(2)}) collective-permute-start(bf16[2,256,256]{2,1,0:T(8,128)(2,1)S(1)} %get-tuple-element.22), channel_id=1, source_target_pairs={{0,1},{1,0},{2,3},{3,2},{4,5},{5,4},{6,7},{7,6},{8,9},{9,8},{10,11... | collective-permute-start | bytes 786440 | tf_op jit(solution)/shard_map/ppermute | solution.py:19
  14.8 32.6 %copy-start.4 = (bf16[512,256]{1,0:T(8,128)(2,1)S(1)}, bf16[512,256]{1,0:T(8,128)(2,1)}, u32[]{:S(2)}) copy-start(bf16[512,256]{1,0:T(8,128)(2,1)} %w_own.1) | copy-start | bytes 786436
  14.8 32.6 %copy-start.5 = (bf16[1280,256]{1,0:T(8,128)(2,1)S(1)}, bf16[1280,256]{1,0:T(8,128)(2,1)}, u32[]{:S(2)}) copy-start(bf16[1280,256]{1,0:T(8,128)(2,1)} %cot_ref.1) | copy-start | bytes 1966084
  14.8 13.7 %collective-permute-start.4 = (bf16[2,256,256]{2,1,0:T(8,128)(2,1)S(1)}, bf16[2,256,256]{2,1,0:T(8,128)(2,1)S(1)}, u32[]{:S(2)}, u32[]{:S(2)}) collective-permute-start(bf16[2,256,256]{2,1,0:T(8,128)(2,1)S(1)} %pad_maximum_fusion.1), channel_id=1, source_target_pairs={{0,4},{5,1},{2,6},{7,3},{4,8},{9,5},{6,10},{11,7},{8,12},{13,9},{1... | collective-permute-start | bytes 786440 | tf_op jit(solution)/shard_map/ppermute | solution.py:28
  19.2 11.3 %collective-permute-start.3 = (bf16[2,256,256]{2,1,0:T(8,128)(2,1)S(1)}, bf16[2,256,256]{2,1,0:T(8,128)(2,1)S(1)}, u32[]{:S(2)}, u32[]{:S(2)}) collective-permute-start(bf16[2,256,256]{2,1,0:T(8,128)(2,1)S(1)} %pad_maximum_fusion), channel_id=1, source_target_pairs={{0,2},{3,1},{2,4},{5,3},{4,6},{7,5},{6,8},{9,7},{8,10},{11,9},{10,... | collective-permute-start | bytes 786440 | tf_op jit(solution)/shard_map/ppermute | solution.py:28
  30.6 1.6 %collective-permute-start.5 = (bf16[2,256,256]{2,1,0:T(8,128)(2,1)S(1)}, bf16[2,256,256]{2,1,0:T(8,128)(2,1)S(1)}, u32[]{:S(2)}, u32[]{:S(2)}) collective-permute-start(bf16[2,256,256]{2,1,0:T(8,128)(2,1)S(1)} %pad_maximum_fusion.2), channel_id=1, source_target_pairs={{0,1},{1,0},{2,3},{3,2},{4,5},{5,4},{6,7},{7,6},{8,9},{9,8},{10,11... | collective-permute-start | bytes 786440 | tf_op jit(solution)/shard_map/ppermute | solution.py:19
  30.7 1.7 %collective-permute-start = (bf16[256,256]{1,0:T(8,128)(2,1)S(1)}, bf16[256,256]{1,0:T(8,128)(2,1)S(1)}, u32[]{:S(2)}, u32[]{:S(2)}) collective-permute-start(bf16[256,256]{1,0:T(8,128)(2,1)S(1)} %copy-done.9), channel_id=1, source_target_pairs={{0,1},{1,0},{2,3},{3,2},{4,5},{5,4},{6,7},{7,6},{8,9},{9,8},{10,11... | collective-permute-start | bytes 393224 | tf_op jit(solution)/shard_map/ppermute | solution.py:19
  32.5 8.3 %collective-permute-start.6 = (bf16[2,256,256]{2,1,0:T(8,128)(2,1)S(1)}, bf16[2,256,256]{2,1,0:T(8,128)(2,1)S(1)}, u32[]{:S(2)}, u32[]{:S(2)}) collective-permute-start(bf16[2,256,256]{2,1,0:T(8,128)(2,1)S(1)} %add_convert_fusion.m), channel_id=1, source_target_pairs={{0,2},{3,1},{2,4},{5,3},{4,6},{7,5},{6,8},{9,7},{8,10},{11,9},{10,... | collective-permute-start | bytes 786440 | tf_op jit(solution)/shard_map/ppermute | solution.py:28
  35.9 9.9 %collective-permute-start.7 = (bf16[2,256,256]{2,1,0:T(8,128)(2,1)S(1)}, bf16[2,256,256]{2,1,0:T(8,128)(2,1)S(1)}, u32[]{:S(2)}, u32[]{:S(2)}) collective-permute-start(bf16[2,256,256]{2,1,0:T(8,128)(2,1)S(1)} %add_convert_fusion.m), channel_id=1, source_target_pairs={{0,4},{5,1},{2,6},{7,3},{4,8},{9,5},{6,10},{11,7},{8,12},{13,9},{1... | collective-permute-start | bytes 786440 | tf_op jit(solution)/shard_map/ppermute | solution.py:28
  40.8 5.0 %collective-permute-start.8 = (bf16[2,256,256]{2,1,0:T(8,128)(2,1)S(1)}, bf16[2,256,256]{2,1,0:T(8,128)(2,1)S(1)}, u32[]{:S(2)}, u32[]{:S(2)}) collective-permute-start(bf16[2,256,256]{2,1,0:T(8,128)(2,1)S(1)} %collective-permute-done.6.q1), channel_id=1, source_target_pairs={{0,1},{1,0},{2,3},{3,2},{4,5},{5,4},{6,7},{7,6},{8,9},{9,8},{10,11... | collective-permute-start | bytes 786440 | tf_op jit(solution)/shard_map/ppermute | solution.py:19
  45.8 1.5 collective-permute-start.9
  56.9 1.5 collective-permute-start.10
  58.5 15.0 %collective-permute-start.12 = (bf16[2,256,256]{2,1,0:T(8,128)(2,1)S(1)}, bf16[2,256,256]{2,1,0:T(8,128)(2,1)S(1)}, u32[]{:S(2)}, u32[]{:S(2)}) collective-permute-start(bf16[2,256,256]{2,1,0:T(8,128)(2,1)S(1)} %pad_maximum_fusion.4), channel_id=1, source_target_pairs={{0,4},{5,1},{2,6},{7,3},{4,8},{9,5},{6,10},{11,7},{8,12},{13,9},{1... | collective-permute-start | bytes 786440 | tf_op jit(solution)/shard_map/ppermute | solution.py:28
  64.5 11.4 %collective-permute-start.11 = (bf16[2,256,256]{2,1,0:T(8,128)(2,1)S(1)}, bf16[2,256,256]{2,1,0:T(8,128)(2,1)S(1)}, u32[]{:S(2)}, u32[]{:S(2)}) collective-permute-start(bf16[2,256,256]{2,1,0:T(8,128)(2,1)S(1)} %pad_maximum_fusion.3), channel_id=1, source_target_pairs={{0,2},{3,1},{2,4},{5,3},{4,6},{7,5},{6,8},{9,7},{8,10},{11,9},{10,... | collective-permute-start | bytes 786440 | tf_op jit(solution)/shard_map/ppermute | solution.py:28
  67.6 8.5 %collective-permute-start.14 = (bf16[512,256]{1,0:T(8,128)(2,1)S(1)}, bf16[512,256]{1,0:T(8,128)(2,1)S(1)}, u32[]{:S(2)}, u32[]{:S(2)}) collective-permute-start(bf16[512,256]{1,0:T(8,128)(2,1)S(1)} %copy-done.4), channel_id=1, source_target_pairs={{0,1},{1,0},{2,3},{3,2},{4,5},{5,4},{6,7},{7,6},{8,9},{9,8},{10,11... | collective-permute-start | bytes 786440 | tf_op jit(solution)/shard_map/ppermute | solution.py:19
  71.3 21.5 %copy-start.3 = (bf16[5120,256]{1,0:T(8,128)(2,1)S(1)}, bf16[5120,256]{1,0:T(8,128)(2,1)}, u32[]{:S(2)}) copy-start(bf16[5120,256]{1,0:T(8,128)(2,1)} %copy-done.2) | copy-start | bytes 7864324
  71.3 21.5 %copy-start.8 = (s32[10]{0:T(128)S(1)}, s32[10]{0:T(128)}, u32[]{:S(2)}) copy-start(s32[10]{0:T(128)} %pc.5) | copy-start | bytes 124
  76.0 1.6 %collective-permute-start.13 = (bf16[2,256,256]{2,1,0:T(8,128)(2,1)S(1)}, bf16[2,256,256]{2,1,0:T(8,128)(2,1)S(1)}, u32[]{:S(2)}, u32[]{:S(2)}) collective-permute-start(bf16[2,256,256]{2,1,0:T(8,128)(2,1)S(1)} %pad_maximum_fusion.5.s), channel_id=1, source_target_pairs={{0,1},{1,0},{2,3},{3,2},{4,5},{5,4},{6,7},{7,6},{8,9},{9,8},{10,11... | collective-permute-start | bytes 786440 | tf_op jit(solution)/shard_map/ppermute | solution.py:19
  78.0 8.3 %collective-permute-start.15 = (bf16[2,256,256]{2,1,0:T(8,128)(2,1)S(1)}, bf16[2,256,256]{2,1,0:T(8,128)(2,1)S(1)}, u32[]{:S(2)}, u32[]{:S(2)}) collective-permute-start(bf16[2,256,256]{2,1,0:T(8,128)(2,1)S(1)} %shard_map.106.m), channel_id=1, source_target_pairs={{0,2},{3,1},{2,4},{5,3},{4,6},{7,5},{6,8},{9,7},{8,10},{11,9},{10,... | collective-permute-start | bytes 786440 | tf_op jit(solution)/shard_map/ppermute | solution.py:28
  81.4 9.9 %collective-permute-start.16 = (bf16[2,256,256]{2,1,0:T(8,128)(2,1)S(1)}, bf16[2,256,256]{2,1,0:T(8,128)(2,1)S(1)}, u32[]{:S(2)}, u32[]{:S(2)}) collective-permute-start(bf16[2,256,256]{2,1,0:T(8,128)(2,1)S(1)} %shard_map.106.m), channel_id=1, source_target_pairs={{0,4},{5,1},{2,6},{7,3},{4,8},{9,5},{6,10},{11,7},{8,12},{13,9},{1... | collective-permute-start | bytes 786440 | tf_op jit(solution)/shard_map/ppermute | solution.py:28
  86.3 5.0 %collective-permute-start.17 = (bf16[2,256,256]{2,1,0:T(8,128)(2,1)S(1)}, bf16[2,256,256]{2,1,0:T(8,128)(2,1)S(1)}, u32[]{:S(2)}, u32[]{:S(2)}) collective-permute-start(bf16[2,256,256]{2,1,0:T(8,128)(2,1)S(1)} %collective-permute-done.15.q1), channel_id=1, source_target_pairs={{0,1},{1,0},{2,3},{3,2},{4,5},{5,4},{6,7},{7,6},{8,9},{9,8},{10,11... | collective-permute-start | bytes 786440 | tf_op jit(solution)/shard_map/ppermute | solution.py:19
  91.3 1.5 collective-permute-start.18

commit v4 on v3

v4 whole, which is shorter than its diff:
```python
import jax
import jax.numpy as jnp
from jax import lax
from jax.experimental import pallas as pl
from jax.experimental.pallas import tpu as pltpu
from jax.sharding import PartitionSpec as P

REACH = 2
NEAR = 2 * REACH + 1
OWNER_BLOCKS = 2

FL, BF = jnp.float32, jnp.bfloat16
ROWS_BY_ROWS = (((0,), (0,)), ((), ()))
COLS_BY_COLS = (((1,), (1,)), ((), ()))


def dot(left, right, dims=(((1,), (0,)), ((), ()))):
    return lax.dot_general(left, right, dims, preferred_element_type=FL)


def swap(value):
    return lax.ppermute(value, "mp", [(0, 1), (1, 0)])


def outward(value, steps):
    count = lax.axis_size("band")
    pairs = []
    for band in range(count - steps):
        pairs.append((2 * band, 2 * (band + steps)))
        pairs.append((2 * (band + steps) + 1, 2 * band + 1))
    return lax.ppermute(value, ("band", "mp"), pairs)


def place(pm, block, slot, facing):
    target = pm[slot, block]
    offset = target // OWNER_BLOCKS - lax.axis_index("band")
    along = jnp.where(lax.axis_index("mp") == 0, offset, -offset) * facing
    along = jnp.clip(along, -REACH, REACH)
    stored = jnp.where(along >= 0, along, REACH - along)
    return stored * OWNER_BLOCKS + target % OWNER_BLOCKS


def live_of(pc, block, slot):
    return jnp.where(slot < pc[block], 1.0, 0.0).astype(FL)


def split_slabs(total, own, mine, other):
    blocks = own.shape[0] // total.shape[1]
    own[...] = total[:blocks].reshape(own.shape).astype(own.dtype)
    mine[...] = total[blocks : 3 * blocks].reshape(mine.shape).astype(mine.dtype)
    other[...] = total[3 * blocks :].reshape(other.shape).astype(other.dtype)


def sigmoid(value):
    return 0.5 * jnp.tanh(0.5 * value) + 0.5


def fetch(pairs, sems):
    copies = [pltpu.make_async_copy(src, dst, sems.at[at]) for at, (src, dst) in enumerate(pairs)]
    for copy in copies:
        copy.start()
    return copies


def encode_kernel(
    pm, pc, a_hbm, g_hbm, w_hbm, g_other, a_ref, x_ref, slope_ref, own, mine, other,
    total, g_ref, w_ref, sems,
):
    blocks, slots, rows, points = a_ref.shape
    pairs = slots * rows
    early = min(2, blocks)
    head, tail = pl.ds(0, early), pl.ds(early, blocks - early)
    copies = fetch(
        [(g_hbm, g_ref), (a_hbm.at[head], a_ref.at[head]), (w_hbm, w_ref), (a_hbm.at[tail], a_ref.at[tail])],
        sems,
    )
    total[...] = jnp.zeros_like(total)
    first = lax.axis_index("mp") == 0
    for copy in copies[:3]:
        copy.wait()
    for block in range(blocks):
        if block == early:
            copies[3].wait()
        span = slice(block * points, (block + 1) * points)
        g_own, g_far = g_ref[span], g_other[span]
        low, high = jnp.where(first, g_own, g_far), jnp.where(first, g_far, g_own)
        weights = a_ref[block].reshape(pairs, points)
        x = dot(weights, jnp.concatenate([low, high], axis=1)).astype(BF)
        x_ref[block * pairs : (block + 1) * pairs] = x
        u = dot(x, w_ref[...])
        for slot in range(slots):
            part = u[slot * rows : (slot + 1) * rows]
            sig = sigmoid(part)
            edge = part * sig
            live = live_of(pc, block, slot)
            total[place(pm, block, slot, 1)] += edge * live
            slope = (sig + edge * (1.0 - sig)) * (0.25 * live)
            slope_ref[block * pairs + slot * rows : block * pairs + (slot + 1) * rows] = slope.astype(BF)
    split_slabs(total, own, mine, other)


def gather_near(near, refs, picks):
    blocks = near.shape[0] // len(refs)
    rows, width = near.shape[1], near.shape[2] // 2

    def fill(own_at):
        for at, (ref, pick) in enumerate(zip(refs, picks)):
            for half in range(2):
                column = (own_at + half) % 2 * width
                value = ref[half ^ pick].reshape(blocks, rows, width)
                near[at * blocks : (at + 1) * blocks, :, column : column + width] = value

    core = lax.axis_index("mp")
    pl.when(core == 0)(lambda: fill(0))
    pl.when(core == 1)(lambda: fill(1))


def decode_kernel(
    pm, pc, a_ref, g_ref, cot_ref, w_ref, m, q1, q2, t1, t2,
    out_ref, y_ref, dz_ref, own, mine, other, near, total,
):
    blocks, slots, rows, points = a_ref.shape
    pairs = slots * points
    total[...] = jnp.zeros_like(total)
    gather_near(near, (m, q1, q2, t1, t2), (0, 0, 0, 1, 1))
    for block in range(blocks):
        for slot in range(slots):
            chosen = near[place(pm, block, slot, -1)]
            y = dot(a_ref[block, slot], chosen, ROWS_BY_ROWS).astype(BF)
            y_ref[block * pairs + slot * points : block * pairs + (slot + 1) * points] = y
        span = slice(block * points, (block + 1) * points)
        z = dot(y_ref[block * pairs : (block + 1) * pairs], w_ref[...])
        result = g_ref[span].astype(FL)
        upstream = cot_ref[span].astype(FL)
        for slot in range(slots):
            part = z[slot * points : (slot + 1) * points]
            sig = sigmoid(part)
            edge = part * sig
            live = live_of(pc, block, slot)
            result = result + edge * live
            slope = sig + edge * (1.0 - sig)
            dz = ((upstream * live) * slope).astype(BF)
            dz_ref[block * pairs + slot * points : block * pairs + (slot + 1) * points] = dz
            total[place(pm, block, slot, 1)] += dot(a_ref[block, slot], dz)
        out_ref[span] = result.astype(BF)
    split_slabs(total, own, mine, other)


def outer_kernel(left_ref, right_ref, out_ref):
    out_ref[...] = dot(right_ref[...], left_ref[...], ROWS_BY_ROWS)


def mesh_grad_kernel(s, t, w_own, w_other, out):
    half = out.shape[2]
    lift_own = (s[0].astype(FL) + t[1].astype(FL)).astype(BF)
    lift_other = (s[1].astype(FL) + t[0].astype(FL)).astype(BF)
    grad = dot(lift_own, w_own[...], COLS_BY_COLS) + dot(lift_other, w_other[...], COLS_BY_COLS)
    grad = grad.astype(BF)
    core = lax.axis_index("mp")

    @pl.when(core == 0)
    def _():
        out[0], out[1] = grad[:, :half], grad[:, half:]

    @pl.when(core == 1)
    def _():
        out[0], out[1] = grad[:, half:], grad[:, :half]


def encoder_grad_kernel(
    pm, pc, x_ref, slope_ref, m, q1, q2, t1, t2, dec_ref, out_ref, near, total
):
    slots, blocks = pm.shape
    rows = near.shape[1]
    pairs = slots * rows
    for at, ref in enumerate((m, q1, q2, t1, t2)):
        near[at * OWNER_BLOCKS : (at + 1) * OWNER_BLOCKS] = ref[at // 3].reshape(OWNER_BLOCKS, rows, -1)
    for block in range(blocks):
        parts = []
        for slot in range(slots):
            picked = near[place(pm, block, slot, -1)].astype(FL)
            start = block * pairs + slot * rows
            parts.append((picked * slope_ref[start : start + rows].astype(FL)).astype(BF))
        term = dot(jnp.concatenate(parts, axis=0), x_ref[block * pairs : (block + 1) * pairs], ROWS_BY_ROWS)
        total[...] = term if block == 0 else total[...] + term
    count, width = total.shape
    lanes = out_ref.shape[1]
    for at, value in enumerate((total, dec_ref)):
        for tile in range(width // lanes):
            start = (at * width // lanes + tile) * count
            out_ref[start : start + count] = value[:, tile * lanes : (tile + 1) * lanes].astype(BF)


def sum_kernel(parts_ref, out_ref):
    total = parts_ref[...].astype(FL).sum(axis=0).astype(BF)
    out_ref[...] = jnp.broadcast_to(total[None], out_ref.shape)


def finish_kernel(flat_ref, enc_ref, dec_ref):
    lanes = flat_ref.shape[1]
    width, count = enc_ref.shape
    for at, out in enumerate((enc_ref, dec_ref)):
        for tile in range(width // lanes):
            start = (at * width // lanes + tile) * count
            piece = flat_ref[start : start + count].astype(FL)
            out[tile * lanes : (tile + 1) * lanes] = piece.T


def plane_groups(count):
    across = min(16, count // 2)
    plane = [list(range(at, at + across)) for at in range(0, count, across)]
    line = [list(range(at, count, across)) for at in range(across)]
    return plane, line


def exchange(value, groups):
    return lax.all_to_all(value, "band", 0, 0, tiled=True, axis_index_groups=groups)


def params():
    return pltpu.CompilerParams(vmem_limit_bytes=40 * 2**20)


def shape_of(*shape, dtype=BF):
    return jax.ShapeDtypeStruct(shape, dtype)


def simple(kernel, out_shape):
    return pl.pallas_call(kernel, out_shape=out_shape, compiler_params=params())


def combine(own, parts):
    first, second = (part.astype(FL) for part in parts)
    total = first + second
    return jnp.stack([total[0] + own.astype(FL), total[1]]).astype(BF)


def reduce_to_owner(own, mine, other, beside=None):
    got = swap(other)
    parts = [outward(jnp.stack([mine[i], got[i]]), i + 1) for i in range(REACH)]
    parts, beside = lax.optimization_barrier((parts, beside))
    sums = combine(own, parts)
    return sums, swap(sums), beside


def spread_from_owner(value):
    near = [outward(value, i + 1) for i in range(REACH)]
    return [value, *near, *(swap(part) for part in near)]


VMEM, ANY, SMEM = (pl.BlockSpec(memory_space=space) for space in (pltpu.VMEM, pl.ANY, pltpu.SMEM))


def held(kernel, in_specs, out_shape, scratch=(), cost=None):
    return pl.pallas_call(
        kernel,
        in_specs=in_specs,
        out_specs=jax.tree.map(lambda _: VMEM, out_shape),
        out_shape=out_shape,
        scratch_shapes=scratch,
        compiler_params=params(),
        cost_estimate=cost,
    )


def slab_shapes(owner_rows, half):
    return [shape_of(*lead, owner_rows, half) for lead in ((), (REACH,), (REACH,))]


def encode(pair_mesh, pair_count, interp, grid, grid_other, w_enc):
    blocks, slots, rows, points = interp.shape
    full, half = w_enc.shape
    pairs = blocks * slots * rows
    return held(
        encode_kernel,
        [SMEM, SMEM, ANY, ANY, ANY, VMEM],
        [
            shape_of(*interp.shape), shape_of(pairs, full), shape_of(pairs, half),
            *slab_shapes(OWNER_BLOCKS * rows, half),
        ],
        [
            pltpu.VMEM((NEAR * OWNER_BLOCKS, rows, half), FL), pltpu.VMEM(grid.shape, BF),
            pltpu.VMEM(w_enc.shape, BF), pltpu.SemaphoreType.DMA((4,)),
        ],
    )(pair_mesh, pair_count, interp, grid, w_enc, grid_other)


def decode(pair_mesh, pair_count, interp, grid, cotangent, w_dec, near):
    blocks, slots, rows, points = interp.shape
    full, half = w_dec.shape
    pairs = blocks * slots * points
    return held(
        decode_kernel,
        [SMEM, SMEM, *[VMEM] * (4 + NEAR)],
        [
            shape_of(*grid.shape), shape_of(pairs, full), shape_of(pairs, half),
            *slab_shapes(OWNER_BLOCKS * rows, half),
        ],
        [
            pltpu.VMEM((NEAR * OWNER_BLOCKS, rows, full), BF),
            pltpu.VMEM((NEAR * OWNER_BLOCKS, rows, half), FL),
        ],
    )(pair_mesh, pair_count, interp, grid, cotangent, w_dec, *near)


def outer(y, dz):
    pairs, full = y.shape
    half = dz.shape[1]
    cost = pl.CostEstimate(
        flops=2 * pairs * full * half, bytes_accessed=2 * pairs * (full + half), transcendentals=0
    )
    return held(outer_kernel, [VMEM, VMEM], shape_of(half, full, dtype=FL), cost=cost)(y, dz)


def encoder_grad(pair_mesh, pair_count, x, slope, near, grad_dec):
    full, half = x.shape[1], slope.shape[1]
    rows = near[0].shape[1] // OWNER_BLOCKS
    return held(
        encoder_grad_kernel,
        [SMEM, SMEM, *[VMEM] * (3 + NEAR)],
        shape_of(4 * full, half // 2),
        [pltpu.VMEM((NEAR * OWNER_BLOCKS, rows, half), BF), pltpu.VMEM((half, full), FL)],
    )(pair_mesh, pair_count, x, slope, *near, grad_dec)


def local(grid, interp, mesh_init, w_enc, w_dec, cotangent, pair_mesh, pair_count):
    full, half = w_enc.shape
    pair_mesh = pair_mesh.T
    grid_other = swap(grid)
    mesh_both = jnp.stack([mesh_init, swap(mesh_init)])
    w_dec_other = swap(w_dec)

    interp, x, slope, own, mine, other = encode(pair_mesh, pair_count, interp, grid, grid_other, w_enc)
    sums, got, _ = reduce_to_owner(own, mine, other)
    agg = sums.astype(FL) + got.astype(FL)[::-1]
    mesh_lat = (mesh_both.astype(FL) + 0.25 * agg).astype(BF)
    near = spread_from_owner(mesh_lat)

    out, y, dz, own, mine, other = decode(
        pair_mesh, pair_count, interp, grid, cotangent, w_dec, near
    )
    sums, got, grad_dec = reduce_to_owner(own, mine, other, outer(y, dz))
    grad_mesh = simple(mesh_grad_kernel, shape_of(*sums.shape))(sums, got, w_dec, w_dec_other)
    near = spread_from_owner(grad_mesh)
    flat = encoder_grad(pair_mesh, pair_count, x, slope, near, grad_dec)

    plane, line = plane_groups(lax.axis_size("band"))
    across = len(plane[0])
    chunks = exchange(flat.reshape(across, -1, half // 2), plane)
    piece = simple(sum_kernel, shape_of(len(line[0]), *chunks.shape[1:]))(chunks)
    pieces = exchange(piece, line)
    spread = simple(sum_kernel, shape_of(*chunks.shape))(pieces)
    flat = exchange(spread, plane).reshape(flat.shape)
    grads = [shape_of(full, half, dtype=FL)] * 2
    grad_enc, grad_dec = simple(finish_kernel, grads)(flat)
    return (out, grad_enc, grad_dec)


def solution(mesh):
    placed = (
        P("band", "mp"),
        P("band", None, None, None),
        P("band", "mp"),
        P(None, "mp"),
        P(None, "mp"),
        P("band", "mp"),
        P("band", None),
        P("band"),
    )
    return jax.shard_map(
        local,
        mesh=mesh,
        in_specs=placed,
        out_specs=(P("band", "mp"), P(None, "mp"), P(None, "mp")),
        check_vma=False,
    )
```

time: 158 us -> 155 us (0.981)
  Pallas kernels: 25.3 us -> 19.4 us
  waiting for transfers between devices: 34.9 us -> 37.8 us
    pallas_call x5, Pallas kernels: 24.2 us -> 18.1 us  [the longest x1 8.73 us: decode(): held(decode_kernel, [SMEM, SMEM, *[VMEM] * (4 + NEAR)], [shape_of(*grid.s...]
    ppermute x8, waiting for transfers between devices: 24.9 us -> 27 us  [outward(): return lax.ppermute(value, ('band', 'mp'), pairs)]
    unnamed x21 -> x26, local copies, waits for them, and re-layouts: 4.81 us -> 4.73 us
  transfers between devices with their start and end apart: 19 -> 19, of which waited for: 16 -> 16; matrix products, arithmetic and copies ran while one was open for 1% -> 0% of each run, Pallas kernels for 2% -> 1%
where the time goes in v4:
time: 155 us
  blocking collectives  59.3 us (38%)
  waiting for transfers between devices  37.8 us (24%)
  starting transfers between devices  32 us (21%)
  Pallas kernels  19.4 us (13%)
  local copies, waits for them, and re-layouts  4.84 us (3%)
    all_to_all x3, blocking collectives, exchange(): lax.all_to_all(value, 'band', 0, 0, tiled=True, axis_index_groups=groups)  59.3 us
    ppermute x8, starting transfers between devices, outward(): return lax.ppermute(value, ('band', 'mp'), pairs)  30.8 us
    ppermute x8, waiting for transfers between devices, outward(): return lax.ppermute(value, ('band', 'mp'), pairs)  27 us
    ppermute x11, waiting for transfers between devices, swap(): return lax.ppermute(value, 'mp', [(0, 1), (1, 0)])  10.8 us
    pallas_call x1, Pallas kernels, decode(): held(decode_kernel, [SMEM, SMEM, *[VMEM] * (4 + NEAR)], [shape_of(*grid.s...  8.73 us
    pallas_call x1, Pallas kernels, encode(): held(encode_kernel, [SMEM, SMEM, ANY, ANY, ANY, VMEM], [shape_of(*interp....  5.34 us
    unnamed x26, local copies, waits for them, and re-layouts  4.73 us
  transfers between devices with their start and end apart: 19, of which 16 were waited for; matrix products, arithmetic and copies ran while one was open for 0% of the time, Pallas kernels for 1%

profile of v4, /device:TPU:8, one launch (start us, length us, event | category | flops | bytes accessed | tf_op | source)
XLA Modules:
  0.0 154.8 jit_solution(9203297854824474813)
XLA Ops:
  0.7 2.3 %collective-permute-done.g_other = bf16[1280,256]{1,0:T(8,128)(2,1)S(1)} collective-permute-done((bf16[1280,256]{1,0:T(8,128)(2,1)}, bf16[1280,256]{1,0:T(8,128)(2,1)S(1)}, u32[]{:S(2)}, u32[]{:S(2)}) %collective-permute-start) | collective-permute-done | bytes 655392 | tf_op jit(solution)/shard_map/ppermute | solution.py:22
  3.0 1.1 copy-done.2
  4.1 1.3 copy-done.4
  7.7 5.3 %shard_map.103 = (bf16[10,4,128,128]{3,2,1,0:T(8,128)(2,1)S(1)}, bf16[5120,512]{1,0:T(8,128)(2,1)S(1)}, bf16[5120,256]{1,0:T(8,128)(2,1)S(1)}, bf16[256,256]{1,0...) custom-call(s32[4,10]{1,0:T(4,128)S(1)} %bitcast.27, s32[10]{0:T(128)S(1)} %copy-done.10, ...), custom_call_target="tpu_custom_call" | custom-call | tf_op jit(solution)/shard_map/pallas_call | solution.py:274
  13.3 1.4 collective-permute-done.2
  14.8 4.3 %collective-permute-start.4 = (bf16[2,256,256]{2,1,0:T(8,128)(2,1)S(1)}, bf16[2,256,256]{2,1,0:T(8,128)(2,1)S(1)}, u32[]{:S(2)}, u32[]{:S(2)}) collective-permute-start(bf16[2,256,256]{2,1,0:T(8,128)(2,1)S(1)} %pad_maximum_fusion.1), channel_id=1, source_target_pairs={{0,4},{5,1},{2,6},{7,3},{4,8},{9,5},{6,10},{11,7},{8,12},{13,9},{1... | collective-permute-start | bytes 786440 | tf_op jit(solution)/shard_map/ppermute | solution.py:31
  19.2 2.4 %collective-permute-start.3 = (bf16[2,256,256]{2,1,0:T(8,128)(2,1)S(1)}, bf16[2,256,256]{2,1,0:T(8,128)(2,1)S(1)}, u32[]{:S(2)}, u32[]{:S(2)}) collective-permute-start(bf16[2,256,256]{2,1,0:T(8,128)(2,1)S(1)} %pad_maximum_fusion), channel_id=1, source_target_pairs={{0,2},{3,1},{2,4},{5,3},{4,6},{7,5},{6,8},{9,7},{8,10},{11,9},{10,... | collective-permute-start | bytes 786440 | tf_op jit(solution)/shard_map/ppermute | solution.py:31
  21.6 6.8 %collective-permute-done.4 = bf16[2,256,256]{2,1,0:T(8,128)(2,1)S(1)} collective-permute-done((bf16[2,256,256]{2,1,0:T(8,128)(2,1)S(1)}, bf16[2,256,256]{2,1,0:T(8,128)(2,1)S(1)}, u32[]{:S(2)}, u32[]{:S(2)}) %collective-permute-start.4) | collective-permute-done | bytes 262176 | tf_op jit(solution)/shard_map/ppermute | solution.py:31
  28.5 2.0 %collective-permute-done.3 = bf16[2,256,256]{2,1,0:T(8,128)(2,1)S(1)} collective-permute-done((bf16[2,256,256]{2,1,0:T(8,128)(2,1)S(1)}, bf16[2,256,256]{2,1,0:T(8,128)(2,1)S(1)}, u32[]{:S(2)}, u32[]{:S(2)}) %collective-permute-start.3) | collective-permute-done | bytes 262176 | tf_op jit(solution)/shard_map/ppermute | solution.py:31
  31.2 1.0 collective-permute-done.5
  32.5 3.3 %collective-permute-start.6 = (bf16[2,256,256]{2,1,0:T(8,128)(2,1)S(1)}, bf16[2,256,256]{2,1,0:T(8,128)(2,1)S(1)}, u32[]{:S(2)}, u32[]{:S(2)}) collective-permute-start(bf16[2,256,256]{2,1,0:T(8,128)(2,1)S(1)} %add_convert_fusion.m), channel_id=1, source_target_pairs={{0,2},{3,1},{2,4},{5,3},{4,6},{7,5},{6,8},{9,7},{8,10},{11,9},{10,... | collective-permute-start | bytes 786440 | tf_op jit(solution)/shard_map/ppermute | solution.py:31
  35.9 3.9 %collective-permute-start.7 = (bf16[2,256,256]{2,1,0:T(8,128)(2,1)S(1)}, bf16[2,256,256]{2,1,0:T(8,128)(2,1)S(1)}, u32[]{:S(2)}, u32[]{:S(2)}) collective-permute-start(bf16[2,256,256]{2,1,0:T(8,128)(2,1)S(1)} %add_convert_fusion.m), channel_id=1, source_target_pairs={{0,4},{5,1},{2,6},{7,3},{4,8},{9,5},{6,10},{11,7},{8,12},{13,9},{1... | collective-permute-start | bytes 786440 | tf_op jit(solution)/shard_map/ppermute | solution.py:31
  39.8 1.0 collective-permute-done.6.q1
  40.8 5.0 %collective-permute-done.7.q2 = bf16[2,256,256]{2,1,0:T(8,128)(2,1)S(1)} collective-permute-done((bf16[2,256,256]{2,1,0:T(8,128)(2,1)S(1)}, bf16[2,256,256]{2,1,0:T(8,128)(2,1)S(1)}, u32[]{:S(2)}, u32[]{:S(2)}) %collective-permute-start.7) | collective-permute-done | bytes 262176 | tf_op jit(solution)/shard_map/ppermute | solution.py:31
  45.8 1.5 collective-permute-done.9.t2
  47.4 8.7 %shard_map.104 = (bf16[1280,256]{1,0:T(8,128)(2,1)}, bf16[5120,512]{1,0:T(8,128)(2,1)S(1)}, bf16[5120,256]{1,0:T(8,128)(2,1)S(1)}, bf16[256,256]{1,0:T(8,128)(2,...) custom-call(s32[4,10]{1,0:T(4,128)S(1)} %bitcast.28, s32[10]{0:T(128)S(1)} %copy-done.10, ...), custom_call_target="tpu_custom_call" | custom-call | tf_op jit(solution)/shard_map/pallas_call | solution.py:292
  56.2 1.4 collective-permute-done.10
  57.7 6.0 %collective-permute-start.12 = (bf16[2,256,256]{2,1,0:T(8,128)(2,1)S(1)}, bf16[2,256,256]{2,1,0:T(8,128)(2,1)S(1)}, u32[]{:S(2)}, u32[]{:S(2)}) collective-permute-start(bf16[2,256,256]{2,1,0:T(8,128)(2,1)S(1)} %pad_maximum_fusion.4), channel_id=1, source_target_pairs={{0,4},{5,1},{2,6},{7,3},{4,8},{9,5},{6,10},{11,7},{8,12},{13,9},{1... | collective-permute-start | bytes 786440 | tf_op jit(solution)/shard_map/ppermute | solution.py:31
  63.7 3.1 %collective-permute-start.11 = (bf16[2,256,256]{2,1,0:T(8,128)(2,1)S(1)}, bf16[2,256,256]{2,1,0:T(8,128)(2,1)S(1)}, u32[]{:S(2)}, u32[]{:S(2)}) collective-permute-start(bf16[2,256,256]{2,1,0:T(8,128)(2,1)S(1)} %pad_maximum_fusion.3), channel_id=1, source_target_pairs={{0,2},{3,1},{2,4},{5,3},{4,6},{7,5},{6,8},{9,7},{8,10},{11,9},{10,... | collective-permute-start | bytes 786440 | tf_op jit(solution)/shard_map/ppermute | solution.py:31
  66.9 1.5 shard_map.105.dec_ref
  68.5 4.3 %collective-permute-done.12 = bf16[2,256,256]{2,1,0:T(8,128)(2,1)S(1)} collective-permute-done((bf16[2,256,256]{2,1,0:T(8,128)(2,1)S(1)}, bf16[2,256,256]{2,1,0:T(8,128)(2,1)S(1)}, u32[]{:S(2)}, u32[]{:S(2)}) %collective-permute-start.12) | collective-permute-done | bytes 262176 | tf_op jit(solution)/shard_map/ppermute | solution.py:31
  72.7 2.4 %collective-permute-done.11 = bf16[2,256,256]{2,1,0:T(8,128)(2,1)S(1)} collective-permute-done((bf16[2,256,256]{2,1,0:T(8,128)(2,1)S(1)}, bf16[2,256,256]{2,1,0:T(8,128)(2,1)S(1)}, u32[]{:S(2)}, u32[]{:S(2)}) %collective-permute-start.11) | collective-permute-done | bytes 262176 | tf_op jit(solution)/shard_map/ppermute | solution.py:31
  75.4 1.5 collective-permute-done.13.t
  77.2 3.3 %collective-permute-start.15 = (bf16[2,256,256]{2,1,0:T(8,128)(2,1)S(1)}, bf16[2,256,256]{2,1,0:T(8,128)(2,1)S(1)}, u32[]{:S(2)}, u32[]{:S(2)}) collective-permute-start(bf16[2,256,256]{2,1,0:T(8,128)(2,1)S(1)} %shard_map.106.m), channel_id=1, source_target_pairs={{0,2},{3,1},{2,4},{5,3},{4,6},{7,5},{6,8},{9,7},{8,10},{11,9},{10,... | collective-permute-start | bytes 786440 | tf_op jit(solution)/shard_map/ppermute | solution.py:31
  80.6 4.4 %collective-permute-start.16 = (bf16[2,256,256]{2,1,0:T(8,128)(2,1)S(1)}, bf16[2,256,256]{2,1,0:T(8,128)(2,1)S(1)}, u32[]{:S(2)}, u32[]{:S(2)}) collective-permute-start(bf16[2,256,256]{2,1,0:T(8,128)(2,1)S(1)} %shard_map.106.m), channel_id=1, source_target_pairs={{0,4},{5,1},{2,6},{7,3},{4,8},{9,5},{6,10},{11,7},{8,12},{13,9},{1... | collective-permute-start | bytes 786440 | tf_op jit(solution)/shard_map/ppermute | solution.py:31
  85.5 5.0 %collective-permute-done.16.q2 = bf16[2,256,256]{2,1,0:T(8,128)(2,1)S(1)} collective-permute-done((bf16[2,256,256]{2,1,0:T(8,128)(2,1)S(1)}, bf16[2,256,256]{2,1,0:T(8,128)(2,1)S(1)}, u32[]{:S(2)}, u32[]{:S(2)}) %collective-permute-start.16) | collective-permute-done | bytes 262176 | tf_op jit(solution)/shard_map/ppermute | solution.py:31
  90.5 1.5 collective-permute-done.18.t2
  92.1 2.2 %shard_map.107 = bf16[2048,128]{1,0:T(8,128)(2,1)S(1)} custom-call(s32[4,10]{1,0:T(4,128)S(1)} %bitcast.29, s32[10]{0:T(128)S(1)} %copy-done.11, bf16[5120,512]{1,0:T(8,128)(2,1)S(1)} %get-tuple-element.29.x_ref, bf16[5120,256]{1,0:T(8,128)(2,1)S(1)} %copy-done.1, bf16[2,256,256]{2,1,0:T(8,128)(2,1)S(1)} %shard_map.106.m, ...), custom_call_target="tpu_custom_call" | custom-call | tf_op jit(solution)/shard_map/pallas_call | solution.py:318
  94.2 23.7 %all_to_all.15.parts_ref = bf16[16,128,128]{2,1,0:T(8,128)(2,1)S(1)} all-to-all(bf16[16,128,128]{2,1,0:T(8,128)(2,1)S(1)} %bitcast.25), channel_id=1, replica_groups={{0,2,4,6,8,10,12,14,16,18,20,22,24,26,28,30},{32,34,36,38,40,42,44,46,4..., dimensions={0} | all-to-all | bytes 1048576 | tf_op jit(solution)/shard_map/all_to_all | solution.py:217
  118.0 21.3 %all_to_all.16.parts_ref = bf16[8,128,128]{2,1,0:T(8,128)(2,1)S(1)} all-to-all(bf16[8,128,128]{2,1,0:T(8,128)(2,1)S(1)} %shard_map.108), channel_id=1, replica_groups={{0,32,64,96,128,160,192,224},{2,34,66,98,130,162,194,226},{4,36,68,100,..., dimensions={0} | all-to-all | bytes 524288 | tf_op jit(solution)/shard_map/all_to_all | solution.py:217
  139.4 14.3 %all_to_all.17 = bf16[16,128,128]{2,1,0:T(8,128)(2,1)S(1)} all-to-all(bf16[16,128,128]{2,1,0:T(8,128)(2,1)S(1)} %shard_map.109), channel_id=1, replica_groups={{0,2,4,6,8,10,12,14,16,18,20,22,24,26,28,30},{32,34,36,38,40,42,44,46,4..., dimensions={0} | all-to-all | bytes 1048576 | tf_op jit(solution)/shard_map/all_to_all | solution.py:217
  153.7 1.1 shard_map.110
  (61 shorter events, 5.3 us)
Async XLA Ops:
  0.6 2.4 %collective-permute-start = (bf16[1280,256]{1,0:T(8,128)(2,1)}, bf16[1280,256]{1,0:T(8,128)(2,1)S(1)}, u32[]{:S(2)}, u32[]{:S(2)}) collective-permute-start(bf16[1280,256]{1,0:T(8,128)(2,1)} %g_ref.1), channel_id=1, source_target_pairs={{0,1},{1,0},{2,3},{3,2},{4,5},{5,4},{6,7},{7,6},{8,9},{9,8},{10,11... | collective-permute-start | bytes 1966088 | tf_op jit(solution)/shard_map/ppermute | solution.py:22
  3.0 1.1 copy-start.2
  4.1 1.3 copy-start.4
  5.4 0.9 copy-start.7
  6.4 0.7 copy-start.8
  7.1 0.7 copy-start.10
  13.1 19.2 %copy-start = (bf16[5120,256]{1,0:T(8,128)(2,1)}, bf16[5120,256]{1,0:T(8,128)(2,1)S(1)}, u32[]{:S(2)}) copy-start(bf16[5120,256]{1,0:T(8,128)(2,1)S(1)} %get-tuple-element.30.slope_ref) | copy-start | bytes 7864324
  13.1 17.7 %copy-start.12 = (bf16[256,256]{1,0:T(8,128)(2,1)S(1)}, bf16[256,256]{1,0:T(8,128)(2,1)}, u32[]{:S(2)}) copy-start(bf16[256,256]{1,0:T(8,128)(2,1)} %param.10) | copy-start | bytes 393220
  13.1 1.6 %collective-permute-start.2 = (bf16[2,256,256]{2,1,0:T(8,128)(2,1)S(1)}, bf16[2,256,256]{2,1,0:T(8,128)(2,1)S(1)}, u32[]{:S(2)}, u32[]{:S(2)}) collective-permute-start(bf16[2,256,256]{2,1,0:T(8,128)(2,1)S(1)} %get-tuple-element.24), channel_id=1, source_target_pairs={{0,1},{1,0},{2,3},{3,2},{4,5},{5,4},{6,7},{7,6},{8,9},{9,8},{10,11... | collective-permute-start | bytes 786440 | tf_op jit(solution)/shard_map/ppermute | solution.py:22
  14.8 32.6 %copy-start.3 = (bf16[1280,256]{1,0:T(8,128)(2,1)S(1)}, bf16[1280,256]{1,0:T(8,128)(2,1)}, u32[]{:S(2)}) copy-start(bf16[1280,256]{1,0:T(8,128)(2,1)} %g_ref.1) | copy-start | bytes 1966084
  14.8 32.6 %copy-start.5 = (bf16[512,256]{1,0:T(8,128)(2,1)S(1)}, bf16[512,256]{1,0:T(8,128)(2,1)}, u32[]{:S(2)}) copy-start(bf16[512,256]{1,0:T(8,128)(2,1)} %w_own.1) | copy-start | bytes 786436
  14.8 32.6 %copy-start.6 = (bf16[1280,256]{1,0:T(8,128)(2,1)S(1)}, bf16[1280,256]{1,0:T(8,128)(2,1)}, u32[]{:S(2)}) copy-start(bf16[1280,256]{1,0:T(8,128)(2,1)} %cot_ref.1) | copy-start | bytes 1966084
  14.8 13.7 %collective-permute-start.4 = (bf16[2,256,256]{2,1,0:T(8,128)(2,1)S(1)}, bf16[2,256,256]{2,1,0:T(8,128)(2,1)S(1)}, u32[]{:S(2)}, u32[]{:S(2)}) collective-permute-start(bf16[2,256,256]{2,1,0:T(8,128)(2,1)S(1)} %pad_maximum_fusion.1), channel_id=1, source_target_pairs={{0,4},{5,1},{2,6},{7,3},{4,8},{9,5},{6,10},{11,7},{8,12},{13,9},{1... | collective-permute-start | bytes 786440 | tf_op jit(solution)/shard_map/ppermute | solution.py:31
  19.2 11.3 %collective-permute-start.3 = (bf16[2,256,256]{2,1,0:T(8,128)(2,1)S(1)}, bf16[2,256,256]{2,1,0:T(8,128)(2,1)S(1)}, u32[]{:S(2)}, u32[]{:S(2)}) collective-permute-start(bf16[2,256,256]{2,1,0:T(8,128)(2,1)S(1)} %pad_maximum_fusion), channel_id=1, source_target_pairs={{0,2},{3,1},{2,4},{5,3},{4,6},{7,5},{6,8},{9,7},{8,10},{11,9},{10,... | collective-permute-start | bytes 786440 | tf_op jit(solution)/shard_map/ppermute | solution.py:31
  30.6 1.6 %collective-permute-start.5 = (bf16[2,256,256]{2,1,0:T(8,128)(2,1)S(1)}, bf16[2,256,256]{2,1,0:T(8,128)(2,1)S(1)}, u32[]{:S(2)}, u32[]{:S(2)}) collective-permute-start(bf16[2,256,256]{2,1,0:T(8,128)(2,1)S(1)} %pad_maximum_fusion.2), channel_id=1, source_target_pairs={{0,1},{1,0},{2,3},{3,2},{4,5},{5,4},{6,7},{7,6},{8,9},{9,8},{10,11... | collective-permute-start | bytes 786440 | tf_op jit(solution)/shard_map/ppermute | solution.py:22
  30.7 1.7 %collective-permute-start.1 = (bf16[256,256]{1,0:T(8,128)(2,1)S(1)}, bf16[256,256]{1,0:T(8,128)(2,1)S(1)}, u32[]{:S(2)}, u32[]{:S(2)}) collective-permute-start(bf16[256,256]{1,0:T(8,128)(2,1)S(1)} %copy-done.12), channel_id=1, source_target_pairs={{0,1},{1,0},{2,3},{3,2},{4,5},{5,4},{6,7},{7,6},{8,9},{9,8},{10,11... | collective-permute-start | bytes 393224 | tf_op jit(solution)/shard_map/ppermute | solution.py:22
  32.5 8.3 %collective-permute-start.6 = (bf16[2,256,256]{2,1,0:T(8,128)(2,1)S(1)}, bf16[2,256,256]{2,1,0:T(8,128)(2,1)S(1)}, u32[]{:S(2)}, u32[]{:S(2)}) collective-permute-start(bf16[2,256,256]{2,1,0:T(8,128)(2,1)S(1)} %add_convert_fusion.m), channel_id=1, source_target_pairs={{0,2},{3,1},{2,4},{5,3},{4,6},{7,5},{6,8},{9,7},{8,10},{11,9},{10,... | collective-permute-start | bytes 786440 | tf_op jit(solution)/shard_map/ppermute | solution.py:31
  35.9 9.9 %collective-permute-start.7 = (bf16[2,256,256]{2,1,0:T(8,128)(2,1)S(1)}, bf16[2,256,256]{2,1,0:T(8,128)(2,1)S(1)}, u32[]{:S(2)}, u32[]{:S(2)}) collective-permute-start(bf16[2,256,256]{2,1,0:T(8,128)(2,1)S(1)} %add_convert_fusion.m), channel_id=1, source_target_pairs={{0,4},{5,1},{2,6},{7,3},{4,8},{9,5},{6,10},{11,7},{8,12},{13,9},{1... | collective-permute-start | bytes 786440 | tf_op jit(solution)/shard_map/ppermute | solution.py:31
  40.8 5.0 %collective-permute-start.8 = (bf16[2,256,256]{2,1,0:T(8,128)(2,1)S(1)}, bf16[2,256,256]{2,1,0:T(8,128)(2,1)S(1)}, u32[]{:S(2)}, u32[]{:S(2)}) collective-permute-start(bf16[2,256,256]{2,1,0:T(8,128)(2,1)S(1)} %collective-permute-done.6.q1), channel_id=1, source_target_pairs={{0,1},{1,0},{2,3},{3,2},{4,5},{5,4},{6,7},{7,6},{8,9},{9,8},{10,11... | collective-permute-start | bytes 786440 | tf_op jit(solution)/shard_map/ppermute | solution.py:22
  45.8 1.5 collective-permute-start.9
  56.1 1.5 collective-permute-start.10
  57.7 15.0 %collective-permute-start.12 = (bf16[2,256,256]{2,1,0:T(8,128)(2,1)S(1)}, bf16[2,256,256]{2,1,0:T(8,128)(2,1)S(1)}, u32[]{:S(2)}, u32[]{:S(2)}) collective-permute-start(bf16[2,256,256]{2,1,0:T(8,128)(2,1)S(1)} %pad_maximum_fusion.4), channel_id=1, source_target_pairs={{0,4},{5,1},{2,6},{7,3},{4,8},{9,5},{6,10},{11,7},{8,12},{13,9},{1... | collective-permute-start | bytes 786440 | tf_op jit(solution)/shard_map/ppermute | solution.py:31
  63.7 11.4 %collective-permute-start.11 = (bf16[2,256,256]{2,1,0:T(8,128)(2,1)S(1)}, bf16[2,256,256]{2,1,0:T(8,128)(2,1)S(1)}, u32[]{:S(2)}, u32[]{:S(2)}) collective-permute-start(bf16[2,256,256]{2,1,0:T(8,128)(2,1)S(1)} %pad_maximum_fusion.3), channel_id=1, source_target_pairs={{0,2},{3,1},{2,4},{5,3},{4,6},{7,5},{6,8},{9,7},{8,10},{11,9},{10,... | collective-permute-start | bytes 786440 | tf_op jit(solution)/shard_map/ppermute | solution.py:31
  66.8 8.6 %collective-permute-start.14 = (bf16[512,256]{1,0:T(8,128)(2,1)S(1)}, bf16[512,256]{1,0:T(8,128)(2,1)S(1)}, u32[]{:S(2)}, u32[]{:S(2)}) collective-permute-start(bf16[512,256]{1,0:T(8,128)(2,1)S(1)} %copy-done.5), channel_id=1, source_target_pairs={{0,1},{1,0},{2,3},{3,2},{4,5},{5,4},{6,7},{7,6},{8,9},{9,8},{10,11... | collective-permute-start | bytes 786440 | tf_op jit(solution)/shard_map/ppermute | solution.py:22
  68.4 23.6 %copy-start.1 = (bf16[5120,256]{1,0:T(8,128)(2,1)S(1)}, bf16[5120,256]{1,0:T(8,128)(2,1)}, u32[]{:S(2)}) copy-start(bf16[5120,256]{1,0:T(8,128)(2,1)} %copy-done) | copy-start | bytes 7864324
  68.4 23.6 %copy-start.9 = (s32[10,4]{0,1:T(4,128)S(1)}, s32[10,4]{0,1:T(4,128)}, u32[]{:S(2)}) copy-start(s32[10,4]{0,1:T(4,128)} %param.14) | copy-start | bytes 484
  68.4 23.6 %copy-start.11 = (s32[10]{0:T(128)S(1)}, s32[10]{0:T(128)}, u32[]{:S(2)}) copy-start(s32[10]{0:T(128)} %pc.5) | copy-start | bytes 124
  75.2 1.6 %collective-permute-start.13 = (bf16[2,256,256]{2,1,0:T(8,128)(2,1)S(1)}, bf16[2,256,256]{2,1,0:T(8,128)(2,1)S(1)}, u32[]{:S(2)}, u32[]{:S(2)}) collective-permute-start(bf16[2,256,256]{2,1,0:T(8,128)(2,1)S(1)} %pad_maximum_fusion.5.s), channel_id=1, source_target_pairs={{0,1},{1,0},{2,3},{3,2},{4,5},{5,4},{6,7},{7,6},{8,9},{9,8},{10,11... | collective-permute-start | bytes 786440 | tf_op jit(solution)/shard_map/ppermute | solution.py:22
  77.2 8.3 %collective-permute-start.15 = (bf16[2,256,256]{2,1,0:T(8,128)(2,1)S(1)}, bf16[2,256,256]{2,1,0:T(8,128)(2,1)S(1)}, u32[]{:S(2)}, u32[]{:S(2)}) collective-permute-start(bf16[2,256,256]{2,1,0:T(8,128)(2,1)S(1)} %shard_map.106.m), channel_id=1, source_target_pairs={{0,2},{3,1},{2,4},{5,3},{4,6},{7,5},{6,8},{9,7},{8,10},{11,9},{10,... | collective-permute-start | bytes 786440 | tf_op jit(solution)/shard_map/ppermute | solution.py:31
  80.6 9.9 %collective-permute-start.16 = (bf16[2,256,256]{2,1,0:T(8,128)(2,1)S(1)}, bf16[2,256,256]{2,1,0:T(8,128)(2,1)S(1)}, u32[]{:S(2)}, u32[]{:S(2)}) collective-permute-start(bf16[2,256,256]{2,1,0:T(8,128)(2,1)S(1)} %shard_map.106.m), channel_id=1, source_target_pairs={{0,4},{5,1},{2,6},{7,3},{4,8},{9,5},{6,10},{11,7},{8,12},{13,9},{1... | collective-permute-start | bytes 786440 | tf_op jit(solution)/shard_map/ppermute | solution.py:31
  85.5 5.0 %collective-permute-start.17 = (bf16[2,256,256]{2,1,0:T(8,128)(2,1)S(1)}, bf16[2,256,256]{2,1,0:T(8,128)(2,1)S(1)}, u32[]{:S(2)}, u32[]{:S(2)}) collective-permute-start(bf16[2,256,256]{2,1,0:T(8,128)(2,1)S(1)} %collective-permute-done.15.q1), channel_id=1, source_target_pairs={{0,1},{1,0},{2,3},{3,2},{4,5},{5,4},{6,7},{7,6},{8,9},{9,8},{10,11... | collective-permute-start | bytes 786440 | tf_op jit(solution)/shard_map/ppermute | solution.py:22
  90.5 1.5 collective-permute-start.18

commit v5 on v4

--- a/solution.py
+++ b/solution.py
@@ -62,32 +62,46 @@
     return copies
 
 
+def lift_kernel(a_hbm, g_hbm, w_hbm, pm_hbm, pc_hbm, a_ref, w_ref, x_ref, pm_ref, pc_ref, g_ref, sems):
+    blocks, slots, rows, points = a_ref.shape
+    pairs = slots * rows
+    early = min(3, blocks)
+    head, tail = pl.ds(0, early), pl.ds(early, blocks - early)
+    copies = fetch(
+        [
+            (g_hbm, g_ref), (a_hbm.at[head], a_ref.at[head]), (a_hbm.at[tail], a_ref.at[tail]),
+            (w_hbm, w_ref), (pm_hbm, pm_ref), (pc_hbm, pc_ref),
+        ],
+        sems,
+    )
+    for copy in copies[:2]:
+        copy.wait()
+    for block in range(blocks):
+        if block == early:
+            copies[2].wait()
+        weights = a_ref[block].reshape(pairs, points)
+        x = dot(weights, g_ref[block * points : (block + 1) * points])
+        x_ref[block * pairs : (block + 1) * pairs] = x.astype(BF)
+    for copy in copies[3:]:
+        copy.wait()
+
+
 def encode_kernel(
-    pm, pc, a_hbm, g_hbm, w_hbm, g_other, a_ref, x_ref, slope_ref, own, mine, other,
-    total, g_ref, w_ref, sems,
+    pm, pc, a_ref, w_ref, x_own, g_other, x_other, slope_ref, own, mine, other, total
 ):
     blocks, slots, rows, points = a_ref.shape
     pairs = slots * rows
-    early = min(2, blocks)
-    head, tail = pl.ds(0, early), pl.ds(early, blocks - early)
-    copies = fetch(
-        [(g_hbm, g_ref), (a_hbm.at[head], a_ref.at[head]), (w_hbm, w_ref), (a_hbm.at[tail], a_ref.at[tail])],
-        sems,
-    )
+    half = x_own.shape[1]
+    core = lax.axis_index("mp")
+    w_own = w_ref[pl.ds(pl.multiple_of(core * half, half), half)]
+    w_far = w_ref[pl.ds(pl.multiple_of((1 - core) * half, half), half)]
     total[...] = jnp.zeros_like(total)
-    first = lax.axis_index("mp") == 0
-    for copy in copies[:3]:
-        copy.wait()
     for block in range(blocks):
-        if block == early:
-            copies[3].wait()
-        span = slice(block * points, (block + 1) * points)
-        g_own, g_far = g_ref[span], g_other[span]
-        low, high = jnp.where(first, g_own, g_far), jnp.where(first, g_far, g_own)
+        span = slice(block * pairs, (block + 1) * pairs)
         weights = a_ref[block].reshape(pairs, points)
-        x = dot(weights, jnp.concatenate([low, high], axis=1)).astype(BF)
-        x_ref[block * pairs : (block + 1) * pairs] = x
-        u = dot(x, w_ref[...])
+        x = dot(weights, g_other[block * points : (block + 1) * points]).astype(BF)
+        x_other[span] = x
+        u = dot(x_own[span], w_own) + dot(x, w_far)
         for slot in range(slots):
             part = u[slot * rows : (slot + 1) * rows]
             sig = sigmoid(part)
@@ -146,8 +160,9 @@
     split_slabs(total, own, mine, other)
 
 
-def outer_kernel(left_ref, right_ref, out_ref):
+def outer_kernel(left_ref, right_ref, made_ref, out_ref, sent_ref):
     out_ref[...] = dot(right_ref[...], left_ref[...], ROWS_BY_ROWS)
+    sent_ref[...] = made_ref[...]
 
 
 def mesh_grad_kernel(s, t, w_own, w_other, out):
@@ -168,7 +183,7 @@
 
 
 def encoder_grad_kernel(
-    pm, pc, x_ref, slope_ref, m, q1, q2, t1, t2, dec_ref, out_ref, near, total
+    pm, pc, x_own, x_other, slope_ref, m, q1, q2, t1, t2, dec_ref, out_ref, near, total
 ):
     slots, blocks = pm.shape
     rows = near.shape[1]
@@ -181,14 +196,27 @@
             picked = near[place(pm, block, slot, -1)].astype(FL)
             start = block * pairs + slot * rows
             parts.append((picked * slope_ref[start : start + rows].astype(FL)).astype(BF))
-        term = dot(jnp.concatenate(parts, axis=0), x_ref[block * pairs : (block + 1) * pairs], ROWS_BY_ROWS)
-        total[...] = term if block == 0 else total[...] + term
-    count, width = total.shape
+        du = jnp.concatenate(parts, axis=0)
+        for at, x_ref in enumerate((x_own, x_other)):
+            term = dot(du, x_ref[block * pairs : (block + 1) * pairs], ROWS_BY_ROWS)
+            total[at] = term if block == 0 else total[at] + term
+    count, half = total.shape[1:]
     lanes = out_ref.shape[1]
-    for at, value in enumerate((total, dec_ref)):
-        for tile in range(width // lanes):
-            start = (at * width // lanes + tile) * count
-            out_ref[start : start + count] = value[:, tile * lanes : (tile + 1) * lanes].astype(BF)
+    tiles = half // lanes
+
+    def store(tile, value):
+        out_ref[tile * count : (tile + 1) * count] = value.astype(BF)
+
+    def store_encoder(order):
+        for at, side in enumerate(order):
+            for tile in range(tiles):
+                store(at * tiles + tile, total[side, :, tile * lanes : (tile + 1) * lanes])
+
+    core = lax.axis_index("mp")
+    pl.when(core == 0)(lambda: store_encoder((0, 1)))
+    pl.when(core == 1)(lambda: store_encoder((1, 0)))
+    for tile in range(2 * tiles):
+        store(2 * tiles + tile, dec_ref[:, tile * lanes : (tile + 1) * lanes])
 
 
 def sum_kernel(parts_ref, out_ref):
@@ -218,7 +246,7 @@
 
 
 def params():
-    return pltpu.CompilerParams(vmem_limit_bytes=40 * 2**20)
+    return pltpu.CompilerParams(vmem_limit_bytes=24 * 2**20)
 
 
 def shape_of(*shape, dtype=BF):
@@ -248,7 +276,7 @@
     return [value, *near, *(swap(part) for part in near)]
 
 
-VMEM, ANY, SMEM = (pl.BlockSpec(memory_space=space) for space in (pltpu.VMEM, pl.ANY, pltpu.SMEM))
+VMEM, HBM, SMEM = (pl.BlockSpec(memory_space=space) for space in (pltpu.VMEM, pltpu.HBM, pltpu.SMEM))
 
 
 def held(kernel, in_specs, out_shape, scratch=(), cost=None):
@@ -267,22 +295,33 @@
     return [shape_of(*lead, owner_rows, half) for lead in ((), (REACH,), (REACH,))]
 
 
-def encode(pair_mesh, pair_count, interp, grid, grid_other, w_enc):
+def lift_own(*given):
+    interp, grid, w_enc, pair_mesh, pair_count = given
     blocks, slots, rows, points = interp.shape
-    full, half = w_enc.shape
+    half = w_enc.shape[1]
     pairs = blocks * slots * rows
+    cost = pl.CostEstimate(flops=2 * pairs * points * half, bytes_accessed=4 * 2**20, transcendentals=0)
+    fixed = [jax.ShapeDtypeStruct(value.shape, value.dtype) for value in (pair_mesh, pair_count)]
+    return pl.pallas_call(
+        lift_kernel,
+        in_specs=[HBM] * 5,
+        out_specs=[VMEM, VMEM, VMEM, SMEM, SMEM],
+        out_shape=[shape_of(*interp.shape), shape_of(*w_enc.shape), shape_of(pairs, half), *fixed],
+        scratch_shapes=[pltpu.VMEM(grid.shape, BF), pltpu.SemaphoreType.DMA((6,))],
+        compiler_params=params(),
+        cost_estimate=cost,
+    )(*(pltpu.with_memory_space_constraint(value, pltpu.HBM) for value in given))
+
+
+def encode(pair_mesh, pair_count, interp, w_enc, x_own, grid_other):
+    blocks, slots, rows, points = interp.shape
+    pairs, half = x_own.shape
     return held(
         encode_kernel,
-        [SMEM, SMEM, ANY, ANY, ANY, VMEM],
-        [
-            shape_of(*interp.shape), shape_of(pairs, full), shape_of(pairs, half),
-            *slab_shapes(OWNER_BLOCKS * rows, half),
-        ],
-        [
-            pltpu.VMEM((NEAR * OWNER_BLOCKS, rows, half), FL), pltpu.VMEM(grid.shape, BF),
-            pltpu.VMEM(w_enc.shape, BF), pltpu.SemaphoreType.DMA((4,)),
-        ],
-    )(pair_mesh, pair_count, interp, grid, w_enc, grid_other)
+        [SMEM, SMEM, *[VMEM] * 4],
+        [shape_of(pairs, half), shape_of(pairs, half), *slab_shapes(OWNER_BLOCKS * rows, half)],
+        [pltpu.VMEM((NEAR * OWNER_BLOCKS, rows, half), FL)],
+    )(pair_mesh, pair_count, interp, w_enc, x_own, grid_other)
 
 
 def decode(pair_mesh, pair_count, interp, grid, cotangent, w_dec, near):
@@ -303,24 +342,25 @@
     )(pair_mesh, pair_count, interp, grid, cotangent, w_dec, *near)
 
 
-def outer(y, dz):
+def outer(y, dz, made):
     pairs, full = y.shape
     half = dz.shape[1]
     cost = pl.CostEstimate(
         flops=2 * pairs * full * half, bytes_accessed=2 * pairs * (full + half), transcendentals=0
     )
-    return held(outer_kernel, [VMEM, VMEM], shape_of(half, full, dtype=FL), cost=cost)(y, dz)
-
-
-def encoder_grad(pair_mesh, pair_count, x, slope, near, grad_dec):
-    full, half = x.shape[1], slope.shape[1]
+    outs = [shape_of(half, full, dtype=FL), shape_of(*made.shape)]
+    return held(outer_kernel, [VMEM] * 3, outs, cost=cost)(y, dz, made)
+
+
+def encoder_grad(pair_mesh, pair_count, x_own, x_other, slope, near, grad_dec):
+    half = slope.shape[1]
     rows = near[0].shape[1] // OWNER_BLOCKS
     return held(
         encoder_grad_kernel,
-        [SMEM, SMEM, *[VMEM] * (3 + NEAR)],
-        shape_of(4 * full, half // 2),
-        [pltpu.VMEM((NEAR * OWNER_BLOCKS, rows, half), BF), pltpu.VMEM((half, full), FL)],
-    )(pair_mesh, pair_count, x, slope, *near, grad_dec)
+        [SMEM, SMEM, *[VMEM] * (4 + NEAR)],
+        shape_of(8 * half, half // 2),
+        [pltpu.VMEM((NEAR * OWNER_BLOCKS, rows, half), BF), pltpu.VMEM((2, half, half), FL)],
+    )(pair_mesh, pair_count, x_own, x_other, slope, *near, grad_dec)
 
 
 def local(grid, interp, mesh_init, w_enc, w_dec, cotangent, pair_mesh, pair_count):
@@ -330,7 +370,10 @@
     mesh_both = jnp.stack([mesh_init, swap(mesh_init)])
     w_dec_other = swap(w_dec)
 
-    interp, x, slope, own, mine, other = encode(pair_mesh, pair_count, interp, grid, grid_other, w_enc)
+    interp, w_enc, x_own, pair_mesh, pair_count = lift_own(interp, grid, w_enc, pair_mesh, pair_count)
+    x_other, slope, own, mine, other = encode(
+        pair_mesh, pair_count, interp, w_enc, x_own, grid_other
+    )
     sums, got, _ = reduce_to_owner(own, mine, other)
     agg = sums.astype(FL) + got.astype(FL)[::-1]
     mesh_lat = (mesh_both.astype(FL) + 0.25 * agg).astype(BF)
@@ -339,10 +382,10 @@
     out, y, dz, own, mine, other = decode(
         pair_mesh, pair_count, interp, grid, cotangent, w_dec, near
     )
-    sums, got, grad_dec = reduce_to_owner(own, mine, other, outer(y, dz))
+    sums, got, (grad_dec, out) = reduce_to_owner(own, mine, other, outer(y, dz, out))
     grad_mesh = simple(mesh_grad_kernel, shape_of(*sums.shape))(sums, got, w_dec, w_dec_other)
     near = spread_from_owner(grad_mesh)
-    flat = encoder_grad(pair_mesh, pair_count, x, slope, near, grad_dec)
+    flat = encoder_grad(pair_mesh, pair_count, x_own, x_other, slope, near, grad_dec)
 
     plane, line = plane_groups(lax.axis_size("band"))
     across = len(plane[0])

time: 155 us -> 150 us (0.968)
  local copies, waits for them, and re-layouts: 4.84 us -> 0.13 us
  waiting for transfers between devices: 37.8 us -> 34.6 us
  Pallas kernels: 19.4 us -> 21.8 us
    unnamed x26 -> x8, local copies, waits for them, and re-layouts: 4.73 us -> 0.03 us
    pallas_call x3 -> x4, Pallas kernels: 9.04 us -> 12.1 us  [the longest x1 4.54 us: encode(): held(encode_kernel, [SMEM, SMEM, *[VMEM] * 4], [shape_of(pairs, half), sh...]
    ppermute x11, waiting for transfers between devices: 10.8 us -> 8.28 us  [swap(): return lax.ppermute(value, 'mp', [(0, 1), (1, 0)])]
  transfers between devices with their start and end apart: 19 -> 19, of which waited for: 16 -> 15; matrix products, arithmetic and copies ran while one was open for 0% -> 0% of each run, Pallas kernels for 1% -> 4%
where the time goes in v5:
time: 150 us
  blocking collectives  59.1 us (39%)
  waiting for transfers between devices  34.6 us (23%)
  starting transfers between devices  32.5 us (22%)
  Pallas kernels  21.8 us (15%)
    all_to_all x3, blocking collectives, exchange(): lax.all_to_all(value, 'band', 0, 0, tiled=True, axis_index_groups=groups)  59.1 us
    ppermute x8, starting transfers between devices, outward(): return lax.ppermute(value, ('band', 'mp'), pairs)  30.8 us
    ppermute x8, waiting for transfers between devices, outward(): return lax.ppermute(value, ('band', 'mp'), pairs)  26.3 us
    ppermute x11, waiting for transfers between devices, swap(): return lax.ppermute(value, 'mp', [(0, 1), (1, 0)])  8.28 us
    pallas_call x1, Pallas kernels, decode(): held(decode_kernel, [SMEM, SMEM, *[VMEM] * (4 + NEAR)], [shape_of(*grid.s...  8.08 us
    pallas_call x1, Pallas kernels, encode(): held(encode_kernel, [SMEM, SMEM, *[VMEM] * 4], [shape_of(pairs, half), sh...  4.54 us
    pallas_call x1, Pallas kernels, lift_own(): pl.pallas_call(lift_kernel, in_specs=[HBM] * 5, out_specs=[VMEM, VMEM, VM...  3.02 us
  transfers between devices with their start and end apart: 19, of which 15 were waited for; matrix products, arithmetic and copies ran while one was open for 0% of the time, Pallas kernels for 4%

profile of v5, /device:TPU:8, one launch (start us, length us, event | category | flops | bytes accessed | tf_op | source)
XLA Modules:
  0.0 149.5 jit_solution(13635407935902432589)
XLA Ops:
  0.7 3.0 %shard_map.103 = (bf16[10,4,128,128]{3,2,1,0:T(8,128)(2,1)S(1)}, bf16[512,256]{1,0:T(8,128)(2,1)S(1)}, bf16[5120,256]{1,0:T(8,128)(2,1)S(1)}, s32[4,10]{1,0:T(4,128)S(1)}, s32[10]{0:T(128)S(1)}) custom-call(bf16[10,4,128,128]{3,2,1,0:T(8,128)(2,1)} %a_hbm.1, bf16[1280,256]{1,0:T(8,128)(2,1)} %g_ref.1, bf16[512,256]{1,0:T(8,128)(2,1)} %w_hbm.1, ...), custom_call_target="tpu_custom_call" | custom-call | flops 335544320 | bytes 4194304 | tf_op jit(solution)/shard_map/pallas_call | solution.py:305
  3.8 4.5 %shard_map.104 = (bf16[5120,256]{1,0:T(8,128)(2,1)S(1)}, bf16[5120,256]{1,0:T(8,128)(2,1)S(1)}, bf16[256,256]{1,0:T(8,128)(2,1)S(1)}, bf16[2,256,256]{2,1,0:T(8,128)(2,1)S(1)}, bf16[2,256,256]{2,1,0:T(8,128)(2,1)S(1)}) custom-call(s32[4,10]{1,0:T(4,128)S(1)} %get-tuple-element.29.pm, s32[10]{0:T(128)S(1)} %get-tuple-element.30.pc, ...), custom_call_target="tpu_custom_call" | custom-call | tf_op jit(solution)/shard_map/pallas_call | solution.py:319
  8.3 0.6 collective-permute-start.2
  8.9 1.1 collective-permute-done.2
  10.2 4.3 %collective-permute-start.4 = (bf16[2,256,256]{2,1,0:T(8,128)(2,1)S(1)}, bf16[2,256,256]{2,1,0:T(8,128)(2,1)S(1)}, u32[]{:S(2)}, u32[]{:S(2)}) collective-permute-start(bf16[2,256,256]{2,1,0:T(8,128)(2,1)S(1)} %pad_maximum_fusion.1), channel_id=1, source_target_pairs={{0,4},{5,1},{2,6},{7,3},{4,8},{9,5},{6,10},{11,7},{8,12},{13,9},{1... | collective-permute-start | bytes 786440 | tf_op jit(solution)/shard_map/ppermute | solution.py:31
  14.6 2.4 %collective-permute-start.3 = (bf16[2,256,256]{2,1,0:T(8,128)(2,1)S(1)}, bf16[2,256,256]{2,1,0:T(8,128)(2,1)S(1)}, u32[]{:S(2)}, u32[]{:S(2)}) collective-permute-start(bf16[2,256,256]{2,1,0:T(8,128)(2,1)S(1)} %pad_maximum_fusion), channel_id=1, source_target_pairs={{0,2},{3,1},{2,4},{5,3},{4,6},{7,5},{6,8},{9,7},{8,10},{11,9},{10,... | collective-permute-start | bytes 786440 | tf_op jit(solution)/shard_map/ppermute | solution.py:31
  17.0 6.6 %collective-permute-done.4 = bf16[2,256,256]{2,1,0:T(8,128)(2,1)S(1)} collective-permute-done((bf16[2,256,256]{2,1,0:T(8,128)(2,1)S(1)}, bf16[2,256,256]{2,1,0:T(8,128)(2,1)S(1)}, u32[]{:S(2)}, u32[]{:S(2)}) %collective-permute-start.4) | collective-permute-done | bytes 262176 | tf_op jit(solution)/shard_map/ppermute | solution.py:31
  23.6 2.2 %collective-permute-done.3 = bf16[2,256,256]{2,1,0:T(8,128)(2,1)S(1)} collective-permute-done((bf16[2,256,256]{2,1,0:T(8,128)(2,1)S(1)}, bf16[2,256,256]{2,1,0:T(8,128)(2,1)S(1)}, u32[]{:S(2)}, u32[]{:S(2)}) %collective-permute-start.3) | collective-permute-done | bytes 262176 | tf_op jit(solution)/shard_map/ppermute | solution.py:31
  26.6 1.0 collective-permute-done.5
  27.9 3.3 %collective-permute-start.6 = (bf16[2,256,256]{2,1,0:T(8,128)(2,1)S(1)}, bf16[2,256,256]{2,1,0:T(8,128)(2,1)S(1)}, u32[]{:S(2)}, u32[]{:S(2)}) collective-permute-start(bf16[2,256,256]{2,1,0:T(8,128)(2,1)S(1)} %add_convert_fusion.m), channel_id=1, source_target_pairs={{0,2},{3,1},{2,4},{5,3},{4,6},{7,5},{6,8},{9,7},{8,10},{11,9},{10,... | collective-permute-start | bytes 786440 | tf_op jit(solution)/shard_map/ppermute | solution.py:31
  31.3 3.9 %collective-permute-start.7 = (bf16[2,256,256]{2,1,0:T(8,128)(2,1)S(1)}, bf16[2,256,256]{2,1,0:T(8,128)(2,1)S(1)}, u32[]{:S(2)}, u32[]{:S(2)}) collective-permute-start(bf16[2,256,256]{2,1,0:T(8,128)(2,1)S(1)} %add_convert_fusion.m), channel_id=1, source_target_pairs={{0,4},{5,1},{2,6},{7,3},{4,8},{9,5},{6,10},{11,7},{8,12},{13,9},{1... | collective-permute-start | bytes 786440 | tf_op jit(solution)/shard_map/ppermute | solution.py:31
  35.2 1.0 collective-permute-done.6.q1
  36.2 5.0 %collective-permute-done.7.q2 = bf16[2,256,256]{2,1,0:T(8,128)(2,1)S(1)} collective-permute-done((bf16[2,256,256]{2,1,0:T(8,128)(2,1)S(1)}, bf16[2,256,256]{2,1,0:T(8,128)(2,1)S(1)}, u32[]{:S(2)}, u32[]{:S(2)}) %collective-permute-start.7) | collective-permute-done | bytes 262176 | tf_op jit(solution)/shard_map/ppermute | solution.py:31
  41.2 1.5 %collective-permute-done.9.t2 = bf16[2,256,256]{2,1,0:T(8,128)(2,1)S(1)} collective-permute-done((bf16[2,256,256]{2,1,0:T(8,128)(2,1)S(1)}, bf16[2,256,256]{2,1,0:T(8,128)(2,1)S(1)}, u32[]{:S(2)}, u32[]{:S(2)}) %collective-permute-start.9) | collective-permute-done | bytes 262176 | tf_op jit(solution)/shard_map/ppermute | solution.py:22
  42.7 8.1 %shard_map.105 = (bf16[1280,256]{1,0:T(8,128)(2,1)S(1)}, bf16[5120,512]{1,0:T(8,128)(2,1)S(1)}, bf16[5120,256]{1,0:T(8,128)(2,1)S(1)}, bf16[256,256]{1,0:T(8,128...) custom-call(s32[4,10]{1,0:T(4,128)S(1)} %get-tuple-element.29.pm, ...), custom_call_target="tpu_custom_call" | custom-call | tf_op jit(solution)/shard_map/pallas_call | solution.py:331
  51.1 1.4 collective-permute-done.10
  52.5 6.0 %collective-permute-start.12 = (bf16[2,256,256]{2,1,0:T(8,128)(2,1)S(1)}, bf16[2,256,256]{2,1,0:T(8,128)(2,1)S(1)}, u32[]{:S(2)}, u32[]{:S(2)}) collective-permute-start(bf16[2,256,256]{2,1,0:T(8,128)(2,1)S(1)} %pad_maximum_fusion.4), channel_id=1, source_target_pairs={{0,4},{5,1},{2,6},{7,3},{4,8},{9,5},{6,10},{11,7},{8,12},{13,9},{1... | collective-permute-start | bytes 786440 | tf_op jit(solution)/shard_map/ppermute | solution.py:31
  58.5 3.1 %collective-permute-start.11 = (bf16[2,256,256]{2,1,0:T(8,128)(2,1)S(1)}, bf16[2,256,256]{2,1,0:T(8,128)(2,1)S(1)}, u32[]{:S(2)}, u32[]{:S(2)}) collective-permute-start(bf16[2,256,256]{2,1,0:T(8,128)(2,1)S(1)} %pad_maximum_fusion.3), channel_id=1, source_target_pairs={{0,2},{3,1},{2,4},{5,3},{4,6},{7,5},{6,8},{9,7},{8,10},{11,9},{10,... | collective-permute-start | bytes 786440 | tf_op jit(solution)/shard_map/ppermute | solution.py:31
  61.7 2.3 %shard_map.106 = (f32[256,512]{1,0:T(8,128)S(1)}, bf16[1280,256]{1,0:T(8,128)(2,1)}) custom-call(bf16[5120,512]{1,0:T(8,128)(2,1)S(1)} %get-tuple-element.41.left_ref, bf16[5120,256]{1,0:T(8,128)(2,1)S(1)} %get-tuple-element.42.right_ref, bf16[1280,256]{1,0:T(8,128)(2,1)S(1)} %get-tuple-element.43.made_ref), custom_call_target="tpu_custom_call" | custom-call | flops 1342177280 | bytes 7864320 | tf_op jit(solution)/shard_map/pallas_call | solution.py:352
  64.0 3.6 %collective-permute-done.12 = bf16[2,256,256]{2,1,0:T(8,128)(2,1)S(1)} collective-permute-done((bf16[2,256,256]{2,1,0:T(8,128)(2,1)S(1)}, bf16[2,256,256]{2,1,0:T(8,128)(2,1)S(1)}, u32[]{:S(2)}, u32[]{:S(2)}) %collective-permute-start.12) | collective-permute-done | bytes 262176 | tf_op jit(solution)/shard_map/ppermute | solution.py:31
  67.5 2.4 %collective-permute-done.11 = bf16[2,256,256]{2,1,0:T(8,128)(2,1)S(1)} collective-permute-done((bf16[2,256,256]{2,1,0:T(8,128)(2,1)S(1)}, bf16[2,256,256]{2,1,0:T(8,128)(2,1)S(1)}, u32[]{:S(2)}, u32[]{:S(2)}) %collective-permute-start.11) | collective-permute-done | bytes 262176 | tf_op jit(solution)/shard_map/ppermute | solution.py:31
  70.2 1.5 %collective-permute-done.13.t = bf16[2,256,256]{2,1,0:T(8,128)(2,1)S(1)} collective-permute-done((bf16[2,256,256]{2,1,0:T(8,128)(2,1)S(1)}, bf16[2,256,256]{2,1,0:T(8,128)(2,1)S(1)}, u32[]{:S(2)}, u32[]{:S(2)}) %collective-permute-start.13) | collective-permute-done | bytes 262176 | tf_op jit(solution)/shard_map/ppermute | solution.py:22
  72.1 3.3 %collective-permute-start.15 = (bf16[2,256,256]{2,1,0:T(8,128)(2,1)S(1)}, bf16[2,256,256]{2,1,0:T(8,128)(2,1)S(1)}, u32[]{:S(2)}, u32[]{:S(2)}) collective-permute-start(bf16[2,256,256]{2,1,0:T(8,128)(2,1)S(1)} %shard_map.107.m), channel_id=1, source_target_pairs={{0,2},{3,1},{2,4},{5,3},{4,6},{7,5},{6,8},{9,7},{8,10},{11,9},{10,... | collective-permute-start | bytes 786440 | tf_op jit(solution)/shard_map/ppermute | solution.py:31
  75.4 4.4 %collective-permute-start.16 = (bf16[2,256,256]{2,1,0:T(8,128)(2,1)S(1)}, bf16[2,256,256]{2,1,0:T(8,128)(2,1)S(1)}, u32[]{:S(2)}, u32[]{:S(2)}) collective-permute-start(bf16[2,256,256]{2,1,0:T(8,128)(2,1)S(1)} %shard_map.107.m), channel_id=1, source_target_pairs={{0,4},{5,1},{2,6},{7,3},{4,8},{9,5},{6,10},{11,7},{8,12},{13,9},{1... | collective-permute-start | bytes 786440 | tf_op jit(solution)/shard_map/ppermute | solution.py:31
  79.8 0.5 collective-permute-done.15.q1
  80.3 5.0 %collective-permute-done.16.q2 = bf16[2,256,256]{2,1,0:T(8,128)(2,1)S(1)} collective-permute-done((bf16[2,256,256]{2,1,0:T(8,128)(2,1)S(1)}, bf16[2,256,256]{2,1,0:T(8,128)(2,1)S(1)}, u32[]{:S(2)}, u32[]{:S(2)}) %collective-permute-start.16) | collective-permute-done | bytes 262176 | tf_op jit(solution)/shard_map/ppermute | solution.py:31
  85.3 1.5 %collective-permute-done.18.t2 = bf16[2,256,256]{2,1,0:T(8,128)(2,1)S(1)} collective-permute-done((bf16[2,256,256]{2,1,0:T(8,128)(2,1)S(1)}, bf16[2,256,256]{2,1,0:T(8,128)(2,1)S(1)}, u32[]{:S(2)}, u32[]{:S(2)}) %collective-permute-start.18) | collective-permute-done | bytes 262176 | tf_op jit(solution)/shard_map/ppermute | solution.py:22
  86.9 2.3 %shard_map.108 = bf16[2048,128]{1,0:T(8,128)(2,1)S(1)} custom-call(s32[4,10]{1,0:T(4,128)S(1)} %get-tuple-element.29.pm, s32[10]{0:T(128)S(1)} %get-tuple-element.30.pc, bf16[5120,256]{1,0:T(8,128)(2,1)S(1)} %get-tuple-element.33.x_own, bf16[5120,256]{1,0:T(8,128)(2,1)S(1)} %get-tuple-element.47.x_other, bf16[5120,256]{1,0:T(8,128)(2,1)S(1)} %get-tuple-element.48.slope_ref, ...), custom_call_target="tpu_custom_call" | custom-call | tf_op jit(solution)/shard_map/pallas_call | solution.py:358
  89.2 23.8 %all_to_all.15.parts_ref = bf16[16,128,128]{2,1,0:T(8,128)(2,1)S(1)} all-to-all(bf16[16,128,128]{2,1,0:T(8,128)(2,1)S(1)} %bitcast.25), channel_id=1, replica_groups={{0,2,4,6,8,10,12,14,16,18,20,22,24,26,28,30},{32,34,36,38,40,42,44,46,4..., dimensions={0} | all-to-all | bytes 1048576 | tf_op jit(solution)/shard_map/all_to_all | solution.py:245
  113.0 21.3 %all_to_all.16.parts_ref = bf16[8,128,128]{2,1,0:T(8,128)(2,1)S(1)} all-to-all(bf16[8,128,128]{2,1,0:T(8,128)(2,1)S(1)} %shard_map.109), channel_id=1, replica_groups={{0,32,64,96,128,160,192,224},{2,34,66,98,130,162,194,226},{4,36,68,100,..., dimensions={0} | all-to-all | bytes 524288 | tf_op jit(solution)/shard_map/all_to_all | solution.py:245
  134.3 14.1 %all_to_all.17 = bf16[16,128,128]{2,1,0:T(8,128)(2,1)S(1)} all-to-all(bf16[16,128,128]{2,1,0:T(8,128)(2,1)S(1)} %shard_map.110), channel_id=1, replica_groups={{0,2,4,6,8,10,12,14,16,18,20,22,24,26,28,30},{32,34,36,38,40,42,44,46,4..., dimensions={0} | all-to-all | bytes 1048576 | tf_op jit(solution)/shard_map/all_to_all | solution.py:245
  148.4 1.1 shard_map.111
  (44 shorter events, 2.4 us)
Async XLA Ops:
  0.6 3.1 %collective-permute-start.1 = (bf16[1280,256]{1,0:T(8,128)(2,1)}, bf16[1280,256]{1,0:T(8,128)(2,1)S(1)}, u32[]{:S(2)}, u32[]{:S(2)}) collective-permute-start(bf16[1280,256]{1,0:T(8,128)(2,1)} %g_ref.1), channel_id=1, source_target_pairs={{0,1},{1,0},{2,3},{3,2},{4,5},{5,4},{6,7},{7,6},{8,9},{9,8},{10,11... | collective-permute-start | bytes 1966088 | tf_op jit(solution)/shard_map/ppermute | solution.py:22
  8.3 17.8 %copy-start.3 = (bf16[256,256]{1,0:T(8,128)(2,1)S(1)}, bf16[256,256]{1,0:T(8,128)(2,1)}, u32[]{:S(2)}) copy-start(bf16[256,256]{1,0:T(8,128)(2,1)} %param.10) | copy-start | bytes 393220
  8.3 1.7 %collective-permute-start.2 = (bf16[2,256,256]{2,1,0:T(8,128)(2,1)S(1)}, bf16[2,256,256]{2,1,0:T(8,128)(2,1)S(1)}, u32[]{:S(2)}, u32[]{:S(2)}) collective-permute-start(bf16[2,256,256]{2,1,0:T(8,128)(2,1)S(1)} %get-tuple-element.35), channel_id=1, source_target_pairs={{0,1},{1,0},{2,3},{3,2},{4,5},{5,4},{6,7},{7,6},{8,9},{9,8},{10,11... | collective-permute-start | bytes 786440 | tf_op jit(solution)/shard_map/ppermute | solution.py:22
  10.1 32.6 %copy-start = (bf16[1280,256]{1,0:T(8,128)(2,1)S(1)}, bf16[1280,256]{1,0:T(8,128)(2,1)}, u32[]{:S(2)}) copy-start(bf16[1280,256]{1,0:T(8,128)(2,1)} %g_ref.1) | copy-start | bytes 1966084
  10.1 32.6 %copy-start.1 = (bf16[512,256]{1,0:T(8,128)(2,1)S(1)}, bf16[512,256]{1,0:T(8,128)(2,1)}, u32[]{:S(2)}) copy-start(bf16[512,256]{1,0:T(8,128)(2,1)} %w_own.1) | copy-start | bytes 786436
  10.2 32.6 %copy-start.2 = (bf16[1280,256]{1,0:T(8,128)(2,1)S(1)}, bf16[1280,256]{1,0:T(8,128)(2,1)}, u32[]{:S(2)}) copy-start(bf16[1280,256]{1,0:T(8,128)(2,1)} %cot_ref.1) | copy-start | bytes 1966084
  10.2 13.5 %collective-permute-start.4 = (bf16[2,256,256]{2,1,0:T(8,128)(2,1)S(1)}, bf16[2,256,256]{2,1,0:T(8,128)(2,1)S(1)}, u32[]{:S(2)}, u32[]{:S(2)}) collective-permute-start(bf16[2,256,256]{2,1,0:T(8,128)(2,1)S(1)} %pad_maximum_fusion.1), channel_id=1, source_target_pairs={{0,4},{5,1},{2,6},{7,3},{4,8},{9,5},{6,10},{11,7},{8,12},{13,9},{1... | collective-permute-start | bytes 786440 | tf_op jit(solution)/shard_map/ppermute | solution.py:31
  14.6 11.3 %collective-permute-start.3 = (bf16[2,256,256]{2,1,0:T(8,128)(2,1)S(1)}, bf16[2,256,256]{2,1,0:T(8,128)(2,1)S(1)}, u32[]{:S(2)}, u32[]{:S(2)}) collective-permute-start(bf16[2,256,256]{2,1,0:T(8,128)(2,1)S(1)} %pad_maximum_fusion), channel_id=1, source_target_pairs={{0,2},{3,1},{2,4},{5,3},{4,6},{7,5},{6,8},{9,7},{8,10},{11,9},{10,... | collective-permute-start | bytes 786440 | tf_op jit(solution)/shard_map/ppermute | solution.py:31
  26.0 1.6 %collective-permute-start.5 = (bf16[2,256,256]{2,1,0:T(8,128)(2,1)S(1)}, bf16[2,256,256]{2,1,0:T(8,128)(2,1)S(1)}, u32[]{:S(2)}, u32[]{:S(2)}) collective-permute-start(bf16[2,256,256]{2,1,0:T(8,128)(2,1)S(1)} %pad_maximum_fusion.2), channel_id=1, source_target_pairs={{0,1},{1,0},{2,3},{3,2},{4,5},{5,4},{6,7},{7,6},{8,9},{9,8},{10,11... | collective-permute-start | bytes 786440 | tf_op jit(solution)/shard_map/ppermute | solution.py:22
  26.1 1.7 %collective-permute-start = (bf16[256,256]{1,0:T(8,128)(2,1)S(1)}, bf16[256,256]{1,0:T(8,128)(2,1)S(1)}, u32[]{:S(2)}, u32[]{:S(2)}) collective-permute-start(bf16[256,256]{1,0:T(8,128)(2,1)S(1)} %copy-done.3), channel_id=1, source_target_pairs={{0,1},{1,0},{2,3},{3,2},{4,5},{5,4},{6,7},{7,6},{8,9},{9,8},{10,11... | collective-permute-start | bytes 393224 | tf_op jit(solution)/shard_map/ppermute | solution.py:22
  27.9 8.3 %collective-permute-start.6 = (bf16[2,256,256]{2,1,0:T(8,128)(2,1)S(1)}, bf16[2,256,256]{2,1,0:T(8,128)(2,1)S(1)}, u32[]{:S(2)}, u32[]{:S(2)}) collective-permute-start(bf16[2,256,256]{2,1,0:T(8,128)(2,1)S(1)} %add_convert_fusion.m), channel_id=1, source_target_pairs={{0,2},{3,1},{2,4},{5,3},{4,6},{7,5},{6,8},{9,7},{8,10},{11,9},{10,... | collective-permute-start | bytes 786440 | tf_op jit(solution)/shard_map/ppermute | solution.py:31
  31.3 9.9 %collective-permute-start.7 = (bf16[2,256,256]{2,1,0:T(8,128)(2,1)S(1)}, bf16[2,256,256]{2,1,0:T(8,128)(2,1)S(1)}, u32[]{:S(2)}, u32[]{:S(2)}) collective-permute-start(bf16[2,256,256]{2,1,0:T(8,128)(2,1)S(1)} %add_convert_fusion.m), channel_id=1, source_target_pairs={{0,4},{5,1},{2,6},{7,3},{4,8},{9,5},{6,10},{11,7},{8,12},{13,9},{1... | collective-permute-start | bytes 786440 | tf_op jit(solution)/shard_map/ppermute | solution.py:31
  36.2 5.0 %collective-permute-start.8 = (bf16[2,256,256]{2,1,0:T(8,128)(2,1)S(1)}, bf16[2,256,256]{2,1,0:T(8,128)(2,1)S(1)}, u32[]{:S(2)}, u32[]{:S(2)}) collective-permute-start(bf16[2,256,256]{2,1,0:T(8,128)(2,1)S(1)} %collective-permute-done.6.q1), channel_id=1, source_target_pairs={{0,1},{1,0},{2,3},{3,2},{4,5},{5,4},{6,7},{7,6},{8,9},{9,8},{10,11... | collective-permute-start | bytes 786440 | tf_op jit(solution)/shard_map/ppermute | solution.py:22
  41.2 1.5 %collective-permute-start.9 = (bf16[2,256,256]{2,1,0:T(8,128)(2,1)S(1)}, bf16[2,256,256]{2,1,0:T(8,128)(2,1)S(1)}, u32[]{:S(2)}, u32[]{:S(2)}) collective-permute-start(bf16[2,256,256]{2,1,0:T(8,128)(2,1)S(1)} %collective-permute-done.7.q2), channel_id=1, source_target_pairs={{0,1},{1,0},{2,3},{3,2},{4,5},{5,4},{6,7},{7,6},{8,9},{9,8},{10,11... | collective-permute-start | bytes 786440 | tf_op jit(solution)/shard_map/ppermute | solution.py:22
  50.8 1.6 %collective-permute-start.10 = (bf16[2,256,256]{2,1,0:T(8,128)(2,1)S(1)}, bf16[2,256,256]{2,1,0:T(8,128)(2,1)S(1)}, u32[]{:S(2)}, u32[]{:S(2)}) collective-permute-start(bf16[2,256,256]{2,1,0:T(8,128)(2,1)S(1)} %get-tuple-element.40), channel_id=1, source_target_pairs={{0,1},{1,0},{2,3},{3,2},{4,5},{5,4},{6,7},{7,6},{8,9},{9,8},{10,11... | collective-permute-start | bytes 786440 | tf_op jit(solution)/shard_map/ppermute | solution.py:22
  52.5 15.0 %collective-permute-start.12 = (bf16[2,256,256]{2,1,0:T(8,128)(2,1)S(1)}, bf16[2,256,256]{2,1,0:T(8,128)(2,1)S(1)}, u32[]{:S(2)}, u32[]{:S(2)}) collective-permute-start(bf16[2,256,256]{2,1,0:T(8,128)(2,1)S(1)} %pad_maximum_fusion.4), channel_id=1, source_target_pairs={{0,4},{5,1},{2,6},{7,3},{4,8},{9,5},{6,10},{11,7},{8,12},{13,9},{1... | collective-permute-start | bytes 786440 | tf_op jit(solution)/shard_map/ppermute | solution.py:31
  58.5 11.4 %collective-permute-start.11 = (bf16[2,256,256]{2,1,0:T(8,128)(2,1)S(1)}, bf16[2,256,256]{2,1,0:T(8,128)(2,1)S(1)}, u32[]{:S(2)}, u32[]{:S(2)}) collective-permute-start(bf16[2,256,256]{2,1,0:T(8,128)(2,1)S(1)} %pad_maximum_fusion.3), channel_id=1, source_target_pairs={{0,2},{3,1},{2,4},{5,3},{4,6},{7,5},{6,8},{9,7},{8,10},{11,9},{10,... | collective-permute-start | bytes 786440 | tf_op jit(solution)/shard_map/ppermute | solution.py:31
  61.6 8.6 %collective-permute-start.14 = (bf16[512,256]{1,0:T(8,128)(2,1)S(1)}, bf16[512,256]{1,0:T(8,128)(2,1)S(1)}, u32[]{:S(2)}, u32[]{:S(2)}) collective-permute-start(bf16[512,256]{1,0:T(8,128)(2,1)S(1)} %copy-done.1), channel_id=1, source_target_pairs={{0,1},{1,0},{2,3},{3,2},{4,5},{5,4},{6,7},{7,6},{8,9},{9,8},{10,11... | collective-permute-start | bytes 786440 | tf_op jit(solution)/shard_map/ppermute | solution.py:22
  70.1 1.6 %collective-permute-start.13 = (bf16[2,256,256]{2,1,0:T(8,128)(2,1)S(1)}, bf16[2,256,256]{2,1,0:T(8,128)(2,1)S(1)}, u32[]{:S(2)}, u32[]{:S(2)}) collective-permute-start(bf16[2,256,256]{2,1,0:T(8,128)(2,1)S(1)} %pad_maximum_fusion.5.s), channel_id=1, source_target_pairs={{0,1},{1,0},{2,3},{3,2},{4,5},{5,4},{6,7},{7,6},{8,9},{9,8},{10,11... | collective-permute-start | bytes 786440 | tf_op jit(solution)/shard_map/ppermute | solution.py:22
  72.1 8.3 %collective-permute-start.15 = (bf16[2,256,256]{2,1,0:T(8,128)(2,1)S(1)}, bf16[2,256,256]{2,1,0:T(8,128)(2,1)S(1)}, u32[]{:S(2)}, u32[]{:S(2)}) collective-permute-start(bf16[2,256,256]{2,1,0:T(8,128)(2,1)S(1)} %shard_map.107.m), channel_id=1, source_target_pairs={{0,2},{3,1},{2,4},{5,3},{4,6},{7,5},{6,8},{9,7},{8,10},{11,9},{10,... | collective-permute-start | bytes 786440 | tf_op jit(solution)/shard_map/ppermute | solution.py:31
  75.4 9.9 %collective-permute-start.16 = (bf16[2,256,256]{2,1,0:T(8,128)(2,1)S(1)}, bf16[2,256,256]{2,1,0:T(8,128)(2,1)S(1)}, u32[]{:S(2)}, u32[]{:S(2)}) collective-permute-start(bf16[2,256,256]{2,1,0:T(8,128)(2,1)S(1)} %shard_map.107.m), channel_id=1, source_target_pairs={{0,4},{5,1},{2,6},{7,3},{4,8},{9,5},{6,10},{11,7},{8,12},{13,9},{1... | collective-permute-start | bytes 786440 | tf_op jit(solution)/shard_map/ppermute | solution.py:31
  80.3 5.0 %collective-permute-start.17 = (bf16[2,256,256]{2,1,0:T(8,128)(2,1)S(1)}, bf16[2,256,256]{2,1,0:T(8,128)(2,1)S(1)}, u32[]{:S(2)}, u32[]{:S(2)}) collective-permute-start(bf16[2,256,256]{2,1,0:T(8,128)(2,1)S(1)} %collective-permute-done.15.q1), channel_id=1, source_target_pairs={{0,1},{1,0},{2,3},{3,2},{4,5},{5,4},{6,7},{7,6},{8,9},{9,8},{10,11... | collective-permute-start | bytes 786440 | tf_op jit(solution)/shard_map/ppermute | solution.py:22
  85.3 1.5 %collective-permute-start.18 = (bf16[2,256,256]{2,1,0:T(8,128)(2,1)S(1)}, bf16[2,256,256]{2,1,0:T(8,128)(2,1)S(1)}, u32[]{:S(2)}, u32[]{:S(2)}) collective-permute-start(bf16[2,256,256]{2,1,0:T(8,128)(2,1)S(1)} %collective-permute-done.16.q2), channel_id=1, source_target_pairs={{0,1},{1,0},{2,3},{3,2},{4,5},{5,4},{6,7},{7,6},{8,9},{9,8},{10,11... | collective-permute-start | bytes 786440 | tf_op jit(solution)/shard_map/ppermute | solution.py:22

commit v6 on v5

--- a/solution.py
+++ b/solution.py
@@ -8,6 +8,7 @@
 REACH = 2
 NEAR = 2 * REACH + 1
 OWNER_BLOCKS = 2
+SLOTS = 4
 
 FL, BF = jnp.float32, jnp.bfloat16
 ROWS_BY_ROWS = (((0,), (0,)), ((), ()))
@@ -65,36 +66,38 @@
 def lift_kernel(a_hbm, g_hbm, w_hbm, pm_hbm, pc_hbm, a_ref, w_ref, x_ref, pm_ref, pc_ref, g_ref, sems):
     blocks, slots, rows, points = a_ref.shape
     pairs = slots * rows
-    early = min(3, blocks)
-    head, tail = pl.ds(0, early), pl.ds(early, blocks - early)
-    copies = fetch(
-        [
-            (g_hbm, g_ref), (a_hbm.at[head], a_ref.at[head]), (a_hbm.at[tail], a_ref.at[tail]),
-            (w_hbm, w_ref), (pm_hbm, pm_ref), (pc_hbm, pc_ref),
-        ],
-        sems,
-    )
+    early = 2
+    parts = []
+    for start, size in ((0, early), (early, blocks - early)):
+        points_at, blocks_at = pl.ds(start * points, size * points), pl.ds(start, size)
+        parts.append((g_hbm.at[points_at], g_ref.at[points_at]))
+        parts.append((a_hbm.at[blocks_at], a_ref.at[blocks_at]))
+    copies = fetch([*parts, (w_hbm, w_ref), (pm_hbm, pm_ref), (pc_hbm, pc_ref)], sems)
     for copy in copies[:2]:
         copy.wait()
     for block in range(blocks):
         if block == early:
-            copies[2].wait()
+            for copy in copies[2:4]:
+                copy.wait()
         weights = a_ref[block].reshape(pairs, points)
         x = dot(weights, g_ref[block * points : (block + 1) * points])
         x_ref[block * pairs : (block + 1) * pairs] = x.astype(BF)
-    for copy in copies[3:]:
+    for copy in copies[4:]:
         copy.wait()
 
 
+def by_side(w_ref):
+    half = w_ref.shape[0] // 2
+    core = lax.axis_index("mp")
+    return [w_ref[pl.ds(pl.multiple_of(side * half, half), half)] for side in (core, 1 - core)]
+
+
 def encode_kernel(
-    pm, pc, a_ref, w_ref, x_own, g_other, x_other, slope_ref, own, mine, other, total
+    pm, pc, a_ref, w_ref, x_own, g_other, x_other, own, mine, other, total
 ):
     blocks, slots, rows, points = a_ref.shape
     pairs = slots * rows
-    half = x_own.shape[1]
-    core = lax.axis_index("mp")
-    w_own = w_ref[pl.ds(pl.multiple_of(core * half, half), half)]
-    w_far = w_ref[pl.ds(pl.multiple_of((1 - core) * half, half), half)]
+    w_own, w_far = by_side(w_ref)
     total[...] = jnp.zeros_like(total)
     for block in range(blocks):
         span = slice(block * pairs, (block + 1) * pairs)
@@ -105,12 +108,23 @@
         for slot in range(slots):
             part = u[slot * rows : (slot + 1) * rows]
             sig = sigmoid(part)
-            edge = part * sig
-            live = live_of(pc, block, slot)
-            total[place(pm, block, slot, 1)] += edge * live
-            slope = (sig + edge * (1.0 - sig)) * (0.25 * live)
+            total[place(pm, block, slot, 1)] += part * sig * live_of(pc, block, slot)
+    split_slabs(total, own, mine, other)
+
+
+def slope_kernel(pc, w_ref, x_own, x_other, slope_ref):
+    blocks = pc.shape[0]
+    pairs = x_own.shape[0] // blocks
+    rows = pairs // SLOTS
+    w_own, w_far = by_side(w_ref)
+    for block in range(blocks):
+        span = slice(block * pairs, (block + 1) * pairs)
+        u = dot(x_own[span], w_own) + dot(x_other[span], w_far)
+        for slot in range(SLOTS):
+            part = u[slot * rows : (slot + 1) * rows]
+            sig = sigmoid(part)
+            slope = (sig + part * sig * (1.0 - sig)) * (0.25 * live_of(pc, block, slot))
             slope_ref[block * pairs + slot * rows : block * pairs + (slot + 1) * rows] = slope.astype(BF)
-    split_slabs(total, own, mine, other)
 
 
 def gather_near(near, refs, picks):
@@ -155,8 +169,11 @@
             slope = sig + edge * (1.0 - sig)
             dz = ((upstream * live) * slope).astype(BF)
             dz_ref[block * pairs + slot * points : block * pairs + (slot + 1) * points] = dz
+        out_ref[span] = result.astype(BF)
+    for block in range(blocks):
+        for slot in range(slots):
+            dz = dz_ref[block * pairs + slot * points : block * pairs + (slot + 1) * points]
             total[place(pm, block, slot, 1)] += dot(a_ref[block, slot], dz)
-        out_ref[span] = result.astype(BF)
     split_slabs(total, own, mine, other)
 
 
@@ -307,7 +324,7 @@
         in_specs=[HBM] * 5,
         out_specs=[VMEM, VMEM, VMEM, SMEM, SMEM],
         out_shape=[shape_of(*interp.shape), shape_of(*w_enc.shape), shape_of(pairs, half), *fixed],
-        scratch_shapes=[pltpu.VMEM(grid.shape, BF), pltpu.SemaphoreType.DMA((6,))],
+        scratch_shapes=[pltpu.VMEM(grid.shape, BF), pltpu.SemaphoreType.DMA((7,))],
         compiler_params=params(),
         cost_estimate=cost,
     )(*(pltpu.with_memory_space_constraint(value, pltpu.HBM) for value in given))
@@ -319,9 +336,19 @@
     return held(
         encode_kernel,
         [SMEM, SMEM, *[VMEM] * 4],
-        [shape_of(pairs, half), shape_of(pairs, half), *slab_shapes(OWNER_BLOCKS * rows, half)],
+        [shape_of(pairs, half), *slab_shapes(OWNER_BLOCKS * rows, half)],
         [pltpu.VMEM((NEAR * OWNER_BLOCKS, rows, half), FL)],
     )(pair_mesh, pair_count, interp, w_enc, x_own, grid_other)
+
+
+def slopes(pair_count, w_enc, x_own, x_other):
+    pairs, half = x_own.shape
+    cost = pl.CostEstimate(
+        flops=4 * pairs * half * half, bytes_accessed=6 * pairs * half, transcendentals=pairs * half
+    )
+    return held(slope_kernel, [SMEM, *[VMEM] * 3], shape_of(pairs, half), cost=cost)(
+        pair_count, w_enc, x_own, x_other
+    )
 
 
 def decode(pair_mesh, pair_count, interp, grid, cotangent, w_dec, near):
@@ -371,10 +398,9 @@
     w_dec_other = swap(w_dec)
 
     interp, w_enc, x_own, pair_mesh, pair_count = lift_own(interp, grid, w_enc, pair_mesh, pair_count)
-    x_other, slope, own, mine, other = encode(
-        pair_mesh, pair_count, interp, w_enc, x_own, grid_other
-    )
-    sums, got, _ = reduce_to_owner(own, mine, other)
+    x_other, own, mine, other = encode(pair_mesh, pair_count, interp, w_enc, x_own, grid_other)
+    slope = slopes(pair_count, w_enc, x_own, x_other)
+    sums, got, slope = reduce_to_owner(own, mine, other, slope)
     agg = sums.astype(FL) + got.astype(FL)[::-1]
     mesh_lat = (mesh_both.astype(FL) + 0.25 * agg).astype(BF)
     near = spread_from_owner(mesh_lat)

time: 150 us -> 146 us (0.973)
  waiting for transfers between devices: 34.6 us -> 31.6 us
    ppermute x8, waiting for transfers between devices: 26.3 us -> 23.3 us  [outward(): return lax.ppermute(value, ('band', 'mp'), pairs)]
    pallas_call x1, Pallas kernels: 8.08 us -> 5.51 us  [decode(): held(decode_kernel, [SMEM, SMEM, *[VMEM] * (4 + NEAR)], [shape_of(*grid.s...]
    pallas_call x1 -> x2, Pallas kernels: 4.54 us -> 6.56 us  [the longest x1 3.62 us: encode(): held(encode_kernel, [SMEM, SMEM, *[VMEM] * 4], [shape_of(pairs, half), *s...]
  transfers between devices with their start and end apart: 19 -> 19, of which waited for: 15 -> 15; matrix products, arithmetic and copies ran while one was open for 0% -> 0% of each run, Pallas kernels for 4% -> 6%
where the time goes in v6:
time: 146 us
  blocking collectives  59.1 us (40%)
  starting transfers between devices  32.3 us (22%)
  waiting for transfers between devices  31.6 us (22%)
  Pallas kernels  21.2 us (15%)
    all_to_all x3, blocking collectives, exchange(): lax.all_to_all(value, 'band', 0, 0, tiled=True, axis_index_groups=groups)  59.1 us
    ppermute x8, starting transfers between devices, outward(): return lax.ppermute(value, ('band', 'mp'), pairs)  30.7 us
    ppermute x8, waiting for transfers between devices, outward(): return lax.ppermute(value, ('band', 'mp'), pairs)  23.3 us
    ppermute x11, waiting for transfers between devices, swap(): return lax.ppermute(value, 'mp', [(0, 1), (1, 0)])  8.28 us
    pallas_call x1, Pallas kernels, decode(): held(decode_kernel, [SMEM, SMEM, *[VMEM] * (4 + NEAR)], [shape_of(*grid.s...  5.51 us
    pallas_call x1, Pallas kernels, encode(): held(encode_kernel, [SMEM, SMEM, *[VMEM] * 4], [shape_of(pairs, half), *s...  3.62 us
    pallas_call x1, Pallas kernels, lift_own(): pl.pallas_call(lift_kernel, in_specs=[HBM] * 5, out_specs=[VMEM, VMEM, VM...  2.95 us
    pallas_call x1, Pallas kernels, slopes(): held(slope_kernel, [SMEM, *[VMEM] * 3], shape_of(pairs, half), cost=cost)  2.95 us
  transfers between devices with their start and end apart: 19, of which 15 were waited for; matrix products, arithmetic and copies ran while one was open for 0% of the time, Pallas kernels for 6%

profile of v6, /device:TPU:8, one launch (start us, length us, event | category | flops | bytes accessed | tf_op | source)
XLA Modules:
  0.0 145.8 jit_solution(3499867551156438630)
XLA Ops:
  0.7 3.0 %shard_map.103 = (bf16[10,4,128,128]{3,2,1,0:T(8,128)(2,1)S(1)}, bf16[512,256]{1,0:T(8,128)(2,1)S(1)}, bf16[5120,256]{1,0:T(8,128)(2,1)S(1)}, s32[4,10]{1,0:T(4,128)S(1)}, s32[10]{0:T(128)S(1)}) custom-call(bf16[10,4,128,128]{3,2,1,0:T(8,128)(2,1)} %a_hbm.1, bf16[1280,256]{1,0:T(8,128)(2,1)} %g_ref.1, bf16[512,256]{1,0:T(8,128)(2,1)} %w_hbm.1, ...), custom_call_target="tpu_custom_call" | custom-call | flops 335544320 | bytes 4194304 | tf_op jit(solution)/shard_map/pallas_call | solution.py:322
  3.7 3.6 %shard_map.104 = (bf16[5120,256]{1,0:T(8,128)(2,1)S(1)}, bf16[256,256]{1,0:T(8,128)(2,1)S(1)}, bf16[2,256,256]{2,1,0:T(8,128)(2,1)S(1)}, bf16[2,256,256]{2,1,0:T(8,128)(2,1)S(1)}) custom-call(s32[4,10]{1,0:T(4,128)S(1)} %get-tuple-element.29.pm, s32[10]{0:T(128)S(1)} %get-tuple-element.30.pc, bf16[10,4,128,128]{3,2,1,0:T(8,128)(2,1)S(1)} %get-tuple-element.31.a_ref, ...), custom_call_target="tpu_custom_call" | custom-call | tf_op jit(solution)/shard_map/pallas_call | solution.py:336
  7.3 0.6 collective-permute-start.2
  7.9 1.1 collective-permute-done.2
  9.1 4.2 %collective-permute-start.4 = (bf16[2,256,256]{2,1,0:T(8,128)(2,1)S(1)}, bf16[2,256,256]{2,1,0:T(8,128)(2,1)S(1)}, u32[]{:S(2)}, u32[]{:S(2)}) collective-permute-start(bf16[2,256,256]{2,1,0:T(8,128)(2,1)S(1)} %pad_maximum_fusion.1), channel_id=1, source_target_pairs={{0,4},{5,1},{2,6},{7,3},{4,8},{9,5},{6,10},{11,7},{8,12},{13,9},{1... | collective-permute-start | bytes 786440 | tf_op jit(solution)/shard_map/ppermute | solution.py:32
  13.4 2.4 %collective-permute-start.3 = (bf16[2,256,256]{2,1,0:T(8,128)(2,1)S(1)}, bf16[2,256,256]{2,1,0:T(8,128)(2,1)S(1)}, u32[]{:S(2)}, u32[]{:S(2)}) collective-permute-start(bf16[2,256,256]{2,1,0:T(8,128)(2,1)S(1)} %pad_maximum_fusion), channel_id=1, source_target_pairs={{0,2},{3,1},{2,4},{5,3},{4,6},{7,5},{6,8},{9,7},{8,10},{11,9},{10,... | collective-permute-start | bytes 786440 | tf_op jit(solution)/shard_map/ppermute | solution.py:32
  15.8 2.9 %shard_map.105.slope_ref = bf16[5120,256]{1,0:T(8,128)(2,1)S(1)} custom-call(s32[10]{0:T(128)S(1)} %get-tuple-element.30.pc, bf16[512,256]{1,0:T(8,128)(2,1)S(1)} %get-tuple-element.32.w_ref, bf16[5120,256]{1,0:T(8,128)(2,1)S(1)} %get-tuple-element.33.x_own, bf16[5120,256]{1,0:T(8,128)(2,1)S(1)} %get-tuple-element.36.x_other), custom_call_target="tpu_custom_call" | custom-call | flops 1342177280 | bytes 7864320 | tf_op jit(solution)/shard_map/pallas_call | solution.py:349
  18.8 3.6 %collective-permute-done.4 = bf16[2,256,256]{2,1,0:T(8,128)(2,1)S(1)} collective-permute-done((bf16[2,256,256]{2,1,0:T(8,128)(2,1)S(1)}, bf16[2,256,256]{2,1,0:T(8,128)(2,1)S(1)}, u32[]{:S(2)}, u32[]{:S(2)}) %collective-permute-start.4) | collective-permute-done | bytes 262176 | tf_op jit(solution)/shard_map/ppermute | solution.py:32
  22.5 2.2 %collective-permute-done.3 = bf16[2,256,256]{2,1,0:T(8,128)(2,1)S(1)} collective-permute-done((bf16[2,256,256]{2,1,0:T(8,128)(2,1)S(1)}, bf16[2,256,256]{2,1,0:T(8,128)(2,1)S(1)}, u32[]{:S(2)}, u32[]{:S(2)}) %collective-permute-start.3) | collective-permute-done | bytes 262176 | tf_op jit(solution)/shard_map/ppermute | solution.py:32
  25.4 1.0 collective-permute-done.5
  26.8 3.3 %collective-permute-start.6 = (bf16[2,256,256]{2,1,0:T(8,128)(2,1)S(1)}, bf16[2,256,256]{2,1,0:T(8,128)(2,1)S(1)}, u32[]{:S(2)}, u32[]{:S(2)}) collective-permute-start(bf16[2,256,256]{2,1,0:T(8,128)(2,1)S(1)} %add_convert_fusion.m), channel_id=1, source_target_pairs={{0,2},{3,1},{2,4},{5,3},{4,6},{7,5},{6,8},{9,7},{8,10},{11,9},{10,... | collective-permute-start | bytes 786440 | tf_op jit(solution)/shard_map/ppermute | solution.py:32
  30.1 3.9 %collective-permute-start.7 = (bf16[2,256,256]{2,1,0:T(8,128)(2,1)S(1)}, bf16[2,256,256]{2,1,0:T(8,128)(2,1)S(1)}, u32[]{:S(2)}, u32[]{:S(2)}) collective-permute-start(bf16[2,256,256]{2,1,0:T(8,128)(2,1)S(1)} %add_convert_fusion.m), channel_id=1, source_target_pairs={{0,4},{5,1},{2,6},{7,3},{4,8},{9,5},{6,10},{11,7},{8,12},{13,9},{1... | collective-permute-start | bytes 786440 | tf_op jit(solution)/shard_map/ppermute | solution.py:32
  34.0 1.0 collective-permute-done.6.q1
  35.0 5.0 %collective-permute-done.7.q2 = bf16[2,256,256]{2,1,0:T(8,128)(2,1)S(1)} collective-permute-done((bf16[2,256,256]{2,1,0:T(8,128)(2,1)S(1)}, bf16[2,256,256]{2,1,0:T(8,128)(2,1)S(1)}, u32[]{:S(2)}, u32[]{:S(2)}) %collective-permute-start.7) | collective-permute-done | bytes 262176 | tf_op jit(solution)/shard_map/ppermute | solution.py:32
  40.0 1.5 %collective-permute-done.9.t2 = bf16[2,256,256]{2,1,0:T(8,128)(2,1)S(1)} collective-permute-done((bf16[2,256,256]{2,1,0:T(8,128)(2,1)S(1)}, bf16[2,256,256]{2,1,0:T(8,128)(2,1)S(1)}, u32[]{:S(2)}, u32[]{:S(2)}) %collective-permute-start.9) | collective-permute-done | bytes 262176 | tf_op jit(solution)/shard_map/ppermute | solution.py:23
  41.6 5.5 %shard_map.106 = (bf16[1280,256]{1,0:T(8,128)(2,1)S(1)}, bf16[5120,512]{1,0:T(8,128)(2,1)S(1)}, bf16[5120,256]{1,0:T(8,128)(2,1)S(1)}, bf16[256,256]{1,0:T(8,128...) custom-call(s32[4,10]{1,0:T(4,128)S(1)} %get-tuple-element.29.pm, ...), custom_call_target="tpu_custom_call" | custom-call | tf_op jit(solution)/shard_map/pallas_call | solution.py:358
  47.3 1.4 collective-permute-done.10
  48.8 6.0 %collective-permute-start.12 = (bf16[2,256,256]{2,1,0:T(8,128)(2,1)S(1)}, bf16[2,256,256]{2,1,0:T(8,128)(2,1)S(1)}, u32[]{:S(2)}, u32[]{:S(2)}) collective-permute-start(bf16[2,256,256]{2,1,0:T(8,128)(2,1)S(1)} %pad_maximum_fusion.4), channel_id=1, source_target_pairs={{0,4},{5,1},{2,6},{7,3},{4,8},{9,5},{6,10},{11,7},{8,12},{13,9},{1... | collective-permute-start | bytes 786440 | tf_op jit(solution)/shard_map/ppermute | solution.py:32
  54.8 3.1 %collective-permute-start.11 = (bf16[2,256,256]{2,1,0:T(8,128)(2,1)S(1)}, bf16[2,256,256]{2,1,0:T(8,128)(2,1)S(1)}, u32[]{:S(2)}, u32[]{:S(2)}) collective-permute-start(bf16[2,256,256]{2,1,0:T(8,128)(2,1)S(1)} %pad_maximum_fusion.3), channel_id=1, source_target_pairs={{0,2},{3,1},{2,4},{5,3},{4,6},{7,5},{6,8},{9,7},{8,10},{11,9},{10,... | collective-permute-start | bytes 786440 | tf_op jit(solution)/shard_map/ppermute | solution.py:32
  58.0 2.3 %shard_map.107 = (f32[256,512]{1,0:T(8,128)S(1)}, bf16[1280,256]{1,0:T(8,128)(2,1)}) custom-call(bf16[5120,512]{1,0:T(8,128)(2,1)S(1)} %get-tuple-element.42.left_ref, bf16[5120,256]{1,0:T(8,128)(2,1)S(1)} %get-tuple-element.43.right_ref, bf16[1280,256]{1,0:T(8,128)(2,1)S(1)} %get-tuple-element.44.made_ref), custom_call_target="tpu_custom_call" | custom-call | flops 1342177280 | bytes 7864320 | tf_op jit(solution)/shard_map/pallas_call | solution.py:379
  60.2 3.6 %collective-permute-done.12 = bf16[2,256,256]{2,1,0:T(8,128)(2,1)S(1)} collective-permute-done((bf16[2,256,256]{2,1,0:T(8,128)(2,1)S(1)}, bf16[2,256,256]{2,1,0:T(8,128)(2,1)S(1)}, u32[]{:S(2)}, u32[]{:S(2)}) %collective-permute-start.12) | collective-permute-done | bytes 262176 | tf_op jit(solution)/shard_map/ppermute | solution.py:32
  63.8 2.3 %collective-permute-done.11 = bf16[2,256,256]{2,1,0:T(8,128)(2,1)S(1)} collective-permute-done((bf16[2,256,256]{2,1,0:T(8,128)(2,1)S(1)}, bf16[2,256,256]{2,1,0:T(8,128)(2,1)S(1)}, u32[]{:S(2)}, u32[]{:S(2)}) %collective-permute-start.11) | collective-permute-done | bytes 262176 | tf_op jit(solution)/shard_map/ppermute | solution.py:32
  66.4 1.5 %collective-permute-done.13.t = bf16[2,256,256]{2,1,0:T(8,128)(2,1)S(1)} collective-permute-done((bf16[2,256,256]{2,1,0:T(8,128)(2,1)S(1)}, bf16[2,256,256]{2,1,0:T(8,128)(2,1)S(1)}, u32[]{:S(2)}, u32[]{:S(2)}) %collective-permute-start.13) | collective-permute-done | bytes 262176 | tf_op jit(solution)/shard_map/ppermute | solution.py:23
  68.3 3.3 %collective-permute-start.15 = (bf16[2,256,256]{2,1,0:T(8,128)(2,1)S(1)}, bf16[2,256,256]{2,1,0:T(8,128)(2,1)S(1)}, u32[]{:S(2)}, u32[]{:S(2)}) collective-permute-start(bf16[2,256,256]{2,1,0:T(8,128)(2,1)S(1)} %shard_map.108.m), channel_id=1, source_target_pairs={{0,2},{3,1},{2,4},{5,3},{4,6},{7,5},{6,8},{9,7},{8,10},{11,9},{10,... | collective-permute-start | bytes 786440 | tf_op jit(solution)/shard_map/ppermute | solution.py:32
  71.6 4.4 %collective-permute-start.16 = (bf16[2,256,256]{2,1,0:T(8,128)(2,1)S(1)}, bf16[2,256,256]{2,1,0:T(8,128)(2,1)S(1)}, u32[]{:S(2)}, u32[]{:S(2)}) collective-permute-start(bf16[2,256,256]{2,1,0:T(8,128)(2,1)S(1)} %shard_map.108.m), channel_id=1, source_target_pairs={{0,4},{5,1},{2,6},{7,3},{4,8},{9,5},{6,10},{11,7},{8,12},{13,9},{1... | collective-permute-start | bytes 786440 | tf_op jit(solution)/shard_map/ppermute | solution.py:32
  76.6 5.0 %collective-permute-done.16.q2 = bf16[2,256,256]{2,1,0:T(8,128)(2,1)S(1)} collective-permute-done((bf16[2,256,256]{2,1,0:T(8,128)(2,1)S(1)}, bf16[2,256,256]{2,1,0:T(8,128)(2,1)S(1)}, u32[]{:S(2)}, u32[]{:S(2)}) %collective-permute-start.16) | collective-permute-done | bytes 262176 | tf_op jit(solution)/shard_map/ppermute | solution.py:32
  81.6 1.5 %collective-permute-done.18.t2 = bf16[2,256,256]{2,1,0:T(8,128)(2,1)S(1)} collective-permute-done((bf16[2,256,256]{2,1,0:T(8,128)(2,1)S(1)}, bf16[2,256,256]{2,1,0:T(8,128)(2,1)S(1)}, u32[]{:S(2)}, u32[]{:S(2)}) %collective-permute-start.18) | collective-permute-done | bytes 262176 | tf_op jit(solution)/shard_map/ppermute | solution.py:23
  83.1 2.3 %shard_map.109 = bf16[2048,128]{1,0:T(8,128)(2,1)S(1)} custom-call(s32[4,10]{1,0:T(4,128)S(1)} %get-tuple-element.29.pm, s32[10]{0:T(128)S(1)} %get-tuple-element.30.pc, bf16[5120,256]{1,0:T(8,128)(2,1)S(1)} %get-tuple-element.33.x_own, bf16[5120,256]{1,0:T(8,128)(2,1)S(1)} %get-tuple-element.36.x_other, bf16[5120,256]{1,0:T(8,128)(2,1)S(1)} %shard_map.105.slope_ref, ...), custom_call_target="tpu_custom_call" | custom-call | tf_op jit(solution)/shard_map/pallas_call | solution.py:385
  85.4 23.8 %all_to_all.15.parts_ref = bf16[16,128,128]{2,1,0:T(8,128)(2,1)S(1)} all-to-all(bf16[16,128,128]{2,1,0:T(8,128)(2,1)S(1)} %bitcast.25), channel_id=1, replica_groups={{0,2,4,6,8,10,12,14,16,18,20,22,24,26,28,30},{32,34,36,38,40,42,44,46,4..., dimensions={0} | all-to-all | bytes 1048576 | tf_op jit(solution)/shard_map/all_to_all | solution.py:262
  109.3 21.3 %all_to_all.16.parts_ref = bf16[8,128,128]{2,1,0:T(8,128)(2,1)S(1)} all-to-all(bf16[8,128,128]{2,1,0:T(8,128)(2,1)S(1)} %shard_map.110), channel_id=1, replica_groups={{0,32,64,96,128,160,192,224},{2,34,66,98,130,162,194,226},{4,36,68,100,..., dimensions={0} | all-to-all | bytes 524288 | tf_op jit(solution)/shard_map/all_to_all | solution.py:262
  130.6 14.1 %all_to_all.17 = bf16[16,128,128]{2,1,0:T(8,128)(2,1)S(1)} all-to-all(bf16[16,128,128]{2,1,0:T(8,128)(2,1)S(1)} %shard_map.111), channel_id=1, replica_groups={{0,2,4,6,8,10,12,14,16,18,20,22,24,26,28,30},{32,34,36,38,40,42,44,46,4..., dimensions={0} | all-to-all | bytes 1048576 | tf_op jit(solution)/shard_map/all_to_all | solution.py:262
  144.7 1.1 shard_map.112
  (45 shorter events, 2.9 us)
Async XLA Ops:
  0.6 3.1 %collective-permute-start.1 = (bf16[1280,256]{1,0:T(8,128)(2,1)}, bf16[1280,256]{1,0:T(8,128)(2,1)S(1)}, u32[]{:S(2)}, u32[]{:S(2)}) collective-permute-start(bf16[1280,256]{1,0:T(8,128)(2,1)} %g_ref.1), channel_id=1, source_target_pairs={{0,1},{1,0},{2,3},{3,2},{4,5},{5,4},{6,7},{7,6},{8,9},{9,8},{10,11... | collective-permute-start | bytes 1966088 | tf_op jit(solution)/shard_map/ppermute | solution.py:23
  7.3 1.7 %collective-permute-start.2 = (bf16[2,256,256]{2,1,0:T(8,128)(2,1)S(1)}, bf16[2,256,256]{2,1,0:T(8,128)(2,1)S(1)}, u32[]{:S(2)}, u32[]{:S(2)}) collective-permute-start(bf16[2,256,256]{2,1,0:T(8,128)(2,1)S(1)} %get-tuple-element.35), channel_id=1, source_target_pairs={{0,1},{1,0},{2,3},{3,2},{4,5},{5,4},{6,7},{7,6},{8,9},{9,8},{10,11... | collective-permute-start | bytes 786440 | tf_op jit(solution)/shard_map/ppermute | solution.py:23
  9.1 13.3 %collective-permute-start.4 = (bf16[2,256,256]{2,1,0:T(8,128)(2,1)S(1)}, bf16[2,256,256]{2,1,0:T(8,128)(2,1)S(1)}, u32[]{:S(2)}, u32[]{:S(2)}) collective-permute-start(bf16[2,256,256]{2,1,0:T(8,128)(2,1)S(1)} %pad_maximum_fusion.1), channel_id=1, source_target_pairs={{0,4},{5,1},{2,6},{7,3},{4,8},{9,5},{6,10},{11,7},{8,12},{13,9},{1... | collective-permute-start | bytes 786440 | tf_op jit(solution)/shard_map/ppermute | solution.py:32
  13.4 11.3 %collective-permute-start.3 = (bf16[2,256,256]{2,1,0:T(8,128)(2,1)S(1)}, bf16[2,256,256]{2,1,0:T(8,128)(2,1)S(1)}, u32[]{:S(2)}, u32[]{:S(2)}) collective-permute-start(bf16[2,256,256]{2,1,0:T(8,128)(2,1)S(1)} %pad_maximum_fusion), channel_id=1, source_target_pairs={{0,2},{3,1},{2,4},{5,3},{4,6},{7,5},{6,8},{9,7},{8,10},{11,9},{10,... | collective-permute-start | bytes 786440 | tf_op jit(solution)/shard_map/ppermute | solution.py:32
  15.8 9.1 %copy-start.3 = (bf16[256,256]{1,0:T(8,128)(2,1)S(1)}, bf16[256,256]{1,0:T(8,128)(2,1)}, u32[]{:S(2)}) copy-start(bf16[256,256]{1,0:T(8,128)(2,1)} %param.10) | copy-start | bytes 393220
  18.8 22.8 %copy-start = (bf16[1280,256]{1,0:T(8,128)(2,1)S(1)}, bf16[1280,256]{1,0:T(8,128)(2,1)}, u32[]{:S(2)}) copy-start(bf16[1280,256]{1,0:T(8,128)(2,1)} %g_ref.1) | copy-start | bytes 1966084
  18.8 22.7 %copy-start.1 = (bf16[512,256]{1,0:T(8,128)(2,1)S(1)}, bf16[512,256]{1,0:T(8,128)(2,1)}, u32[]{:S(2)}) copy-start(bf16[512,256]{1,0:T(8,128)(2,1)} %w_own.1) | copy-start | bytes 786436
  18.8 22.7 %copy-start.2 = (bf16[1280,256]{1,0:T(8,128)(2,1)S(1)}, bf16[1280,256]{1,0:T(8,128)(2,1)}, u32[]{:S(2)}) copy-start(bf16[1280,256]{1,0:T(8,128)(2,1)} %cot_ref.1) | copy-start | bytes 1966084
  24.8 1.6 %collective-permute-start.5 = (bf16[2,256,256]{2,1,0:T(8,128)(2,1)S(1)}, bf16[2,256,256]{2,1,0:T(8,128)(2,1)S(1)}, u32[]{:S(2)}, u32[]{:S(2)}) collective-permute-start(bf16[2,256,256]{2,1,0:T(8,128)(2,1)S(1)} %pad_maximum_fusion.2), channel_id=1, source_target_pairs={{0,1},{1,0},{2,3},{3,2},{4,5},{5,4},{6,7},{7,6},{8,9},{9,8},{10,11... | collective-permute-start | bytes 786440 | tf_op jit(solution)/shard_map/ppermute | solution.py:23
  24.9 1.7 %collective-permute-start = (bf16[256,256]{1,0:T(8,128)(2,1)S(1)}, bf16[256,256]{1,0:T(8,128)(2,1)S(1)}, u32[]{:S(2)}, u32[]{:S(2)}) collective-permute-start(bf16[256,256]{1,0:T(8,128)(2,1)S(1)} %copy-done.3), channel_id=1, source_target_pairs={{0,1},{1,0},{2,3},{3,2},{4,5},{5,4},{6,7},{7,6},{8,9},{9,8},{10,11... | collective-permute-start | bytes 393224 | tf_op jit(solution)/shard_map/ppermute | solution.py:23
  26.8 8.3 %collective-permute-start.6 = (bf16[2,256,256]{2,1,0:T(8,128)(2,1)S(1)}, bf16[2,256,256]{2,1,0:T(8,128)(2,1)S(1)}, u32[]{:S(2)}, u32[]{:S(2)}) collective-permute-start(bf16[2,256,256]{2,1,0:T(8,128)(2,1)S(1)} %add_convert_fusion.m), channel_id=1, source_target_pairs={{0,2},{3,1},{2,4},{5,3},{4,6},{7,5},{6,8},{9,7},{8,10},{11,9},{10,... | collective-permute-start | bytes 786440 | tf_op jit(solution)/shard_map/ppermute | solution.py:32
  30.1 9.9 %collective-permute-start.7 = (bf16[2,256,256]{2,1,0:T(8,128)(2,1)S(1)}, bf16[2,256,256]{2,1,0:T(8,128)(2,1)S(1)}, u32[]{:S(2)}, u32[]{:S(2)}) collective-permute-start(bf16[2,256,256]{2,1,0:T(8,128)(2,1)S(1)} %add_convert_fusion.m), channel_id=1, source_target_pairs={{0,4},{5,1},{2,6},{7,3},{4,8},{9,5},{6,10},{11,7},{8,12},{13,9},{1... | collective-permute-start | bytes 786440 | tf_op jit(solution)/shard_map/ppermute | solution.py:32
  35.0 5.0 %collective-permute-start.8 = (bf16[2,256,256]{2,1,0:T(8,128)(2,1)S(1)}, bf16[2,256,256]{2,1,0:T(8,128)(2,1)S(1)}, u32[]{:S(2)}, u32[]{:S(2)}) collective-permute-start(bf16[2,256,256]{2,1,0:T(8,128)(2,1)S(1)} %collective-permute-done.6.q1), channel_id=1, source_target_pairs={{0,1},{1,0},{2,3},{3,2},{4,5},{5,4},{6,7},{7,6},{8,9},{9,8},{10,11... | collective-permute-start | bytes 786440 | tf_op jit(solution)/shard_map/ppermute | solution.py:23
  40.0 1.5 %collective-permute-start.9 = (bf16[2,256,256]{2,1,0:T(8,128)(2,1)S(1)}, bf16[2,256,256]{2,1,0:T(8,128)(2,1)S(1)}, u32[]{:S(2)}, u32[]{:S(2)}) collective-permute-start(bf16[2,256,256]{2,1,0:T(8,128)(2,1)S(1)} %collective-permute-done.7.q2), channel_id=1, source_target_pairs={{0,1},{1,0},{2,3},{3,2},{4,5},{5,4},{6,7},{7,6},{8,9},{9,8},{10,11... | collective-permute-start | bytes 786440 | tf_op jit(solution)/shard_map/ppermute | solution.py:23
  47.1 1.6 %collective-permute-start.10 = (bf16[2,256,256]{2,1,0:T(8,128)(2,1)S(1)}, bf16[2,256,256]{2,1,0:T(8,128)(2,1)S(1)}, u32[]{:S(2)}, u32[]{:S(2)}) collective-permute-start(bf16[2,256,256]{2,1,0:T(8,128)(2,1)S(1)} %get-tuple-element.41), channel_id=1, source_target_pairs={{0,1},{1,0},{2,3},{3,2},{4,5},{5,4},{6,7},{7,6},{8,9},{9,8},{10,11... | collective-permute-start | bytes 786440 | tf_op jit(solution)/shard_map/ppermute | solution.py:23
  48.8 15.0 %collective-permute-start.12 = (bf16[2,256,256]{2,1,0:T(8,128)(2,1)S(1)}, bf16[2,256,256]{2,1,0:T(8,128)(2,1)S(1)}, u32[]{:S(2)}, u32[]{:S(2)}) collective-permute-start(bf16[2,256,256]{2,1,0:T(8,128)(2,1)S(1)} %pad_maximum_fusion.4), channel_id=1, source_target_pairs={{0,4},{5,1},{2,6},{7,3},{4,8},{9,5},{6,10},{11,7},{8,12},{13,9},{1... | collective-permute-start | bytes 786440 | tf_op jit(solution)/shard_map/ppermute | solution.py:32
  54.8 11.4 %collective-permute-start.11 = (bf16[2,256,256]{2,1,0:T(8,128)(2,1)S(1)}, bf16[2,256,256]{2,1,0:T(8,128)(2,1)S(1)}, u32[]{:S(2)}, u32[]{:S(2)}) collective-permute-start(bf16[2,256,256]{2,1,0:T(8,128)(2,1)S(1)} %pad_maximum_fusion.3), channel_id=1, source_target_pairs={{0,2},{3,1},{2,4},{5,3},{4,6},{7,5},{6,8},{9,7},{8,10},{11,9},{10,... | collective-permute-start | bytes 786440 | tf_op jit(solution)/shard_map/ppermute | solution.py:32
  57.9 8.6 %collective-permute-start.14 = (bf16[512,256]{1,0:T(8,128)(2,1)S(1)}, bf16[512,256]{1,0:T(8,128)(2,1)S(1)}, u32[]{:S(2)}, u32[]{:S(2)}) collective-permute-start(bf16[512,256]{1,0:T(8,128)(2,1)S(1)} %copy-done.1), channel_id=1, source_target_pairs={{0,1},{1,0},{2,3},{3,2},{4,5},{5,4},{6,7},{7,6},{8,9},{9,8},{10,11... | collective-permute-start | bytes 786440 | tf_op jit(solution)/shard_map/ppermute | solution.py:23
  66.3 1.6 %collective-permute-start.13 = (bf16[2,256,256]{2,1,0:T(8,128)(2,1)S(1)}, bf16[2,256,256]{2,1,0:T(8,128)(2,1)S(1)}, u32[]{:S(2)}, u32[]{:S(2)}) collective-permute-start(bf16[2,256,256]{2,1,0:T(8,128)(2,1)S(1)} %pad_maximum_fusion.5.s), channel_id=1, source_target_pairs={{0,1},{1,0},{2,3},{3,2},{4,5},{5,4},{6,7},{7,6},{8,9},{9,8},{10,11... | collective-permute-start | bytes 786440 | tf_op jit(solution)/shard_map/ppermute | solution.py:23
  68.3 8.3 %collective-permute-start.15 = (bf16[2,256,256]{2,1,0:T(8,128)(2,1)S(1)}, bf16[2,256,256]{2,1,0:T(8,128)(2,1)S(1)}, u32[]{:S(2)}, u32[]{:S(2)}) collective-permute-start(bf16[2,256,256]{2,1,0:T(8,128)(2,1)S(1)} %shard_map.108.m), channel_id=1, source_target_pairs={{0,2},{3,1},{2,4},{5,3},{4,6},{7,5},{6,8},{9,7},{8,10},{11,9},{10,... | collective-permute-start | bytes 786440 | tf_op jit(solution)/shard_map/ppermute | solution.py:32
  71.6 9.9 %collective-permute-start.16 = (bf16[2,256,256]{2,1,0:T(8,128)(2,1)S(1)}, bf16[2,256,256]{2,1,0:T(8,128)(2,1)S(1)}, u32[]{:S(2)}, u32[]{:S(2)}) collective-permute-start(bf16[2,256,256]{2,1,0:T(8,128)(2,1)S(1)} %shard_map.108.m), channel_id=1, source_target_pairs={{0,4},{5,1},{2,6},{7,3},{4,8},{9,5},{6,10},{11,7},{8,12},{13,9},{1... | collective-permute-start | bytes 786440 | tf_op jit(solution)/shard_map/ppermute | solution.py:32
  76.6 5.0 %collective-permute-start.17 = (bf16[2,256,256]{2,1,0:T(8,128)(2,1)S(1)}, bf16[2,256,256]{2,1,0:T(8,128)(2,1)S(1)}, u32[]{:S(2)}, u32[]{:S(2)}) collective-permute-start(bf16[2,256,256]{2,1,0:T(8,128)(2,1)S(1)} %collective-permute-done.15.q1), channel_id=1, source_target_pairs={{0,1},{1,0},{2,3},{3,2},{4,5},{5,4},{6,7},{7,6},{8,9},{9,8},{10,11... | collective-permute-start | bytes 786440 | tf_op jit(solution)/shard_map/ppermute | solution.py:23
  81.6 1.5 %collective-permute-start.18 = (bf16[2,256,256]{2,1,0:T(8,128)(2,1)S(1)}, bf16[2,256,256]{2,1,0:T(8,128)(2,1)S(1)}, u32[]{:S(2)}, u32[]{:S(2)}) collective-permute-start(bf16[2,256,256]{2,1,0:T(8,128)(2,1)S(1)} %collective-permute-done.16.q2), channel_id=1, source_target_pairs={{0,1},{1,0},{2,3},{3,2},{4,5},{5,4},{6,7},{7,6},{8,9},{9,8},{10,11... | collective-permute-start | bytes 786440 | tf_op jit(solution)/shard_map/ppermute | solution.py:23

commit v7 on v6

--- a/solution.py
+++ b/solution.py
@@ -9,6 +9,7 @@
 NEAR = 2 * REACH + 1
 OWNER_BLOCKS = 2
 SLOTS = 4
+LEAST, USUAL = 2, 3
 
 FL, BF = jnp.float32, jnp.bfloat16
 ROWS_BY_ROWS = (((0,), (0,)), ((), ()))
@@ -43,6 +44,20 @@
 
 def live_of(pc, block, slot):
     return jnp.where(slot < pc[block], 1.0, 0.0).astype(FL)
+
+
+def largest(pc):
+    most = pc[0]
+    for block in range(1, pc.shape[0]):
+        most = jnp.maximum(most, pc[block])
+    return most
+
+
+def by_count(pc, slots, body):
+    most = largest(pc)
+    for used in range(LEAST, slots + 1):
+        fits = most <= used if used == LEAST else (most >= used if used == slots else most == used)
+        pl.when(fits)(lambda used=used: body(used))
 
 
 def split_slabs(total, own, mine, other):
@@ -73,16 +88,21 @@
         parts.append((g_hbm.at[points_at], g_ref.at[points_at]))
         parts.append((a_hbm.at[blocks_at], a_ref.at[blocks_at]))
     copies = fetch([*parts, (w_hbm, w_ref), (pm_hbm, pm_ref), (pc_hbm, pc_ref)], sems)
+    copies[-1].wait()
     for copy in copies[:2]:
         copy.wait()
-    for block in range(blocks):
-        if block == early:
-            for copy in copies[2:4]:
-                copy.wait()
-        weights = a_ref[block].reshape(pairs, points)
-        x = dot(weights, g_ref[block * points : (block + 1) * points])
-        x_ref[block * pairs : (block + 1) * pairs] = x.astype(BF)
-    for copy in copies[4:]:
+
+    def body(used):
+        for block in range(blocks):
+            if block == early:
+                for copy in copies[2:4]:
+                    copy.wait()
+            weights = a_ref[block, :used].reshape(used * rows, points)
+            x = dot(weights, g_ref[block * points : (block + 1) * points])
+            x_ref[block * pairs : block * pairs + used * rows] = x.astype(BF)
+
+    by_count(pc_ref, slots, body)
+    for copy in copies[4:-1]:
         copy.wait()
 
 
@@ -97,18 +117,22 @@
 ):
     blocks, slots, rows, points = a_ref.shape
     pairs = slots * rows
-    w_own, w_far = by_side(w_ref)
     total[...] = jnp.zeros_like(total)
-    for block in range(blocks):
-        span = slice(block * pairs, (block + 1) * pairs)
-        weights = a_ref[block].reshape(pairs, points)
-        x = dot(weights, g_other[block * points : (block + 1) * points]).astype(BF)
-        x_other[span] = x
-        u = dot(x_own[span], w_own) + dot(x, w_far)
-        for slot in range(slots):
-            part = u[slot * rows : (slot + 1) * rows]
-            sig = sigmoid(part)
-            total[place(pm, block, slot, 1)] += part * sig * live_of(pc, block, slot)
+
+    def body(used):
+        w_own, w_far = by_side(w_ref)
+        for block in range(blocks):
+            span = slice(block * pairs, block * pairs + used * rows)
+            weights = a_ref[block, :used].reshape(used * rows, points)
+            x = dot(weights, g_other[block * points : (block + 1) * points]).astype(BF)
+            x_other[span] = x
+            u = dot(x_own[span], w_own) + dot(x, w_far)
+            for slot in range(used):
+                part = u[slot * rows : (slot + 1) * rows]
+                sig = sigmoid(part)
+                total[place(pm, block, slot, 1)] += part * sig * live_of(pc, block, slot)
+
+    by_count(pc, slots, body)
     split_slabs(total, own, mine, other)
 
 
@@ -116,15 +140,20 @@
     blocks = pc.shape[0]
     pairs = x_own.shape[0] // blocks
     rows = pairs // SLOTS
-    w_own, w_far = by_side(w_ref)
-    for block in range(blocks):
-        span = slice(block * pairs, (block + 1) * pairs)
-        u = dot(x_own[span], w_own) + dot(x_other[span], w_far)
-        for slot in range(SLOTS):
-            part = u[slot * rows : (slot + 1) * rows]
-            sig = sigmoid(part)
-            slope = (sig + part * sig * (1.0 - sig)) * (0.25 * live_of(pc, block, slot))
-            slope_ref[block * pairs + slot * rows : block * pairs + (slot + 1) * rows] = slope.astype(BF)
+
+    def body(used):
+        w_own, w_far = by_side(w_ref)
+        for block in range(blocks):
+            span = slice(block * pairs, block * pairs + used * rows)
+            u = dot(x_own[span], w_own) + dot(x_other[span], w_far)
+            for slot in range(used):
+                part = u[slot * rows : (slot + 1) * rows]
+                sig = sigmoid(part)
+                slope = (sig + part * sig * (1.0 - sig)) * (0.25 * live_of(pc, block, slot))
+                at = block * pairs + slot * rows
+                slope_ref[at : at + rows] = slope.astype(BF)
+
+    by_count(pc, SLOTS, body)
 
 
 def gather_near(near, refs, picks):
@@ -151,35 +180,80 @@
     pairs = slots * points
     total[...] = jnp.zeros_like(total)
     gather_near(near, (m, q1, q2, t1, t2), (0, 0, 0, 1, 1))
-    for block in range(blocks):
-        for slot in range(slots):
+
+    def lat(block, slot):
+        at = block * pairs + slot * points
+        return pl.ds(at if isinstance(block, int) else pl.multiple_of(at, points), points)
+
+    def points_of(block):
+        at = block * points
+        return pl.ds(at if isinstance(block, int) else pl.multiple_of(at, points), points)
+
+    def forward(block, first, last):
+        for slot in range(first, last):
             chosen = near[place(pm, block, slot, -1)]
-            y = dot(a_ref[block, slot], chosen, ROWS_BY_ROWS).astype(BF)
-            y_ref[block * pairs + slot * points : block * pairs + (slot + 1) * points] = y
-        span = slice(block * points, (block + 1) * points)
-        z = dot(y_ref[block * pairs : (block + 1) * pairs], w_ref[...])
-        result = g_ref[span].astype(FL)
+            y_ref[lat(block, slot)] = dot(a_ref[block, slot], chosen, ROWS_BY_ROWS).astype(BF)
+        span = points_of(block)
+        z = dot(y_ref[pl.ds(lat(block, first).start, (last - first) * points)], w_ref[...])
+        result = (out_ref[span] if first else g_ref[span]).astype(FL)
         upstream = cot_ref[span].astype(FL)
-        for slot in range(slots):
-            part = z[slot * points : (slot + 1) * points]
+        for slot in range(first, last):
+            part = z[(slot - first) * points : (slot - first + 1) * points]
             sig = sigmoid(part)
             edge = part * sig
             live = live_of(pc, block, slot)
             result = result + edge * live
             slope = sig + edge * (1.0 - sig)
-            dz = ((upstream * live) * slope).astype(BF)
-            dz_ref[block * pairs + slot * points : block * pairs + (slot + 1) * points] = dz
-        out_ref[span] = result.astype(BF)
-    for block in range(blocks):
-        for slot in range(slots):
-            dz = dz_ref[block * pairs + slot * points : block * pairs + (slot + 1) * points]
-            total[place(pm, block, slot, 1)] += dot(a_ref[block, slot], dz)
+            dz_ref[lat(block, slot)] = ((upstream * live) * slope).astype(BF)
+        out_ref[span] = result
+
+    def backward(block, first, last):
+        for slot in range(first, last):
+            lift = dot(a_ref[block, slot], dz_ref[lat(block, slot)])
+            total[place(pm, block, slot, 1)] += lift
+
+    def body(used):
+        for step in (forward, backward):
+            for block in range(blocks):
+                step(block, 0, used)
+
+    def rest(block, _):
+        for slot in range(USUAL, slots):
+            live = slot < pc[block]
+
+            @pl.when(live)
+            def _(slot=slot):
+                forward(block, slot, slot + 1)
+                backward(block, slot, slot + 1)
+
+            @pl.when(jnp.logical_not(live))
+            def _(slot=slot):
+                y_ref[lat(block, slot)] = jnp.zeros((points, y_ref.shape[1]), BF)
+                dz_ref[lat(block, slot)] = jnp.zeros((points, dz_ref.shape[1]), BF)
+
+    most = largest(pc)
+    pl.when(most <= LEAST)(lambda: body(LEAST))
+    pl.when(most > LEAST)(lambda: body(USUAL))
+    pl.when(most > USUAL)(lambda: lax.fori_loop(0, blocks, rest, None))
     split_slabs(total, own, mine, other)
 
 
-def outer_kernel(left_ref, right_ref, made_ref, out_ref, sent_ref):
-    out_ref[...] = dot(right_ref[...], left_ref[...], ROWS_BY_ROWS)
-    sent_ref[...] = made_ref[...]
+def outer_kernel(pc, left_ref, right_ref, made_ref, out_ref, sent_ref):
+    blocks = pc.shape[0]
+    pairs = left_ref.shape[0] // blocks
+    rows = pairs // SLOTS
+
+    def body(used):
+        if used == SLOTS:
+            out_ref[...] = dot(right_ref[...], left_ref[...], ROWS_BY_ROWS)
+            return
+        for block in range(blocks):
+            span = slice(block * pairs, block * pairs + used * rows)
+            term = dot(right_ref[span], left_ref[span], ROWS_BY_ROWS)
+            out_ref[...] = term if block == 0 else out_ref[...] + term
+
+    by_count(pc, SLOTS, body)
+    sent_ref[...] = made_ref[...].astype(BF)
 
 
 def mesh_grad_kernel(s, t, w_own, w_other, out):
@@ -207,16 +281,20 @@
     pairs = slots * rows
     for at, ref in enumerate((m, q1, q2, t1, t2)):
         near[at * OWNER_BLOCKS : (at + 1) * OWNER_BLOCKS] = ref[at // 3].reshape(OWNER_BLOCKS, rows, -1)
-    for block in range(blocks):
-        parts = []
-        for slot in range(slots):
-            picked = near[place(pm, block, slot, -1)].astype(FL)
-            start = block * pairs + slot * rows
-            parts.append((picked * slope_ref[start : start + rows].astype(FL)).astype(BF))
-        du = jnp.concatenate(parts, axis=0)
-        for at, x_ref in enumerate((x_own, x_other)):
-            term = dot(du, x_ref[block * pairs : (block + 1) * pairs], ROWS_BY_ROWS)
-            total[at] = term if block == 0 else total[at] + term
+
+    def body(used):
+        for block in range(blocks):
+            parts = []
+            for slot in range(used):
+                picked = near[place(pm, block, slot, -1)].astype(FL)
+                start = block * pairs + slot * rows
+                parts.append((picked * slope_ref[start : start + rows].astype(FL)).astype(BF))
+            du = jnp.concatenate(parts, axis=0)
+            for at, x_ref in enumerate((x_own, x_other)):
+                term = dot(du, x_ref[block * pairs : block * pairs + used * rows], ROWS_BY_ROWS)
+                total[at] = term if block == 0 else total[at] + term
+
+    by_count(pc, slots, body)
     count, half = total.shape[1:]
     lanes = out_ref.shape[1]
     tiles = half // lanes
@@ -359,7 +437,7 @@
         decode_kernel,
         [SMEM, SMEM, *[VMEM] * (4 + NEAR)],
         [
-            shape_of(*grid.shape), shape_of(pairs, full), shape_of(pairs, half),
+            shape_of(*grid.shape, dtype=FL), shape_of(pairs, full), shape_of(pairs, half),
             *slab_shapes(OWNER_BLOCKS * rows, half),
         ],
         [
@@ -369,14 +447,14 @@
     )(pair_mesh, pair_count, interp, grid, cotangent, w_dec, *near)
 
 
-def outer(y, dz, made):
+def outer(pair_count, y, dz, made):
     pairs, full = y.shape
     half = dz.shape[1]
     cost = pl.CostEstimate(
         flops=2 * pairs * full * half, bytes_accessed=2 * pairs * (full + half), transcendentals=0
     )
     outs = [shape_of(half, full, dtype=FL), shape_of(*made.shape)]
-    return held(outer_kernel, [VMEM] * 3, outs, cost=cost)(y, dz, made)
+    return held(outer_kernel, [SMEM, *[VMEM] * 3], outs, cost=cost)(pair_count, y, dz, made)
 
 
 def encoder_grad(pair_mesh, pair_count, x_own, x_other, slope, near, grad_dec):
@@ -408,7 +486,7 @@
     out, y, dz, own, mine, other = decode(
         pair_mesh, pair_count, interp, grid, cotangent, w_dec, near
     )
-    sums, got, (grad_dec, out) = reduce_to_owner(own, mine, other, outer(y, dz, out))
+    sums, got, (grad_dec, out) = reduce_to_owner(own, mine, other, outer(pair_count, y, dz, out))
     grad_mesh = simple(mesh_grad_kernel, shape_of(*sums.shape))(sums, got, w_dec, w_dec_other)
     near = spread_from_owner(grad_mesh)
     flat = encoder_grad(pair_mesh, pair_count, x_own, x_other, slope, near, grad_dec)

time: 146 us -> 142 us (0.973)
  blocking collectives: 59.1 us -> 56.6 us
    all_to_all x3, blocking collectives: 59.1 us -> 56.6 us  [exchange(): lax.all_to_all(value, 'band', 0, 0, tiled=True, axis_index_groups=groups)]
where the time goes in v7:
time: 142 us
  blocking collectives  56.6 us (40%)
  starting transfers between devices  32.3 us (23%)
  waiting for transfers between devices  31.2 us (22%)
  Pallas kernels  20.1 us (14%)
    all_to_all x3, blocking collectives, exchange(): lax.all_to_all(value, 'band', 0, 0, tiled=True, axis_index_groups=groups)  56.6 us
    ppermute x8, starting transfers between devices, outward(): return lax.ppermute(value, ('band', 'mp'), pairs)  30.7 us
    ppermute x8, waiting for transfers between devices, outward(): return lax.ppermute(value, ('band', 'mp'), pairs)  22.9 us
    ppermute x11, waiting for transfers between devices, swap(): return lax.ppermute(value, 'mp', [(0, 1), (1, 0)])  8.29 us
    pallas_call x1, Pallas kernels, decode(): held(decode_kernel, [SMEM, SMEM, *[VMEM] * (4 + NEAR)], [shape_of(*grid.s...  4.53 us
    pallas_call x1, Pallas kernels, encode(): held(encode_kernel, [SMEM, SMEM, *[VMEM] * 4], [shape_of(pairs, half), *s...  3.15 us
    pallas_call x1, Pallas kernels, outer(): held(outer_kernel, [SMEM, *[VMEM] * 3], outs, cost=cost)  3 us
  transfers between devices with their start and end apart: 19, of which 15 were waited for; matrix products, arithmetic and copies ran while one was open for 0% of the time, Pallas kernels for 6%

profile of v7, /device:TPU:8, one launch (start us, length us, event | category | flops | bytes accessed | tf_op | source)
XLA Modules:
  0.0 141.8 jit_solution(17961233757267599030)
XLA Ops:
  0.7 2.8 %shard_map.103 = (bf16[10,4,128,128]{3,2,1,0:T(8,128)(2,1)S(1)}, bf16[512,256]{1,0:T(8,128)(2,1)S(1)}, bf16[5120,256]{1,0:T(8,128)(2,1)S(1)}, s32[4,10]{1,0:T(4,128)S(1)}, s32[10]{0:T(128)S(1)}) custom-call(bf16[10,4,128,128]{3,2,1,0:T(8,128)(2,1)} %a_hbm.1, bf16[1280,256]{1,0:T(8,128)(2,1)} %g_ref.1, bf16[512,256]{1,0:T(8,128)(2,1)} %w_hbm.1, ...), custom_call_target="tpu_custom_call" | custom-call | flops 335544320 | bytes 4194304 | tf_op jit(solution)/shard_map/pallas_call | solution.py:400
  3.6 3.1 %shard_map.104 = (bf16[5120,256]{1,0:T(8,128)(2,1)S(1)}, bf16[256,256]{1,0:T(8,128)(2,1)S(1)}, bf16[2,256,256]{2,1,0:T(8,128)(2,1)S(1)}, bf16[2,256,256]{2,1,0:T(8,128)(2,1)S(1)}) custom-call(s32[4,10]{1,0:T(4,128)S(1)} %get-tuple-element.29.pm, s32[10]{0:T(128)S(1)} %get-tuple-element.30.pc, bf16[10,4,128,128]{3,2,1,0:T(8,128)(2,1)S(1)} %get-tuple-element.31.a_ref, ...), custom_call_target="tpu_custom_call" | custom-call | tf_op jit(solution)/shard_map/pallas_call | solution.py:414
  6.7 0.6 collective-permute-start.2
  7.3 1.1 collective-permute-done.2
  8.5 4.2 %collective-permute-start.4 = (bf16[2,256,256]{2,1,0:T(8,128)(2,1)S(1)}, bf16[2,256,256]{2,1,0:T(8,128)(2,1)S(1)}, u32[]{:S(2)}, u32[]{:S(2)}) collective-permute-start(bf16[2,256,256]{2,1,0:T(8,128)(2,1)S(1)} %pad_maximum_fusion.1), channel_id=1, source_target_pairs={{0,4},{5,1},{2,6},{7,3},{4,8},{9,5},{6,10},{11,7},{8,12},{13,9},{1... | collective-permute-start | bytes 786440 | tf_op jit(solution)/shard_map/ppermute | solution.py:33
  12.8 2.4 %collective-permute-start.3 = (bf16[2,256,256]{2,1,0:T(8,128)(2,1)S(1)}, bf16[2,256,256]{2,1,0:T(8,128)(2,1)S(1)}, u32[]{:S(2)}, u32[]{:S(2)}) collective-permute-start(bf16[2,256,256]{2,1,0:T(8,128)(2,1)S(1)} %pad_maximum_fusion), channel_id=1, source_target_pairs={{0,2},{3,1},{2,4},{5,3},{4,6},{7,5},{6,8},{9,7},{8,10},{11,9},{10,... | collective-permute-start | bytes 786440 | tf_op jit(solution)/shard_map/ppermute | solution.py:33
  15.2 2.5 %shard_map.105.slope_ref = bf16[5120,256]{1,0:T(8,128)(2,1)S(1)} custom-call(s32[10]{0:T(128)S(1)} %get-tuple-element.30.pc, bf16[512,256]{1,0:T(8,128)(2,1)S(1)} %get-tuple-element.32.w_ref, bf16[5120,256]{1,0:T(8,128)(2,1)S(1)} %get-tuple-element.33.x_own, bf16[5120,256]{1,0:T(8,128)(2,1)S(1)} %get-tuple-element.36.x_other), custom_call_target="tpu_custom_call" | custom-call | flops 1342177280 | bytes 7864320 | tf_op jit(solution)/shard_map/pallas_call | solution.py:427
  17.8 4.0 %collective-permute-done.4 = bf16[2,256,256]{2,1,0:T(8,128)(2,1)S(1)} collective-permute-done((bf16[2,256,256]{2,1,0:T(8,128)(2,1)S(1)}, bf16[2,256,256]{2,1,0:T(8,128)(2,1)S(1)}, u32[]{:S(2)}, u32[]{:S(2)}) %collective-permute-start.4) | collective-permute-done | bytes 262176 | tf_op jit(solution)/shard_map/ppermute | solution.py:33
  21.8 2.3 %collective-permute-done.3 = bf16[2,256,256]{2,1,0:T(8,128)(2,1)S(1)} collective-permute-done((bf16[2,256,256]{2,1,0:T(8,128)(2,1)S(1)}, bf16[2,256,256]{2,1,0:T(8,128)(2,1)S(1)}, u32[]{:S(2)}, u32[]{:S(2)}) %collective-permute-start.3) | collective-permute-done | bytes 262176 | tf_op jit(solution)/shard_map/ppermute | solution.py:33
  24.8 1.0 collective-permute-done.5
  26.1 3.3 %collective-permute-start.6 = (bf16[2,256,256]{2,1,0:T(8,128)(2,1)S(1)}, bf16[2,256,256]{2,1,0:T(8,128)(2,1)S(1)}, u32[]{:S(2)}, u32[]{:S(2)}) collective-permute-start(bf16[2,256,256]{2,1,0:T(8,128)(2,1)S(1)} %add_convert_fusion.m), channel_id=1, source_target_pairs={{0,2},{3,1},{2,4},{5,3},{4,6},{7,5},{6,8},{9,7},{8,10},{11,9},{10,... | collective-permute-start | bytes 786440 | tf_op jit(solution)/shard_map/ppermute | solution.py:33
  29.5 3.9 %collective-permute-start.7 = (bf16[2,256,256]{2,1,0:T(8,128)(2,1)S(1)}, bf16[2,256,256]{2,1,0:T(8,128)(2,1)S(1)}, u32[]{:S(2)}, u32[]{:S(2)}) collective-permute-start(bf16[2,256,256]{2,1,0:T(8,128)(2,1)S(1)} %add_convert_fusion.m), channel_id=1, source_target_pairs={{0,4},{5,1},{2,6},{7,3},{4,8},{9,5},{6,10},{11,7},{8,12},{13,9},{1... | collective-permute-start | bytes 786440 | tf_op jit(solution)/shard_map/ppermute | solution.py:33
  33.4 1.0 collective-permute-done.6.q1
  34.4 5.0 %collective-permute-done.7.q2 = bf16[2,256,256]{2,1,0:T(8,128)(2,1)S(1)} collective-permute-done((bf16[2,256,256]{2,1,0:T(8,128)(2,1)S(1)}, bf16[2,256,256]{2,1,0:T(8,128)(2,1)S(1)}, u32[]{:S(2)}, u32[]{:S(2)}) %collective-permute-start.7) | collective-permute-done | bytes 262176 | tf_op jit(solution)/shard_map/ppermute | solution.py:33
  39.4 1.5 %collective-permute-done.9.t2 = bf16[2,256,256]{2,1,0:T(8,128)(2,1)S(1)} collective-permute-done((bf16[2,256,256]{2,1,0:T(8,128)(2,1)S(1)}, bf16[2,256,256]{2,1,0:T(8,128)(2,1)S(1)}, u32[]{:S(2)}, u32[]{:S(2)}) %collective-permute-start.9) | collective-permute-done | bytes 262176 | tf_op jit(solution)/shard_map/ppermute | solution.py:24
  41.0 4.5 %shard_map.106 = (f32[1280,256]{1,0:T(8,128)S(1)}, bf16[5120,512]{1,0:T(8,128)(2,1)S(1)}, bf16[5120,256]{1,0:T(8,128)(2,1)S(1)}, bf16[256,256]{1,0:T(8,128)(2,1)...) custom-call(s32[4,10]{1,0:T(4,128)S(1)} %get-tuple-element.29.pm, s32[10]{0:T(128)S(1)} %get-tuple-element.30.pc, ...), custom_call_target="tpu_custom_call" | custom-call | tf_op jit(solution)/shard_map/pallas_call | solution.py:436
  45.7 1.4 collective-permute-done.10
  47.2 6.0 %collective-permute-start.12 = (bf16[2,256,256]{2,1,0:T(8,128)(2,1)S(1)}, bf16[2,256,256]{2,1,0:T(8,128)(2,1)S(1)}, u32[]{:S(2)}, u32[]{:S(2)}) collective-permute-start(bf16[2,256,256]{2,1,0:T(8,128)(2,1)S(1)} %pad_maximum_fusion.4), channel_id=1, source_target_pairs={{0,4},{5,1},{2,6},{7,3},{4,8},{9,5},{6,10},{11,7},{8,12},{13,9},{1... | collective-permute-start | bytes 786440 | tf_op jit(solution)/shard_map/ppermute | solution.py:33
  53.2 3.1 %collective-permute-start.11 = (bf16[2,256,256]{2,1,0:T(8,128)(2,1)S(1)}, bf16[2,256,256]{2,1,0:T(8,128)(2,1)S(1)}, u32[]{:S(2)}, u32[]{:S(2)}) collective-permute-start(bf16[2,256,256]{2,1,0:T(8,128)(2,1)S(1)} %pad_maximum_fusion.3), channel_id=1, source_target_pairs={{0,2},{3,1},{2,4},{5,3},{4,6},{7,5},{6,8},{9,7},{8,10},{11,9},{10,... | collective-permute-start | bytes 786440 | tf_op jit(solution)/shard_map/ppermute | solution.py:33
  56.4 3.0 %shard_map.107 = (f32[256,512]{1,0:T(8,128)S(1)}, bf16[1280,256]{1,0:T(8,128)(2,1)}) custom-call(s32[10]{0:T(128)S(1)} %get-tuple-element.30.pc, bf16[5120,512]{1,0:T(8,128)(2,1)S(1)} %get-tuple-element.42.left_ref, bf16[5120,256]{1,0:T(8,128)(2,1)S(1)} %get-tuple-element.43.right_ref, f32[1280,256]{1,0:T(8,128)S(1)} %get-tuple-element.44.made_ref), custom_call_target="tpu_custom_call" | custom-call | flops 1342177280 | bytes 7864320 | tf_op jit(solution)/shard_map/pallas_call | solution.py:457
  59.4 3.1 %collective-permute-done.12 = bf16[2,256,256]{2,1,0:T(8,128)(2,1)S(1)} collective-permute-done((bf16[2,256,256]{2,1,0:T(8,128)(2,1)S(1)}, bf16[2,256,256]{2,1,0:T(8,128)(2,1)S(1)}, u32[]{:S(2)}, u32[]{:S(2)}) %collective-permute-start.12) | collective-permute-done | bytes 262176 | tf_op jit(solution)/shard_map/ppermute | solution.py:33
  62.4 2.1 %collective-permute-done.11 = bf16[2,256,256]{2,1,0:T(8,128)(2,1)S(1)} collective-permute-done((bf16[2,256,256]{2,1,0:T(8,128)(2,1)S(1)}, bf16[2,256,256]{2,1,0:T(8,128)(2,1)S(1)}, u32[]{:S(2)}, u32[]{:S(2)}) %collective-permute-start.11) | collective-permute-done | bytes 262176 | tf_op jit(solution)/shard_map/ppermute | solution.py:33
  64.8 1.5 %collective-permute-done.13.t = bf16[2,256,256]{2,1,0:T(8,128)(2,1)S(1)} collective-permute-done((bf16[2,256,256]{2,1,0:T(8,128)(2,1)S(1)}, bf16[2,256,256]{2,1,0:T(8,128)(2,1)S(1)}, u32[]{:S(2)}, u32[]{:S(2)}) %collective-permute-start.13) | collective-permute-done | bytes 262176 | tf_op jit(solution)/shard_map/ppermute | solution.py:24
  66.7 3.3 %collective-permute-start.15 = (bf16[2,256,256]{2,1,0:T(8,128)(2,1)S(1)}, bf16[2,256,256]{2,1,0:T(8,128)(2,1)S(1)}, u32[]{:S(2)}, u32[]{:S(2)}) collective-permute-start(bf16[2,256,256]{2,1,0:T(8,128)(2,1)S(1)} %shard_map.108.m), channel_id=1, source_target_pairs={{0,2},{3,1},{2,4},{5,3},{4,6},{7,5},{6,8},{9,7},{8,10},{11,9},{10,... | collective-permute-start | bytes 786440 | tf_op jit(solution)/shard_map/ppermute | solution.py:33
  70.1 4.4 %collective-permute-start.16 = (bf16[2,256,256]{2,1,0:T(8,128)(2,1)S(1)}, bf16[2,256,256]{2,1,0:T(8,128)(2,1)S(1)}, u32[]{:S(2)}, u32[]{:S(2)}) collective-permute-start(bf16[2,256,256]{2,1,0:T(8,128)(2,1)S(1)} %shard_map.108.m), channel_id=1, source_target_pairs={{0,4},{5,1},{2,6},{7,3},{4,8},{9,5},{6,10},{11,7},{8,12},{13,9},{1... | collective-permute-start | bytes 786440 | tf_op jit(solution)/shard_map/ppermute | solution.py:33
  75.0 4.9 %collective-permute-done.16.q2 = bf16[2,256,256]{2,1,0:T(8,128)(2,1)S(1)} collective-permute-done((bf16[2,256,256]{2,1,0:T(8,128)(2,1)S(1)}, bf16[2,256,256]{2,1,0:T(8,128)(2,1)S(1)}, u32[]{:S(2)}, u32[]{:S(2)}) %collective-permute-start.16) | collective-permute-done | bytes 262176 | tf_op jit(solution)/shard_map/ppermute | solution.py:33
  79.9 1.5 %collective-permute-done.18.t2 = bf16[2,256,256]{2,1,0:T(8,128)(2,1)S(1)} collective-permute-done((bf16[2,256,256]{2,1,0:T(8,128)(2,1)S(1)}, bf16[2,256,256]{2,1,0:T(8,128)(2,1)S(1)}, u32[]{:S(2)}, u32[]{:S(2)}) %collective-permute-start.18) | collective-permute-done | bytes 262176 | tf_op jit(solution)/shard_map/ppermute | solution.py:24
  81.4 2.6 %shard_map.109 = bf16[2048,128]{1,0:T(8,128)(2,1)S(1)} custom-call(s32[4,10]{1,0:T(4,128)S(1)} %get-tuple-element.29.pm, s32[10]{0:T(128)S(1)} %get-tuple-element.30.pc, bf16[5120,256]{1,0:T(8,128)(2,1)S(1)} %get-tuple-element.33.x_own, bf16[5120,256]{1,0:T(8,128)(2,1)S(1)} %get-tuple-element.36.x_other, bf16[5120,256]{1,0:T(8,128)(2,1)S(1)} %shard_map.105.slope_ref, ...), custom_call_target="tpu_custom_call" | custom-call | tf_op jit(solution)/shard_map/pallas_call | solution.py:463
  84.0 23.8 %all_to_all.15.parts_ref = bf16[16,128,128]{2,1,0:T(8,128)(2,1)S(1)} all-to-all(bf16[16,128,128]{2,1,0:T(8,128)(2,1)S(1)} %bitcast.25), channel_id=1, replica_groups={{0,2,4,6,8,10,12,14,16,18,20,22,24,26,28,30},{32,34,36,38,40,42,44,46,4..., dimensions={0} | all-to-all | bytes 1048576 | tf_op jit(solution)/shard_map/all_to_all | solution.py:340
  107.9 18.7 %all_to_all.16.parts_ref = bf16[8,128,128]{2,1,0:T(8,128)(2,1)S(1)} all-to-all(bf16[8,128,128]{2,1,0:T(8,128)(2,1)S(1)} %shard_map.110), channel_id=1, replica_groups={{0,32,64,96,128,160,192,224},{2,34,66,98,130,162,194,226},{4,36,68,100,..., dimensions={0} | all-to-all | bytes 524288 | tf_op jit(solution)/shard_map/all_to_all | solution.py:340
  126.6 14.1 %all_to_all.17 = bf16[16,128,128]{2,1,0:T(8,128)(2,1)S(1)} all-to-all(bf16[16,128,128]{2,1,0:T(8,128)(2,1)S(1)} %shard_map.111), channel_id=1, replica_groups={{0,2,4,6,8,10,12,14,16,18,20,22,24,26,28,30},{32,34,36,38,40,42,44,46,4..., dimensions={0} | all-to-all | bytes 1048576 | tf_op jit(solution)/shard_map/all_to_all | solution.py:340
  140.7 1.1 shard_map.112
  (45 shorter events, 2.9 us)
Async XLA Ops:
  0.6 2.9 %collective-permute-start.1 = (bf16[1280,256]{1,0:T(8,128)(2,1)}, bf16[1280,256]{1,0:T(8,128)(2,1)S(1)}, u32[]{:S(2)}, u32[]{:S(2)}) collective-permute-start(bf16[1280,256]{1,0:T(8,128)(2,1)} %g_ref.1), channel_id=1, source_target_pairs={{0,1},{1,0},{2,3},{3,2},{4,5},{5,4},{6,7},{7,6},{8,9},{9,8},{10,11... | collective-permute-start | bytes 1966088 | tf_op jit(solution)/shard_map/ppermute | solution.py:24
  6.7 1.7 %collective-permute-start.2 = (bf16[2,256,256]{2,1,0:T(8,128)(2,1)S(1)}, bf16[2,256,256]{2,1,0:T(8,128)(2,1)S(1)}, u32[]{:S(2)}, u32[]{:S(2)}) collective-permute-start(bf16[2,256,256]{2,1,0:T(8,128)(2,1)S(1)} %get-tuple-element.35), channel_id=1, source_target_pairs={{0,1},{1,0},{2,3},{3,2},{4,5},{5,4},{6,7},{7,6},{8,9},{9,8},{10,11... | collective-permute-start | bytes 786440 | tf_op jit(solution)/shard_map/ppermute | solution.py:24
  8.5 13.2 %collective-permute-start.4 = (bf16[2,256,256]{2,1,0:T(8,128)(2,1)S(1)}, bf16[2,256,256]{2,1,0:T(8,128)(2,1)S(1)}, u32[]{:S(2)}, u32[]{:S(2)}) collective-permute-start(bf16[2,256,256]{2,1,0:T(8,128)(2,1)S(1)} %pad_maximum_fusion.1), channel_id=1, source_target_pairs={{0,4},{5,1},{2,6},{7,3},{4,8},{9,5},{6,10},{11,7},{8,12},{13,9},{1... | collective-permute-start | bytes 786440 | tf_op jit(solution)/shard_map/ppermute | solution.py:33
  12.8 11.3 %collective-permute-start.3 = (bf16[2,256,256]{2,1,0:T(8,128)(2,1)S(1)}, bf16[2,256,256]{2,1,0:T(8,128)(2,1)S(1)}, u32[]{:S(2)}, u32[]{:S(2)}) collective-permute-start(bf16[2,256,256]{2,1,0:T(8,128)(2,1)S(1)} %pad_maximum_fusion), channel_id=1, source_target_pairs={{0,2},{3,1},{2,4},{5,3},{4,6},{7,5},{6,8},{9,7},{8,10},{11,9},{10,... | collective-permute-start | bytes 786440 | tf_op jit(solution)/shard_map/ppermute | solution.py:33
  15.2 9.1 %copy-start.3 = (bf16[256,256]{1,0:T(8,128)(2,1)S(1)}, bf16[256,256]{1,0:T(8,128)(2,1)}, u32[]{:S(2)}) copy-start(bf16[256,256]{1,0:T(8,128)(2,1)} %param.10) | copy-start | bytes 393220
  17.7 23.2 %copy-start = (bf16[1280,256]{1,0:T(8,128)(2,1)S(1)}, bf16[1280,256]{1,0:T(8,128)(2,1)}, u32[]{:S(2)}) copy-start(bf16[1280,256]{1,0:T(8,128)(2,1)} %g_ref.1) | copy-start | bytes 1966084
  17.8 23.2 %copy-start.1 = (bf16[512,256]{1,0:T(8,128)(2,1)S(1)}, bf16[512,256]{1,0:T(8,128)(2,1)}, u32[]{:S(2)}) copy-start(bf16[512,256]{1,0:T(8,128)(2,1)} %w_own.1) | copy-start | bytes 786436
  17.8 23.2 %copy-start.2 = (bf16[1280,256]{1,0:T(8,128)(2,1)S(1)}, bf16[1280,256]{1,0:T(8,128)(2,1)}, u32[]{:S(2)}) copy-start(bf16[1280,256]{1,0:T(8,128)(2,1)} %cot_ref.1) | copy-start | bytes 1966084
  24.2 1.6 %collective-permute-start.5 = (bf16[2,256,256]{2,1,0:T(8,128)(2,1)S(1)}, bf16[2,256,256]{2,1,0:T(8,128)(2,1)S(1)}, u32[]{:S(2)}, u32[]{:S(2)}) collective-permute-start(bf16[2,256,256]{2,1,0:T(8,128)(2,1)S(1)} %pad_maximum_fusion.2), channel_id=1, source_target_pairs={{0,1},{1,0},{2,3},{3,2},{4,5},{5,4},{6,7},{7,6},{8,9},{9,8},{10,11... | collective-permute-start | bytes 786440 | tf_op jit(solution)/shard_map/ppermute | solution.py:24
  24.3 1.7 %collective-permute-start = (bf16[256,256]{1,0:T(8,128)(2,1)S(1)}, bf16[256,256]{1,0:T(8,128)(2,1)S(1)}, u32[]{:S(2)}, u32[]{:S(2)}) collective-permute-start(bf16[256,256]{1,0:T(8,128)(2,1)S(1)} %copy-done.3), channel_id=1, source_target_pairs={{0,1},{1,0},{2,3},{3,2},{4,5},{5,4},{6,7},{7,6},{8,9},{9,8},{10,11... | collective-permute-start | bytes 393224 | tf_op jit(solution)/shard_map/ppermute | solution.py:24
  26.1 8.3 %collective-permute-start.6 = (bf16[2,256,256]{2,1,0:T(8,128)(2,1)S(1)}, bf16[2,256,256]{2,1,0:T(8,128)(2,1)S(1)}, u32[]{:S(2)}, u32[]{:S(2)}) collective-permute-start(bf16[2,256,256]{2,1,0:T(8,128)(2,1)S(1)} %add_convert_fusion.m), channel_id=1, source_target_pairs={{0,2},{3,1},{2,4},{5,3},{4,6},{7,5},{6,8},{9,7},{8,10},{11,9},{10,... | collective-permute-start | bytes 786440 | tf_op jit(solution)/shard_map/ppermute | solution.py:33
  29.5 9.9 %collective-permute-start.7 = (bf16[2,256,256]{2,1,0:T(8,128)(2,1)S(1)}, bf16[2,256,256]{2,1,0:T(8,128)(2,1)S(1)}, u32[]{:S(2)}, u32[]{:S(2)}) collective-permute-start(bf16[2,256,256]{2,1,0:T(8,128)(2,1)S(1)} %add_convert_fusion.m), channel_id=1, source_target_pairs={{0,4},{5,1},{2,6},{7,3},{4,8},{9,5},{6,10},{11,7},{8,12},{13,9},{1... | collective-permute-start | bytes 786440 | tf_op jit(solution)/shard_map/ppermute | solution.py:33
  34.4 5.0 %collective-permute-start.8 = (bf16[2,256,256]{2,1,0:T(8,128)(2,1)S(1)}, bf16[2,256,256]{2,1,0:T(8,128)(2,1)S(1)}, u32[]{:S(2)}, u32[]{:S(2)}) collective-permute-start(bf16[2,256,256]{2,1,0:T(8,128)(2,1)S(1)} %collective-permute-done.6.q1), channel_id=1, source_target_pairs={{0,1},{1,0},{2,3},{3,2},{4,5},{5,4},{6,7},{7,6},{8,9},{9,8},{10,11... | collective-permute-start | bytes 786440 | tf_op jit(solution)/shard_map/ppermute | solution.py:24
  39.4 1.5 %collective-permute-start.9 = (bf16[2,256,256]{2,1,0:T(8,128)(2,1)S(1)}, bf16[2,256,256]{2,1,0:T(8,128)(2,1)S(1)}, u32[]{:S(2)}, u32[]{:S(2)}) collective-permute-start(bf16[2,256,256]{2,1,0:T(8,128)(2,1)S(1)} %collective-permute-done.7.q2), channel_id=1, source_target_pairs={{0,1},{1,0},{2,3},{3,2},{4,5},{5,4},{6,7},{7,6},{8,9},{9,8},{10,11... | collective-permute-start | bytes 786440 | tf_op jit(solution)/shard_map/ppermute | solution.py:24
  45.5 1.6 %collective-permute-start.10 = (bf16[2,256,256]{2,1,0:T(8,128)(2,1)S(1)}, bf16[2,256,256]{2,1,0:T(8,128)(2,1)S(1)}, u32[]{:S(2)}, u32[]{:S(2)}) collective-permute-start(bf16[2,256,256]{2,1,0:T(8,128)(2,1)S(1)} %get-tuple-element.41), channel_id=1, source_target_pairs={{0,1},{1,0},{2,3},{3,2},{4,5},{5,4},{6,7},{7,6},{8,9},{9,8},{10,11... | collective-permute-start | bytes 786440 | tf_op jit(solution)/shard_map/ppermute | solution.py:24
  47.2 15.3 %collective-permute-start.12 = (bf16[2,256,256]{2,1,0:T(8,128)(2,1)S(1)}, bf16[2,256,256]{2,1,0:T(8,128)(2,1)S(1)}, u32[]{:S(2)}, u32[]{:S(2)}) collective-permute-start(bf16[2,256,256]{2,1,0:T(8,128)(2,1)S(1)} %pad_maximum_fusion.4), channel_id=1, source_target_pairs={{0,4},{5,1},{2,6},{7,3},{4,8},{9,5},{6,10},{11,7},{8,12},{13,9},{1... | collective-permute-start | bytes 786440 | tf_op jit(solution)/shard_map/ppermute | solution.py:33
  53.2 11.4 %collective-permute-start.11 = (bf16[2,256,256]{2,1,0:T(8,128)(2,1)S(1)}, bf16[2,256,256]{2,1,0:T(8,128)(2,1)S(1)}, u32[]{:S(2)}, u32[]{:S(2)}) collective-permute-start(bf16[2,256,256]{2,1,0:T(8,128)(2,1)S(1)} %pad_maximum_fusion.3), channel_id=1, source_target_pairs={{0,2},{3,1},{2,4},{5,3},{4,6},{7,5},{6,8},{9,7},{8,10},{11,9},{10,... | collective-permute-start | bytes 786440 | tf_op jit(solution)/shard_map/ppermute | solution.py:33
  56.3 8.6 %collective-permute-start.14 = (bf16[512,256]{1,0:T(8,128)(2,1)S(1)}, bf16[512,256]{1,0:T(8,128)(2,1)S(1)}, u32[]{:S(2)}, u32[]{:S(2)}) collective-permute-start(bf16[512,256]{1,0:T(8,128)(2,1)S(1)} %copy-done.1), channel_id=1, source_target_pairs={{0,1},{1,0},{2,3},{3,2},{4,5},{5,4},{6,7},{7,6},{8,9},{9,8},{10,11... | collective-permute-start | bytes 786440 | tf_op jit(solution)/shard_map/ppermute | solution.py:24
  64.7 1.6 %collective-permute-start.13 = (bf16[2,256,256]{2,1,0:T(8,128)(2,1)S(1)}, bf16[2,256,256]{2,1,0:T(8,128)(2,1)S(1)}, u32[]{:S(2)}, u32[]{:S(2)}) collective-permute-start(bf16[2,256,256]{2,1,0:T(8,128)(2,1)S(1)} %pad_maximum_fusion.5.s), channel_id=1, source_target_pairs={{0,1},{1,0},{2,3},{3,2},{4,5},{5,4},{6,7},{7,6},{8,9},{9,8},{10,11... | collective-permute-start | bytes 786440 | tf_op jit(solution)/shard_map/ppermute | solution.py:24
  66.7 8.3 %collective-permute-start.15 = (bf16[2,256,256]{2,1,0:T(8,128)(2,1)S(1)}, bf16[2,256,256]{2,1,0:T(8,128)(2,1)S(1)}, u32[]{:S(2)}, u32[]{:S(2)}) collective-permute-start(bf16[2,256,256]{2,1,0:T(8,128)(2,1)S(1)} %shard_map.108.m), channel_id=1, source_target_pairs={{0,2},{3,1},{2,4},{5,3},{4,6},{7,5},{6,8},{9,7},{8,10},{11,9},{10,... | collective-permute-start | bytes 786440 | tf_op jit(solution)/shard_map/ppermute | solution.py:33
  70.1 9.8 %collective-permute-start.16 = (bf16[2,256,256]{2,1,0:T(8,128)(2,1)S(1)}, bf16[2,256,256]{2,1,0:T(8,128)(2,1)S(1)}, u32[]{:S(2)}, u32[]{:S(2)}) collective-permute-start(bf16[2,256,256]{2,1,0:T(8,128)(2,1)S(1)} %shard_map.108.m), channel_id=1, source_target_pairs={{0,4},{5,1},{2,6},{7,3},{4,8},{9,5},{6,10},{11,7},{8,12},{13,9},{1... | collective-permute-start | bytes 786440 | tf_op jit(solution)/shard_map/ppermute | solution.py:33
  75.0 4.9 %collective-permute-start.17 = (bf16[2,256,256]{2,1,0:T(8,128)(2,1)S(1)}, bf16[2,256,256]{2,1,0:T(8,128)(2,1)S(1)}, u32[]{:S(2)}, u32[]{:S(2)}) collective-permute-start(bf16[2,256,256]{2,1,0:T(8,128)(2,1)S(1)} %collective-permute-done.15.q1), channel_id=1, source_target_pairs={{0,1},{1,0},{2,3},{3,2},{4,5},{5,4},{6,7},{7,6},{8,9},{9,8},{10,11... | collective-permute-start | bytes 786440 | tf_op jit(solution)/shard_map/ppermute | solution.py:24
  79.9 1.5 %collective-permute-start.18 = (bf16[2,256,256]{2,1,0:T(8,128)(2,1)S(1)}, bf16[2,256,256]{2,1,0:T(8,128)(2,1)S(1)}, u32[]{:S(2)}, u32[]{:S(2)}) collective-permute-start(bf16[2,256,256]{2,1,0:T(8,128)(2,1)S(1)} %collective-permute-done.16.q2), channel_id=1, source_target_pairs={{0,1},{1,0},{2,3},{3,2},{4,5},{5,4},{6,7},{7,6},{8,9},{9,8},{10,11... | collective-permute-start | bytes 786440 | tf_op jit(solution)/shard_map/ppermute | solution.py:24

commit v8 on v7

--- a/solution.py
+++ b/solution.py
@@ -99,7 +99,7 @@
                     copy.wait()
             weights = a_ref[block, :used].reshape(used * rows, points)
             x = dot(weights, g_ref[block * points : (block + 1) * points])
-            x_ref[block * pairs : block * pairs + used * rows] = x.astype(BF)
+            x_ref[block * used * rows : (block + 1) * used * rows] = x.astype(BF)
 
     by_count(pc_ref, slots, body)
     for copy in copies[4:-1]:
@@ -122,7 +122,7 @@
     def body(used):
         w_own, w_far = by_side(w_ref)
         for block in range(blocks):
-            span = slice(block * pairs, block * pairs + used * rows)
+            span = slice(block * used * rows, (block + 1) * used * rows)
             weights = a_ref[block, :used].reshape(used * rows, points)
             x = dot(weights, g_other[block * points : (block + 1) * points]).astype(BF)
             x_other[span] = x
@@ -144,13 +144,13 @@
     def body(used):
         w_own, w_far = by_side(w_ref)
         for block in range(blocks):
-            span = slice(block * pairs, block * pairs + used * rows)
+            span = slice(block * used * rows, (block + 1) * used * rows)
             u = dot(x_own[span], w_own) + dot(x_other[span], w_far)
             for slot in range(used):
                 part = u[slot * rows : (slot + 1) * rows]
                 sig = sigmoid(part)
                 slope = (sig + part * sig * (1.0 - sig)) * (0.25 * live_of(pc, block, slot))
-                at = block * pairs + slot * rows
+                at = (block * used + slot) * rows
                 slope_ref[at : at + rows] = slope.astype(BF)
 
     by_count(pc, SLOTS, body)
@@ -278,21 +278,23 @@
 ):
     slots, blocks = pm.shape
     rows = near.shape[1]
-    pairs = slots * rows
     for at, ref in enumerate((m, q1, q2, t1, t2)):
-        near[at * OWNER_BLOCKS : (at + 1) * OWNER_BLOCKS] = ref[at // 3].reshape(OWNER_BLOCKS, rows, -1)
+        half = ref[0] if at < 3 else ref[...]
+        near[at * OWNER_BLOCKS : (at + 1) * OWNER_BLOCKS] = half.reshape(OWNER_BLOCKS, rows, -1)
 
     def body(used):
-        for block in range(blocks):
+        for first in range(0, blocks, 2):
+            last = min(first + 2, blocks)
             parts = []
-            for slot in range(used):
-                picked = near[place(pm, block, slot, -1)].astype(FL)
-                start = block * pairs + slot * rows
-                parts.append((picked * slope_ref[start : start + rows].astype(FL)).astype(BF))
+            for block in range(first, last):
+                for slot in range(used):
+                    picked = near[place(pm, block, slot, -1)].astype(FL)
+                    start = (block * used + slot) * rows
+                    parts.append((picked * slope_ref[start : start + rows].astype(FL)).astype(BF))
             du = jnp.concatenate(parts, axis=0)
             for at, x_ref in enumerate((x_own, x_other)):
-                term = dot(du, x_ref[block * pairs : block * pairs + used * rows], ROWS_BY_ROWS)
-                total[at] = term if block == 0 else total[at] + term
+                term = dot(du, x_ref[first * used * rows : last * used * rows], ROWS_BY_ROWS)
+                total[at] = term if first == 0 else total[at] + term
 
     by_count(pc, slots, body)
     count, half = total.shape[1:]
@@ -366,9 +368,9 @@
     return sums, swap(sums), beside
 
 
-def spread_from_owner(value):
+def spread_from_owner(value, wanted=lambda part: part):
     near = [outward(value, i + 1) for i in range(REACH)]
-    return [value, *near, *(swap(part) for part in near)]
+    return [value, *near, *(swap(wanted(part)) for part in near)]
 
 
 VMEM, HBM, SMEM = (pl.BlockSpec(memory_space=space) for space in (pltpu.VMEM, pltpu.HBM, pltpu.SMEM))
@@ -471,9 +473,9 @@
 def local(grid, interp, mesh_init, w_enc, w_dec, cotangent, pair_mesh, pair_count):
     full, half = w_enc.shape
     pair_mesh = pair_mesh.T
-    grid_other = swap(grid)
-    mesh_both = jnp.stack([mesh_init, swap(mesh_init)])
-    w_dec_other = swap(w_dec)
+    swapped = [swap(value) for value in (grid, mesh_init, w_dec)]
+    grid_other, mesh_other, w_dec_other = lax.optimization_barrier(swapped)
+    mesh_both = jnp.stack([mesh_init, mesh_other])
 
     interp, w_enc, x_own, pair_mesh, pair_count = lift_own(interp, grid, w_enc, pair_mesh, pair_count)
     x_other, own, mine, other = encode(pair_mesh, pair_count, interp, w_enc, x_own, grid_other)
@@ -488,7 +490,7 @@
     )
     sums, got, (grad_dec, out) = reduce_to_owner(own, mine, other, outer(pair_count, y, dz, out))
     grad_mesh = simple(mesh_grad_kernel, shape_of(*sums.shape))(sums, got, w_dec, w_dec_other)
-    near = spread_from_owner(grad_mesh)
+    near = spread_from_owner(grad_mesh, lambda part: part[1])
     flat = encoder_grad(pair_mesh, pair_count, x_own, x_other, slope, near, grad_dec)
 
     plane, line = plane_groups(lax.axis_size("band"))

time: 142 us -> 144 us (1.014)
  starting transfers between devices: 32.3 us -> 35.2 us
    ppermute x8, starting transfers between devices: 30.7 us -> 33.2 us  [outward(): return lax.ppermute(value, ('band', 'mp'), pairs)]
  transfers between devices with their start and end apart: 19 -> 19, of which waited for: 15 -> 12; matrix products, arithmetic and copies ran while one was open for 0% -> 0% of each run, Pallas kernels for 6% -> 6%
where the time goes in v8:
time: 144 us; the launch traced here: 143 us
  blocking collectives  55.6 us (39%)
  starting transfers between devices  35.2 us (24%)
  waiting for transfers between devices  31.6 us (22%)
  Pallas kernels  19.3 us (13%)
    all_to_all x3, blocking collectives, exchange(): lax.all_to_all(value, 'band', 0, 0, tiled=True, axis_index_groups=groups)  55.6 us
    ppermute x8, starting transfers between devices, outward(): return lax.ppermute(value, ('band', 'mp'), pairs)  33.2 us
    ppermute x8, waiting for transfers between devices, outward(): return lax.ppermute(value, ('band', 'mp'), pairs)  23.1 us
    ppermute x11, waiting for transfers between devices, swap(): return lax.ppermute(value, 'mp', [(0, 1), (1, 0)])  8.44 us
    pallas_call x1, Pallas kernels, decode(): held(decode_kernel, [SMEM, SMEM, *[VMEM] * (4 + NEAR)], [shape_of(*grid.s...  4.3 us
    pallas_call x1, Pallas kernels, encode(): held(encode_kernel, [SMEM, SMEM, *[VMEM] * 4], [shape_of(pairs, half), *s...  3.14 us
    pallas_call x1, Pallas kernels, outer(): held(outer_kernel, [SMEM, *[VMEM] * 3], outs, cost=cost)  3 us
  transfers between devices with their start and end apart: 19, of which 12 were waited for; matrix products, arithmetic and copies ran while one was open for 0% of the time, Pallas kernels for 6%

profile of v8, /device:TPU:8, one launch (start us, length us, event | category | flops | bytes accessed | tf_op | source)
XLA Modules:
  0.0 143.3 jit_solution(16322355091802246728)
XLA Ops:
  0.7 0.5 collective-permute-start.2
  1.3 2.8 %shard_map.103 = (bf16[10,4,128,128]{3,2,1,0:T(8,128)(2,1)S(1)}, bf16[512,256]{1,0:T(8,128)(2,1)S(1)}, bf16[5120,256]{1,0:T(8,128)(2,1)S(1)}, s32[4,10]{1,0:T(4,128)S(1)}, s32[10]{0:T(128)S(1)}) custom-call(bf16[10,4,128,128]{3,2,1,0:T(8,128)(2,1)} %a_hbm.1, bf16[1280,256]{1,0:T(8,128)(2,1)} %g_ref.1, bf16[512,256]{1,0:T(8,128)(2,1)} %w_hbm.1, ...), custom_call_target="tpu_custom_call" | custom-call | flops 335544320 | bytes 4194304 | tf_op jit(solution)/shard_map/pallas_call | solution.py:402
  4.2 3.1 %shard_map.104 = (bf16[5120,256]{1,0:T(8,128)(2,1)S(1)}, bf16[256,256]{1,0:T(8,128)(2,1)S(1)}, bf16[2,256,256]{2,1,0:T(8,128)(2,1)S(1)}, bf16[2,256,256]{2,1,0:T(8,128)(2,1)S(1)}) custom-call(s32[4,10]{1,0:T(4,128)S(1)} %get-tuple-element.32.pm, s32[10]{0:T(128)S(1)} %get-tuple-element.33.pc, bf16[10,4,128,128]{3,2,1,0:T(8,128)(2,1)S(1)} %get-tuple-element.34.a_ref, ...), custom_call_target="tpu_custom_call" | custom-call | tf_op jit(solution)/shard_map/pallas_call | solution.py:416
  7.3 0.5 collective-permute-start.3
  7.8 1.1 collective-permute-done.3
  9.0 3.5 %collective-permute-start.4 = (bf16[2,256,256]{2,1,0:T(8,128)(2,1)S(1)}, bf16[2,256,256]{2,1,0:T(8,128)(2,1)S(1)}, u32[]{:S(2)}, u32[]{:S(2)}) collective-permute-start(bf16[2,256,256]{2,1,0:T(8,128)(2,1)S(1)} %pad_maximum_fusion), channel_id=1, source_target_pairs={{0,2},{3,1},{2,4},{5,3},{4,6},{7,5},{6,8},{9,7},{8,10},{11,9},{10,... | collective-permute-start | bytes 786440 | tf_op jit(solution)/shard_map/ppermute | solution.py:33
  12.6 3.8 %collective-permute-start.5 = (bf16[2,256,256]{2,1,0:T(8,128)(2,1)S(1)}, bf16[2,256,256]{2,1,0:T(8,128)(2,1)S(1)}, u32[]{:S(2)}, u32[]{:S(2)}) collective-permute-start(bf16[2,256,256]{2,1,0:T(8,128)(2,1)S(1)} %pad_maximum_fusion.1), channel_id=1, source_target_pairs={{0,4},{5,1},{2,6},{7,3},{4,8},{9,5},{6,10},{11,7},{8,12},{13,9},{1... | collective-permute-start | bytes 786440 | tf_op jit(solution)/shard_map/ppermute | solution.py:33
  16.4 2.5 %shard_map.105.slope_ref = bf16[5120,256]{1,0:T(8,128)(2,1)S(1)} custom-call(s32[10]{0:T(128)S(1)} %get-tuple-element.33.pc, bf16[512,256]{1,0:T(8,128)(2,1)S(1)} %get-tuple-element.36.w_ref, bf16[5120,256]{1,0:T(8,128)(2,1)S(1)} %get-tuple-element.37.x_own, bf16[5120,256]{1,0:T(8,128)(2,1)S(1)} %get-tuple-element.41.x_other), custom_call_target="tpu_custom_call" | custom-call | flops 1342177280 | bytes 7864320 | tf_op jit(solution)/shard_map/pallas_call | solution.py:429
  18.9 3.8 %collective-permute-done.5 = bf16[2,256,256]{2,1,0:T(8,128)(2,1)S(1)} collective-permute-done((bf16[2,256,256]{2,1,0:T(8,128)(2,1)S(1)}, bf16[2,256,256]{2,1,0:T(8,128)(2,1)S(1)}, u32[]{:S(2)}, u32[]{:S(2)}) %collective-permute-start.5) | collective-permute-done | bytes 262176 | tf_op jit(solution)/shard_map/ppermute | solution.py:33
  23.0 1.5 %collective-permute-done.6 = bf16[2,256,256]{2,1,0:T(8,128)(2,1)S(1)} collective-permute-done((bf16[2,256,256]{2,1,0:T(8,128)(2,1)S(1)}, bf16[2,256,256]{2,1,0:T(8,128)(2,1)S(1)}, u32[]{:S(2)}, u32[]{:S(2)}) %collective-permute-start.6) | collective-permute-done | bytes 262176 | tf_op jit(solution)/shard_map/ppermute | solution.py:24
  24.7 5.9 %collective-permute-start.8 = (bf16[2,256,256]{2,1,0:T(8,128)(2,1)S(1)}, bf16[2,256,256]{2,1,0:T(8,128)(2,1)S(1)}, u32[]{:S(2)}, u32[]{:S(2)}) collective-permute-start(bf16[2,256,256]{2,1,0:T(8,128)(2,1)S(1)} %add_convert_fusion.m), channel_id=1, source_target_pairs={{0,4},{5,1},{2,6},{7,3},{4,8},{9,5},{6,10},{11,7},{8,12},{13,9},{1... | collective-permute-start | bytes 786440 | tf_op jit(solution)/shard_map/ppermute | solution.py:33
  30.6 3.1 %collective-permute-start.7 = (bf16[2,256,256]{2,1,0:T(8,128)(2,1)S(1)}, bf16[2,256,256]{2,1,0:T(8,128)(2,1)S(1)}, u32[]{:S(2)}, u32[]{:S(2)}) collective-permute-start(bf16[2,256,256]{2,1,0:T(8,128)(2,1)S(1)} %add_convert_fusion.m), channel_id=1, source_target_pairs={{0,2},{3,1},{2,4},{5,3},{4,6},{7,5},{6,8},{9,7},{8,10},{11,9},{10,... | collective-permute-start | bytes 786440 | tf_op jit(solution)/shard_map/ppermute | solution.py:33
  33.8 5.9 %collective-permute-done.8.q2 = bf16[2,256,256]{2,1,0:T(8,128)(2,1)S(1)} collective-permute-done((bf16[2,256,256]{2,1,0:T(8,128)(2,1)S(1)}, bf16[2,256,256]{2,1,0:T(8,128)(2,1)S(1)}, u32[]{:S(2)}, u32[]{:S(2)}) %collective-permute-start.8) | collective-permute-done | bytes 262176 | tf_op jit(solution)/shard_map/ppermute | solution.py:33
  39.7 2.4 %collective-permute-done.7.q1 = bf16[2,256,256]{2,1,0:T(8,128)(2,1)S(1)} collective-permute-done((bf16[2,256,256]{2,1,0:T(8,128)(2,1)S(1)}, bf16[2,256,256]{2,1,0:T(8,128)(2,1)S(1)}, u32[]{:S(2)}, u32[]{:S(2)}) %collective-permute-start.7) | collective-permute-done | bytes 262176 | tf_op jit(solution)/shard_map/ppermute | solution.py:33
  42.1 1.5 %collective-permute-done.9.t1 = bf16[2,256,256]{2,1,0:T(8,128)(2,1)S(1)} collective-permute-done((bf16[2,256,256]{2,1,0:T(8,128)(2,1)S(1)}, bf16[2,256,256]{2,1,0:T(8,128)(2,1)S(1)}, u32[]{:S(2)}, u32[]{:S(2)}) %collective-permute-start.9) | collective-permute-done | bytes 262176 | tf_op jit(solution)/shard_map/ppermute | solution.py:24
  43.6 4.3 %shard_map.106 = (f32[1280,256]{1,0:T(8,128)S(1)}, bf16[5120,512]{1,0:T(8,128)(2,1)S(1)}, bf16[5120,256]{1,0:T(8,128)(2,1)S(1)}, bf16[256,256]{1,0:T(8,128)(2,1)...) custom-call(s32[4,10]{1,0:T(4,128)S(1)} %get-tuple-element.32.pm, s32[10]{0:T(128)S(1)} %get-tuple-element.33.pc, ...), custom_call_target="tpu_custom_call" | custom-call | tf_op jit(solution)/shard_map/pallas_call | solution.py:438
  48.4 1.4 collective-permute-done.11
  49.8 3.3 %collective-permute-start.12 = (bf16[2,256,256]{2,1,0:T(8,128)(2,1)S(1)}, bf16[2,256,256]{2,1,0:T(8,128)(2,1)S(1)}, u32[]{:S(2)}, u32[]{:S(2)}) collective-permute-start(bf16[2,256,256]{2,1,0:T(8,128)(2,1)S(1)} %pad_maximum_fusion.3), channel_id=1, source_target_pairs={{0,2},{3,1},{2,4},{5,3},{4,6},{7,5},{6,8},{9,7},{8,10},{11,9},{10,... | collective-permute-start | bytes 786440 | tf_op jit(solution)/shard_map/ppermute | solution.py:33
  53.2 4.4 %collective-permute-start.13 = (bf16[2,256,256]{2,1,0:T(8,128)(2,1)S(1)}, bf16[2,256,256]{2,1,0:T(8,128)(2,1)S(1)}, u32[]{:S(2)}, u32[]{:S(2)}) collective-permute-start(bf16[2,256,256]{2,1,0:T(8,128)(2,1)S(1)} %pad_maximum_fusion.4), channel_id=1, source_target_pairs={{0,4},{5,1},{2,6},{7,3},{4,8},{9,5},{6,10},{11,7},{8,12},{13,9},{1... | collective-permute-start | bytes 786440 | tf_op jit(solution)/shard_map/ppermute | solution.py:33
  57.6 3.0 %shard_map.107 = (f32[256,512]{1,0:T(8,128)S(1)}, bf16[1280,256]{1,0:T(8,128)(2,1)}) custom-call(s32[10]{0:T(128)S(1)} %get-tuple-element.33.pc, bf16[5120,512]{1,0:T(8,128)(2,1)S(1)} %get-tuple-element.47.left_ref, bf16[5120,256]{1,0:T(8,128)(2,1)S(1)} %get-tuple-element.48.right_ref, f32[1280,256]{1,0:T(8,128)S(1)} %get-tuple-element.49.made_ref), custom_call_target="tpu_custom_call" | custom-call | flops 1342177280 | bytes 7864320 | tf_op jit(solution)/shard_map/pallas_call | solution.py:459
  60.6 2.9 %collective-permute-done.13 = bf16[2,256,256]{2,1,0:T(8,128)(2,1)S(1)} collective-permute-done((bf16[2,256,256]{2,1,0:T(8,128)(2,1)S(1)}, bf16[2,256,256]{2,1,0:T(8,128)(2,1)S(1)}, u32[]{:S(2)}, u32[]{:S(2)}) %collective-permute-start.13) | collective-permute-done | bytes 262176 | tf_op jit(solution)/shard_map/ppermute | solution.py:33
  63.7 1.5 %collective-permute-done.14.t = bf16[2,256,256]{2,1,0:T(8,128)(2,1)S(1)} collective-permute-done((bf16[2,256,256]{2,1,0:T(8,128)(2,1)S(1)}, bf16[2,256,256]{2,1,0:T(8,128)(2,1)S(1)}, u32[]{:S(2)}, u32[]{:S(2)}) %collective-permute-start.14) | collective-permute-done | bytes 262176 | tf_op jit(solution)/shard_map/ppermute | solution.py:24
  65.6 6.0 %collective-permute-start.16 = (bf16[2,256,256]{2,1,0:T(8,128)(2,1)S(1)}, bf16[2,256,256]{2,1,0:T(8,128)(2,1)S(1)}, u32[]{:S(2)}, u32[]{:S(2)}) collective-permute-start(bf16[2,256,256]{2,1,0:T(8,128)(2,1)S(1)} %shard_map.108.m), channel_id=1, source_target_pairs={{0,4},{5,1},{2,6},{7,3},{4,8},{9,5},{6,10},{11,7},{8,12},{13,9},{1... | collective-permute-start | bytes 786440 | tf_op jit(solution)/shard_map/ppermute | solution.py:33
  71.6 3.1 %collective-permute-start.15 = (bf16[2,256,256]{2,1,0:T(8,128)(2,1)S(1)}, bf16[2,256,256]{2,1,0:T(8,128)(2,1)S(1)}, u32[]{:S(2)}, u32[]{:S(2)}) collective-permute-start(bf16[2,256,256]{2,1,0:T(8,128)(2,1)S(1)} %shard_map.108.m), channel_id=1, source_target_pairs={{0,2},{3,1},{2,4},{5,3},{4,6},{7,5},{6,8},{9,7},{8,10},{11,9},{10,... | collective-permute-start | bytes 786440 | tf_op jit(solution)/shard_map/ppermute | solution.py:33
  74.7 5.9 %collective-permute-done.16.q2 = bf16[2,256,256]{2,1,0:T(8,128)(2,1)S(1)} collective-permute-done((bf16[2,256,256]{2,1,0:T(8,128)(2,1)S(1)}, bf16[2,256,256]{2,1,0:T(8,128)(2,1)S(1)}, u32[]{:S(2)}, u32[]{:S(2)}) %collective-permute-start.16) | collective-permute-done | bytes 262176 | tf_op jit(solution)/shard_map/ppermute | solution.py:33
  80.7 2.3 %collective-permute-done.15.q1 = bf16[2,256,256]{2,1,0:T(8,128)(2,1)S(1)} collective-permute-done((bf16[2,256,256]{2,1,0:T(8,128)(2,1)S(1)}, bf16[2,256,256]{2,1,0:T(8,128)(2,1)S(1)}, u32[]{:S(2)}, u32[]{:S(2)}) %collective-permute-start.15) | collective-permute-done | bytes 262176 | tf_op jit(solution)/shard_map/ppermute | solution.py:33
  83.1 1.3 collective-permute-done.17.t1
  84.4 2.0 %shard_map.109 = bf16[2048,128]{1,0:T(8,128)(2,1)S(1)} custom-call(s32[4,10]{1,0:T(4,128)S(1)} %get-tuple-element.32.pm, s32[10]{0:T(128)S(1)} %get-tuple-element.33.pc, bf16[5120,256]{1,0:T(8,128)(2,1)S(1)} %get-tuple-element.37.x_own, bf16[5120,256]{1,0:T(8,128)(2,1)S(1)} %get-tuple-element.41.x_other, bf16[5120,256]{1,0:T(8,128)(2,1)S(1)} %shard_map.105.slope_ref, ...), custom_call_target="tpu_custom_call" | custom-call | tf_op jit(solution)/shard_map/pallas_call | solution.py:465
  86.4 23.6 %all_to_all.15.parts_ref = bf16[16,128,128]{2,1,0:T(8,128)(2,1)S(1)} all-to-all(bf16[16,128,128]{2,1,0:T(8,128)(2,1)S(1)} %bitcast.29), channel_id=1, replica_groups={{0,2,4,6,8,10,12,14,16,18,20,22,24,26,28,30},{32,34,36,38,40,42,44,46,4..., dimensions={0} | all-to-all | bytes 1048576 | tf_op jit(solution)/shard_map/all_to_all | solution.py:342
  110.1 17.9 %all_to_all.16.parts_ref = bf16[8,128,128]{2,1,0:T(8,128)(2,1)S(1)} all-to-all(bf16[8,128,128]{2,1,0:T(8,128)(2,1)S(1)} %shard_map.110), channel_id=1, replica_groups={{0,32,64,96,128,160,192,224},{2,34,66,98,130,162,194,226},{4,36,68,100,..., dimensions={0} | all-to-all | bytes 524288 | tf_op jit(solution)/shard_map/all_to_all | solution.py:342
  128.1 14.0 %all_to_all.17 = bf16[16,128,128]{2,1,0:T(8,128)(2,1)S(1)} all-to-all(bf16[16,128,128]{2,1,0:T(8,128)(2,1)S(1)} %shard_map.111), channel_id=1, replica_groups={{0,2,4,6,8,10,12,14,16,18,20,22,24,26,28,30},{32,34,36,38,40,42,44,46,4..., dimensions={0} | all-to-all | bytes 1048576 | tf_op jit(solution)/shard_map/all_to_all | solution.py:342
  142.2 1.1 shard_map.112
  (47 shorter events, 2.2 us)
Async XLA Ops:
  0.6 3.5 %collective-permute-start = (bf16[1280,256]{1,0:T(8,128)(2,1)}, bf16[1280,256]{1,0:T(8,128)(2,1)S(1)}, u32[]{:S(2)}, u32[]{:S(2)}) collective-permute-start(bf16[1280,256]{1,0:T(8,128)(2,1)} %g_ref.1), channel_id=1, source_target_pairs={{0,1},{1,0},{2,3},{3,2},{4,5},{5,4},{6,7},{7,6},{8,9},{9,8},{10,11... | collective-permute-start | bytes 1966088 | tf_op jit(solution)/shard_map/ppermute | solution.py:24
  0.7 3.4 %collective-permute-start.2 = (bf16[512,256]{1,0:T(8,128)(2,1)}, bf16[512,256]{1,0:T(8,128)(2,1)S(1)}, u32[]{:S(2)}, u32[]{:S(2)}) collective-permute-start(bf16[512,256]{1,0:T(8,128)(2,1)} %w_own.1), channel_id=1, source_target_pairs={{0,1},{1,0},{2,3},{3,2},{4,5},{5,4},{6,7},{7,6},{8,9},{9,8},{10,11... | collective-permute-start | bytes 786440 | tf_op jit(solution)/shard_map/ppermute | solution.py:24
  1.2 2.9 %collective-permute-start.1 = (bf16[256,256]{1,0:T(8,128)(2,1)}, bf16[256,256]{1,0:T(8,128)(2,1)S(1)}, u32[]{:S(2)}, u32[]{:S(2)}) collective-permute-start(bf16[256,256]{1,0:T(8,128)(2,1)} %param.10), channel_id=1, source_target_pairs={{0,1},{1,0},{2,3},{3,2},{4,5},{5,4},{6,7},{7,6},{8,9},{9,8},{10,11... | collective-permute-start | bytes 393224 | tf_op jit(solution)/shard_map/ppermute | solution.py:24
  7.3 1.7 %collective-permute-start.3 = (bf16[2,256,256]{2,1,0:T(8,128)(2,1)S(1)}, bf16[2,256,256]{2,1,0:T(8,128)(2,1)S(1)}, u32[]{:S(2)}, u32[]{:S(2)}) collective-permute-start(bf16[2,256,256]{2,1,0:T(8,128)(2,1)S(1)} %get-tuple-element.40), channel_id=1, source_target_pairs={{0,1},{1,0},{2,3},{3,2},{4,5},{5,4},{6,7},{7,6},{8,9},{9,8},{10,11... | collective-permute-start | bytes 786440 | tf_op jit(solution)/shard_map/ppermute | solution.py:24
  9.0 9.9 %collective-permute-start.4 = (bf16[2,256,256]{2,1,0:T(8,128)(2,1)S(1)}, bf16[2,256,256]{2,1,0:T(8,128)(2,1)S(1)}, u32[]{:S(2)}, u32[]{:S(2)}) collective-permute-start(bf16[2,256,256]{2,1,0:T(8,128)(2,1)S(1)} %pad_maximum_fusion), channel_id=1, source_target_pairs={{0,2},{3,1},{2,4},{5,3},{4,6},{7,5},{6,8},{9,7},{8,10},{11,9},{10,... | collective-permute-start | bytes 786440 | tf_op jit(solution)/shard_map/ppermute | solution.py:33
  12.6 10.2 %collective-permute-start.5 = (bf16[2,256,256]{2,1,0:T(8,128)(2,1)S(1)}, bf16[2,256,256]{2,1,0:T(8,128)(2,1)S(1)}, u32[]{:S(2)}, u32[]{:S(2)}) collective-permute-start(bf16[2,256,256]{2,1,0:T(8,128)(2,1)S(1)} %pad_maximum_fusion.1), channel_id=1, source_target_pairs={{0,4},{5,1},{2,6},{7,3},{4,8},{9,5},{6,10},{11,7},{8,12},{13,9},{1... | collective-permute-start | bytes 786440 | tf_op jit(solution)/shard_map/ppermute | solution.py:33
  18.9 5.7 %copy-start.3 = (bf16[256,256]{1,0:T(8,128)(2,1)S(1)}, bf16[256,256]{1,0:T(8,128)(2,1)}, u32[]{:S(2)}) copy-start(bf16[256,256]{1,0:T(8,128)(2,1)} %param.10) | copy-start | bytes 393220
  18.9 24.7 %copy-start = (bf16[1280,256]{1,0:T(8,128)(2,1)S(1)}, bf16[1280,256]{1,0:T(8,128)(2,1)}, u32[]{:S(2)}) copy-start(bf16[1280,256]{1,0:T(8,128)(2,1)} %g_ref.1) | copy-start | bytes 1966084
  18.9 24.7 %copy-start.1 = (bf16[512,256]{1,0:T(8,128)(2,1)S(1)}, bf16[512,256]{1,0:T(8,128)(2,1)}, u32[]{:S(2)}) copy-start(bf16[512,256]{1,0:T(8,128)(2,1)} %w_own.1) | copy-start | bytes 786436
  18.9 24.7 %copy-start.2 = (bf16[1280,256]{1,0:T(8,128)(2,1)S(1)}, bf16[1280,256]{1,0:T(8,128)(2,1)}, u32[]{:S(2)}) copy-start(bf16[1280,256]{1,0:T(8,128)(2,1)} %cot_ref.1) | copy-start | bytes 1966084
  22.9 1.6 %collective-permute-start.6 = (bf16[2,256,256]{2,1,0:T(8,128)(2,1)S(1)}, bf16[2,256,256]{2,1,0:T(8,128)(2,1)S(1)}, u32[]{:S(2)}, u32[]{:S(2)}) collective-permute-start(bf16[2,256,256]{2,1,0:T(8,128)(2,1)S(1)} %pad_maximum_fusion.2), channel_id=1, source_target_pairs={{0,1},{1,0},{2,3},{3,2},{4,5},{5,4},{6,7},{7,6},{8,9},{9,8},{10,11... | collective-permute-start | bytes 786440 | tf_op jit(solution)/shard_map/ppermute | solution.py:24
  24.7 15.0 %collective-permute-start.8 = (bf16[2,256,256]{2,1,0:T(8,128)(2,1)S(1)}, bf16[2,256,256]{2,1,0:T(8,128)(2,1)S(1)}, u32[]{:S(2)}, u32[]{:S(2)}) collective-permute-start(bf16[2,256,256]{2,1,0:T(8,128)(2,1)S(1)} %add_convert_fusion.m), channel_id=1, source_target_pairs={{0,4},{5,1},{2,6},{7,3},{4,8},{9,5},{6,10},{11,7},{8,12},{13,9},{1... | collective-permute-start | bytes 786440 | tf_op jit(solution)/shard_map/ppermute | solution.py:33
  30.6 11.4 %collective-permute-start.7 = (bf16[2,256,256]{2,1,0:T(8,128)(2,1)S(1)}, bf16[2,256,256]{2,1,0:T(8,128)(2,1)S(1)}, u32[]{:S(2)}, u32[]{:S(2)}) collective-permute-start(bf16[2,256,256]{2,1,0:T(8,128)(2,1)S(1)} %add_convert_fusion.m), channel_id=1, source_target_pairs={{0,2},{3,1},{2,4},{5,3},{4,6},{7,5},{6,8},{9,7},{8,10},{11,9},{10,... | collective-permute-start | bytes 786440 | tf_op jit(solution)/shard_map/ppermute | solution.py:33
  39.7 2.4 %collective-permute-start.10 = (bf16[2,256,256]{2,1,0:T(8,128)(2,1)S(1)}, bf16[2,256,256]{2,1,0:T(8,128)(2,1)S(1)}, u32[]{:S(2)}, u32[]{:S(2)}) collective-permute-start(bf16[2,256,256]{2,1,0:T(8,128)(2,1)S(1)} %collective-permute-done.8.q2), channel_id=1, source_target_pairs={{0,1},{1,0},{2,3},{3,2},{4,5},{5,4},{6,7},{7,6},{8,9},{9,8},{10,11... | collective-permute-start | bytes 786440 | tf_op jit(solution)/shard_map/ppermute | solution.py:24
  42.1 1.5 %collective-permute-start.9 = (bf16[2,256,256]{2,1,0:T(8,128)(2,1)S(1)}, bf16[2,256,256]{2,1,0:T(8,128)(2,1)S(1)}, u32[]{:S(2)}, u32[]{:S(2)}) collective-permute-start(bf16[2,256,256]{2,1,0:T(8,128)(2,1)S(1)} %collective-permute-done.7.q1), channel_id=1, source_target_pairs={{0,1},{1,0},{2,3},{3,2},{4,5},{5,4},{6,7},{7,6},{8,9},{9,8},{10,11... | collective-permute-start | bytes 786440 | tf_op jit(solution)/shard_map/ppermute | solution.py:24
  47.9 1.8 %collective-permute-start.11 = (bf16[2,256,256]{2,1,0:T(8,128)(2,1)S(1)}, bf16[2,256,256]{2,1,0:T(8,128)(2,1)S(1)}, u32[]{:S(2)}, u32[]{:S(2)}) collective-permute-start(bf16[2,256,256]{2,1,0:T(8,128)(2,1)S(1)} %get-tuple-element.46), channel_id=1, source_target_pairs={{0,1},{1,0},{2,3},{3,2},{4,5},{5,4},{6,7},{7,6},{8,9},{9,8},{10,11... | collective-permute-start | bytes 786440 | tf_op jit(solution)/shard_map/ppermute | solution.py:24
  49.8 10.8 %collective-permute-start.12 = (bf16[2,256,256]{2,1,0:T(8,128)(2,1)S(1)}, bf16[2,256,256]{2,1,0:T(8,128)(2,1)S(1)}, u32[]{:S(2)}, u32[]{:S(2)}) collective-permute-start(bf16[2,256,256]{2,1,0:T(8,128)(2,1)S(1)} %pad_maximum_fusion.3), channel_id=1, source_target_pairs={{0,2},{3,1},{2,4},{5,3},{4,6},{7,5},{6,8},{9,7},{8,10},{11,9},{10,... | collective-permute-start | bytes 786440 | tf_op jit(solution)/shard_map/ppermute | solution.py:33
  53.2 10.3 %collective-permute-start.13 = (bf16[2,256,256]{2,1,0:T(8,128)(2,1)S(1)}, bf16[2,256,256]{2,1,0:T(8,128)(2,1)S(1)}, u32[]{:S(2)}, u32[]{:S(2)}) collective-permute-start(bf16[2,256,256]{2,1,0:T(8,128)(2,1)S(1)} %pad_maximum_fusion.4), channel_id=1, source_target_pairs={{0,4},{5,1},{2,6},{7,3},{4,8},{9,5},{6,10},{11,7},{8,12},{13,9},{1... | collective-permute-start | bytes 786440 | tf_op jit(solution)/shard_map/ppermute | solution.py:33
  63.6 1.6 %collective-permute-start.14 = (bf16[2,256,256]{2,1,0:T(8,128)(2,1)S(1)}, bf16[2,256,256]{2,1,0:T(8,128)(2,1)S(1)}, u32[]{:S(2)}, u32[]{:S(2)}) collective-permute-start(bf16[2,256,256]{2,1,0:T(8,128)(2,1)S(1)} %pad_maximum_fusion.5.s), channel_id=1, source_target_pairs={{0,1},{1,0},{2,3},{3,2},{4,5},{5,4},{6,7},{7,6},{8,9},{9,8},{10,11... | collective-permute-start | bytes 786440 | tf_op jit(solution)/shard_map/ppermute | solution.py:24
  65.6 15.0 %collective-permute-start.16 = (bf16[2,256,256]{2,1,0:T(8,128)(2,1)S(1)}, bf16[2,256,256]{2,1,0:T(8,128)(2,1)S(1)}, u32[]{:S(2)}, u32[]{:S(2)}) collective-permute-start(bf16[2,256,256]{2,1,0:T(8,128)(2,1)S(1)} %shard_map.108.m), channel_id=1, source_target_pairs={{0,4},{5,1},{2,6},{7,3},{4,8},{9,5},{6,10},{11,7},{8,12},{13,9},{1... | collective-permute-start | bytes 786440 | tf_op jit(solution)/shard_map/ppermute | solution.py:33
  71.6 11.4 %collective-permute-start.15 = (bf16[2,256,256]{2,1,0:T(8,128)(2,1)S(1)}, bf16[2,256,256]{2,1,0:T(8,128)(2,1)S(1)}, u32[]{:S(2)}, u32[]{:S(2)}) collective-permute-start(bf16[2,256,256]{2,1,0:T(8,128)(2,1)S(1)} %shard_map.108.m), channel_id=1, source_target_pairs={{0,2},{3,1},{2,4},{5,3},{4,6},{7,5},{6,8},{9,7},{8,10},{11,9},{10,... | collective-permute-start | bytes 786440 | tf_op jit(solution)/shard_map/ppermute | solution.py:33
  80.6 2.5 %collective-permute-start.18 = (bf16[256,256]{1,0:T(8,128)(2,1)S(1)}, bf16[256,256]{1,0:T(8,128)(2,1)S(1)}, u32[]{:S(2)}, u32[]{:S(2)}) collective-permute-start(bf16[256,256]{1,0:T(8,128)(2,1)S(1)} %slice_bitcast_fusion.2), channel_id=1, source_target_pairs={{0,1},{1,0},{2,3},{3,2},{4,5},{5,4},{6,7},{7,6},{8,9},{9,8},{10,11... | collective-permute-start | bytes 393224 | tf_op jit(solution)/shard_map/ppermute | solution.py:24
  83.0 1.4 %collective-permute-start.17 = (bf16[256,256]{1,0:T(8,128)(2,1)S(1)}, bf16[256,256]{1,0:T(8,128)(2,1)S(1)}, u32[]{:S(2)}, u32[]{:S(2)}) collective-permute-start(bf16[256,256]{1,0:T(8,128)(2,1)S(1)} %slice_bitcast_fusion.3), channel_id=1, source_target_pairs={{0,1},{1,0},{2,3},{3,2},{4,5},{5,4},{6,7},{7,6},{8,9},{9,8},{10,11... | collective-permute-start | bytes 393224 | tf_op jit(solution)/shard_map/ppermute | solution.py:24

commit v9 on v8

--- a/solution.py
+++ b/solution.py
@@ -370,7 +370,11 @@
 
 def spread_from_owner(value, wanted=lambda part: part):
     near = [outward(value, i + 1) for i in range(REACH)]
-    return [value, *near, *(swap(wanted(part)) for part in near)]
+    swapped = [swap(wanted(near[0]))]
+    for part in near[1:]:
+        part, swapped[-1] = lax.optimization_barrier((part, swapped[-1]))
+        swapped.append(swap(wanted(part)))
+    return [value, *near, *swapped]
 
 
 VMEM, HBM, SMEM = (pl.BlockSpec(memory_space=space) for space in (pltpu.VMEM, pltpu.HBM, pltpu.SMEM))

time: 144 us -> 146 us (1.014)
  waiting for transfers between devices: 31.6 us -> 26.2 us
  blocking collectives: 55.6 us -> 59.8 us
  starting transfers between devices: 35.2 us -> 38.4 us
    ppermute x8, waiting for transfers between devices: 23.1 us -> 17.7 us  [outward(): return lax.ppermute(value, ('band', 'mp'), pairs)]
    all_to_all x3, blocking collectives: 55.6 us -> 59.8 us  [exchange(): lax.all_to_all(value, 'band', 0, 0, tiled=True, axis_index_groups=groups)]
    ppermute x8, starting transfers between devices: 33.2 us -> 36.3 us  [outward(): return lax.ppermute(value, ('band', 'mp'), pairs)]
  transfers between devices with their start and end apart: 19 -> 19, of which waited for: 12 -> 10; matrix products, arithmetic and copies ran while one was open for 0% -> 0% of each run, Pallas kernels for 6% -> 6%
where the time goes in v9:
time: 146 us; the launch traced here: 145 us
  blocking collectives  59.8 us (41%)
  starting transfers between devices  38.4 us (26%)
  waiting for transfers between devices  26.2 us (18%)
  Pallas kernels  19.3 us (13%)
    all_to_all x3, blocking collectives, exchange(): lax.all_to_all(value, 'band', 0, 0, tiled=True, axis_index_groups=groups)  59.8 us
    ppermute x8, starting transfers between devices, outward(): return lax.ppermute(value, ('band', 'mp'), pairs)  36.3 us
    ppermute x8, waiting for transfers between devices, outward(): return lax.ppermute(value, ('band', 'mp'), pairs)  17.7 us
    ppermute x11, waiting for transfers between devices, swap(): return lax.ppermute(value, 'mp', [(0, 1), (1, 0)])  8.46 us
    pallas_call x1, Pallas kernels, decode(): held(decode_kernel, [SMEM, SMEM, *[VMEM] * (4 + NEAR)], [shape_of(*grid.s...  4.3 us
    pallas_call x1, Pallas kernels, encode(): held(encode_kernel, [SMEM, SMEM, *[VMEM] * 4], [shape_of(pairs, half), *s...  3.14 us
    pallas_call x1, Pallas kernels, outer(): held(outer_kernel, [SMEM, *[VMEM] * 3], outs, cost=cost)  3 us
  transfers between devices with their start and end apart: 19, of which 10 were waited for; matrix products, arithmetic and copies ran while one was open for 0% of the time, Pallas kernels for 6%

profile of v9, /device:TPU:8, one launch (start us, length us, event | category | flops | bytes accessed | tf_op | source)
XLA Modules:
  0.0 145.4 jit_solution(15815441894173095020)
XLA Ops:
  0.7 0.5 collective-permute-start.2
  1.3 2.8 %shard_map.103 = (bf16[10,4,128,128]{3,2,1,0:T(8,128)(2,1)S(1)}, bf16[512,256]{1,0:T(8,128)(2,1)S(1)}, bf16[5120,256]{1,0:T(8,128)(2,1)S(1)}, s32[4,10]{1,0:T(4,128)S(1)}, s32[10]{0:T(128)S(1)}) custom-call(bf16[10,4,128,128]{3,2,1,0:T(8,128)(2,1)} %a_hbm.1, bf16[1280,256]{1,0:T(8,128)(2,1)} %g_ref.1, bf16[512,256]{1,0:T(8,128)(2,1)} %w_hbm.1, ...), custom_call_target="tpu_custom_call" | custom-call | flops 335544320 | bytes 4194304 | tf_op jit(solution)/shard_map/pallas_call | solution.py:406
  4.2 3.1 %shard_map.104 = (bf16[5120,256]{1,0:T(8,128)(2,1)S(1)}, bf16[256,256]{1,0:T(8,128)(2,1)S(1)}, bf16[2,256,256]{2,1,0:T(8,128)(2,1)S(1)}, bf16[2,256,256]{2,1,0:T(8,128)(2,1)S(1)}) custom-call(s32[4,10]{1,0:T(4,128)S(1)} %get-tuple-element.36.pm, s32[10]{0:T(128)S(1)} %get-tuple-element.37.pc, bf16[10,4,128,128]{3,2,1,0:T(8,128)(2,1)S(1)} %get-tuple-element.38.a_ref, ...), custom_call_target="tpu_custom_call" | custom-call | tf_op jit(solution)/shard_map/pallas_call | solution.py:420
  7.3 0.5 collective-permute-start.3
  7.8 1.1 collective-permute-done.3
  9.0 3.5 %collective-permute-start.4 = (bf16[2,256,256]{2,1,0:T(8,128)(2,1)S(1)}, bf16[2,256,256]{2,1,0:T(8,128)(2,1)S(1)}, u32[]{:S(2)}, u32[]{:S(2)}) collective-permute-start(bf16[2,256,256]{2,1,0:T(8,128)(2,1)S(1)} %pad_maximum_fusion), channel_id=1, source_target_pairs={{0,2},{3,1},{2,4},{5,3},{4,6},{7,5},{6,8},{9,7},{8,10},{11,9},{10,... | collective-permute-start | bytes 786440 | tf_op jit(solution)/shard_map/ppermute | solution.py:33
  12.6 3.8 %collective-permute-start.5 = (bf16[2,256,256]{2,1,0:T(8,128)(2,1)S(1)}, bf16[2,256,256]{2,1,0:T(8,128)(2,1)S(1)}, u32[]{:S(2)}, u32[]{:S(2)}) collective-permute-start(bf16[2,256,256]{2,1,0:T(8,128)(2,1)S(1)} %pad_maximum_fusion.1), channel_id=1, source_target_pairs={{0,4},{5,1},{2,6},{7,3},{4,8},{9,5},{6,10},{11,7},{8,12},{13,9},{1... | collective-permute-start | bytes 786440 | tf_op jit(solution)/shard_map/ppermute | solution.py:33
  16.4 2.5 %shard_map.105.slope_ref = bf16[5120,256]{1,0:T(8,128)(2,1)S(1)} custom-call(s32[10]{0:T(128)S(1)} %get-tuple-element.37.pc, bf16[512,256]{1,0:T(8,128)(2,1)S(1)} %get-tuple-element.40.w_ref, bf16[5120,256]{1,0:T(8,128)(2,1)S(1)} %get-tuple-element.41.x_own, bf16[5120,256]{1,0:T(8,128)(2,1)S(1)} %get-tuple-element.45.x_other), custom_call_target="tpu_custom_call" | custom-call | flops 1342177280 | bytes 7864320 | tf_op jit(solution)/shard_map/pallas_call | solution.py:433
  18.9 3.8 %collective-permute-done.5 = bf16[2,256,256]{2,1,0:T(8,128)(2,1)S(1)} collective-permute-done((bf16[2,256,256]{2,1,0:T(8,128)(2,1)S(1)}, bf16[2,256,256]{2,1,0:T(8,128)(2,1)S(1)}, u32[]{:S(2)}, u32[]{:S(2)}) %collective-permute-start.5) | collective-permute-done | bytes 262176 | tf_op jit(solution)/shard_map/ppermute | solution.py:33
  23.0 1.5 %collective-permute-done.6 = bf16[2,256,256]{2,1,0:T(8,128)(2,1)S(1)} collective-permute-done((bf16[2,256,256]{2,1,0:T(8,128)(2,1)S(1)}, bf16[2,256,256]{2,1,0:T(8,128)(2,1)S(1)}, u32[]{:S(2)}, u32[]{:S(2)}) %collective-permute-start.6) | collective-permute-done | bytes 262176 | tf_op jit(solution)/shard_map/ppermute | solution.py:24
  24.7 5.3 %collective-permute-start.7 = (bf16[2,256,256]{2,1,0:T(8,128)(2,1)S(1)}, bf16[2,256,256]{2,1,0:T(8,128)(2,1)S(1)}, u32[]{:S(2)}, u32[]{:S(2)}) collective-permute-start(bf16[2,256,256]{2,1,0:T(8,128)(2,1)S(1)} %add_convert_fusion.m), channel_id=1, source_target_pairs={{0,2},{3,1},{2,4},{5,3},{4,6},{7,5},{6,8},{9,7},{8,10},{11,9},{10,... | collective-permute-start | bytes 786440 | tf_op jit(solution)/shard_map/ppermute | solution.py:33
  30.0 4.4 %collective-permute-start.8 = (bf16[2,256,256]{2,1,0:T(8,128)(2,1)S(1)}, bf16[2,256,256]{2,1,0:T(8,128)(2,1)S(1)}, u32[]{:S(2)}, u32[]{:S(2)}) collective-permute-start(bf16[2,256,256]{2,1,0:T(8,128)(2,1)S(1)} %add_convert_fusion.m), channel_id=1, source_target_pairs={{0,4},{5,1},{2,6},{7,3},{4,8},{9,5},{6,10},{11,7},{8,12},{13,9},{1... | collective-permute-start | bytes 786440 | tf_op jit(solution)/shard_map/ppermute | solution.py:33
  34.5 5.4 %collective-permute-done.8.q2 = bf16[2,256,256]{2,1,0:T(8,128)(2,1)S(1)} collective-permute-done((bf16[2,256,256]{2,1,0:T(8,128)(2,1)S(1)}, bf16[2,256,256]{2,1,0:T(8,128)(2,1)S(1)}, u32[]{:S(2)}, u32[]{:S(2)}) %collective-permute-start.8) | collective-permute-done | bytes 262176 | tf_op jit(solution)/shard_map/ppermute | solution.py:33
  39.8 1.5 %collective-permute-done.10.t2 = bf16[2,256,256]{2,1,0:T(8,128)(2,1)S(1)} collective-permute-done((bf16[2,256,256]{2,1,0:T(8,128)(2,1)S(1)}, bf16[2,256,256]{2,1,0:T(8,128)(2,1)S(1)}, u32[]{:S(2)}, u32[]{:S(2)}) %collective-permute-start.10) | collective-permute-done | bytes 262176 | tf_op jit(solution)/shard_map/ppermute | solution.py:24
  41.4 4.3 %shard_map.106 = (f32[1280,256]{1,0:T(8,128)S(1)}, bf16[5120,512]{1,0:T(8,128)(2,1)S(1)}, bf16[5120,256]{1,0:T(8,128)(2,1)S(1)}, bf16[256,256]{1,0:T(8,128)(2,1)...) custom-call(s32[4,10]{1,0:T(4,128)S(1)} %get-tuple-element.36.pm, s32[10]{0:T(128)S(1)} %get-tuple-element.37.pc, ...), custom_call_target="tpu_custom_call" | custom-call | tf_op jit(solution)/shard_map/pallas_call | solution.py:442
  45.7 0.4 collective-permute-start.11
  46.2 1.4 collective-permute-done.11
  47.6 5.3 %collective-permute-start.12 = (bf16[2,256,256]{2,1,0:T(8,128)(2,1)S(1)}, bf16[2,256,256]{2,1,0:T(8,128)(2,1)S(1)}, u32[]{:S(2)}, u32[]{:S(2)}) collective-permute-start(bf16[2,256,256]{2,1,0:T(8,128)(2,1)S(1)} %pad_maximum_fusion.3), channel_id=1, source_target_pairs={{0,2},{3,1},{2,4},{5,3},{4,6},{7,5},{6,8},{9,7},{8,10},{11,9},{10,... | collective-permute-start | bytes 786440 | tf_op jit(solution)/shard_map/ppermute | solution.py:33
  53.0 4.7 %collective-permute-start.13 = (bf16[2,256,256]{2,1,0:T(8,128)(2,1)S(1)}, bf16[2,256,256]{2,1,0:T(8,128)(2,1)S(1)}, u32[]{:S(2)}, u32[]{:S(2)}) collective-permute-start(bf16[2,256,256]{2,1,0:T(8,128)(2,1)S(1)} %pad_maximum_fusion.4), channel_id=1, source_target_pairs={{0,4},{5,1},{2,6},{7,3},{4,8},{9,5},{6,10},{11,7},{8,12},{13,9},{1... | collective-permute-start | bytes 786440 | tf_op jit(solution)/shard_map/ppermute | solution.py:33
  57.6 3.0 %shard_map.107 = (f32[256,512]{1,0:T(8,128)S(1)}, bf16[1280,256]{1,0:T(8,128)(2,1)}) custom-call(s32[10]{0:T(128)S(1)} %get-tuple-element.37.pc, bf16[5120,512]{1,0:T(8,128)(2,1)S(1)} %get-tuple-element.53.left_ref, bf16[5120,256]{1,0:T(8,128)(2,1)S(1)} %get-tuple-element.54.right_ref, f32[1280,256]{1,0:T(8,128)S(1)} %get-tuple-element.55.made_ref), custom_call_target="tpu_custom_call" | custom-call | flops 1342177280 | bytes 7864320 | tf_op jit(solution)/shard_map/pallas_call | solution.py:463
  60.6 3.0 %collective-permute-done.13 = bf16[2,256,256]{2,1,0:T(8,128)(2,1)S(1)} collective-permute-done((bf16[2,256,256]{2,1,0:T(8,128)(2,1)S(1)}, bf16[2,256,256]{2,1,0:T(8,128)(2,1)S(1)}, u32[]{:S(2)}, u32[]{:S(2)}) %collective-permute-start.13) | collective-permute-done | bytes 262176 | tf_op jit(solution)/shard_map/ppermute | solution.py:33
  63.9 1.5 %collective-permute-done.14.t = bf16[2,256,256]{2,1,0:T(8,128)(2,1)S(1)} collective-permute-done((bf16[2,256,256]{2,1,0:T(8,128)(2,1)S(1)}, bf16[2,256,256]{2,1,0:T(8,128)(2,1)S(1)}, u32[]{:S(2)}, u32[]{:S(2)}) %collective-permute-start.14) | collective-permute-done | bytes 262176 | tf_op jit(solution)/shard_map/ppermute | solution.py:24
  65.4 0.4 shard_map.108.m
  65.8 4.4 %collective-permute-start.15 = (bf16[2,256,256]{2,1,0:T(8,128)(2,1)S(1)}, bf16[2,256,256]{2,1,0:T(8,128)(2,1)S(1)}, u32[]{:S(2)}, u32[]{:S(2)}) collective-permute-start(bf16[2,256,256]{2,1,0:T(8,128)(2,1)S(1)} %shard_map.108.m), channel_id=1, source_target_pairs={{0,2},{3,1},{2,4},{5,3},{4,6},{7,5},{6,8},{9,7},{8,10},{11,9},{10,... | collective-permute-start | bytes 786440 | tf_op jit(solution)/shard_map/ppermute | solution.py:33
  70.2 4.9 %collective-permute-start.16 = (bf16[2,256,256]{2,1,0:T(8,128)(2,1)S(1)}, bf16[2,256,256]{2,1,0:T(8,128)(2,1)S(1)}, u32[]{:S(2)}, u32[]{:S(2)}) collective-permute-start(bf16[2,256,256]{2,1,0:T(8,128)(2,1)S(1)} %shard_map.108.m), channel_id=1, source_target_pairs={{0,4},{5,1},{2,6},{7,3},{4,8},{9,5},{6,10},{11,7},{8,12},{13,9},{1... | collective-permute-start | bytes 786440 | tf_op jit(solution)/shard_map/ppermute | solution.py:33
  75.3 5.6 %collective-permute-done.16.q2 = bf16[2,256,256]{2,1,0:T(8,128)(2,1)S(1)} collective-permute-done((bf16[2,256,256]{2,1,0:T(8,128)(2,1)S(1)}, bf16[2,256,256]{2,1,0:T(8,128)(2,1)S(1)}, u32[]{:S(2)}, u32[]{:S(2)}) %collective-permute-start.16) | collective-permute-done | bytes 262176 | tf_op jit(solution)/shard_map/ppermute | solution.py:33
  81.0 1.3 collective-permute-done.18.t2
  82.3 2.0 %shard_map.109 = bf16[2048,128]{1,0:T(8,128)(2,1)S(1)} custom-call(s32[4,10]{1,0:T(4,128)S(1)} %get-tuple-element.36.pm, s32[10]{0:T(128)S(1)} %get-tuple-element.37.pc, bf16[5120,256]{1,0:T(8,128)(2,1)S(1)} %get-tuple-element.41.x_own, bf16[5120,256]{1,0:T(8,128)(2,1)S(1)} %get-tuple-element.45.x_other, bf16[5120,256]{1,0:T(8,128)(2,1)S(1)} %shard_map.105.slope_ref, ...), custom_call_target="tpu_custom_call" | custom-call | tf_op jit(solution)/shard_map/pallas_call | solution.py:469
  84.3 26.5 %all_to_all.15.parts_ref = bf16[16,128,128]{2,1,0:T(8,128)(2,1)S(1)} all-to-all(bf16[16,128,128]{2,1,0:T(8,128)(2,1)S(1)} %bitcast.29), channel_id=1, replica_groups={{0,2,4,6,8,10,12,14,16,18,20,22,24,26,28,30},{32,34,36,38,40,42,44,46,4..., dimensions={0} | all-to-all | bytes 1048576 | tf_op jit(solution)/shard_map/all_to_all | solution.py:342
  110.9 19.1 %all_to_all.16.parts_ref = bf16[8,128,128]{2,1,0:T(8,128)(2,1)S(1)} all-to-all(bf16[8,128,128]{2,1,0:T(8,128)(2,1)S(1)} %shard_map.110), channel_id=1, replica_groups={{0,32,64,96,128,160,192,224},{2,34,66,98,130,162,194,226},{4,36,68,100,..., dimensions={0} | all-to-all | bytes 524288 | tf_op jit(solution)/shard_map/all_to_all | solution.py:342
  130.0 14.3 %all_to_all.17 = bf16[16,128,128]{2,1,0:T(8,128)(2,1)S(1)} all-to-all(bf16[16,128,128]{2,1,0:T(8,128)(2,1)S(1)} %shard_map.111), channel_id=1, replica_groups={{0,2,4,6,8,10,12,14,16,18,20,22,24,26,28,30},{32,34,36,38,40,42,44,46,4..., dimensions={0} | all-to-all | bytes 1048576 | tf_op jit(solution)/shard_map/all_to_all | solution.py:342
  144.3 1.1 shard_map.112
  (47 shorter events, 1.5 us)
Async XLA Ops:
  0.6 3.5 %collective-permute-start = (bf16[1280,256]{1,0:T(8,128)(2,1)}, bf16[1280,256]{1,0:T(8,128)(2,1)S(1)}, u32[]{:S(2)}, u32[]{:S(2)}) collective-permute-start(bf16[1280,256]{1,0:T(8,128)(2,1)} %g_ref.1), channel_id=1, source_target_pairs={{0,1},{1,0},{2,3},{3,2},{4,5},{5,4},{6,7},{7,6},{8,9},{9,8},{10,11... | collective-permute-start | bytes 1966088 | tf_op jit(solution)/shard_map/ppermute | solution.py:24
  0.7 3.4 %collective-permute-start.2 = (bf16[512,256]{1,0:T(8,128)(2,1)}, bf16[512,256]{1,0:T(8,128)(2,1)S(1)}, u32[]{:S(2)}, u32[]{:S(2)}) collective-permute-start(bf16[512,256]{1,0:T(8,128)(2,1)} %w_own.1), channel_id=1, source_target_pairs={{0,1},{1,0},{2,3},{3,2},{4,5},{5,4},{6,7},{7,6},{8,9},{9,8},{10,11... | collective-permute-start | bytes 786440 | tf_op jit(solution)/shard_map/ppermute | solution.py:24
  1.2 2.9 %collective-permute-start.1 = (bf16[256,256]{1,0:T(8,128)(2,1)}, bf16[256,256]{1,0:T(8,128)(2,1)S(1)}, u32[]{:S(2)}, u32[]{:S(2)}) collective-permute-start(bf16[256,256]{1,0:T(8,128)(2,1)} %param.10), channel_id=1, source_target_pairs={{0,1},{1,0},{2,3},{3,2},{4,5},{5,4},{6,7},{7,6},{8,9},{9,8},{10,11... | collective-permute-start | bytes 393224 | tf_op jit(solution)/shard_map/ppermute | solution.py:24
  7.3 1.7 %collective-permute-start.3 = (bf16[2,256,256]{2,1,0:T(8,128)(2,1)S(1)}, bf16[2,256,256]{2,1,0:T(8,128)(2,1)S(1)}, u32[]{:S(2)}, u32[]{:S(2)}) collective-permute-start(bf16[2,256,256]{2,1,0:T(8,128)(2,1)S(1)} %get-tuple-element.44), channel_id=1, source_target_pairs={{0,1},{1,0},{2,3},{3,2},{4,5},{5,4},{6,7},{7,6},{8,9},{9,8},{10,11... | collective-permute-start | bytes 786440 | tf_op jit(solution)/shard_map/ppermute | solution.py:24
  9.0 9.9 %collective-permute-start.4 = (bf16[2,256,256]{2,1,0:T(8,128)(2,1)S(1)}, bf16[2,256,256]{2,1,0:T(8,128)(2,1)S(1)}, u32[]{:S(2)}, u32[]{:S(2)}) collective-permute-start(bf16[2,256,256]{2,1,0:T(8,128)(2,1)S(1)} %pad_maximum_fusion), channel_id=1, source_target_pairs={{0,2},{3,1},{2,4},{5,3},{4,6},{7,5},{6,8},{9,7},{8,10},{11,9},{10,... | collective-permute-start | bytes 786440 | tf_op jit(solution)/shard_map/ppermute | solution.py:33
  12.6 10.2 %collective-permute-start.5 = (bf16[2,256,256]{2,1,0:T(8,128)(2,1)S(1)}, bf16[2,256,256]{2,1,0:T(8,128)(2,1)S(1)}, u32[]{:S(2)}, u32[]{:S(2)}) collective-permute-start(bf16[2,256,256]{2,1,0:T(8,128)(2,1)S(1)} %pad_maximum_fusion.1), channel_id=1, source_target_pairs={{0,4},{5,1},{2,6},{7,3},{4,8},{9,5},{6,10},{11,7},{8,12},{13,9},{1... | collective-permute-start | bytes 786440 | tf_op jit(solution)/shard_map/ppermute | solution.py:33
  18.9 5.7 %copy-start.3 = (bf16[256,256]{1,0:T(8,128)(2,1)S(1)}, bf16[256,256]{1,0:T(8,128)(2,1)}, u32[]{:S(2)}) copy-start(bf16[256,256]{1,0:T(8,128)(2,1)} %param.10) | copy-start | bytes 393220
  18.9 22.5 %copy-start = (bf16[1280,256]{1,0:T(8,128)(2,1)S(1)}, bf16[1280,256]{1,0:T(8,128)(2,1)}, u32[]{:S(2)}) copy-start(bf16[1280,256]{1,0:T(8,128)(2,1)} %g_ref.1) | copy-start | bytes 1966084
  18.9 22.5 %copy-start.1 = (bf16[512,256]{1,0:T(8,128)(2,1)S(1)}, bf16[512,256]{1,0:T(8,128)(2,1)}, u32[]{:S(2)}) copy-start(bf16[512,256]{1,0:T(8,128)(2,1)} %w_own.1) | copy-start | bytes 786436
  18.9 22.5 %copy-start.2 = (bf16[1280,256]{1,0:T(8,128)(2,1)S(1)}, bf16[1280,256]{1,0:T(8,128)(2,1)}, u32[]{:S(2)}) copy-start(bf16[1280,256]{1,0:T(8,128)(2,1)} %cot_ref.1) | copy-start | bytes 1966084
  22.9 1.6 %collective-permute-start.6 = (bf16[2,256,256]{2,1,0:T(8,128)(2,1)S(1)}, bf16[2,256,256]{2,1,0:T(8,128)(2,1)S(1)}, u32[]{:S(2)}, u32[]{:S(2)}) collective-permute-start(bf16[2,256,256]{2,1,0:T(8,128)(2,1)S(1)} %pad_maximum_fusion.2), channel_id=1, source_target_pairs={{0,1},{1,0},{2,3},{3,2},{4,5},{5,4},{6,7},{7,6},{8,9},{9,8},{10,11... | collective-permute-start | bytes 786440 | tf_op jit(solution)/shard_map/ppermute | solution.py:24
  24.7 9.7 %collective-permute-start.7 = (bf16[2,256,256]{2,1,0:T(8,128)(2,1)S(1)}, bf16[2,256,256]{2,1,0:T(8,128)(2,1)S(1)}, u32[]{:S(2)}, u32[]{:S(2)}) collective-permute-start(bf16[2,256,256]{2,1,0:T(8,128)(2,1)S(1)} %add_convert_fusion.m), channel_id=1, source_target_pairs={{0,2},{3,1},{2,4},{5,3},{4,6},{7,5},{6,8},{9,7},{8,10},{11,9},{10,... | collective-permute-start | bytes 786440 | tf_op jit(solution)/shard_map/ppermute | solution.py:33
  30.0 9.8 %collective-permute-start.8 = (bf16[2,256,256]{2,1,0:T(8,128)(2,1)S(1)}, bf16[2,256,256]{2,1,0:T(8,128)(2,1)S(1)}, u32[]{:S(2)}, u32[]{:S(2)}) collective-permute-start(bf16[2,256,256]{2,1,0:T(8,128)(2,1)S(1)} %add_convert_fusion.m), channel_id=1, source_target_pairs={{0,4},{5,1},{2,6},{7,3},{4,8},{9,5},{6,10},{11,7},{8,12},{13,9},{1... | collective-permute-start | bytes 786440 | tf_op jit(solution)/shard_map/ppermute | solution.py:33
  34.4 5.5 %collective-permute-start.9 = (bf16[2,256,256]{2,1,0:T(8,128)(2,1)S(1)}, bf16[2,256,256]{2,1,0:T(8,128)(2,1)S(1)}, u32[]{:S(2)}, u32[]{:S(2)}) collective-permute-start(bf16[2,256,256]{2,1,0:T(8,128)(2,1)S(1)} %collective-permute-done.7.q1), channel_id=1, source_target_pairs={{0,1},{1,0},{2,3},{3,2},{4,5},{5,4},{6,7},{7,6},{8,9},{9,8},{10,11... | collective-permute-start | bytes 786440 | tf_op jit(solution)/shard_map/ppermute | solution.py:24
  39.8 1.5 %collective-permute-start.10 = (bf16[2,256,256]{2,1,0:T(8,128)(2,1)S(1)}, bf16[2,256,256]{2,1,0:T(8,128)(2,1)S(1)}, u32[]{:S(2)}, u32[]{:S(2)}) collective-permute-start(bf16[2,256,256]{2,1,0:T(8,128)(2,1)S(1)} %collective-permute-done.8.q2), channel_id=1, source_target_pairs={{0,1},{1,0},{2,3},{3,2},{4,5},{5,4},{6,7},{7,6},{8,9},{9,8},{10,11... | collective-permute-start | bytes 786440 | tf_op jit(solution)/shard_map/ppermute | solution.py:24
  45.7 1.8 %collective-permute-start.11 = (bf16[2,256,256]{2,1,0:T(8,128)(2,1)S(1)}, bf16[2,256,256]{2,1,0:T(8,128)(2,1)S(1)}, u32[]{:S(2)}, u32[]{:S(2)}) collective-permute-start(bf16[2,256,256]{2,1,0:T(8,128)(2,1)S(1)} %get-tuple-element.52), channel_id=1, source_target_pairs={{0,1},{1,0},{2,3},{3,2},{4,5},{5,4},{6,7},{7,6},{8,9},{9,8},{10,11... | collective-permute-start | bytes 786440 | tf_op jit(solution)/shard_map/ppermute | solution.py:24
  47.6 13.0 %collective-permute-start.12 = (bf16[2,256,256]{2,1,0:T(8,128)(2,1)S(1)}, bf16[2,256,256]{2,1,0:T(8,128)(2,1)S(1)}, u32[]{:S(2)}, u32[]{:S(2)}) collective-permute-start(bf16[2,256,256]{2,1,0:T(8,128)(2,1)S(1)} %pad_maximum_fusion.3), channel_id=1, source_target_pairs={{0,2},{3,1},{2,4},{5,3},{4,6},{7,5},{6,8},{9,7},{8,10},{11,9},{10,... | collective-permute-start | bytes 786440 | tf_op jit(solution)/shard_map/ppermute | solution.py:33
  53.0 10.7 %collective-permute-start.13 = (bf16[2,256,256]{2,1,0:T(8,128)(2,1)S(1)}, bf16[2,256,256]{2,1,0:T(8,128)(2,1)S(1)}, u32[]{:S(2)}, u32[]{:S(2)}) collective-permute-start(bf16[2,256,256]{2,1,0:T(8,128)(2,1)S(1)} %pad_maximum_fusion.4), channel_id=1, source_target_pairs={{0,4},{5,1},{2,6},{7,3},{4,8},{9,5},{6,10},{11,7},{8,12},{13,9},{1... | collective-permute-start | bytes 786440 | tf_op jit(solution)/shard_map/ppermute | solution.py:33
  63.8 1.6 %collective-permute-start.14 = (bf16[2,256,256]{2,1,0:T(8,128)(2,1)S(1)}, bf16[2,256,256]{2,1,0:T(8,128)(2,1)S(1)}, u32[]{:S(2)}, u32[]{:S(2)}) collective-permute-start(bf16[2,256,256]{2,1,0:T(8,128)(2,1)S(1)} %pad_maximum_fusion.5.s), channel_id=1, source_target_pairs={{0,1},{1,0},{2,3},{3,2},{4,5},{5,4},{6,7},{7,6},{8,9},{9,8},{10,11... | collective-permute-start | bytes 786440 | tf_op jit(solution)/shard_map/ppermute | solution.py:24
  65.8 9.4 %collective-permute-start.15 = (bf16[2,256,256]{2,1,0:T(8,128)(2,1)S(1)}, bf16[2,256,256]{2,1,0:T(8,128)(2,1)S(1)}, u32[]{:S(2)}, u32[]{:S(2)}) collective-permute-start(bf16[2,256,256]{2,1,0:T(8,128)(2,1)S(1)} %shard_map.108.m), channel_id=1, source_target_pairs={{0,2},{3,1},{2,4},{5,3},{4,6},{7,5},{6,8},{9,7},{8,10},{11,9},{10,... | collective-permute-start | bytes 786440 | tf_op jit(solution)/shard_map/ppermute | solution.py:33
  70.2 10.7 %collective-permute-start.16 = (bf16[2,256,256]{2,1,0:T(8,128)(2,1)S(1)}, bf16[2,256,256]{2,1,0:T(8,128)(2,1)S(1)}, u32[]{:S(2)}, u32[]{:S(2)}) collective-permute-start(bf16[2,256,256]{2,1,0:T(8,128)(2,1)S(1)} %shard_map.108.m), channel_id=1, source_target_pairs={{0,4},{5,1},{2,6},{7,3},{4,8},{9,5},{6,10},{11,7},{8,12},{13,9},{1... | collective-permute-start | bytes 786440 | tf_op jit(solution)/shard_map/ppermute | solution.py:33
  75.2 5.7 %collective-permute-start.17 = (bf16[256,256]{1,0:T(8,128)(2,1)S(1)}, bf16[256,256]{1,0:T(8,128)(2,1)S(1)}, u32[]{:S(2)}, u32[]{:S(2)}) collective-permute-start(bf16[256,256]{1,0:T(8,128)(2,1)S(1)} %slice_bitcast_fusion.2), channel_id=1, source_target_pairs={{0,1},{1,0},{2,3},{3,2},{4,5},{5,4},{6,7},{7,6},{8,9},{9,8},{10,11... | collective-permute-start | bytes 393224 | tf_op jit(solution)/shard_map/ppermute | solution.py:24
  80.9 1.4 collective-permute-start.18

commit v10 on v8

--- a/solution.py
+++ b/solution.py
@@ -355,15 +355,17 @@
 
 
 def combine(own, parts):
-    first, second = (part.astype(FL) for part in parts)
-    total = first + second
-    return jnp.stack([total[0] + own.astype(FL), total[1]]).astype(BF)
+    near, far = parts
+    near = near.astype(FL)
+    base = jnp.stack([near[0] + own.astype(FL), near[1]])
+    base, far = lax.optimization_barrier((base, far))
+    return (base + far.astype(FL)).astype(BF)
 
 
 def reduce_to_owner(own, mine, other, beside=None):
     got = swap(other)
     parts = [outward(jnp.stack([mine[i], got[i]]), i + 1) for i in range(REACH)]
-    parts, beside = lax.optimization_barrier((parts, beside))
+    parts[1], beside = lax.optimization_barrier((parts[1], beside))
     sums = combine(own, parts)
     return sums, swap(sums), beside
 

time: 144 us -> 140 us (0.972)
  starting transfers between devices: 35.2 us -> 28.5 us
  waiting for transfers between devices: 31.6 us -> 37.8 us
  blocking collectives: 55.6 us -> 52.2 us
    ppermute x8, starting transfers between devices: 33.2 us -> 26.5 us  [outward(): return lax.ppermute(value, ('band', 'mp'), pairs)]
    ppermute x8, waiting for transfers between devices: 23.1 us -> 29.4 us  [outward(): return lax.ppermute(value, ('band', 'mp'), pairs)]
    all_to_all x3, blocking collectives: 55.6 us -> 52.2 us  [exchange(): lax.all_to_all(value, 'band', 0, 0, tiled=True, axis_index_groups=groups)]
  transfers between devices with their start and end apart: 19 -> 19, of which waited for: 12 -> 14; matrix products, arithmetic and copies ran while one was open for 0% -> 0% of each run, Pallas kernels for 6% -> 6%
where the time goes in v10:
time: 140 us
  blocking collectives  52.2 us (37%)
  waiting for transfers between devices  37.8 us (27%)
  starting transfers between devices  28.5 us (20%)
  Pallas kernels  19.3 us (14%)
    all_to_all x3, blocking collectives, exchange(): lax.all_to_all(value, 'band', 0, 0, tiled=True, axis_index_groups=groups)  52.2 us
    ppermute x8, waiting for transfers between devices, outward(): return lax.ppermute(value, ('band', 'mp'), pairs)  29.4 us
    ppermute x8, starting transfers between devices, outward(): return lax.ppermute(value, ('band', 'mp'), pairs)  26.5 us
    ppermute x11, waiting for transfers between devices, swap(): return lax.ppermute(value, 'mp', [(0, 1), (1, 0)])  8.45 us
    pallas_call x1, Pallas kernels, decode(): held(decode_kernel, [SMEM, SMEM, *[VMEM] * (4 + NEAR)], [shape_of(*grid.s...  4.31 us
    pallas_call x1, Pallas kernels, encode(): held(encode_kernel, [SMEM, SMEM, *[VMEM] * 4], [shape_of(pairs, half), *s...  3.14 us
    pallas_call x1, Pallas kernels, outer(): held(outer_kernel, [SMEM, *[VMEM] * 3], outs, cost=cost)  3 us
  transfers between devices with their start and end apart: 19, of which 14 were waited for; matrix products, arithmetic and copies ran while one was open for 0% of the time, Pallas kernels for 6%

profile of v10, /device:TPU:8, one launch (start us, length us, event | category | flops | bytes accessed | tf_op | source)
XLA Modules:
  0.0 139.7 jit_solution(2839445063978090146)
XLA Ops:
  1.3 2.8 %shard_map.103 = (bf16[10,4,128,128]{3,2,1,0:T(8,128)(2,1)S(1)}, bf16[512,256]{1,0:T(8,128)(2,1)S(1)}, bf16[5120,256]{1,0:T(8,128)(2,1)S(1)}, s32[4,10]{1,0:T(4,128)S(1)}, s32[10]{0:T(128)S(1)}) custom-call(bf16[10,4,128,128]{3,2,1,0:T(8,128)(2,1)} %a_hbm.1, bf16[1280,256]{1,0:T(8,128)(2,1)} %g_ref.1, bf16[512,256]{1,0:T(8,128)(2,1)} %w_hbm.1, ...), custom_call_target="tpu_custom_call" | custom-call | flops 335544320 | bytes 4194304 | tf_op jit(solution)/shard_map/pallas_call | solution.py:404
  4.2 3.1 %shard_map.104 = (bf16[5120,256]{1,0:T(8,128)(2,1)S(1)}, bf16[256,256]{1,0:T(8,128)(2,1)S(1)}, bf16[2,256,256]{2,1,0:T(8,128)(2,1)S(1)}, bf16[2,256,256]{2,1,0:T(8,128)(2,1)S(1)}) custom-call(s32[4,10]{1,0:T(4,128)S(1)} %get-tuple-element.34.pm, s32[10]{0:T(128)S(1)} %get-tuple-element.35.pc, bf16[10,4,128,128]{3,2,1,0:T(8,128)(2,1)S(1)} %get-tuple-element.36.a_ref, ...), custom_call_target="tpu_custom_call" | custom-call | tf_op jit(solution)/shard_map/pallas_call | solution.py:418
  7.8 1.1 collective-permute-done.3
  9.0 4.2 %collective-permute-start.5 = (bf16[2,256,256]{2,1,0:T(8,128)(2,1)S(1)}, bf16[2,256,256]{2,1,0:T(8,128)(2,1)S(1)}, u32[]{:S(2)}, u32[]{:S(2)}) collective-permute-start(bf16[2,256,256]{2,1,0:T(8,128)(2,1)S(1)} %pad_maximum_fusion.3), channel_id=1, source_target_pairs={{0,4},{5,1},{2,6},{7,3},{4,8},{9,5},{6,10},{11,7},{8,12},{13,9},{1... | collective-permute-start | bytes 786440 | tf_op jit(solution)/shard_map/ppermute | solution.py:33
  13.3 2.4 %collective-permute-start.4 = (bf16[2,256,256]{2,1,0:T(8,128)(2,1)S(1)}, bf16[2,256,256]{2,1,0:T(8,128)(2,1)S(1)}, u32[]{:S(2)}, u32[]{:S(2)}) collective-permute-start(bf16[2,256,256]{2,1,0:T(8,128)(2,1)S(1)} %pad_maximum_fusion.2), channel_id=1, source_target_pairs={{0,2},{3,1},{2,4},{5,3},{4,6},{7,5},{6,8},{9,7},{8,10},{11,9},{10,... | collective-permute-start | bytes 786440 | tf_op jit(solution)/shard_map/ppermute | solution.py:33
  15.7 2.5 %shard_map.105.slope_ref = bf16[5120,256]{1,0:T(8,128)(2,1)S(1)} custom-call(s32[10]{0:T(128)S(1)} %get-tuple-element.35.pc, bf16[512,256]{1,0:T(8,128)(2,1)S(1)} %get-tuple-element.38.w_ref, bf16[5120,256]{1,0:T(8,128)(2,1)S(1)} %get-tuple-element.39.x_own, bf16[5120,256]{1,0:T(8,128)(2,1)S(1)} %get-tuple-element.44.x_other), custom_call_target="tpu_custom_call" | custom-call | flops 1342177280 | bytes 7864320 | tf_op jit(solution)/shard_map/pallas_call | solution.py:431
  18.3 4.0 %collective-permute-done.5 = bf16[2,256,256]{2,1,0:T(8,128)(2,1)S(1)} collective-permute-done((bf16[2,256,256]{2,1,0:T(8,128)(2,1)S(1)}, bf16[2,256,256]{2,1,0:T(8,128)(2,1)S(1)}, u32[]{:S(2)}, u32[]{:S(2)}) %collective-permute-start.5) | collective-permute-done | bytes 262176 | tf_op jit(solution)/shard_map/ppermute | solution.py:33
  22.3 2.3 %collective-permute-done.4 = bf16[2,256,256]{2,1,0:T(8,128)(2,1)S(1)} collective-permute-done((bf16[2,256,256]{2,1,0:T(8,128)(2,1)S(1)}, bf16[2,256,256]{2,1,0:T(8,128)(2,1)S(1)}, u32[]{:S(2)}, u32[]{:S(2)}) %collective-permute-start.4) | collective-permute-done | bytes 262176 | tf_op jit(solution)/shard_map/ppermute | solution.py:33
  24.9 1.5 %collective-permute-done.6 = bf16[2,256,256]{2,1,0:T(8,128)(2,1)S(1)} collective-permute-done((bf16[2,256,256]{2,1,0:T(8,128)(2,1)S(1)}, bf16[2,256,256]{2,1,0:T(8,128)(2,1)S(1)}, u32[]{:S(2)}, u32[]{:S(2)}) %collective-permute-start.6) | collective-permute-done | bytes 262176 | tf_op jit(solution)/shard_map/ppermute | solution.py:24
  26.6 4.1 %collective-permute-start.8 = (bf16[2,256,256]{2,1,0:T(8,128)(2,1)S(1)}, bf16[2,256,256]{2,1,0:T(8,128)(2,1)S(1)}, u32[]{:S(2)}, u32[]{:S(2)}) collective-permute-start(bf16[2,256,256]{2,1,0:T(8,128)(2,1)S(1)} %add_convert_fusion.1.m), channel_id=1, source_target_pairs={{0,4},{5,1},{2,6},{7,3},{4,8},{9,5},{6,10},{11,7},{8,12},{13,9},{1... | collective-permute-start | bytes 786440 | tf_op jit(solution)/shard_map/ppermute | solution.py:33
  30.7 2.6 %collective-permute-start.7 = (bf16[2,256,256]{2,1,0:T(8,128)(2,1)S(1)}, bf16[2,256,256]{2,1,0:T(8,128)(2,1)S(1)}, u32[]{:S(2)}, u32[]{:S(2)}) collective-permute-start(bf16[2,256,256]{2,1,0:T(8,128)(2,1)S(1)} %add_convert_fusion.1.m), channel_id=1, source_target_pairs={{0,2},{3,1},{2,4},{5,3},{4,6},{7,5},{6,8},{9,7},{8,10},{11,9},{10,... | collective-permute-start | bytes 786440 | tf_op jit(solution)/shard_map/ppermute | solution.py:33
  33.3 6.6 %collective-permute-done.8.q2 = bf16[2,256,256]{2,1,0:T(8,128)(2,1)S(1)} collective-permute-done((bf16[2,256,256]{2,1,0:T(8,128)(2,1)S(1)}, bf16[2,256,256]{2,1,0:T(8,128)(2,1)S(1)}, u32[]{:S(2)}, u32[]{:S(2)}) %collective-permute-start.8) | collective-permute-done | bytes 262176 | tf_op jit(solution)/shard_map/ppermute | solution.py:33
  39.9 2.1 %collective-permute-done.7.q1 = bf16[2,256,256]{2,1,0:T(8,128)(2,1)S(1)} collective-permute-done((bf16[2,256,256]{2,1,0:T(8,128)(2,1)S(1)}, bf16[2,256,256]{2,1,0:T(8,128)(2,1)S(1)}, u32[]{:S(2)}, u32[]{:S(2)}) %collective-permute-start.7) | collective-permute-done | bytes 262176 | tf_op jit(solution)/shard_map/ppermute | solution.py:33
  42.0 1.5 %collective-permute-done.9.t1 = bf16[2,256,256]{2,1,0:T(8,128)(2,1)S(1)} collective-permute-done((bf16[2,256,256]{2,1,0:T(8,128)(2,1)S(1)}, bf16[2,256,256]{2,1,0:T(8,128)(2,1)S(1)}, u32[]{:S(2)}, u32[]{:S(2)}) %collective-permute-start.9) | collective-permute-done | bytes 262176 | tf_op jit(solution)/shard_map/ppermute | solution.py:24
  43.6 4.3 %shard_map.106 = (f32[1280,256]{1,0:T(8,128)S(1)}, bf16[5120,512]{1,0:T(8,128)(2,1)S(1)}, bf16[5120,256]{1,0:T(8,128)(2,1)S(1)}, bf16[256,256]{1,0:T(8,128)(2,1)...) custom-call(s32[4,10]{1,0:T(4,128)S(1)} %get-tuple-element.34.pm, s32[10]{0:T(128)S(1)} %get-tuple-element.35.pc, ...), custom_call_target="tpu_custom_call" | custom-call | tf_op jit(solution)/shard_map/pallas_call | solution.py:440
  48.3 1.4 %collective-permute-done.11 = bf16[2,256,256]{2,1,0:T(8,128)(2,1)S(1)} collective-permute-done((bf16[2,256,256]{2,1,0:T(8,128)(2,1)S(1)}, bf16[2,256,256]{2,1,0:T(8,128)(2,1)S(1)}, u32[]{:S(2)}, u32[]{:S(2)}) %collective-permute-start.11) | collective-permute-done | bytes 262176 | tf_op jit(solution)/shard_map/ppermute | solution.py:24
  49.8 4.5 %collective-permute-start.12 = (bf16[2,256,256]{2,1,0:T(8,128)(2,1)S(1)}, bf16[2,256,256]{2,1,0:T(8,128)(2,1)S(1)}, u32[]{:S(2)}, u32[]{:S(2)}) collective-permute-start(bf16[2,256,256]{2,1,0:T(8,128)(2,1)S(1)} %pad_maximum_fusion.4), channel_id=1, source_target_pairs={{0,4},{5,1},{2,6},{7,3},{4,8},{9,5},{6,10},{11,7},{8,12},{13,9},{1... | collective-permute-start | bytes 786440 | tf_op jit(solution)/shard_map/ppermute | solution.py:33
  54.4 2.0 %collective-permute-start.13 = (bf16[2,256,256]{2,1,0:T(8,128)(2,1)S(1)}, bf16[2,256,256]{2,1,0:T(8,128)(2,1)S(1)}, u32[]{:S(2)}, u32[]{:S(2)}) collective-permute-start(bf16[2,256,256]{2,1,0:T(8,128)(2,1)S(1)} %pad_maximum_fusion.5), channel_id=1, source_target_pairs={{0,2},{3,1},{2,4},{5,3},{4,6},{7,5},{6,8},{9,7},{8,10},{11,9},{10,... | collective-permute-start | bytes 786440 | tf_op jit(solution)/shard_map/ppermute | solution.py:33
  56.4 3.0 %shard_map.107 = (f32[256,512]{1,0:T(8,128)S(1)}, bf16[1280,256]{1,0:T(8,128)(2,1)}) custom-call(s32[10]{0:T(128)S(1)} %get-tuple-element.35.pc, bf16[5120,512]{1,0:T(8,128)(2,1)S(1)} %get-tuple-element.50.left_ref, bf16[5120,256]{1,0:T(8,128)(2,1)S(1)} %get-tuple-element.51.right_ref, f32[1280,256]{1,0:T(8,128)S(1)} %get-tuple-element.52.made_ref), custom_call_target="tpu_custom_call" | custom-call | flops 1342177280 | bytes 7864320 | tf_op jit(solution)/shard_map/pallas_call | solution.py:461
  59.4 4.3 %collective-permute-done.12 = bf16[2,256,256]{2,1,0:T(8,128)(2,1)S(1)} collective-permute-done((bf16[2,256,256]{2,1,0:T(8,128)(2,1)S(1)}, bf16[2,256,256]{2,1,0:T(8,128)(2,1)S(1)}, u32[]{:S(2)}, u32[]{:S(2)}) %collective-permute-start.12) | collective-permute-done | bytes 262176 | tf_op jit(solution)/shard_map/ppermute | solution.py:33
  63.7 1.4 %collective-permute-done.13 = bf16[2,256,256]{2,1,0:T(8,128)(2,1)S(1)} collective-permute-done((bf16[2,256,256]{2,1,0:T(8,128)(2,1)S(1)}, bf16[2,256,256]{2,1,0:T(8,128)(2,1)S(1)}, u32[]{:S(2)}, u32[]{:S(2)}) %collective-permute-start.13) | collective-permute-done | bytes 262176 | tf_op jit(solution)/shard_map/ppermute | solution.py:33
  65.5 1.5 %collective-permute-done.14.t = bf16[2,256,256]{2,1,0:T(8,128)(2,1)S(1)} collective-permute-done((bf16[2,256,256]{2,1,0:T(8,128)(2,1)S(1)}, bf16[2,256,256]{2,1,0:T(8,128)(2,1)S(1)}, u32[]{:S(2)}, u32[]{:S(2)}) %collective-permute-start.14) | collective-permute-done | bytes 262176 | tf_op jit(solution)/shard_map/ppermute | solution.py:24
  67.4 4.6 %collective-permute-start.16 = (bf16[2,256,256]{2,1,0:T(8,128)(2,1)S(1)}, bf16[2,256,256]{2,1,0:T(8,128)(2,1)S(1)}, u32[]{:S(2)}, u32[]{:S(2)}) collective-permute-start(bf16[2,256,256]{2,1,0:T(8,128)(2,1)S(1)} %shard_map.108.m), channel_id=1, source_target_pairs={{0,4},{5,1},{2,6},{7,3},{4,8},{9,5},{6,10},{11,7},{8,12},{13,9},{1... | collective-permute-start | bytes 786440 | tf_op jit(solution)/shard_map/ppermute | solution.py:33
  72.0 2.0 %collective-permute-start.15 = (bf16[2,256,256]{2,1,0:T(8,128)(2,1)S(1)}, bf16[2,256,256]{2,1,0:T(8,128)(2,1)S(1)}, u32[]{:S(2)}, u32[]{:S(2)}) collective-permute-start(bf16[2,256,256]{2,1,0:T(8,128)(2,1)S(1)} %shard_map.108.m), channel_id=1, source_target_pairs={{0,2},{3,1},{2,4},{5,3},{4,6},{7,5},{6,8},{9,7},{8,10},{11,9},{10,... | collective-permute-start | bytes 786440 | tf_op jit(solution)/shard_map/ppermute | solution.py:33
  74.1 7.4 %collective-permute-done.16.q2 = bf16[2,256,256]{2,1,0:T(8,128)(2,1)S(1)} collective-permute-done((bf16[2,256,256]{2,1,0:T(8,128)(2,1)S(1)}, bf16[2,256,256]{2,1,0:T(8,128)(2,1)S(1)}, u32[]{:S(2)}, u32[]{:S(2)}) %collective-permute-start.16) | collective-permute-done | bytes 262176 | tf_op jit(solution)/shard_map/ppermute | solution.py:33
  81.5 1.2 collective-permute-done.15.q1
  82.9 1.3 collective-permute-done.17.t1
  84.2 2.0 %shard_map.109 = bf16[2048,128]{1,0:T(8,128)(2,1)S(1)} custom-call(s32[4,10]{1,0:T(4,128)S(1)} %get-tuple-element.34.pm, s32[10]{0:T(128)S(1)} %get-tuple-element.35.pc, bf16[5120,256]{1,0:T(8,128)(2,1)S(1)} %get-tuple-element.39.x_own, bf16[5120,256]{1,0:T(8,128)(2,1)S(1)} %get-tuple-element.44.x_other, bf16[5120,256]{1,0:T(8,128)(2,1)S(1)} %shard_map.105.slope_ref, ...), custom_call_target="tpu_custom_call" | custom-call | tf_op jit(solution)/shard_map/pallas_call | solution.py:467
  86.2 18.1 %all_to_all.15.parts_ref = bf16[16,128,128]{2,1,0:T(8,128)(2,1)S(1)} all-to-all(bf16[16,128,128]{2,1,0:T(8,128)(2,1)S(1)} %bitcast.25), channel_id=1, replica_groups={{0,2,4,6,8,10,12,14,16,18,20,22,24,26,28,30},{32,34,36,38,40,42,44,46,4..., dimensions={0} | all-to-all | bytes 1048576 | tf_op jit(solution)/shard_map/all_to_all | solution.py:342
  104.4 20.0 %all_to_all.16.parts_ref = bf16[8,128,128]{2,1,0:T(8,128)(2,1)S(1)} all-to-all(bf16[8,128,128]{2,1,0:T(8,128)(2,1)S(1)} %shard_map.110), channel_id=1, replica_groups={{0,32,64,96,128,160,192,224},{2,34,66,98,130,162,194,226},{4,36,68,100,..., dimensions={0} | all-to-all | bytes 524288 | tf_op jit(solution)/shard_map/all_to_all | solution.py:342
  124.4 14.1 %all_to_all.17 = bf16[16,128,128]{2,1,0:T(8,128)(2,1)S(1)} all-to-all(bf16[16,128,128]{2,1,0:T(8,128)(2,1)S(1)} %shard_map.111), channel_id=1, replica_groups={{0,2,4,6,8,10,12,14,16,18,20,22,24,26,28,30},{32,34,36,38,40,42,44,46,4..., dimensions={0} | all-to-all | bytes 1048576 | tf_op jit(solution)/shard_map/all_to_all | solution.py:342
  138.6 1.1 shard_map.112
  (49 shorter events, 3.3 us)
Async XLA Ops:
  0.6 3.5 %collective-permute-start = (bf16[1280,256]{1,0:T(8,128)(2,1)}, bf16[1280,256]{1,0:T(8,128)(2,1)S(1)}, u32[]{:S(2)}, u32[]{:S(2)}) collective-permute-start(bf16[1280,256]{1,0:T(8,128)(2,1)} %g_ref.1), channel_id=1, source_target_pairs={{0,1},{1,0},{2,3},{3,2},{4,5},{5,4},{6,7},{7,6},{8,9},{9,8},{10,11... | collective-permute-start | bytes 1966088 | tf_op jit(solution)/shard_map/ppermute | solution.py:24
  0.7 3.4 %collective-permute-start.2 = (bf16[512,256]{1,0:T(8,128)(2,1)}, bf16[512,256]{1,0:T(8,128)(2,1)S(1)}, u32[]{:S(2)}, u32[]{:S(2)}) collective-permute-start(bf16[512,256]{1,0:T(8,128)(2,1)} %w_own.1), channel_id=1, source_target_pairs={{0,1},{1,0},{2,3},{3,2},{4,5},{5,4},{6,7},{7,6},{8,9},{9,8},{10,11... | collective-permute-start | bytes 786440 | tf_op jit(solution)/shard_map/ppermute | solution.py:24
  1.2 2.9 %collective-permute-start.1 = (bf16[256,256]{1,0:T(8,128)(2,1)}, bf16[256,256]{1,0:T(8,128)(2,1)S(1)}, u32[]{:S(2)}, u32[]{:S(2)}) collective-permute-start(bf16[256,256]{1,0:T(8,128)(2,1)} %param.10), channel_id=1, source_target_pairs={{0,1},{1,0},{2,3},{3,2},{4,5},{5,4},{6,7},{7,6},{8,9},{9,8},{10,11... | collective-permute-start | bytes 393224 | tf_op jit(solution)/shard_map/ppermute | solution.py:24
  7.3 1.7 %collective-permute-start.3 = (bf16[2,256,256]{2,1,0:T(8,128)(2,1)S(1)}, bf16[2,256,256]{2,1,0:T(8,128)(2,1)S(1)}, u32[]{:S(2)}, u32[]{:S(2)}) collective-permute-start(bf16[2,256,256]{2,1,0:T(8,128)(2,1)S(1)} %get-tuple-element.42), channel_id=1, source_target_pairs={{0,1},{1,0},{2,3},{3,2},{4,5},{5,4},{6,7},{7,6},{8,9},{9,8},{10,11... | collective-permute-start | bytes 786440 | tf_op jit(solution)/shard_map/ppermute | solution.py:24
  9.0 13.3 %collective-permute-start.5 = (bf16[2,256,256]{2,1,0:T(8,128)(2,1)S(1)}, bf16[2,256,256]{2,1,0:T(8,128)(2,1)S(1)}, u32[]{:S(2)}, u32[]{:S(2)}) collective-permute-start(bf16[2,256,256]{2,1,0:T(8,128)(2,1)S(1)} %pad_maximum_fusion.3), channel_id=1, source_target_pairs={{0,4},{5,1},{2,6},{7,3},{4,8},{9,5},{6,10},{11,7},{8,12},{13,9},{1... | collective-permute-start | bytes 786440 | tf_op jit(solution)/shard_map/ppermute | solution.py:33
  13.3 11.3 %collective-permute-start.4 = (bf16[2,256,256]{2,1,0:T(8,128)(2,1)S(1)}, bf16[2,256,256]{2,1,0:T(8,128)(2,1)S(1)}, u32[]{:S(2)}, u32[]{:S(2)}) collective-permute-start(bf16[2,256,256]{2,1,0:T(8,128)(2,1)S(1)} %pad_maximum_fusion.2), channel_id=1, source_target_pairs={{0,2},{3,1},{2,4},{5,3},{4,6},{7,5},{6,8},{9,7},{8,10},{11,9},{10,... | collective-permute-start | bytes 786440 | tf_op jit(solution)/shard_map/ppermute | solution.py:33
  18.3 8.2 %copy-start.3 = (bf16[256,256]{1,0:T(8,128)(2,1)S(1)}, bf16[256,256]{1,0:T(8,128)(2,1)}, u32[]{:S(2)}) copy-start(bf16[256,256]{1,0:T(8,128)(2,1)} %param.10) | copy-start | bytes 393220
  24.6 18.9 %copy-start = (bf16[1280,256]{1,0:T(8,128)(2,1)S(1)}, bf16[1280,256]{1,0:T(8,128)(2,1)}, u32[]{:S(2)}) copy-start(bf16[1280,256]{1,0:T(8,128)(2,1)} %g_ref.1) | copy-start | bytes 1966084
  24.6 18.9 %copy-start.1 = (bf16[512,256]{1,0:T(8,128)(2,1)S(1)}, bf16[512,256]{1,0:T(8,128)(2,1)}, u32[]{:S(2)}) copy-start(bf16[512,256]{1,0:T(8,128)(2,1)} %w_own.1) | copy-start | bytes 786436
  24.6 18.9 %copy-start.2 = (bf16[1280,256]{1,0:T(8,128)(2,1)S(1)}, bf16[1280,256]{1,0:T(8,128)(2,1)}, u32[]{:S(2)}) copy-start(bf16[1280,256]{1,0:T(8,128)(2,1)} %cot_ref.1) | copy-start | bytes 1966084
  24.8 1.6 %collective-permute-start.6 = (bf16[2,256,256]{2,1,0:T(8,128)(2,1)S(1)}, bf16[2,256,256]{2,1,0:T(8,128)(2,1)S(1)}, u32[]{:S(2)}, u32[]{:S(2)}) collective-permute-start(bf16[2,256,256]{2,1,0:T(8,128)(2,1)S(1)} %add_convert_fusion.2), channel_id=1, source_target_pairs={{0,1},{1,0},{2,3},{3,2},{4,5},{5,4},{6,7},{7,6},{8,9},{9,8},{10,11... | collective-permute-start | bytes 786440 | tf_op jit(solution)/shard_map/ppermute | solution.py:24
  26.6 13.3 %collective-permute-start.8 = (bf16[2,256,256]{2,1,0:T(8,128)(2,1)S(1)}, bf16[2,256,256]{2,1,0:T(8,128)(2,1)S(1)}, u32[]{:S(2)}, u32[]{:S(2)}) collective-permute-start(bf16[2,256,256]{2,1,0:T(8,128)(2,1)S(1)} %add_convert_fusion.1.m), channel_id=1, source_target_pairs={{0,4},{5,1},{2,6},{7,3},{4,8},{9,5},{6,10},{11,7},{8,12},{13,9},{1... | collective-permute-start | bytes 786440 | tf_op jit(solution)/shard_map/ppermute | solution.py:33
  30.7 11.3 %collective-permute-start.7 = (bf16[2,256,256]{2,1,0:T(8,128)(2,1)S(1)}, bf16[2,256,256]{2,1,0:T(8,128)(2,1)S(1)}, u32[]{:S(2)}, u32[]{:S(2)}) collective-permute-start(bf16[2,256,256]{2,1,0:T(8,128)(2,1)S(1)} %add_convert_fusion.1.m), channel_id=1, source_target_pairs={{0,2},{3,1},{2,4},{5,3},{4,6},{7,5},{6,8},{9,7},{8,10},{11,9},{10,... | collective-permute-start | bytes 786440 | tf_op jit(solution)/shard_map/ppermute | solution.py:33
  39.9 2.1 %collective-permute-start.10 = (bf16[2,256,256]{2,1,0:T(8,128)(2,1)S(1)}, bf16[2,256,256]{2,1,0:T(8,128)(2,1)S(1)}, u32[]{:S(2)}, u32[]{:S(2)}) collective-permute-start(bf16[2,256,256]{2,1,0:T(8,128)(2,1)S(1)} %collective-permute-done.8.q2), channel_id=1, source_target_pairs={{0,1},{1,0},{2,3},{3,2},{4,5},{5,4},{6,7},{7,6},{8,9},{9,8},{10,11... | collective-permute-start | bytes 786440 | tf_op jit(solution)/shard_map/ppermute | solution.py:24
  42.0 1.5 %collective-permute-start.9 = (bf16[2,256,256]{2,1,0:T(8,128)(2,1)S(1)}, bf16[2,256,256]{2,1,0:T(8,128)(2,1)S(1)}, u32[]{:S(2)}, u32[]{:S(2)}) collective-permute-start(bf16[2,256,256]{2,1,0:T(8,128)(2,1)S(1)} %collective-permute-done.7.q1), channel_id=1, source_target_pairs={{0,1},{1,0},{2,3},{3,2},{4,5},{5,4},{6,7},{7,6},{8,9},{9,8},{10,11... | collective-permute-start | bytes 786440 | tf_op jit(solution)/shard_map/ppermute | solution.py:24
  47.9 1.8 %collective-permute-start.11 = (bf16[2,256,256]{2,1,0:T(8,128)(2,1)S(1)}, bf16[2,256,256]{2,1,0:T(8,128)(2,1)S(1)}, u32[]{:S(2)}, u32[]{:S(2)}) collective-permute-start(bf16[2,256,256]{2,1,0:T(8,128)(2,1)S(1)} %get-tuple-element.49), channel_id=1, source_target_pairs={{0,1},{1,0},{2,3},{3,2},{4,5},{5,4},{6,7},{7,6},{8,9},{9,8},{10,11... | collective-permute-start | bytes 786440 | tf_op jit(solution)/shard_map/ppermute | solution.py:24
  49.8 13.9 %collective-permute-start.12 = (bf16[2,256,256]{2,1,0:T(8,128)(2,1)S(1)}, bf16[2,256,256]{2,1,0:T(8,128)(2,1)S(1)}, u32[]{:S(2)}, u32[]{:S(2)}) collective-permute-start(bf16[2,256,256]{2,1,0:T(8,128)(2,1)S(1)} %pad_maximum_fusion.4), channel_id=1, source_target_pairs={{0,4},{5,1},{2,6},{7,3},{4,8},{9,5},{6,10},{11,7},{8,12},{13,9},{1... | collective-permute-start | bytes 786440 | tf_op jit(solution)/shard_map/ppermute | solution.py:33
  54.4 10.8 %collective-permute-start.13 = (bf16[2,256,256]{2,1,0:T(8,128)(2,1)S(1)}, bf16[2,256,256]{2,1,0:T(8,128)(2,1)S(1)}, u32[]{:S(2)}, u32[]{:S(2)}) collective-permute-start(bf16[2,256,256]{2,1,0:T(8,128)(2,1)S(1)} %pad_maximum_fusion.5), channel_id=1, source_target_pairs={{0,2},{3,1},{2,4},{5,3},{4,6},{7,5},{6,8},{9,7},{8,10},{11,9},{10,... | collective-permute-start | bytes 786440 | tf_op jit(solution)/shard_map/ppermute | solution.py:33
  65.4 1.6 %collective-permute-start.14 = (bf16[2,256,256]{2,1,0:T(8,128)(2,1)S(1)}, bf16[2,256,256]{2,1,0:T(8,128)(2,1)S(1)}, u32[]{:S(2)}, u32[]{:S(2)}) collective-permute-start(bf16[2,256,256]{2,1,0:T(8,128)(2,1)S(1)} %add_convert_fusion.s), channel_id=1, source_target_pairs={{0,1},{1,0},{2,3},{3,2},{4,5},{5,4},{6,7},{7,6},{8,9},{9,8},{10,11... | collective-permute-start | bytes 786440 | tf_op jit(solution)/shard_map/ppermute | solution.py:24
  67.4 14.0 %collective-permute-start.16 = (bf16[2,256,256]{2,1,0:T(8,128)(2,1)S(1)}, bf16[2,256,256]{2,1,0:T(8,128)(2,1)S(1)}, u32[]{:S(2)}, u32[]{:S(2)}) collective-permute-start(bf16[2,256,256]{2,1,0:T(8,128)(2,1)S(1)} %shard_map.108.m), channel_id=1, source_target_pairs={{0,4},{5,1},{2,6},{7,3},{4,8},{9,5},{6,10},{11,7},{8,12},{13,9},{1... | collective-permute-start | bytes 786440 | tf_op jit(solution)/shard_map/ppermute | solution.py:33
  72.0 10.7 %collective-permute-start.15 = (bf16[2,256,256]{2,1,0:T(8,128)(2,1)S(1)}, bf16[2,256,256]{2,1,0:T(8,128)(2,1)S(1)}, u32[]{:S(2)}, u32[]{:S(2)}) collective-permute-start(bf16[2,256,256]{2,1,0:T(8,128)(2,1)S(1)} %shard_map.108.m), channel_id=1, source_target_pairs={{0,2},{3,1},{2,4},{5,3},{4,6},{7,5},{6,8},{9,7},{8,10},{11,9},{10,... | collective-permute-start | bytes 786440 | tf_op jit(solution)/shard_map/ppermute | solution.py:33
  81.4 1.4 %collective-permute-start.18 = (bf16[256,256]{1,0:T(8,128)(2,1)S(1)}, bf16[256,256]{1,0:T(8,128)(2,1)S(1)}, u32[]{:S(2)}, u32[]{:S(2)}) collective-permute-start(bf16[256,256]{1,0:T(8,128)(2,1)S(1)} %slice_bitcast_fusion.2), channel_id=1, source_target_pairs={{0,1},{1,0},{2,3},{3,2},{4,5},{5,4},{6,7},{7,6},{8,9},{9,8},{10,11... | collective-permute-start | bytes 393224 | tf_op jit(solution)/shard_map/ppermute | solution.py:24
  82.8 1.4 %collective-permute-start.17 = (bf16[256,256]{1,0:T(8,128)(2,1)S(1)}, bf16[256,256]{1,0:T(8,128)(2,1)S(1)}, u32[]{:S(2)}, u32[]{:S(2)}) collective-permute-start(bf16[256,256]{1,0:T(8,128)(2,1)S(1)} %slice_bitcast_fusion.3), channel_id=1, source_target_pairs={{0,1},{1,0},{2,3},{3,2},{4,5},{5,4},{6,7},{7,6},{8,9},{9,8},{10,11... | collective-permute-start | bytes 393224 | tf_op jit(solution)/shard_map/ppermute | solution.py:24

commit v11 on v10

--- a/solution.py
+++ b/solution.py
@@ -28,15 +28,15 @@
     count = lax.axis_size("band")
     pairs = []
     for band in range(count - steps):
-        pairs.append((2 * band, 2 * (band + steps)))
-        pairs.append((2 * (band + steps) + 1, 2 * band + 1))
+        low, high = 2 * band, 2 * (band + steps) + 1
+        pairs += [(low, high), (high, low)]
     return lax.ppermute(value, ("band", "mp"), pairs)
 
 
-def place(pm, block, slot, facing):
+def place(pm, block, slot):
     target = pm[slot, block]
     offset = target // OWNER_BLOCKS - lax.axis_index("band")
-    along = jnp.where(lax.axis_index("mp") == 0, offset, -offset) * facing
+    along = jnp.where(lax.axis_index("mp") == 0, offset, -offset)
     along = jnp.clip(along, -REACH, REACH)
     stored = jnp.where(along >= 0, along, REACH - along)
     return stored * OWNER_BLOCKS + target % OWNER_BLOCKS
@@ -130,7 +130,7 @@
             for slot in range(used):
                 part = u[slot * rows : (slot + 1) * rows]
                 sig = sigmoid(part)
-                total[place(pm, block, slot, 1)] += part * sig * live_of(pc, block, slot)
+                total[place(pm, block, slot)] += part * sig * live_of(pc, block, slot)
 
     by_count(pc, slots, body)
     split_slabs(total, own, mine, other)
@@ -179,7 +179,7 @@
     blocks, slots, rows, points = a_ref.shape
     pairs = slots * points
     total[...] = jnp.zeros_like(total)
-    gather_near(near, (m, q1, q2, t1, t2), (0, 0, 0, 1, 1))
+    gather_near(near, (m, q1, q2, t1, t2), (0, 1, 1, 0, 0))
 
     def lat(block, slot):
         at = block * pairs + slot * points
@@ -191,7 +191,7 @@
 
     def forward(block, first, last):
         for slot in range(first, last):
-            chosen = near[place(pm, block, slot, -1)]
+            chosen = near[place(pm, block, slot)]
             y_ref[lat(block, slot)] = dot(a_ref[block, slot], chosen, ROWS_BY_ROWS).astype(BF)
         span = points_of(block)
         z = dot(y_ref[pl.ds(lat(block, first).start, (last - first) * points)], w_ref[...])
@@ -210,7 +210,7 @@
     def backward(block, first, last):
         for slot in range(first, last):
             lift = dot(a_ref[block, slot], dz_ref[lat(block, slot)])
-            total[place(pm, block, slot, 1)] += lift
+            total[place(pm, block, slot)] += lift
 
     def body(used):
         for step in (forward, backward):
@@ -279,7 +279,7 @@
     slots, blocks = pm.shape
     rows = near.shape[1]
     for at, ref in enumerate((m, q1, q2, t1, t2)):
-        half = ref[0] if at < 3 else ref[...]
+        half = ref[...] if at > REACH else ref[min(at, 1)]
         near[at * OWNER_BLOCKS : (at + 1) * OWNER_BLOCKS] = half.reshape(OWNER_BLOCKS, rows, -1)
 
     def body(used):
@@ -288,7 +288,7 @@
             parts = []
             for block in range(first, last):
                 for slot in range(used):
-                    picked = near[place(pm, block, slot, -1)].astype(FL)
+                    picked = near[place(pm, block, slot)].astype(FL)
                     start = (block * used + slot) * rows
                     parts.append((picked * slope_ref[start : start + rows].astype(FL)).astype(BF))
             du = jnp.concatenate(parts, axis=0)
@@ -357,9 +357,9 @@
 def combine(own, parts):
     near, far = parts
     near = near.astype(FL)
-    base = jnp.stack([near[0] + own.astype(FL), near[1]])
+    base = jnp.stack([near[1] + own.astype(FL), near[0]])
     base, far = lax.optimization_barrier((base, far))
-    return (base + far.astype(FL)).astype(BF)
+    return (base + far.astype(FL)[::-1]).astype(BF)
 
 
 def reduce_to_owner(own, mine, other, beside=None):
@@ -492,7 +492,7 @@
     )
     sums, got, (grad_dec, out) = reduce_to_owner(own, mine, other, outer(pair_count, y, dz, out))
     grad_mesh = simple(mesh_grad_kernel, shape_of(*sums.shape))(sums, got, w_dec, w_dec_other)
-    near = spread_from_owner(grad_mesh, lambda part: part[1])
+    near = spread_from_owner(grad_mesh, lambda part: part[0])
     flat = encoder_grad(pair_mesh, pair_count, x_own, x_other, slope, near, grad_dec)
 
     plane, line = plane_groups(lax.axis_size("band"))

time: 140 us -> 141 us (level)
  waiting for transfers between devices: 37.8 us -> 26.8 us
  starting transfers between devices: 28.5 us -> 37.7 us
  blocking collectives: 52.2 us -> 54.8 us
    ppermute x8, waiting for transfers between devices: 29.4 us -> 20 us  [outward(): return lax.ppermute(value, ('band', 'mp'), pairs)]
    ppermute x8, starting transfers between devices: 26.5 us -> 31.9 us  [outward(): return lax.ppermute(value, ('band', 'mp'), pairs)]
    ppermute x11, starting transfers between devices: 1.98 us -> 5.72 us  [swap(): return lax.ppermute(value, 'mp', [(0, 1), (1, 0)])]
    all_to_all x3, blocking collectives: 52.2 us -> 54.8 us  [exchange(): lax.all_to_all(value, 'band', 0, 0, tiled=True, axis_index_groups=groups)]
    ppermute x11, waiting for transfers between devices: 8.45 us -> 6.76 us  [swap(): return lax.ppermute(value, 'mp', [(0, 1), (1, 0)])]
where the time goes in v11:
time: 141 us; the launch traced here: 140 us
  blocking collectives  54.8 us (39%)
  starting transfers between devices  37.7 us (27%)
  waiting for transfers between devices  26.8 us (19%)
  Pallas kernels  19.3 us (14%)
    all_to_all x3, blocking collectives, exchange(): lax.all_to_all(value, 'band', 0, 0, tiled=True, axis_index_groups=groups)  54.8 us
    ppermute x8, starting transfers between devices, outward(): return lax.ppermute(value, ('band', 'mp'), pairs)  31.9 us
    ppermute x8, waiting for transfers between devices, outward(): return lax.ppermute(value, ('band', 'mp'), pairs)  20 us
    ppermute x11, waiting for transfers between devices, swap(): return lax.ppermute(value, 'mp', [(0, 1), (1, 0)])  6.76 us
    ppermute x11, starting transfers between devices, swap(): return lax.ppermute(value, 'mp', [(0, 1), (1, 0)])  5.72 us
    pallas_call x1, Pallas kernels, decode(): held(decode_kernel, [SMEM, SMEM, *[VMEM] * (4 + NEAR)], [shape_of(*grid.s...  4.29 us
    pallas_call x1, Pallas kernels, encode(): held(encode_kernel, [SMEM, SMEM, *[VMEM] * 4], [shape_of(pairs, half), *s...  3.14 us
    pallas_call x1, Pallas kernels, outer(): held(outer_kernel, [SMEM, *[VMEM] * 3], outs, cost=cost)  3 us
  transfers between devices with their start and end apart: 19, of which 14 were waited for; matrix products, arithmetic and copies ran while one was open for 0% of the time, Pallas kernels for 6%

profile of v11, /device:TPU:8, one launch (start us, length us, event | category | flops | bytes accessed | tf_op | source)
XLA Modules:
  0.0 140.5 jit_solution(4987504568349470832)
XLA Ops:
  1.3 2.8 %shard_map.103 = (bf16[10,4,128,128]{3,2,1,0:T(8,128)(2,1)S(1)}, bf16[512,256]{1,0:T(8,128)(2,1)S(1)}, bf16[5120,256]{1,0:T(8,128)(2,1)S(1)}, s32[4,10]{1,0:T(4,128)S(1)}, s32[10]{0:T(128)S(1)}) custom-call(bf16[10,4,128,128]{3,2,1,0:T(8,128)(2,1)} %a_hbm.1, bf16[1280,256]{1,0:T(8,128)(2,1)} %g_ref.1, bf16[512,256]{1,0:T(8,128)(2,1)} %w_hbm.1, ...), custom_call_target="tpu_custom_call" | custom-call | flops 335544320 | bytes 4194304 | tf_op jit(solution)/shard_map/pallas_call | solution.py:404
  4.2 3.1 %shard_map.104 = (bf16[5120,256]{1,0:T(8,128)(2,1)S(1)}, bf16[256,256]{1,0:T(8,128)(2,1)S(1)}, bf16[2,256,256]{2,1,0:T(8,128)(2,1)S(1)}, bf16[2,256,256]{2,1,0:T(8,128)(2,1)S(1)}) custom-call(s32[4,10]{1,0:T(4,128)S(1)} %get-tuple-element.34.pm, s32[10]{0:T(128)S(1)} %get-tuple-element.35.pc, bf16[10,4,128,128]{3,2,1,0:T(8,128)(2,1)S(1)} %get-tuple-element.36.a_ref, ...), custom_call_target="tpu_custom_call" | custom-call | tf_op jit(solution)/shard_map/pallas_call | solution.py:418
  7.8 1.1 collective-permute-done.3
  9.0 4.2 %collective-permute-start.5 = (bf16[2,256,256]{2,1,0:T(8,128)(2,1)S(1)}, bf16[2,256,256]{2,1,0:T(8,128)(2,1)S(1)}, u32[]{:S(2)}, u32[]{:S(2)}) collective-permute-start(bf16[2,256,256]{2,1,0:T(8,128)(2,1)S(1)} %pad_maximum_fusion.3), channel_id=1, source_target_pairs={{0,5},{5,0},{2,7},{7,2},{4,9},{9,4},{6,11},{11,6},{8,13},{13,8},{1... | collective-permute-start | bytes 786440 | tf_op jit(solution)/shard_map/ppermute | solution.py:33
  13.3 3.7 %collective-permute-start.4 = (bf16[2,256,256]{2,1,0:T(8,128)(2,1)S(1)}, bf16[2,256,256]{2,1,0:T(8,128)(2,1)S(1)}, u32[]{:S(2)}, u32[]{:S(2)}) collective-permute-start(bf16[2,256,256]{2,1,0:T(8,128)(2,1)S(1)} %pad_maximum_fusion.2), channel_id=1, source_target_pairs={{0,3},{3,0},{2,5},{5,2},{4,7},{7,4},{6,9},{9,6},{8,11},{11,8},{10,... | collective-permute-start | bytes 786440 | tf_op jit(solution)/shard_map/ppermute | solution.py:33
  17.0 2.5 %shard_map.105.slope_ref = bf16[5120,256]{1,0:T(8,128)(2,1)S(1)} custom-call(s32[10]{0:T(128)S(1)} %get-tuple-element.35.pc, bf16[512,256]{1,0:T(8,128)(2,1)S(1)} %get-tuple-element.38.w_ref, bf16[5120,256]{1,0:T(8,128)(2,1)S(1)} %get-tuple-element.39.x_own, bf16[5120,256]{1,0:T(8,128)(2,1)S(1)} %get-tuple-element.44.x_other), custom_call_target="tpu_custom_call" | custom-call | flops 1342177280 | bytes 7864320 | tf_op jit(solution)/shard_map/pallas_call | solution.py:431
  19.5 2.7 %collective-permute-done.5 = bf16[2,256,256]{2,1,0:T(8,128)(2,1)S(1)} collective-permute-done((bf16[2,256,256]{2,1,0:T(8,128)(2,1)S(1)}, bf16[2,256,256]{2,1,0:T(8,128)(2,1)S(1)}, u32[]{:S(2)}, u32[]{:S(2)}) %collective-permute-start.5) | collective-permute-done | bytes 262176 | tf_op jit(solution)/shard_map/ppermute | solution.py:33
  22.2 1.3 collective-permute-done.4
  23.8 1.0 collective-permute-start.6
  24.8 1.2 collective-permute-done.6
  26.1 4.8 %collective-permute-start.8 = (bf16[2,256,256]{2,1,0:T(8,128)(2,1)S(1)}, bf16[2,256,256]{2,1,0:T(8,128)(2,1)S(1)}, u32[]{:S(2)}, u32[]{:S(2)}) collective-permute-start(bf16[2,256,256]{2,1,0:T(8,128)(2,1)S(1)} %add_convert_fusion.1.m), channel_id=1, source_target_pairs={{0,5},{5,0},{2,7},{7,2},{4,9},{9,4},{6,11},{11,6},{8,13},{13,8},{1... | collective-permute-start | bytes 786440 | tf_op jit(solution)/shard_map/ppermute | solution.py:33
  30.9 1.9 %collective-permute-start.7 = (bf16[2,256,256]{2,1,0:T(8,128)(2,1)S(1)}, bf16[2,256,256]{2,1,0:T(8,128)(2,1)S(1)}, u32[]{:S(2)}, u32[]{:S(2)}) collective-permute-start(bf16[2,256,256]{2,1,0:T(8,128)(2,1)S(1)} %add_convert_fusion.1.m), channel_id=1, source_target_pairs={{0,3},{3,0},{2,5},{5,2},{4,7},{7,4},{6,9},{9,6},{8,11},{11,8},{10,... | collective-permute-start | bytes 786440 | tf_op jit(solution)/shard_map/ppermute | solution.py:33
  32.8 6.8 %collective-permute-done.8.q2 = bf16[2,256,256]{2,1,0:T(8,128)(2,1)S(1)} collective-permute-done((bf16[2,256,256]{2,1,0:T(8,128)(2,1)S(1)}, bf16[2,256,256]{2,1,0:T(8,128)(2,1)S(1)}, u32[]{:S(2)}, u32[]{:S(2)}) %collective-permute-start.8) | collective-permute-done | bytes 262176 | tf_op jit(solution)/shard_map/ppermute | solution.py:33
  40.4 0.9 collective-permute-start.9
  41.3 1.2 collective-permute-done.9.t1
  42.5 4.3 %shard_map.106 = (f32[1280,256]{1,0:T(8,128)S(1)}, bf16[5120,512]{1,0:T(8,128)(2,1)S(1)}, bf16[5120,256]{1,0:T(8,128)(2,1)S(1)}, bf16[256,256]{1,0:T(8,128)(2,1)...) custom-call(s32[4,10]{1,0:T(4,128)S(1)} %get-tuple-element.34.pm, s32[10]{0:T(128)S(1)} %get-tuple-element.35.pc, ...), custom_call_target="tpu_custom_call" | custom-call | tf_op jit(solution)/shard_map/pallas_call | solution.py:440
  47.5 1.1 collective-permute-done.11
  48.7 5.1 %collective-permute-start.12 = (bf16[2,256,256]{2,1,0:T(8,128)(2,1)S(1)}, bf16[2,256,256]{2,1,0:T(8,128)(2,1)S(1)}, u32[]{:S(2)}, u32[]{:S(2)}) collective-permute-start(bf16[2,256,256]{2,1,0:T(8,128)(2,1)S(1)} %pad_maximum_fusion.4), channel_id=1, source_target_pairs={{0,5},{5,0},{2,7},{7,2},{4,9},{9,4},{6,11},{11,6},{8,13},{13,8},{1... | collective-permute-start | bytes 786440 | tf_op jit(solution)/shard_map/ppermute | solution.py:33
  53.9 5.2 %collective-permute-start.13 = (bf16[2,256,256]{2,1,0:T(8,128)(2,1)S(1)}, bf16[2,256,256]{2,1,0:T(8,128)(2,1)S(1)}, u32[]{:S(2)}, u32[]{:S(2)}) collective-permute-start(bf16[2,256,256]{2,1,0:T(8,128)(2,1)S(1)} %pad_maximum_fusion.5), channel_id=1, source_target_pairs={{0,3},{3,0},{2,5},{5,2},{4,7},{7,4},{6,9},{9,6},{8,11},{11,8},{10,... | collective-permute-start | bytes 786440 | tf_op jit(solution)/shard_map/ppermute | solution.py:33
  59.1 3.0 %shard_map.107 = (f32[256,512]{1,0:T(8,128)S(1)}, bf16[1280,256]{1,0:T(8,128)(2,1)}) custom-call(s32[10]{0:T(128)S(1)} %get-tuple-element.35.pc, bf16[5120,512]{1,0:T(8,128)(2,1)S(1)} %get-tuple-element.50.left_ref, bf16[5120,256]{1,0:T(8,128)(2,1)S(1)} %get-tuple-element.51.right_ref, f32[1280,256]{1,0:T(8,128)S(1)} %get-tuple-element.52.made_ref), custom_call_target="tpu_custom_call" | custom-call | flops 1342177280 | bytes 7864320 | tf_op jit(solution)/shard_map/pallas_call | solution.py:461
  63.6 0.9 collective-permute-start.14
  64.5 1.2 collective-permute-done.14.t
  66.1 5.0 %collective-permute-start.16 = (bf16[2,256,256]{2,1,0:T(8,128)(2,1)S(1)}, bf16[2,256,256]{2,1,0:T(8,128)(2,1)S(1)}, u32[]{:S(2)}, u32[]{:S(2)}) collective-permute-start(bf16[2,256,256]{2,1,0:T(8,128)(2,1)S(1)} %shard_map.108.m), channel_id=1, source_target_pairs={{0,5},{5,0},{2,7},{7,2},{4,9},{9,4},{6,11},{11,6},{8,13},{13,8},{1... | collective-permute-start | bytes 786440 | tf_op jit(solution)/shard_map/ppermute | solution.py:33
  71.1 2.0 %collective-permute-start.15 = (bf16[2,256,256]{2,1,0:T(8,128)(2,1)S(1)}, bf16[2,256,256]{2,1,0:T(8,128)(2,1)S(1)}, u32[]{:S(2)}, u32[]{:S(2)}) collective-permute-start(bf16[2,256,256]{2,1,0:T(8,128)(2,1)S(1)} %shard_map.108.m), channel_id=1, source_target_pairs={{0,3},{3,0},{2,5},{5,2},{4,7},{7,4},{6,9},{9,6},{8,11},{11,8},{10,... | collective-permute-start | bytes 786440 | tf_op jit(solution)/shard_map/ppermute | solution.py:33
  73.1 6.7 %collective-permute-done.16.q2 = bf16[2,256,256]{2,1,0:T(8,128)(2,1)S(1)} collective-permute-done((bf16[2,256,256]{2,1,0:T(8,128)(2,1)S(1)}, bf16[2,256,256]{2,1,0:T(8,128)(2,1)S(1)}, u32[]{:S(2)}, u32[]{:S(2)}) %collective-permute-start.16) | collective-permute-done | bytes 262176 | tf_op jit(solution)/shard_map/ppermute | solution.py:33
  80.4 1.0 collective-permute-start.17
  81.4 1.0 collective-permute-done.17.t1
  82.4 2.0 %shard_map.109 = bf16[2048,128]{1,0:T(8,128)(2,1)S(1)} custom-call(s32[4,10]{1,0:T(4,128)S(1)} %get-tuple-element.34.pm, s32[10]{0:T(128)S(1)} %get-tuple-element.35.pc, bf16[5120,256]{1,0:T(8,128)(2,1)S(1)} %get-tuple-element.39.x_own, bf16[5120,256]{1,0:T(8,128)(2,1)S(1)} %get-tuple-element.44.x_other, bf16[5120,256]{1,0:T(8,128)(2,1)S(1)} %shard_map.105.slope_ref, ...), custom_call_target="tpu_custom_call" | custom-call | tf_op jit(solution)/shard_map/pallas_call | solution.py:467
  84.4 22.3 %all_to_all.15.parts_ref = bf16[16,128,128]{2,1,0:T(8,128)(2,1)S(1)} all-to-all(bf16[16,128,128]{2,1,0:T(8,128)(2,1)S(1)} %bitcast.25), channel_id=1, replica_groups={{0,2,4,6,8,10,12,14,16,18,20,22,24,26,28,30},{32,34,36,38,40,42,44,46,4..., dimensions={0} | all-to-all | bytes 1048576 | tf_op jit(solution)/shard_map/all_to_all | solution.py:342
  106.8 18.6 %all_to_all.16.parts_ref = bf16[8,128,128]{2,1,0:T(8,128)(2,1)S(1)} all-to-all(bf16[8,128,128]{2,1,0:T(8,128)(2,1)S(1)} %shard_map.110), channel_id=1, replica_groups={{0,32,64,96,128,160,192,224},{2,34,66,98,130,162,194,226},{4,36,68,100,..., dimensions={0} | all-to-all | bytes 524288 | tf_op jit(solution)/shard_map/all_to_all | solution.py:342
  125.4 13.9 %all_to_all.17 = bf16[16,128,128]{2,1,0:T(8,128)(2,1)S(1)} all-to-all(bf16[16,128,128]{2,1,0:T(8,128)(2,1)S(1)} %shard_map.111), channel_id=1, replica_groups={{0,2,4,6,8,10,12,14,16,18,20,22,24,26,28,30},{32,34,36,38,40,42,44,46,4..., dimensions={0} | all-to-all | bytes 1048576 | tf_op jit(solution)/shard_map/all_to_all | solution.py:342
  139.4 1.1 shard_map.112
  (51 shorter events, 5.8 us)
Async XLA Ops:
  0.6 3.5 %collective-permute-start = (bf16[1280,256]{1,0:T(8,128)(2,1)}, bf16[1280,256]{1,0:T(8,128)(2,1)S(1)}, u32[]{:S(2)}, u32[]{:S(2)}) collective-permute-start(bf16[1280,256]{1,0:T(8,128)(2,1)} %g_ref.1), channel_id=1, source_target_pairs={{0,1},{1,0},{2,3},{3,2},{4,5},{5,4},{6,7},{7,6},{8,9},{9,8},{10,11... | collective-permute-start | bytes 1966088 | tf_op jit(solution)/shard_map/ppermute | solution.py:24
  0.7 3.4 %collective-permute-start.2 = (bf16[512,256]{1,0:T(8,128)(2,1)}, bf16[512,256]{1,0:T(8,128)(2,1)S(1)}, u32[]{:S(2)}, u32[]{:S(2)}) collective-permute-start(bf16[512,256]{1,0:T(8,128)(2,1)} %w_own.1), channel_id=1, source_target_pairs={{0,1},{1,0},{2,3},{3,2},{4,5},{5,4},{6,7},{7,6},{8,9},{9,8},{10,11... | collective-permute-start | bytes 786440 | tf_op jit(solution)/shard_map/ppermute | solution.py:24
  1.2 2.9 %collective-permute-start.1 = (bf16[256,256]{1,0:T(8,128)(2,1)}, bf16[256,256]{1,0:T(8,128)(2,1)S(1)}, u32[]{:S(2)}, u32[]{:S(2)}) collective-permute-start(bf16[256,256]{1,0:T(8,128)(2,1)} %param.10), channel_id=1, source_target_pairs={{0,1},{1,0},{2,3},{3,2},{4,5},{5,4},{6,7},{7,6},{8,9},{9,8},{10,11... | collective-permute-start | bytes 393224 | tf_op jit(solution)/shard_map/ppermute | solution.py:24
  7.3 1.7 %collective-permute-start.3 = (bf16[2,256,256]{2,1,0:T(8,128)(2,1)S(1)}, bf16[2,256,256]{2,1,0:T(8,128)(2,1)S(1)}, u32[]{:S(2)}, u32[]{:S(2)}) collective-permute-start(bf16[2,256,256]{2,1,0:T(8,128)(2,1)S(1)} %get-tuple-element.42), channel_id=1, source_target_pairs={{0,1},{1,0},{2,3},{3,2},{4,5},{5,4},{6,7},{7,6},{8,9},{9,8},{10,11... | collective-permute-start | bytes 786440 | tf_op jit(solution)/shard_map/ppermute | solution.py:24
  9.0 13.2 %collective-permute-start.5 = (bf16[2,256,256]{2,1,0:T(8,128)(2,1)S(1)}, bf16[2,256,256]{2,1,0:T(8,128)(2,1)S(1)}, u32[]{:S(2)}, u32[]{:S(2)}) collective-permute-start(bf16[2,256,256]{2,1,0:T(8,128)(2,1)S(1)} %pad_maximum_fusion.3), channel_id=1, source_target_pairs={{0,5},{5,0},{2,7},{7,2},{4,9},{9,4},{6,11},{11,6},{8,13},{13,8},{1... | collective-permute-start | bytes 786440 | tf_op jit(solution)/shard_map/ppermute | solution.py:33
  13.3 10.2 %collective-permute-start.4 = (bf16[2,256,256]{2,1,0:T(8,128)(2,1)S(1)}, bf16[2,256,256]{2,1,0:T(8,128)(2,1)S(1)}, u32[]{:S(2)}, u32[]{:S(2)}) collective-permute-start(bf16[2,256,256]{2,1,0:T(8,128)(2,1)S(1)} %pad_maximum_fusion.2), channel_id=1, source_target_pairs={{0,3},{3,0},{2,5},{5,2},{4,7},{7,4},{6,9},{9,6},{8,11},{11,8},{10,... | collective-permute-start | bytes 786440 | tf_op jit(solution)/shard_map/ppermute | solution.py:33
  23.5 2.5 %copy-start.3 = (bf16[256,256]{1,0:T(8,128)(2,1)S(1)}, bf16[256,256]{1,0:T(8,128)(2,1)}, u32[]{:S(2)}) copy-start(bf16[256,256]{1,0:T(8,128)(2,1)} %param.10) | copy-start | bytes 393220
  23.6 18.9 %copy-start = (bf16[1280,256]{1,0:T(8,128)(2,1)S(1)}, bf16[1280,256]{1,0:T(8,128)(2,1)}, u32[]{:S(2)}) copy-start(bf16[1280,256]{1,0:T(8,128)(2,1)} %g_ref.1) | copy-start | bytes 1966084
  23.6 18.9 %copy-start.1 = (bf16[512,256]{1,0:T(8,128)(2,1)S(1)}, bf16[512,256]{1,0:T(8,128)(2,1)}, u32[]{:S(2)}) copy-start(bf16[512,256]{1,0:T(8,128)(2,1)} %w_own.1) | copy-start | bytes 786436
  23.6 18.8 %copy-start.2 = (bf16[1280,256]{1,0:T(8,128)(2,1)S(1)}, bf16[1280,256]{1,0:T(8,128)(2,1)}, u32[]{:S(2)}) copy-start(bf16[1280,256]{1,0:T(8,128)(2,1)} %cot_ref.1) | copy-start | bytes 1966084
  23.8 2.1 %collective-permute-start.6 = (bf16[2,256,256]{2,1,0:T(8,128)(2,1)S(1)}, bf16[2,256,256]{2,1,0:T(8,128)(2,1)S(1)}, u32[]{:S(2)}, u32[]{:S(2)}) collective-permute-start(bf16[2,256,256]{2,1,0:T(8,128)(2,1)S(1)} %add_convert_fusion.2), channel_id=1, source_target_pairs={{0,1},{1,0},{2,3},{3,2},{4,5},{5,4},{6,7},{7,6},{8,9},{9,8},{10,11... | collective-permute-start | bytes 786440 | tf_op jit(solution)/shard_map/ppermute | solution.py:24
  26.1 13.5 %collective-permute-start.8 = (bf16[2,256,256]{2,1,0:T(8,128)(2,1)S(1)}, bf16[2,256,256]{2,1,0:T(8,128)(2,1)S(1)}, u32[]{:S(2)}, u32[]{:S(2)}) collective-permute-start(bf16[2,256,256]{2,1,0:T(8,128)(2,1)S(1)} %add_convert_fusion.1.m), channel_id=1, source_target_pairs={{0,5},{5,0},{2,7},{7,2},{4,9},{9,4},{6,11},{11,6},{8,13},{13,8},{1... | collective-permute-start | bytes 786440 | tf_op jit(solution)/shard_map/ppermute | solution.py:33
  30.9 9.5 %collective-permute-start.7 = (bf16[2,256,256]{2,1,0:T(8,128)(2,1)S(1)}, bf16[2,256,256]{2,1,0:T(8,128)(2,1)S(1)}, u32[]{:S(2)}, u32[]{:S(2)}) collective-permute-start(bf16[2,256,256]{2,1,0:T(8,128)(2,1)S(1)} %add_convert_fusion.1.m), channel_id=1, source_target_pairs={{0,3},{3,0},{2,5},{5,2},{4,7},{7,4},{6,9},{9,6},{8,11},{11,8},{10,... | collective-permute-start | bytes 786440 | tf_op jit(solution)/shard_map/ppermute | solution.py:33
  39.6 1.7 %collective-permute-start.10 = (bf16[2,256,256]{2,1,0:T(8,128)(2,1)S(1)}, bf16[2,256,256]{2,1,0:T(8,128)(2,1)S(1)}, u32[]{:S(2)}, u32[]{:S(2)}) collective-permute-start(bf16[2,256,256]{2,1,0:T(8,128)(2,1)S(1)} %collective-permute-done.8.q2), channel_id=1, source_target_pairs={{0,1},{1,0},{2,3},{3,2},{4,5},{5,4},{6,7},{7,6},{8,9},{9,8},{10,11... | collective-permute-start | bytes 786440 | tf_op jit(solution)/shard_map/ppermute | solution.py:24
  40.4 2.0 %collective-permute-start.9 = (bf16[2,256,256]{2,1,0:T(8,128)(2,1)S(1)}, bf16[2,256,256]{2,1,0:T(8,128)(2,1)S(1)}, u32[]{:S(2)}, u32[]{:S(2)}) collective-permute-start(bf16[2,256,256]{2,1,0:T(8,128)(2,1)S(1)} %collective-permute-done.7.q1), channel_id=1, source_target_pairs={{0,1},{1,0},{2,3},{3,2},{4,5},{5,4},{6,7},{7,6},{8,9},{9,8},{10,11... | collective-permute-start | bytes 786440 | tf_op jit(solution)/shard_map/ppermute | solution.py:24
  46.8 1.9 %collective-permute-start.11 = (bf16[2,256,256]{2,1,0:T(8,128)(2,1)S(1)}, bf16[2,256,256]{2,1,0:T(8,128)(2,1)S(1)}, u32[]{:S(2)}, u32[]{:S(2)}) collective-permute-start(bf16[2,256,256]{2,1,0:T(8,128)(2,1)S(1)} %get-tuple-element.49), channel_id=1, source_target_pairs={{0,1},{1,0},{2,3},{3,2},{4,5},{5,4},{6,7},{7,6},{8,9},{9,8},{10,11... | collective-permute-start | bytes 786440 | tf_op jit(solution)/shard_map/ppermute | solution.py:24
  48.7 13.8 %collective-permute-start.12 = (bf16[2,256,256]{2,1,0:T(8,128)(2,1)S(1)}, bf16[2,256,256]{2,1,0:T(8,128)(2,1)S(1)}, u32[]{:S(2)}, u32[]{:S(2)}) collective-permute-start(bf16[2,256,256]{2,1,0:T(8,128)(2,1)S(1)} %pad_maximum_fusion.4), channel_id=1, source_target_pairs={{0,5},{5,0},{2,7},{7,2},{4,9},{9,4},{6,11},{11,6},{8,13},{13,8},{1... | collective-permute-start | bytes 786440 | tf_op jit(solution)/shard_map/ppermute | solution.py:33
  53.9 9.5 %collective-permute-start.13 = (bf16[2,256,256]{2,1,0:T(8,128)(2,1)S(1)}, bf16[2,256,256]{2,1,0:T(8,128)(2,1)S(1)}, u32[]{:S(2)}, u32[]{:S(2)}) collective-permute-start(bf16[2,256,256]{2,1,0:T(8,128)(2,1)S(1)} %pad_maximum_fusion.5), channel_id=1, source_target_pairs={{0,3},{3,0},{2,5},{5,2},{4,7},{7,4},{6,9},{9,6},{8,11},{11,8},{10,... | collective-permute-start | bytes 786440 | tf_op jit(solution)/shard_map/ppermute | solution.py:33
  63.6 2.1 %collective-permute-start.14 = (bf16[2,256,256]{2,1,0:T(8,128)(2,1)S(1)}, bf16[2,256,256]{2,1,0:T(8,128)(2,1)S(1)}, u32[]{:S(2)}, u32[]{:S(2)}) collective-permute-start(bf16[2,256,256]{2,1,0:T(8,128)(2,1)S(1)} %add_convert_fusion.s), channel_id=1, source_target_pairs={{0,1},{1,0},{2,3},{3,2},{4,5},{5,4},{6,7},{7,6},{8,9},{9,8},{10,11... | collective-permute-start | bytes 786440 | tf_op jit(solution)/shard_map/ppermute | solution.py:24
  66.1 13.8 %collective-permute-start.16 = (bf16[2,256,256]{2,1,0:T(8,128)(2,1)S(1)}, bf16[2,256,256]{2,1,0:T(8,128)(2,1)S(1)}, u32[]{:S(2)}, u32[]{:S(2)}) collective-permute-start(bf16[2,256,256]{2,1,0:T(8,128)(2,1)S(1)} %shard_map.108.m), channel_id=1, source_target_pairs={{0,5},{5,0},{2,7},{7,2},{4,9},{9,4},{6,11},{11,6},{8,13},{13,8},{1... | collective-permute-start | bytes 786440 | tf_op jit(solution)/shard_map/ppermute | solution.py:33
  71.1 9.3 %collective-permute-start.15 = (bf16[2,256,256]{2,1,0:T(8,128)(2,1)S(1)}, bf16[2,256,256]{2,1,0:T(8,128)(2,1)S(1)}, u32[]{:S(2)}, u32[]{:S(2)}) collective-permute-start(bf16[2,256,256]{2,1,0:T(8,128)(2,1)S(1)} %shard_map.108.m), channel_id=1, source_target_pairs={{0,3},{3,0},{2,5},{5,2},{4,7},{7,4},{6,9},{9,6},{8,11},{11,8},{10,... | collective-permute-start | bytes 786440 | tf_op jit(solution)/shard_map/ppermute | solution.py:33
  79.8 1.6 %collective-permute-start.18 = (bf16[256,256]{1,0:T(8,128)(2,1)S(1)}, bf16[256,256]{1,0:T(8,128)(2,1)S(1)}, u32[]{:S(2)}, u32[]{:S(2)}) collective-permute-start(bf16[256,256]{1,0:T(8,128)(2,1)S(1)} %slice_bitcast_fusion.2), channel_id=1, source_target_pairs={{0,1},{1,0},{2,3},{3,2},{4,5},{5,4},{6,7},{7,6},{8,9},{9,8},{10,11... | collective-permute-start | bytes 393224 | tf_op jit(solution)/shard_map/ppermute | solution.py:24
  80.4 2.0 %collective-permute-start.17 = (bf16[256,256]{1,0:T(8,128)(2,1)S(1)}, bf16[256,256]{1,0:T(8,128)(2,1)S(1)}, u32[]{:S(2)}, u32[]{:S(2)}) collective-permute-start(bf16[256,256]{1,0:T(8,128)(2,1)S(1)} %slice_bitcast_fusion.3), channel_id=1, source_target_pairs={{0,1},{1,0},{2,3},{3,2},{4,5},{5,4},{6,7},{7,6},{8,9},{9,8},{10,11... | collective-permute-start | bytes 393224 | tf_op jit(solution)/shard_map/ppermute | solution.py:24
